TPU v7x, 256 devices: a whole 4x4x8 slice. The times are simulated.
256 devices in a mesh: section: 8 (over y, core), expert: 32 (over x, z).
Axes of the slice: x: 4, y: 4, z: 8, core: 2. Of those that a mesh axis runs over, the one named last changes fastest.
Arguments:
- inputs: bfloat16 [8, 512, 768], P('section', None, 'expert'), may hold values from -6 to 6
- routes: int32 [2, 8, 8, 512, 2], P(None, 'section'), may hold values from 0 to 31, all different within a row; in each aligned block of 512 rows (0 to 511, 512 to 1023, ..., all dimensions but the last counted through in order) at most 48 rows name the same one
- norm_gains: bfloat16 [2, 8, 768], P(None, 'section'), may hold values from 0.25 to 1.75
- routers: bfloat16 [2, 8, 32, 768], P(None, 'section', 'expert'), may hold values from -0.21875 to 0.21875
- expert_in: bfloat16 [2, 8, 32, 1536, 768], P(None, 'section', 'expert'), may hold values from -0.21875 to 0.21875
- expert_out: bfloat16 [2, 8, 32, 1536, 768], P(None, 'section', 'expert'), may hold values from -0.15625 to 0.15625
Outputs:
- outputs: bfloat16 [8, 512, 768], P('section', None, 'expert')
Inputs may be any that keep to these rules, and one draw needn't show every extreme that they name: `routes`: in each layer and micro-batch no expert is named by more than 48 tokens; a token's two ids differ.
All inputs are finite; a program needn't handle non-finite values.
Results may differ from a plain program's by a relative error of at most 0.034.
Values may be sent and summed in bfloat16 or wider, within the bound.
No kernel may reach another device: no remote copies, remote signals or barrier semaphores. Data moves between devices by JAX's collectives and lax.ppermute only.
A program may use at most 64 MiB of HBM per device.

v0:
```python
import jax
import jax.numpy as jnp
from jax import lax
from jax.sharding import PartitionSpec as P


def passed_along(value, axis, steps):
    count = lax.axis_size(axis)
    pairs = [(source, (source + steps) % count) for source in range(count)]
    return lax.ppermute(value, axis, pairs)


def from_behind(block, axis, distance):
    devices = range(lax.axis_size(axis))
    route = [(i - distance, i) for i in devices if i - distance in devices]
    return lax.ppermute(block, axis, route)


def place_rows(chosen, experts, capacity):
    flat_ids = chosen.reshape(-1)
    onehot = (flat_ids[:, None] == jnp.arange(experts, dtype=jnp.int32)[None, :]).astype(jnp.int32)
    rank_table = jnp.cumsum(onehot, axis=0) - 1
    slot_ids = jnp.sum(rank_table * onehot, axis=1)
    owners = jnp.arange(flat_ids.shape[0], dtype=jnp.int32) // 2
    slot_table = (
        jnp.full((experts * capacity,), -1, jnp.int32)
        .at[flat_ids * capacity + slot_ids]
        .set(owners)
    )
    return (slot_table.reshape(experts, capacity), flat_ids, slot_ids)


def combine(current, returned, gate_grid, flat_ids, slot_ids, experts):
    flat_index = slot_ids * experts + flat_ids
    picked_vals = returned.reshape(-1, returned.shape[2])[flat_index].astype(jnp.float32)
    weights = gate_grid.reshape(-1)[flat_index].astype(jnp.float32)
    branch_sum = picked_vals.reshape(-1, 2, picked_vals.shape[1]).sum(axis=1)
    gate_sum = weights.reshape(-1, 2).sum(axis=1)
    return (current.astype(jnp.float32) + branch_sum / gate_sum[:, None]).astype(jnp.bfloat16)


def expert_block(row_block, gain_row, column, weight_in, weight_out):
    widened = row_block.astype(jnp.float32)
    mean_square = jnp.mean(widened * widened, axis=1, keepdims=True)
    normed = (widened * lax.rsqrt(mean_square + 1e-06) * gain_row.astype(jnp.float32)).astype(
        jnp.bfloat16
    )
    pre_act = lax.dot_general(
        normed, weight_in, (((1,), (1,)), ((), ())), preferred_element_type=jnp.float32
    )
    active = jax.nn.gelu(pre_act).astype(jnp.bfloat16)
    output = jnp.dot(active, weight_out, preferred_element_type=jnp.float32)
    logit_value = jnp.dot(normed, column, preferred_element_type=jnp.float32)
    gate_value = jax.nn.sigmoid(logit_value).astype(jnp.bfloat16)
    weighted = (output * gate_value.astype(jnp.float32)[:, None]).astype(jnp.bfloat16)
    return (weighted, gate_value)


def mix_layer(current, chosen, gain_row, column, weight_in, weight_out, groups, capacity):
    slot_table, flat_ids, slot_ids = place_rows(chosen, groups, capacity)
    by_slot = jnp.transpose(slot_table, (1, 0))
    picked = jnp.take(current, jnp.maximum(by_slot, 0), axis=0)
    picked = jnp.where((by_slot >= 0)[:, :, None], picked, jnp.zeros_like(picked))
    received = lax.all_to_all(picked, "expert", split_axis=1, concat_axis=1, tiled=True)
    row_block = received.reshape(received.shape[0], -1)
    row_count = row_block.shape[0]
    weighted, gate_value = expert_block(row_block, gain_row, column, weight_in, weight_out)
    spread = weighted.reshape(row_count, groups, -1)
    gate_wide = jnp.broadcast_to(gate_value[:, None], (row_count, groups))
    spread, gate_wide = (spread, gate_wide)
    returned = lax.all_to_all(spread, "expert", split_axis=1, concat_axis=1, tiled=True)
    gate_grid = lax.all_to_all(gate_wide, "expert", split_axis=1, concat_axis=1, tiled=True)
    return combine(current, returned, gate_grid, flat_ids, slot_ids, groups)


def local(inputs, routes, norm_gains, routers, expert_in, expert_out):
    sections = lax.axis_size("section")
    groups = lax.axis_size("expert")
    section_pos = lax.axis_index("section")
    tokens = inputs.shape[1]
    capacity = 3 * tokens // groups
    repeats = expert_in.shape[0]
    total_steps = sections * (repeats + 1) - 1
    last_layer = sections * repeats - 1
    first_slot = inputs[0]
    buffer = first_slot
    carried = jnp.zeros_like(first_slot)

    def advance(step_id, loop_state):
        carried, buffer = loop_state
        position = step_id - jnp.mod(step_id - section_pos, sections)
        micro_id = jnp.clip(step_id - position, 0, sections - 1)
        repeat_id = jnp.clip(position // sections, 0, repeats - 1)
        incoming = buffer
        current = jnp.where((section_pos == 0) & (step_id < sections), incoming, carried)
        chosen = routes[repeat_id, 0, micro_id]
        updated = mix_layer(
            current,
            chosen,
            norm_gains[repeat_id, 0],
            routers[repeat_id, 0, 0],
            expert_in[repeat_id, 0, 0],
            expert_out[repeat_id, 0, 0],
            groups,
            capacity,
        )
        carried = passed_along(updated, "section", 1)
        finished = (section_pos == sections - 1) & (position == last_layer)
        shifted = from_behind(buffer, "section", -1)
        buffer = jnp.where(finished, updated, shifted)
        return (carried, buffer)

    carried, buffer = lax.fori_loop(0, total_steps, advance, (carried, buffer))
    result = buffer[None]
    return result


def solution(mesh):
    return jax.shard_map(
        local,
        mesh=mesh,
        in_specs=(
            P("section", None, "expert"),
            P(None, "section", None, None, None),
            P(None, "section", None),
            P(None, "section", "expert", None),
            P(None, "section", "expert", None, None),
            P(None, "section", "expert", None, None),
        ),
        out_specs=P("section", None, "expert"),
        check_vma=False,
    )
```

profile of v0, /device:TPU:8, one launch (start us, length us, event | category | flops | bytes accessed | tf_op | source)
XLA Modules:
  0.0 1789.1 jit_solution(16144247728431451255)
XLA Ops:
  0.9 1787.5 %while.18 = (s32[]{:T(128)}, bf16[512,24]{1,0:T(8,128)(2,1)S(1)}, bf16[512,24]{1,0:T(8,128)(2,1)S(1)}, pred[]{:T(512)}, s32[]{:T(128)}, /*index=5*/s32[2,1,8,512...) while((s32[]{:T(128)}, bf16[512,24]{1,0:T(8,128)(2,1)S(1)}, ...), condition=%wide.region_8.9_spmd, body=%wide.region_0.8_spmd.sunk | while | flops 232165408 | bytes 8677082 | solution.py:113
  2.4 9.0 reduce-window.24
  21.3 11.3 all-to-all-start
  34.7 8.0 all-to-all-done
  83.3 9.0 reduce-window.24
  111.3 8.1 all-to-all-done
  159.9 9.0 reduce-window.24
  187.9 8.1 all-to-all-done
  236.6 9.0 reduce-window.24
  264.6 8.1 all-to-all-done
  313.3 9.0 reduce-window.24
  341.5 8.0 all-to-all-done
  390.0 9.0 reduce-window.24
  467.1 9.0 reduce-window.24
  544.9 9.0 reduce-window.24
  563.8 7.9 all-to-all-start
  622.7 9.0 reduce-window.24
  641.6 7.9 all-to-all-start
  700.5 9.0 reduce-window.24
  778.3 9.0 reduce-window.24
  856.1 9.0 reduce-window.24
  933.9 9.0 reduce-window.24
  1011.7 9.0 reduce-window.24
  1089.5 9.0 reduce-window.24
  1167.3 9.0 reduce-window.24
  1245.1 9.0 reduce-window.24
  1323.0 9.0 reduce-window.24
  1400.8 9.0 reduce-window.24
  1478.6 9.0 reduce-window.24
  1556.4 9.0 reduce-window.24
  1634.2 9.0 reduce-window.24
  1712.0 9.0 reduce-window.24
  (1490 shorter events, 1506.8 us)
Async XLA Ops:
  21.3 21.4 %all-to-all-start = ((bf16[32,2,576]{2,1,0:T(2,128)(2,1)}), bf16[32,2,576]{2,1,0:T(2,128)(2,1)S(1)}, u32[]{:S(2)}, u32[]{:S(2)}) async-start(bf16[32,2,576]{2,1,0:T(2,128)(2,1)} %reshape.348), calls=%async_computation | async-start | bytes 163840 | tf_op jit(solution)/shard_map/while/body/eval_jaxpr/all_to_all | solution.py:64
  32.6 44.7 %collective-permute-start = (bf16[512,24]{1,0:T(8,128)(2,1)S(1)}, bf16[512,24]{1,0:T(8,128)(2,1)S(1)}, u32[]{:S(2)}, u32[]{:S(2)}) collective-permute-start(bf16[512,24]{1,0:T(8,128)(2,1)S(1)} %get-tuple-element.439), channel_id=1, source_target_pairs={{32,0},{64,32},{96,64},{128,96},{160,128},{192,160},{224,192},{33,... | collective-permute-start | bytes 73736 | tf_op jit(solution)/shard_map/while/body/eval_jaxpr/ppermute | solution.py:16
  109.2 44.7 %collective-permute-start = (bf16[512,24]{1,0:T(8,128)(2,1)S(1)}, bf16[512,24]{1,0:T(8,128)(2,1)S(1)}, u32[]{:S(2)}, u32[]{:S(2)}) collective-permute-start(bf16[512,24]{1,0:T(8,128)(2,1)S(1)} %get-tuple-element.439), channel_id=1, source_target_pairs={{32,0},{64,32},{96,64},{128,96},{160,128},{192,160},{224,192},{33,... | collective-permute-start | bytes 73736 | tf_op jit(solution)/shard_map/while/body/eval_jaxpr/ppermute | solution.py:16
  185.9 44.7 %collective-permute-start = (bf16[512,24]{1,0:T(8,128)(2,1)S(1)}, bf16[512,24]{1,0:T(8,128)(2,1)S(1)}, u32[]{:S(2)}, u32[]{:S(2)}) collective-permute-start(bf16[512,24]{1,0:T(8,128)(2,1)S(1)} %get-tuple-element.439), channel_id=1, source_target_pairs={{32,0},{64,32},{96,64},{128,96},{160,128},{192,160},{224,192},{33,... | collective-permute-start | bytes 73736 | tf_op jit(solution)/shard_map/while/body/eval_jaxpr/ppermute | solution.py:16
  262.6 44.8 %collective-permute-start = (bf16[512,24]{1,0:T(8,128)(2,1)S(1)}, bf16[512,24]{1,0:T(8,128)(2,1)S(1)}, u32[]{:S(2)}, u32[]{:S(2)}) collective-permute-start(bf16[512,24]{1,0:T(8,128)(2,1)S(1)} %get-tuple-element.439), channel_id=1, source_target_pairs={{32,0},{64,32},{96,64},{128,96},{160,128},{192,160},{224,192},{33,... | collective-permute-start | bytes 73736 | tf_op jit(solution)/shard_map/while/body/eval_jaxpr/ppermute | solution.py:16
  339.3 44.7 %collective-permute-start = (bf16[512,24]{1,0:T(8,128)(2,1)S(1)}, bf16[512,24]{1,0:T(8,128)(2,1)S(1)}, u32[]{:S(2)}, u32[]{:S(2)}) collective-permute-start(bf16[512,24]{1,0:T(8,128)(2,1)S(1)} %get-tuple-element.439), channel_id=1, source_target_pairs={{32,0},{64,32},{96,64},{128,96},{160,128},{192,160},{224,192},{33,... | collective-permute-start | bytes 73736 | tf_op jit(solution)/shard_map/while/body/eval_jaxpr/ppermute | solution.py:16
  416.1 44.7 %collective-permute-start = (bf16[512,24]{1,0:T(8,128)(2,1)S(1)}, bf16[512,24]{1,0:T(8,128)(2,1)S(1)}, u32[]{:S(2)}, u32[]{:S(2)}) collective-permute-start(bf16[512,24]{1,0:T(8,128)(2,1)S(1)} %get-tuple-element.439), channel_id=1, source_target_pairs={{32,0},{64,32},{96,64},{128,96},{160,128},{192,160},{224,192},{33,... | collective-permute-start | bytes 73736 | tf_op jit(solution)/shard_map/while/body/eval_jaxpr/ppermute | solution.py:16
  486.0 18.0 %all-to-all-start = ((bf16[32,2,576]{2,1,0:T(2,128)(2,1)}), bf16[32,2,576]{2,1,0:T(2,128)(2,1)S(1)}, u32[]{:S(2)}, u32[]{:S(2)}) async-start(bf16[32,2,576]{2,1,0:T(2,128)(2,1)} %reshape.348), calls=%async_computation | async-start | bytes 163840 | tf_op jit(solution)/shard_map/while/body/eval_jaxpr/all_to_all | solution.py:64
  493.9 44.6 %collective-permute-start = (bf16[512,24]{1,0:T(8,128)(2,1)S(1)}, bf16[512,24]{1,0:T(8,128)(2,1)S(1)}, u32[]{:S(2)}, u32[]{:S(2)}) collective-permute-start(bf16[512,24]{1,0:T(8,128)(2,1)S(1)} %get-tuple-element.439), channel_id=1, source_target_pairs={{32,0},{64,32},{96,64},{128,96},{160,128},{192,160},{224,192},{33,... | collective-permute-start | bytes 73736 | tf_op jit(solution)/shard_map/while/body/eval_jaxpr/ppermute | solution.py:16
  563.8 18.0 %all-to-all-start = ((bf16[32,2,576]{2,1,0:T(2,128)(2,1)}), bf16[32,2,576]{2,1,0:T(2,128)(2,1)S(1)}, u32[]{:S(2)}, u32[]{:S(2)}) async-start(bf16[32,2,576]{2,1,0:T(2,128)(2,1)} %reshape.348), calls=%async_computation | async-start | bytes 163840 | tf_op jit(solution)/shard_map/while/body/eval_jaxpr/all_to_all | solution.py:64
  571.7 44.6 %collective-permute-start = (bf16[512,24]{1,0:T(8,128)(2,1)S(1)}, bf16[512,24]{1,0:T(8,128)(2,1)S(1)}, u32[]{:S(2)}, u32[]{:S(2)}) collective-permute-start(bf16[512,24]{1,0:T(8,128)(2,1)S(1)} %get-tuple-element.439), channel_id=1, source_target_pairs={{32,0},{64,32},{96,64},{128,96},{160,128},{192,160},{224,192},{33,... | collective-permute-start | bytes 73736 | tf_op jit(solution)/shard_map/while/body/eval_jaxpr/ppermute | solution.py:16
  641.6 18.0 %all-to-all-start = ((bf16[32,2,576]{2,1,0:T(2,128)(2,1)}), bf16[32,2,576]{2,1,0:T(2,128)(2,1)S(1)}, u32[]{:S(2)}, u32[]{:S(2)}) async-start(bf16[32,2,576]{2,1,0:T(2,128)(2,1)} %reshape.348), calls=%async_computation | async-start | bytes 163840 | tf_op jit(solution)/shard_map/while/body/eval_jaxpr/all_to_all | solution.py:64
  649.6 44.6 %collective-permute-start = (bf16[512,24]{1,0:T(8,128)(2,1)S(1)}, bf16[512,24]{1,0:T(8,128)(2,1)S(1)}, u32[]{:S(2)}, u32[]{:S(2)}) collective-permute-start(bf16[512,24]{1,0:T(8,128)(2,1)S(1)} %get-tuple-element.439), channel_id=1, source_target_pairs={{32,0},{64,32},{96,64},{128,96},{160,128},{192,160},{224,192},{33,... | collective-permute-start | bytes 73736 | tf_op jit(solution)/shard_map/while/body/eval_jaxpr/ppermute | solution.py:16
  719.4 18.0 %all-to-all-start = ((bf16[32,2,576]{2,1,0:T(2,128)(2,1)}), bf16[32,2,576]{2,1,0:T(2,128)(2,1)S(1)}, u32[]{:S(2)}, u32[]{:S(2)}) async-start(bf16[32,2,576]{2,1,0:T(2,128)(2,1)} %reshape.348), calls=%async_computation | async-start | bytes 163840 | tf_op jit(solution)/shard_map/while/body/eval_jaxpr/all_to_all | solution.py:64
  727.4 44.6 %collective-permute-start = (bf16[512,24]{1,0:T(8,128)(2,1)S(1)}, bf16[512,24]{1,0:T(8,128)(2,1)S(1)}, u32[]{:S(2)}, u32[]{:S(2)}) collective-permute-start(bf16[512,24]{1,0:T(8,128)(2,1)S(1)} %get-tuple-element.439), channel_id=1, source_target_pairs={{32,0},{64,32},{96,64},{128,96},{160,128},{192,160},{224,192},{33,... | collective-permute-start | bytes 73736 | tf_op jit(solution)/shard_map/while/body/eval_jaxpr/ppermute | solution.py:16
  805.2 44.6 %collective-permute-start = (bf16[512,24]{1,0:T(8,128)(2,1)S(1)}, bf16[512,24]{1,0:T(8,128)(2,1)S(1)}, u32[]{:S(2)}, u32[]{:S(2)}) collective-permute-start(bf16[512,24]{1,0:T(8,128)(2,1)S(1)} %get-tuple-element.439), channel_id=1, source_target_pairs={{32,0},{64,32},{96,64},{128,96},{160,128},{192,160},{224,192},{33,... | collective-permute-start | bytes 73736 | tf_op jit(solution)/shard_map/while/body/eval_jaxpr/ppermute | solution.py:16
  883.0 44.6 %collective-permute-start = (bf16[512,24]{1,0:T(8,128)(2,1)S(1)}, bf16[512,24]{1,0:T(8,128)(2,1)S(1)}, u32[]{:S(2)}, u32[]{:S(2)}) collective-permute-start(bf16[512,24]{1,0:T(8,128)(2,1)S(1)} %get-tuple-element.439), channel_id=1, source_target_pairs={{32,0},{64,32},{96,64},{128,96},{160,128},{192,160},{224,192},{33,... | collective-permute-start | bytes 73736 | tf_op jit(solution)/shard_map/while/body/eval_jaxpr/ppermute | solution.py:16
  952.8 18.0 %all-to-all-start = ((bf16[32,2,576]{2,1,0:T(2,128)(2,1)}), bf16[32,2,576]{2,1,0:T(2,128)(2,1)S(1)}, u32[]{:S(2)}, u32[]{:S(2)}) async-start(bf16[32,2,576]{2,1,0:T(2,128)(2,1)} %reshape.348), calls=%async_computation | async-start | bytes 163840 | tf_op jit(solution)/shard_map/while/body/eval_jaxpr/all_to_all | solution.py:64
  960.8 44.6 %collective-permute-start = (bf16[512,24]{1,0:T(8,128)(2,1)S(1)}, bf16[512,24]{1,0:T(8,128)(2,1)S(1)}, u32[]{:S(2)}, u32[]{:S(2)}) collective-permute-start(bf16[512,24]{1,0:T(8,128)(2,1)S(1)} %get-tuple-element.439), channel_id=1, source_target_pairs={{32,0},{64,32},{96,64},{128,96},{160,128},{192,160},{224,192},{33,... | collective-permute-start | bytes 73736 | tf_op jit(solution)/shard_map/while/body/eval_jaxpr/ppermute | solution.py:16
  1038.6 44.6 %collective-permute-start = (bf16[512,24]{1,0:T(8,128)(2,1)S(1)}, bf16[512,24]{1,0:T(8,128)(2,1)S(1)}, u32[]{:S(2)}, u32[]{:S(2)}) collective-permute-start(bf16[512,24]{1,0:T(8,128)(2,1)S(1)} %get-tuple-element.439), channel_id=1, source_target_pairs={{32,0},{64,32},{96,64},{128,96},{160,128},{192,160},{224,192},{33,... | collective-permute-start | bytes 73736 | tf_op jit(solution)/shard_map/while/body/eval_jaxpr/ppermute | solution.py:16
  1108.4 18.0 %all-to-all-start = ((bf16[32,2,576]{2,1,0:T(2,128)(2,1)}), bf16[32,2,576]{2,1,0:T(2,128)(2,1)S(1)}, u32[]{:S(2)}, u32[]{:S(2)}) async-start(bf16[32,2,576]{2,1,0:T(2,128)(2,1)} %reshape.348), calls=%async_computation | async-start | bytes 163840 | tf_op jit(solution)/shard_map/while/body/eval_jaxpr/all_to_all | solution.py:64
  1116.4 44.6 %collective-permute-start = (bf16[512,24]{1,0:T(8,128)(2,1)S(1)}, bf16[512,24]{1,0:T(8,128)(2,1)S(1)}, u32[]{:S(2)}, u32[]{:S(2)}) collective-permute-start(bf16[512,24]{1,0:T(8,128)(2,1)S(1)} %get-tuple-element.439), channel_id=1, source_target_pairs={{32,0},{64,32},{96,64},{128,96},{160,128},{192,160},{224,192},{33,... | collective-permute-start | bytes 73736 | tf_op jit(solution)/shard_map/while/body/eval_jaxpr/ppermute | solution.py:16
  1194.2 44.6 %collective-permute-start = (bf16[512,24]{1,0:T(8,128)(2,1)S(1)}, bf16[512,24]{1,0:T(8,128)(2,1)S(1)}, u32[]{:S(2)}, u32[]{:S(2)}) collective-permute-start(bf16[512,24]{1,0:T(8,128)(2,1)S(1)} %get-tuple-element.439), channel_id=1, source_target_pairs={{32,0},{64,32},{96,64},{128,96},{160,128},{192,160},{224,192},{33,... | collective-permute-start | bytes 73736 | tf_op jit(solution)/shard_map/while/body/eval_jaxpr/ppermute | solution.py:16
  1272.0 44.6 %collective-permute-start = (bf16[512,24]{1,0:T(8,128)(2,1)S(1)}, bf16[512,24]{1,0:T(8,128)(2,1)S(1)}, u32[]{:S(2)}, u32[]{:S(2)}) collective-permute-start(bf16[512,24]{1,0:T(8,128)(2,1)S(1)} %get-tuple-element.439), channel_id=1, source_target_pairs={{32,0},{64,32},{96,64},{128,96},{160,128},{192,160},{224,192},{33,... | collective-permute-start | bytes 73736 | tf_op jit(solution)/shard_map/while/body/eval_jaxpr/ppermute | solution.py:16
  1349.8 44.6 %collective-permute-start = (bf16[512,24]{1,0:T(8,128)(2,1)S(1)}, bf16[512,24]{1,0:T(8,128)(2,1)S(1)}, u32[]{:S(2)}, u32[]{:S(2)}) collective-permute-start(bf16[512,24]{1,0:T(8,128)(2,1)S(1)} %get-tuple-element.439), channel_id=1, source_target_pairs={{32,0},{64,32},{96,64},{128,96},{160,128},{192,160},{224,192},{33,... | collective-permute-start | bytes 73736 | tf_op jit(solution)/shard_map/while/body/eval_jaxpr/ppermute | solution.py:16
  1419.7 18.0 %all-to-all-start = ((bf16[32,2,576]{2,1,0:T(2,128)(2,1)}), bf16[32,2,576]{2,1,0:T(2,128)(2,1)S(1)}, u32[]{:S(2)}, u32[]{:S(2)}) async-start(bf16[32,2,576]{2,1,0:T(2,128)(2,1)} %reshape.348), calls=%async_computation | async-start | bytes 163840 | tf_op jit(solution)/shard_map/while/body/eval_jaxpr/all_to_all | solution.py:64
  1427.6 44.6 %collective-permute-start = (bf16[512,24]{1,0:T(8,128)(2,1)S(1)}, bf16[512,24]{1,0:T(8,128)(2,1)S(1)}, u32[]{:S(2)}, u32[]{:S(2)}) collective-permute-start(bf16[512,24]{1,0:T(8,128)(2,1)S(1)} %get-tuple-element.439), channel_id=1, source_target_pairs={{32,0},{64,32},{96,64},{128,96},{160,128},{192,160},{224,192},{33,... | collective-permute-start | bytes 73736 | tf_op jit(solution)/shard_map/while/body/eval_jaxpr/ppermute | solution.py:16
  1505.4 44.6 %collective-permute-start = (bf16[512,24]{1,0:T(8,128)(2,1)S(1)}, bf16[512,24]{1,0:T(8,128)(2,1)S(1)}, u32[]{:S(2)}, u32[]{:S(2)}) collective-permute-start(bf16[512,24]{1,0:T(8,128)(2,1)S(1)} %get-tuple-element.439), channel_id=1, source_target_pairs={{32,0},{64,32},{96,64},{128,96},{160,128},{192,160},{224,192},{33,... | collective-permute-start | bytes 73736 | tf_op jit(solution)/shard_map/while/body/eval_jaxpr/ppermute | solution.py:16
  1575.3 18.0 %all-to-all-start = ((bf16[32,2,576]{2,1,0:T(2,128)(2,1)}), bf16[32,2,576]{2,1,0:T(2,128)(2,1)S(1)}, u32[]{:S(2)}, u32[]{:S(2)}) async-start(bf16[32,2,576]{2,1,0:T(2,128)(2,1)} %reshape.348), calls=%async_computation | async-start | bytes 163840 | tf_op jit(solution)/shard_map/while/body/eval_jaxpr/all_to_all | solution.py:64
  1583.2 44.6 %collective-permute-start = (bf16[512,24]{1,0:T(8,128)(2,1)S(1)}, bf16[512,24]{1,0:T(8,128)(2,1)S(1)}, u32[]{:S(2)}, u32[]{:S(2)}) collective-permute-start(bf16[512,24]{1,0:T(8,128)(2,1)S(1)} %get-tuple-element.439), channel_id=1, source_target_pairs={{32,0},{64,32},{96,64},{128,96},{160,128},{192,160},{224,192},{33,... | collective-permute-start | bytes 73736 | tf_op jit(solution)/shard_map/while/body/eval_jaxpr/ppermute | solution.py:16
  1661.1 44.6 %collective-permute-start = (bf16[512,24]{1,0:T(8,128)(2,1)S(1)}, bf16[512,24]{1,0:T(8,128)(2,1)S(1)}, u32[]{:S(2)}, u32[]{:S(2)}) collective-permute-start(bf16[512,24]{1,0:T(8,128)(2,1)S(1)} %get-tuple-element.439), channel_id=1, source_target_pairs={{32,0},{64,32},{96,64},{128,96},{160,128},{192,160},{224,192},{33,... | collective-permute-start | bytes 73736 | tf_op jit(solution)/shard_map/while/body/eval_jaxpr/ppermute | solution.py:16
  1738.9 44.6 %collective-permute-start = (bf16[512,24]{1,0:T(8,128)(2,1)S(1)}, bf16[512,24]{1,0:T(8,128)(2,1)S(1)}, u32[]{:S(2)}, u32[]{:S(2)}) collective-permute-start(bf16[512,24]{1,0:T(8,128)(2,1)S(1)} %get-tuple-element.439), channel_id=1, source_target_pairs={{32,0},{64,32},{96,64},{128,96},{160,128},{192,160},{224,192},{33,... | collective-permute-start | bytes 73736 | tf_op jit(solution)/shard_map/while/body/eval_jaxpr/ppermute | solution.py:16
  (129 other events, 2617.4 us)
where the time goes:
time: 1800 us; the launch traced here: 1790 us
  local copies, waits for them, and re-layouts  557 us (31%)
  waiting for transfers between devices  451 us (25%)
  starting transfers between devices  443 us (25%)
  other arithmetic  245 us (14%)
  matrix products  85.5 us (5%)
    another operation x46, other arithmetic  208 us
    all_to_all x23, starting transfers between devices, mix_layer(): lax.all_to_all(picked, 'expert', split_axis=1, concat_axis=1, tiled=True)  182 us
    all_to_all x23, waiting for transfers between devices, mix_layer(): lax.all_to_all(picked, 'expert', split_axis=1, concat_axis=1, tiled=True)  165 us
    gather x23, local copies, waits for them, and re-layouts, combine(): weights = gate_grid.reshape(-1)[flat_index].astype(jnp.float32)  156 us
    all_to_all x23, waiting for transfers between devices, mix_layer(): lax.all_to_all(gate_wide, 'expert', split_axis=1, concat_axis=1, tiled=True)  116 us
    all_to_all x23, starting transfers between devices, mix_layer(): lax.all_to_all(spread, 'expert', split_axis=1, concat_axis=1, tiled=True)  109 us
    ppermute x23, waiting for transfers between devices, passed_along(): return lax.ppermute(value, axis, pairs)  106 us
    scatter x23, local copies, waits for them, and re-layouts, place_rows(): slot_table = jnp.full((experts * capacity,), -1, jnp.int32).at[flat_ids *...  99.3 us
  transfers between devices with their start and end apart: 115, of which 92 were waited for; matrix products, arithmetic and copies ran while one was open for 23% of the time, Pallas kernels for 0%

commit v1 on v0

v1 whole, which is shorter than its diff:
```python
import functools

import jax
import jax.numpy as jnp
import numpy as np
from jax import lax
from jax.experimental import pallas as pl
from jax.experimental.pallas import tpu as pltpu
from jax.sharding import PartitionSpec as P

VMEM_LIMIT = 62 * 1024 * 1024
HBM = pl.BlockSpec(memory_space=pltpu.HBM)
SMEM = pl.BlockSpec(memory_space=pltpu.SMEM)
VMEM = pl.BlockSpec(memory_space=pltpu.VMEM)
DIRS = (1, -1)


def owner_of(layer, sections):
    return (layer % sections) // 2


def ring_plan(sections, layers):
    chips = sections // 2
    held = [
        [{q: 0 for q in range(layers) if owner_of(q, sections) == y} for y in range(chips)]
        for _ in DIRS
    ]
    slots = []
    while any(len(stock) < layers for lane in held for stock in lane):
        moves = []
        for lane, step in enumerate(DIRS):
            for y in range(chips):
                there = held[lane][(y + step) % chips]
                options = [q for q in held[lane][y] if q not in there]
                if options:
                    moves.append((lane, y, (y + step) % chips, min(options)))
        slots.append(moves)
        for lane, y, target, q in moves:
            held[lane][target][q] = len(slots)
    return slots, held


def pick_kernel(row, places, tab_ref, *refs):
    count = len(places)
    sources, out_ref, sem = refs[:count], refs[count], refs[count + 1]
    choice = tab_ref[row]
    for number, (source, place) in enumerate(zip(sources, places)):
        view = source.at[place] if place else source

        @pl.when(choice == number)
        def _(view=view):
            copy = pltpu.make_async_copy(view, out_ref, sem)
            copy.start()
            copy.wait()


def pick(tab, row, sources, places):
    shape = sources[0].shape[-2:]
    size = 2 * shape[0] * shape[1] * 2
    return pl.pallas_call(
        functools.partial(pick_kernel, row, places),
        out_shape=jax.ShapeDtypeStruct(shape, jnp.bfloat16),
        in_specs=[SMEM] + [HBM] * len(sources),
        out_specs=HBM,
        scratch_shapes=[pltpu.SemaphoreType.DMA],
        compiler_params=pltpu.CompilerParams(vmem_limit_bytes=VMEM_LIMIT),
        cost_estimate=pl.CostEstimate(flops=0, bytes_accessed=size, transcendentals=0),
        name="pick",
    )(tab, *sources)


def merge_rows(h_ref, gathered_ref, scale_ref, col_ref, start, size):
    rows = pl.ds(start, size)
    slots = gathered_ref.shape[0]
    lanes = lax.broadcasted_iota(jnp.int32, (size, slots), 1)
    first, second = col_ref[rows, 0:1], col_ref[rows, 1:2]
    onehot = jnp.where((lanes == first) | (lanes == second), 1.0, 0.0).astype(jnp.bfloat16)
    update = jnp.dot(onehot, gathered_ref[...], preferred_element_type=jnp.float32)
    return (h_ref[rows, :].astype(jnp.float32) + update * scale_ref[rows, :]).astype(jnp.bfloat16)


def layer_kernel(
    merge, block, scal_ref, h_ref, gathered_ref, scale_ref, colp_ref, col_ref, row_ref,
    router_ref, gain_ref, lane_ref, other_ref, hnew_ref, weighted_ref, newscale_ref,
    win_ref, wout_ref, normed_ref, gates_ref, sems,
):
    core, expert = scal_ref[0], scal_ref[1]

    @pl.when(core == 0)
    def _():
        pltpu.make_async_copy(lane_ref, win_ref, sems.at[0]).start()
        pltpu.make_async_copy(other_ref, wout_ref, sems.at[1]).start()

    @pl.when(core != 0)
    def _():
        pltpu.make_async_copy(other_ref, win_ref, sems.at[0]).start()
        pltpu.make_async_copy(lane_ref, wout_ref, sems.at[1]).start()

    tokens = h_ref.shape[0]
    experts = router_ref.shape[0]
    capacity = weighted_ref.shape[0]
    gain = gain_ref[...]
    ids = lax.broadcasted_iota(jnp.int32, (block, experts), 1)
    @pl.loop(0, tokens // block)
    def _(turn):
        start = pl.multiple_of(turn * block, block)
        rows = pl.ds(start, block)
        if merge:
            held = merge_rows(h_ref, gathered_ref, scale_ref, colp_ref, start, block)
            hnew_ref[rows, :] = held
        else:
            held = h_ref[rows, :]
            hnew_ref[rows, :] = held
        wide = held.astype(jnp.float32)
        mean_square = jnp.mean(wide * wide, axis=1, keepdims=True)
        normed = (wide * lax.rsqrt(mean_square + 1e-06) * gain).astype(jnp.bfloat16)
        normed_ref[rows, :] = normed
        logits = lax.dot_general(
            normed, router_ref[...], (((1,), (1,)), ((), ())), preferred_element_type=jnp.float32
        )
        gates = jax.nn.sigmoid(logits).astype(jnp.bfloat16)
        gates_ref[rows, :] = gates
        named = (ids == col_ref[rows, 2:3]) | (ids == col_ref[rows, 3:4])
        total = jnp.sum(jnp.where(named, gates.astype(jnp.float32), 0.0), axis=1, keepdims=True)
        newscale_ref[rows, :] = 1.0 / total

    slots = lax.broadcasted_iota(jnp.int32, (capacity, tokens), 0) + expert * capacity
    chosen = (slots == row_ref[0:1, :]) | (slots == row_ref[1:2, :])
    chosen = jnp.where(chosen, 1.0, 0.0).astype(jnp.bfloat16)
    taken = jnp.dot(chosen, normed_ref[...], preferred_element_type=jnp.float32)
    taken = taken.astype(jnp.bfloat16)
    all_gates = jnp.dot(chosen, gates_ref[...], preferred_element_type=jnp.float32)
    own = lax.broadcasted_iota(jnp.int32, all_gates.shape, 1) == expert
    gate = jnp.sum(jnp.where(own, all_gates, 0.0), axis=1, keepdims=True)
    pltpu.make_async_copy(lane_ref, win_ref, sems.at[0]).wait()
    pre_act = lax.dot_general(
        taken, win_ref[...], (((1,), (1,)), ((), ())), preferred_element_type=jnp.float32
    )
    active = jax.nn.gelu(pre_act, approximate=True).astype(jnp.bfloat16)
    pltpu.make_async_copy(lane_ref, wout_ref, sems.at[1]).wait()
    output = jnp.dot(active, wout_ref[...], preferred_element_type=jnp.float32)
    weighted_ref[...] = (output * gate).astype(jnp.bfloat16)


def plane(shape, *lead):
    return pl.BlockSpec((None,) * len(lead) + shape, lambda i: lead + (0,) * len(shape))


def run_layer(layer, scal, h, gathered, scale, cols, rows, routers, gains, lane_w, other_w):
    tokens, width = h.shape
    hidden = lane_w.shape[0]
    experts = routers.shape[1]
    capacity = 3 * tokens // experts
    merge = layer > 0
    before = max(layer - 1, 0)
    operands = (scal, h, gathered, scale, cols, cols, rows, routers, gains, lane_w, other_w)
    flops = 4 * capacity * hidden * width + 2 * tokens * experts * capacity * width
    return pl.pallas_call(
        functools.partial(layer_kernel, merge, min(128, tokens)),
        out_shape=(
            jax.ShapeDtypeStruct((tokens, width), jnp.bfloat16),
            jax.ShapeDtypeStruct((capacity, width), jnp.bfloat16),
            jax.ShapeDtypeStruct((tokens, 1), jnp.float32),
        ),
        grid=(1,),
        in_specs=[
            SMEM, VMEM, VMEM, VMEM,
            plane((tokens, 4), before), plane((tokens, 4), layer), plane((8, tokens), layer),
            plane((experts, width), layer), plane((1, width), layer),
            HBM, HBM,
        ],
        out_specs=(VMEM, VMEM, VMEM),
        scratch_shapes=[
            pltpu.VMEM((hidden, width), jnp.bfloat16),
            pltpu.VMEM((hidden, width), jnp.bfloat16),
            pltpu.VMEM((tokens, width), jnp.bfloat16),
            pltpu.VMEM((tokens, experts), jnp.bfloat16),
            pltpu.SemaphoreType.DMA((2,)),
        ],
        compiler_params=pltpu.CompilerParams(vmem_limit_bytes=VMEM_LIMIT),
        cost_estimate=pl.CostEstimate(
            flops=flops, bytes_accessed=4 * hidden * width + 4 * tokens * width, transcendentals=0
        ),
        name="layer",
    )(*operands)


def final_kernel(block, h_ref, gathered_ref, scale_ref, col_ref, out_ref):
    @pl.loop(0, h_ref.shape[0] // block)
    def _(turn):
        start = pl.multiple_of(turn * block, block)
        out_ref[pl.ds(start, block), :] = merge_rows(
            h_ref, gathered_ref, scale_ref, col_ref, start, block
        )


def run_final(last, h, gathered, scale, cols):
    tokens = h.shape[0]
    return pl.pallas_call(
        functools.partial(final_kernel, min(128, tokens)),
        out_shape=jax.ShapeDtypeStruct(h.shape, jnp.bfloat16),
        grid=(1,),
        in_specs=[VMEM, VMEM, VMEM, plane((tokens, 4), last)],
        out_specs=VMEM,
        compiler_params=pltpu.CompilerParams(vmem_limit_bytes=VMEM_LIMIT),
        name="final",
    )(h, gathered, scale, cols)


def place_tokens(routes, experts, capacity):
    layers, tokens, _ = routes.shape
    ids = jnp.arange(experts, dtype=jnp.int32)
    first = routes[:, :, 0:1] == ids
    second = routes[:, :, 1:2] == ids
    named = (first | second).astype(jnp.bfloat16)
    earlier = jnp.tril(jnp.ones((tokens, tokens), jnp.bfloat16), -1)
    rank = jnp.einsum("ut,lte->lue", earlier, named, preferred_element_type=jnp.float32)
    rank = rank.astype(jnp.int32) + ids * capacity
    slot_first = jnp.sum(jnp.where(first, rank, 0), axis=2)
    slot_second = jnp.sum(jnp.where(second, rank, 0), axis=2)
    cols = jnp.stack([slot_first, slot_second, routes[:, :, 0], routes[:, :, 1]], axis=2)
    blank = jnp.zeros_like(slot_first)
    rows = jnp.stack([slot_first, slot_second] + [blank] * 6, axis=1)
    return cols, rows


def local(inputs, routes, norm_gains, routers, expert_in, expert_out):
    sections = lax.axis_size("section")
    experts = lax.axis_size("expert")
    section_pos = lax.axis_index("section")
    expert_pos = lax.axis_index("expert")
    repeats = expert_in.shape[0]
    layers = repeats * sections
    tokens = inputs.shape[1]
    capacity = 3 * tokens // experts
    slots, held = ring_plan(sections, layers)
    arrival = [max(stock[q] for lane in held for stock in lane) for q in range(layers)]
    scal = jnp.stack([section_pos % 2, expert_pos]).astype(jnp.int32)

    def source_of(lane, y, q):
        if owner_of(q, sections) == y:
            if q % 2 == lane:
                return ("in", "out")[lane], q // sections
            return "swapped", q // sections
        return "ring", held[lane][y][q]

    buffers = {("in", r): (expert_in, (r, 0, 0)) for r in range(repeats)}
    buffers.update({("out", r): (expert_out, (r, 0, 0)) for r in range(repeats)})
    table, wanted = [], []

    def add_pick(by_section):
        names = sorted(set(by_section.values()))
        table.append([names.index(by_section[s]) if s in by_section else 0 for s in range(sections)])
        wanted.append(names)
        return len(table) - 1

    every = [(lane, y) for lane in range(2) for y in range(sections // 2)]
    swap_rows = [
        add_pick({2 * y + lane: (("out", "in")[lane], r) for lane, y in every})
        for r in range(repeats)
    ]
    ring_rows = [
        add_pick({2 * y + lane: source_of(lane, y, q) for lane, y, _, q in moves}) for moves in slots
    ]
    layer_rows = [
        add_pick({2 * y + lane: source_of(lane, y, q) for lane, y in every}) for q in range(layers)
    ]
    tab = jnp.asarray(np.array(table, np.int32).T)[section_pos]

    def picked(row, tab):
        found = [buffers[name] for name in wanted[row]]
        return pick(tab, row, [array for array, _ in found], [place for _, place in found])

    def swapped(value):
        return lax.ppermute(value, "section", [(s, s ^ 1) for s in range(sections)])

    def ring(slot, tab):
        pairs = [(2 * y + lane, 2 * target + lane) for lane, y, target, _ in slots[slot]]
        return lax.ppermute(picked(ring_rows[slot], tab), "section", pairs)

    mine = lax.all_to_all(routes[:, 0], "section", split_axis=1, concat_axis=0, tiled=False)
    mine = jnp.transpose(mine, (1, 0, 2, 3)).reshape(layers, tokens, 2)
    cols, rows = place_tokens(mine, experts, capacity)
    gains = lax.all_gather(norm_gains[:, 0], "section", axis=0)
    gains = jnp.transpose(gains, (1, 0, 2)).reshape(layers, 1, -1).astype(jnp.float32)
    gate_rows = lax.all_gather(routers[:, 0, 0], ("section", "expert"), axis=0)
    gate_rows = gate_rows.reshape(sections, experts, repeats, -1)
    gate_rows = jnp.transpose(gate_rows, (2, 0, 1, 3)).reshape(layers, experts, -1)
    h = lax.all_gather(inputs[0], "expert", axis=1, tiled=True)

    buffers[("swapped", 0)] = (swapped(picked(swap_rows[0], tab)), ())
    later = swapped(picked(swap_rows[1], tab))
    lead = arrival[0]
    for slot in range(lead):
        arrived = ring(slot, tab)
        if slot == 0:
            arrived, later, tab = lax.optimization_barrier((arrived, later, tab))
            buffers[("swapped", 1)] = (later, ())
        else:
            arrived, tab = lax.optimization_barrier((arrived, tab))
        buffers[("ring", slot + 1)] = (arrived, ())
    lane_w = picked(layer_rows[0], tab)
    other_w = swapped(lane_w)
    state = lax.optimization_barrier((lane_w, other_w, tab, cols, rows, gains, gate_rows, h))
    lane_w, other_w, tab, cols, rows, gains, gate_rows, h = state
    gathered = jnp.zeros((8, h.shape[1]), jnp.bfloat16)
    scale = jnp.zeros((8, 1), jnp.float32)

    for q in range(layers):
        slot = lead + q
        arrived = ring(slot, tab) if slot < len(slots) else None
        h, weighted, scale = run_layer(
            q, scal, h, gathered, scale, cols, rows, gate_rows, gains, lane_w, other_w
        )
        weighted, tab = lax.optimization_barrier((weighted, tab))
        gathered = lax.all_gather(weighted, "expert", axis=0, tiled=True)
        early = q + 1 < layers and arrival[q + 1] <= slot
        if early:
            lane_w = picked(layer_rows[q + 1], tab)
            other_w = swapped(lane_w)
        if arrived is not None:
            state = lax.optimization_barrier((gathered, arrived, lane_w, other_w, tab))
            gathered, arrived, lane_w, other_w, tab = state
            buffers[("ring", slot + 1)] = (arrived, ())
        else:
            state = lax.optimization_barrier((gathered, lane_w, other_w, tab))
            gathered, lane_w, other_w, tab = state
        if q + 1 < layers and not early:
            lane_w = picked(layer_rows[q + 1], tab)
            other_w = swapped(lane_w)

    h = run_final(layers - 1, h, gathered, scale, cols)
    width = inputs.shape[2]
    return lax.dynamic_slice(h, (0, expert_pos * width), (tokens, width))[None]


def solution(mesh):
    return jax.shard_map(
        local,
        mesh=mesh,
        in_specs=(
            P("section", None, "expert"),
            P(None, "section", None, None, None),
            P(None, "section", None),
            P(None, "section", "expert", None),
            P(None, "section", "expert", None, None),
            P(None, "section", "expert", None, None),
        ),
        out_specs=P("section", None, "expert"),
        check_vma=False,
    )
```

time: 1800 us -> 3110 us (1.73)
  Pallas kernels: 0 us -> 2480 us
  local copies, waits for them, and re-layouts: 557 us -> 11 us
  starting transfers between devices: 443 us -> 62 us
  other arithmetic: 245 us -> 6.36 us
  blocking collectives: 0 us -> 130 us
  matrix products: 85.5 us -> 0.89 us
  waiting for transfers between devices: 451 us -> 393 us
    pallas_call x0 -> x49, Pallas kernels: none -> 2480 us  [the longest x32 2340 us: pick(): pl.pallas_call(functools.partial(pick_kernel, row, places), out_shape=jax...]
    all_to_all x69 -> x1, starting transfers between devices: 379 us -> 6.48 us  [local(): lax.all_to_all(routes[:, 0], 'section', split_axis=1, concat_axis=0, tile...]
    all_to_all x69 -> x1, waiting for transfers between devices: 344 us -> 0.01 us  [local(): lax.all_to_all(routes[:, 0], 'section', split_axis=1, concat_axis=0, tile...]
    gather x92 -> x0, local copies, waits for them, and re-layouts: 314 us -> none  [the longest x23 156 us: combine(): weights = gate_grid.reshape(-1)[flat_index].astype(jnp.float32)]
    ppermute x46 -> x32, waiting for transfers between devices: 106 us -> 318 us  [the longest x14 261 us: ring(): return lax.ppermute(picked(ring_rows[slot], tab), 'section', pairs)]
    another operation x46 -> x3, other arithmetic: 208 us -> 1.44 us  [the longest x1 0.82 us: place_tokens(): rows = jnp.stack([slot_first, slot_second] + [blank] * 6, axis=1)]
    all_gather x0 -> x3, blocking collectives: none -> 130 us  [the longest x1 66.3 us: local(): gate_rows = lax.all_gather(routers[:, 0, 0], ('section', 'expert'), axis=0)]
    scatter x23 -> x0, local copies, waits for them, and re-layouts: 99.3 us -> none  [place_rows(): slot_table = jnp.full((experts * capacity,), -1, jnp.int32).at[flat_ids *...]
  transfers between devices with their start and end apart: 115 -> 49, of which waited for: 92 -> 22; matrix products, arithmetic and copies ran while one was open for 23% -> 0% of each run, Pallas kernels for 0% -> 59%
where the time goes in v1:
time: 3110 us; the launch traced here: 3100 us
  Pallas kernels  2480 us (80%)
  waiting for transfers between devices  393 us (13%)
  blocking collectives  130 us (4%)
  starting transfers between devices  62 us (2%)
    pallas_call x32, Pallas kernels, pick(): pl.pallas_call(functools.partial(pick_kernel, row, places), out_shape=jax...  2340 us
    ppermute x14, waiting for transfers between devices, ring(): return lax.ppermute(picked(ring_rows[slot], tab), 'section', pairs)  261 us
    pallas_call x16, Pallas kernels, run_layer(): pl.pallas_call(functools.partial(layer_kernel, merge, min(128, tokens)),...  134 us
    all_gather x16, waiting for transfers between devices, local(): gathered = lax.all_gather(weighted, 'expert', axis=0, tiled=True)  74.7 us
    all_gather x1, blocking collectives, local(): gate_rows = lax.all_gather(routers[:, 0, 0], ('section', 'expert'), axis=0)  66.3 us
  transfers between devices with their start and end apart: 49, of which 22 were waited for; matrix products, arithmetic and copies ran while one was open for 0% of the time, Pallas kernels for 59%

profile of v1, /device:TPU:8, one launch (start us, length us, event | category | flops | bytes accessed | tf_op | source)
XLA Modules:
  0.0 3100.5 jit_solution(4620929305444771591)
XLA Ops:
  7.7 73.2 %pick.32 = bf16[1536,768]{1,0:T(8,128)(2,1)} custom-call(s32[32]{0:T(128)} %dynamic-slice_bitcast_fusion.tab_ref, bf16[2,1,1,1536,768]{4,3,2,1,0:T(8,128)(2,1)} %refs_0_.50, bf16[2,1,1,1536,768]{4,3,2,1,0:T(8,128)(2,1)} %refs_0_.51), custom_call_target="tpu_custom_call" | custom-call | bytes 4718592 | tf_op jit(solution)/shard_map/pick/pallas_call | solution.py:60
  81.1 73.2 %pick.34 = bf16[1536,768]{1,0:T(8,128)(2,1)} custom-call(s32[32]{0:T(128)} %dynamic-slice_bitcast_fusion.tab_ref, bf16[2,1,1,1536,768]{4,3,2,1,0:T(8,128)(2,1)} %refs_0_.50, bf16[2,1,1,1536,768]{4,3,2,1,0:T(8,128)(2,1)} %refs_0_.51), custom_call_target="tpu_custom_call" | custom-call | bytes 4718592 | tf_op jit(solution)/shard_map/pick/pallas_call | solution.py:60
  257.6 73.2 %pick.35 = bf16[1536,768]{1,0:T(8,128)(2,1)} custom-call(s32[32]{0:T(128)} %dynamic-slice_bitcast_fusion.tab_ref, bf16[2,1,1,1536,768]{4,3,2,1,0:T(8,128)(2,1)} %refs_0_.51, bf16[1536,768]{1,0:T(8,128)(2,1)} %collective-permute-done.1.refs_1_.refs_0_, bf16[1536,768]{1,0:T(8,128)(2,1)} %collective-permute-done.refs_1_.refs_2_.refs_4_.refs_3_.refs_5_.refs_6_), custom_call_target="tpu_custom_call" | custom-call | bytes 4718592 | tf_op jit(solution)/shard_map/pick/pallas_call | solution.py:60
  361.3 73.2 %pick.36 = bf16[1536,768]{1,0:T(8,128)(2,1)} custom-call(s32[32]{0:T(128)} %dynamic-slice_bitcast_fusion.tab_ref, bf16[1536,768]{1,0:T(8,128)(2,1)} %collective-permute-done.1.refs_1_.refs_0_, bf16[1536,768]{1,0:T(8,128)(2,1)} %collective-permute-done.3.refs_1_.refs_2_), custom_call_target="tpu_custom_call" | custom-call | bytes 4718592 | tf_op jit(solution)/shard_map/pick/pallas_call | solution.py:60
  465.0 73.2 %pick.37.lane_ref = bf16[1536,768]{1,0:T(8,128)(2,1)} custom-call(s32[32]{0:T(128)} %dynamic-slice_bitcast_fusion.tab_ref, bf16[2,1,1,1536,768]{4,3,2,1,0:T(8,128)(2,1)} %refs_0_.50, bf16[1536,768]{1,0:T(8,128)(2,1)} %collective-permute-done.1.refs_1_.refs_0_, bf16[1536,768]{1,0:T(8,128)(2,1)} %collective-permute-done.3.refs_1_.refs_2_, ...), custom_call_target="tpu_custom_call" | custom-call | bytes 4718592 | tf_op jit(solution)/shard_map/pick/pallas_call | solution.py:60
  696.1 73.3 %pick.38 = bf16[1536,768]{1,0:T(8,128)(2,1)} custom-call(s32[32]{0:T(128)} %dynamic-slice_bitcast_fusion.tab_ref, bf16[1536,768]{1,0:T(8,128)(2,1)} %collective-permute-done.1.refs_1_.refs_0_, bf16[1536,768]{1,0:T(8,128)(2,1)} %collective-permute-done.3.refs_1_.refs_2_, bf16[1536,768]{1,0:T(8,128)(2,1)} %collective-permute-done.4.refs_3_.refs_2_, ...), custom_call_target="tpu_custom_call" | custom-call | bytes 4718592 | tf_op jit(solution)/shard_map/pick/pallas_call | solution.py:60
  800.0 73.2 %pick.39.lane_ref = bf16[1536,768]{1,0:T(8,128)(2,1)} custom-call(s32[32]{0:T(128)} %dynamic-slice_bitcast_fusion.tab_ref, bf16[2,1,1,1536,768]{4,3,2,1,0:T(8,128)(2,1)} %refs_0_.51, bf16[1536,768]{1,0:T(8,128)(2,1)} %collective-permute-done.3.refs_1_.refs_2_, bf16[1536,768]{1,0:T(8,128)(2,1)} %collective-permute-done.4.refs_3_.refs_2_, ...), custom_call_target="tpu_custom_call" | custom-call | bytes 4718592 | tf_op jit(solution)/shard_map/pick/pallas_call | solution.py:60
  887.0 73.3 %pick.40 = bf16[1536,768]{1,0:T(8,128)(2,1)} custom-call(s32[32]{0:T(128)} %dynamic-slice_bitcast_fusion.tab_ref, bf16[2,1,1,1536,768]{4,3,2,1,0:T(8,128)(2,1)} %refs_0_.50, bf16[1536,768]{1,0:T(8,128)(2,1)} %collective-permute-done.1.refs_1_.refs_0_, bf16[1536,768]{1,0:T(8,128)(2,1)} %collective-permute-done.4.refs_3_.refs_2_, ...), custom_call_target="tpu_custom_call" | custom-call | bytes 4718592 | tf_op jit(solution)/shard_map/pick/pallas_call | solution.py:60
  960.4 73.2 %pick.41.lane_ref = bf16[1536,768]{1,0:T(8,128)(2,1)} custom-call(s32[32]{0:T(128)} %dynamic-slice_bitcast_fusion.tab_ref, bf16[2,1,1,1536,768]{4,3,2,1,0:T(8,128)(2,1)} %refs_0_.50, bf16[1536,768]{1,0:T(8,128)(2,1)} %collective-permute-done.1.refs_1_.refs_0_, bf16[1536,768]{1,0:T(8,128)(2,1)} %collective-permute-done.3.refs_1_.refs_2_, ...), custom_call_target="tpu_custom_call" | custom-call | bytes 4718592 | tf_op jit(solution)/shard_map/pick/pallas_call | solution.py:60
  1050.0 73.3 %pick.42 = bf16[1536,768]{1,0:T(8,128)(2,1)} custom-call(s32[32]{0:T(128)} %dynamic-slice_bitcast_fusion.tab_ref, bf16[2,1,1,1536,768]{4,3,2,1,0:T(8,128)(2,1)} %refs_0_.50, bf16[2,1,1,1536,768]{4,3,2,1,0:T(8,128)(2,1)} %refs_0_.51, bf16[1536,768]{1,0:T(8,128)(2,1)} %collective-permute-done.6.refs_3_.refs_4_.refs_2_.refs_1_, ...), custom_call_target="tpu_custom_call" | custom-call | bytes 4718592 | tf_op jit(solution)/shard_map/pick/pallas_call | solution.py:60
  1152.5 73.3 %pick.43.lane_ref = bf16[1536,768]{1,0:T(8,128)(2,1)} custom-call(s32[32]{0:T(128)} %dynamic-slice_bitcast_fusion.tab_ref, bf16[2,1,1,1536,768]{4,3,2,1,0:T(8,128)(2,1)} %refs_0_.51, bf16[1536,768]{1,0:T(8,128)(2,1)} %collective-permute-done.3.refs_1_.refs_2_, bf16[1536,768]{1,0:T(8,128)(2,1)} %collective-permute-done.6.refs_3_.refs_4_.refs_2_.refs_1_, ...), custom_call_target="tpu_custom_call" | custom-call | bytes 4718592 | tf_op jit(solution)/shard_map/pick/pallas_call | solution.py:60
  1239.3 73.2 %pick.44 = bf16[1536,768]{1,0:T(8,128)(2,1)} custom-call(s32[32]{0:T(128)} %dynamic-slice_bitcast_fusion.tab_ref, bf16[2,1,1,1536,768]{4,3,2,1,0:T(8,128)(2,1)} %refs_0_.50, bf16[2,1,1,1536,768]{4,3,2,1,0:T(8,128)(2,1)} %refs_0_.51, bf16[1536,768]{1,0:T(8,128)(2,1)} %collective-permute-done.10.refs_4_.refs_2_.refs_3_.refs_1_, ...), custom_call_target="tpu_custom_call" | custom-call | bytes 4718592 | tf_op jit(solution)/shard_map/pick/pallas_call | solution.py:60
  1313.3 73.2 %pick.45.lane_ref = bf16[1536,768]{1,0:T(8,128)(2,1)} custom-call(s32[32]{0:T(128)} %dynamic-slice_bitcast_fusion.tab_ref, bf16[2,1,1,1536,768]{4,3,2,1,0:T(8,128)(2,1)} %refs_0_.50, bf16[1536,768]{1,0:T(8,128)(2,1)} %collective-permute-done.1.refs_1_.refs_0_, bf16[1536,768]{1,0:T(8,128)(2,1)} %collective-permute-done.3.refs_1_.refs_2_, ...), custom_call_target="tpu_custom_call" | custom-call | bytes 4718592 | tf_op jit(solution)/shard_map/pick/pallas_call | solution.py:60
  1400.7 73.2 %pick.46 = bf16[1536,768]{1,0:T(8,128)(2,1)} custom-call(s32[32]{0:T(128)} %dynamic-slice_bitcast_fusion.tab_ref, bf16[2,1,1,1536,768]{4,3,2,1,0:T(8,128)(2,1)} %refs_0_.51, bf16[1536,768]{1,0:T(8,128)(2,1)} %collective-permute-done.12.refs_1_.refs_4_.refs_0_.refs_2_), custom_call_target="tpu_custom_call" | custom-call | bytes 4718592 | tf_op jit(solution)/shard_map/pick/pallas_call | solution.py:60
  1503.3 73.3 %pick.47.lane_ref = bf16[1536,768]{1,0:T(8,128)(2,1)} custom-call(s32[32]{0:T(128)} %dynamic-slice_bitcast_fusion.tab_ref, bf16[2,1,1,1536,768]{4,3,2,1,0:T(8,128)(2,1)} %refs_0_.51, bf16[1536,768]{1,0:T(8,128)(2,1)} %collective-permute-done.3.refs_1_.refs_2_, bf16[1536,768]{1,0:T(8,128)(2,1)} %collective-permute-done.6.refs_3_.refs_4_.refs_2_.refs_1_, ...), custom_call_target="tpu_custom_call" | custom-call | bytes 4718592 | tf_op jit(solution)/shard_map/pick/pallas_call | solution.py:60
  1590.5 73.2 %pick.48 = bf16[1536,768]{1,0:T(8,128)(2,1)} custom-call(s32[32]{0:T(128)} %dynamic-slice_bitcast_fusion.tab_ref, bf16[2,1,1,1536,768]{4,3,2,1,0:T(8,128)(2,1)} %refs_0_.50, bf16[1536,768]{1,0:T(8,128)(2,1)} %collective-permute-done.8.refs_3_.refs_4_.refs_1_.refs_0_.refs_2_, bf16[1536,768]{1,0:T(8,128)(2,1)} %collective-permute-done.10.refs_4_.refs_2_.refs_3_.refs_1_, ...), custom_call_target="tpu_custom_call" | custom-call | bytes 4718592 | tf_op jit(solution)/shard_map/pick/pallas_call | solution.py:60
  1665.7 73.2 %pick.49.lane_ref = bf16[1536,768]{1,0:T(8,128)(2,1)} custom-call(s32[32]{0:T(128)} %dynamic-slice_bitcast_fusion.tab_ref, bf16[2,1,1,1536,768]{4,3,2,1,0:T(8,128)(2,1)} %refs_0_.50, bf16[1536,768]{1,0:T(8,128)(2,1)} %collective-permute-done.1.refs_1_.refs_0_, bf16[1536,768]{1,0:T(8,128)(2,1)} %collective-permute-done.6.refs_3_.refs_4_.refs_2_.refs_1_, ...), custom_call_target="tpu_custom_call" | custom-call | bytes 4718592 | tf_op jit(solution)/shard_map/pick/pallas_call | solution.py:60
  1753.4 73.3 %pick.50 = bf16[1536,768]{1,0:T(8,128)(2,1)} custom-call(s32[32]{0:T(128)} %dynamic-slice_bitcast_fusion.tab_ref, bf16[1536,768]{1,0:T(8,128)(2,1)} %collective-permute-done.8.refs_3_.refs_4_.refs_1_.refs_0_.refs_2_, bf16[1536,768]{1,0:T(8,128)(2,1)} %collective-permute-done.12.refs_1_.refs_4_.refs_0_.refs_2_, ...), custom_call_target="tpu_custom_call" | custom-call | bytes 4718592 | tf_op jit(solution)/shard_map/pick/pallas_call | solution.py:60
  1829.0 73.2 %pick.51.lane_ref = bf16[1536,768]{1,0:T(8,128)(2,1)} custom-call(s32[32]{0:T(128)} %dynamic-slice_bitcast_fusion.tab_ref, bf16[2,1,1,1536,768]{4,3,2,1,0:T(8,128)(2,1)} %refs_0_.51, bf16[1536,768]{1,0:T(8,128)(2,1)} %collective-permute-done.6.refs_3_.refs_4_.refs_2_.refs_1_, ...), custom_call_target="tpu_custom_call" | custom-call | bytes 4718592 | tf_op jit(solution)/shard_map/pick/pallas_call | solution.py:60
  1915.9 73.2 %pick.53.lane_ref = bf16[1536,768]{1,0:T(8,128)(2,1)} custom-call(s32[32]{0:T(128)} %dynamic-slice_bitcast_fusion.tab_ref, bf16[2,1,1,1536,768]{4,3,2,1,0:T(8,128)(2,1)} %refs_0_.50, bf16[1536,768]{1,0:T(8,128)(2,1)} %collective-permute-done.10.refs_4_.refs_2_.refs_3_.refs_1_, bf16[1536,768]{1,0:T(8,128)(2,1)} %collective-permute-done.12.refs_1_.refs_4_.refs_0_.refs_2_, ...), custom_call_target="tpu_custom_call" | custom-call | bytes 4718592 | tf_op jit(solution)/shard_map/pick/pallas_call | solution.py:60
  1989.1 73.2 %pick.52 = bf16[1536,768]{1,0:T(8,128)(2,1)} custom-call(s32[32]{0:T(128)} %dynamic-slice_bitcast_fusion.tab_ref, bf16[1536,768]{1,0:T(8,128)(2,1)} %collective-permute-done.12.refs_1_.refs_4_.refs_0_.refs_2_, bf16[1536,768]{1,0:T(8,128)(2,1)} %collective-permute-done.16.refs_3_.refs_1_.refs_4_.refs_2_, ...), custom_call_target="tpu_custom_call" | custom-call | bytes 4718592 | tf_op jit(solution)/shard_map/pick/pallas_call | solution.py:60
  2103.2 73.2 %pick.55.lane_ref = bf16[1536,768]{1,0:T(8,128)(2,1)} custom-call(s32[32]{0:T(128)} %dynamic-slice_bitcast_fusion.tab_ref, bf16[2,1,1,1536,768]{4,3,2,1,0:T(8,128)(2,1)} %refs_0_.51, bf16[1536,768]{1,0:T(8,128)(2,1)} %collective-permute-done.12.refs_1_.refs_4_.refs_0_.refs_2_, bf16[1536,768]{1,0:T(8,128)(2,1)} %collective-permute-done.14.refs_5_.refs_3_.refs_2_.refs_1_, ...), custom_call_target="tpu_custom_call" | custom-call | bytes 4718592 | tf_op jit(solution)/shard_map/pick/pallas_call | solution.py:60
  2176.4 73.2 %pick.54 = bf16[1536,768]{1,0:T(8,128)(2,1)} custom-call(s32[32]{0:T(128)} %dynamic-slice_bitcast_fusion.tab_ref, bf16[2,1,1,1536,768]{4,3,2,1,0:T(8,128)(2,1)} %refs_0_.51, bf16[1536,768]{1,0:T(8,128)(2,1)} %collective-permute-done.18.refs_2_.refs_1_.refs_4_.refs_3_, bf16[1536,768]{1,0:T(8,128)(2,1)} %collective-permute-done.20.refs_2_.refs_4_.refs_3_.refs_5_, ...), custom_call_target="tpu_custom_call" | custom-call | bytes 4718592 | tf_op jit(solution)/shard_map/pick/pallas_call | solution.py:60
  2288.6 73.2 %pick.57.lane_ref = bf16[1536,768]{1,0:T(8,128)(2,1)} custom-call(s32[32]{0:T(128)} %dynamic-slice_bitcast_fusion.tab_ref, bf16[2,1,1,1536,768]{4,3,2,1,0:T(8,128)(2,1)} %refs_0_.50, bf16[1536,768]{1,0:T(8,128)(2,1)} %collective-permute-done.8.refs_3_.refs_4_.refs_1_.refs_0_.refs_2_, ...), custom_call_target="tpu_custom_call" | custom-call | bytes 4718592 | tf_op jit(solution)/shard_map/pick/pallas_call | solution.py:60
  2361.8 73.2 %pick.56 = bf16[1536,768]{1,0:T(8,128)(2,1)} custom-call(s32[32]{0:T(128)} %dynamic-slice_bitcast_fusion.tab_ref, bf16[1536,768]{1,0:T(8,128)(2,1)} %collective-permute-done.22.refs_0_.refs_4_.refs_3_.refs_5_), custom_call_target="tpu_custom_call" | custom-call | bytes 4718592 | tf_op jit(solution)/shard_map/pick/pallas_call | solution.py:60
  2450.8 73.3 %pick.59.lane_ref = bf16[1536,768]{1,0:T(8,128)(2,1)} custom-call(s32[32]{0:T(128)} %dynamic-slice_bitcast_fusion.tab_ref, bf16[2,1,1,1536,768]{4,3,2,1,0:T(8,128)(2,1)} %refs_0_.51, bf16[1536,768]{1,0:T(8,128)(2,1)} %collective-permute-done.12.refs_1_.refs_4_.refs_0_.refs_2_, bf16[1536,768]{1,0:T(8,128)(2,1)} %collective-permute-done.18.refs_2_.refs_1_.refs_4_.refs_3_, ...), custom_call_target="tpu_custom_call" | custom-call | bytes 4718592 | tf_op jit(solution)/shard_map/pick/pallas_call | solution.py:60
  2524.1 73.2 %pick.58 = bf16[1536,768]{1,0:T(8,128)(2,1)} custom-call(s32[32]{0:T(128)} %dynamic-slice_bitcast_fusion.tab_ref, bf16[1536,768]{1,0:T(8,128)(2,1)} %collective-permute-done.24.refs_0_.refs_4_), custom_call_target="tpu_custom_call" | custom-call | bytes 4718592 | tf_op jit(solution)/shard_map/pick/pallas_call | solution.py:60
  2664.8 73.3 %pick.60.lane_ref = bf16[1536,768]{1,0:T(8,128)(2,1)} custom-call(s32[32]{0:T(128)} %dynamic-slice_bitcast_fusion.tab_ref, bf16[2,1,1,1536,768]{4,3,2,1,0:T(8,128)(2,1)} %refs_0_.50, bf16[1536,768]{1,0:T(8,128)(2,1)} %collective-permute-done.10.refs_4_.refs_2_.refs_3_.refs_1_, bf16[1536,768]{1,0:T(8,128)(2,1)} %collective-permute-done.12.refs_1_.refs_4_.refs_0_.refs_2_, ...), custom_call_target="tpu_custom_call" | custom-call | bytes 4718592 | tf_op jit(solution)/shard_map/pick/pallas_call | solution.py:60
  2751.6 73.3 %pick.61.lane_ref = bf16[1536,768]{1,0:T(8,128)(2,1)} custom-call(s32[32]{0:T(128)} %dynamic-slice_bitcast_fusion.tab_ref, bf16[2,1,1,1536,768]{4,3,2,1,0:T(8,128)(2,1)} %refs_0_.51, bf16[1536,768]{1,0:T(8,128)(2,1)} %collective-permute-done.14.refs_5_.refs_3_.refs_2_.refs_1_, bf16[1536,768]{1,0:T(8,128)(2,1)} %collective-permute-done.18.refs_2_.refs_1_.refs_4_.refs_3_, ...), custom_call_target="tpu_custom_call" | custom-call | bytes 4718592 | tf_op jit(solution)/shard_map/pick/pallas_call | solution.py:60
  2838.5 73.3 %pick.62.lane_ref = bf16[1536,768]{1,0:T(8,128)(2,1)} custom-call(s32[32]{0:T(128)} %dynamic-slice_bitcast_fusion.tab_ref, bf16[2,1,1,1536,768]{4,3,2,1,0:T(8,128)(2,1)} %refs_0_.50, bf16[1536,768]{1,0:T(8,128)(2,1)} %collective-permute-done.8.refs_3_.refs_4_.refs_1_.refs_0_.refs_2_, ...), custom_call_target="tpu_custom_call" | custom-call | bytes 4718592 | tf_op jit(solution)/shard_map/pick/pallas_call | solution.py:60
  2925.4 73.2 %pick.63.lane_ref = bf16[1536,768]{1,0:T(8,128)(2,1)} custom-call(s32[32]{0:T(128)} %dynamic-slice_bitcast_fusion.tab_ref, bf16[2,1,1,1536,768]{4,3,2,1,0:T(8,128)(2,1)} %refs_0_.51, bf16[1536,768]{1,0:T(8,128)(2,1)} %collective-permute-done.16.refs_3_.refs_1_.refs_4_.refs_2_, bf16[1536,768]{1,0:T(8,128)(2,1)} %collective-permute-done.20.refs_2_.refs_4_.refs_3_.refs_5_, ...), custom_call_target="tpu_custom_call" | custom-call | bytes 4718592 | tf_op jit(solution)/shard_map/pick/pallas_call | solution.py:60
  3012.2 74.7 %all-gather.50.cloned.1.call-done.gathered_ref = bf16[1536,768]{1,0:T(8,128)(2,1)} async-done(((bf16[48,768]{1,0:T(8,128)(2,1)}), bf16[1536,768]{1,0:T(8,128)(2,1)}) %all-gather.50.cloned.1.call-update) | async-done | bytes 2359312 | tf_op jit(solution)/shard_map/all_gather | solution.py:316
  (173 shorter events, 740.9 us)
Async XLA Ops:
  81.0 73.9 %collective-permute-start = (bf16[1536,768]{1,0:T(8,128)(2,1)}, bf16[1536,768]{1,0:T(8,128)(2,1)}, u32[]{:S(2)}, u32[]{:S(2)}) collective-permute-start(bf16[1536,768]{1,0:T(8,128)(2,1)} %pick.32), channel_id=1, source_target_pairs={{0,32},{32,0},{64,96},{96,64},{128,160},{160,128},{192,224},{224,1... | collective-permute-start | bytes 7077896 | tf_op jit(solution)/shard_map/ppermute | solution.py:275
  154.3 75.5 %collective-permute-start.2 = (bf16[1536,768]{1,0:T(8,128)(2,1)}, bf16[1536,768]{1,0:T(8,128)(2,1)}, u32[]{:S(2)}, u32[]{:S(2)}) collective-permute-start(bf16[1536,768]{1,0:T(8,128)(2,1)} %pick.34), channel_id=1, source_target_pairs={{0,32},{32,0},{64,96},{96,64},{128,160},{160,128},{192,224},{224,1... | collective-permute-start | bytes 7077896 | tf_op jit(solution)/shard_map/ppermute | solution.py:275
  228.2 29.4 collective-permute-start.1
  330.8 30.4 collective-permute-start.3
  434.6 30.4 collective-permute-start.4
  538.3 148.4 %collective-permute-start.5 = (bf16[1536,768]{1,0:T(8,128)(2,1)}, bf16[1536,768]{1,0:T(8,128)(2,1)}, u32[]{:S(2)}, u32[]{:S(2)}) collective-permute-start(bf16[1536,768]{1,0:T(8,128)(2,1)} %pick.37.lane_ref), channel_id=1, source_target_pairs={{0,32},{32,0},{64,96},{96,64},{128,160},{160,128},{192,224},{224,1... | collective-permute-start | bytes 7077896 | tf_op jit(solution)/shard_map/ppermute | solution.py:275
  539.0 145.8 %all-to-all-start = ((s32[1,2,8,512,2]{3,4,1,0,2:T(2,128)}), s32[1,2,8,512,2]{3,4,1,0,2:T(2,128)S(1)}, u32[]{:S(2)}, u32[]{:S(2)}) async-start(s32[1,2,8,512,2]{3,4,1,0,2:T(2,128)} %bitcast.35), calls=%async_computation | async-start | bytes 131072 | tf_op jit(solution)/shard_map/all_to_all | solution.py:281
  545.5 254.5 %all-gather.20.cloned.1.call-start = ((), (), s32[]{:S(2)}) async-start(), calls=%async_computation.1 | async-start | bytes 2433024 | tf_op jit(solution)/shard_map/all_gather | solution.py:316
  696.1 345.3 %all-gather.22.cloned.1.call-start = ((), (), s32[]{:S(2)}) async-start(), calls=%async_computation.2 | async-start | bytes 2433024 | tf_op jit(solution)/shard_map/all_gather | solution.py:316
  769.4 30.6 collective-permute-start.6
  887.0 265.5 %all-gather.24.cloned.1.call-start = ((), (), s32[]{:S(2)}) async-start(), calls=%async_computation.3 | async-start | bytes 2433024 | tf_op jit(solution)/shard_map/all_gather | solution.py:316
  960.3 76.5 %collective-permute-start.8 = (bf16[1536,768]{1,0:T(8,128)(2,1)}, bf16[1536,768]{1,0:T(8,128)(2,1)}, u32[]{:S(2)}, u32[]{:S(2)}) collective-permute-start(bf16[1536,768]{1,0:T(8,128)(2,1)} %pick.40), channel_id=1, source_target_pairs={{0,64},{64,128},{128,192},{192,0},{32,224},{96,32},{160,96},{224,1... | collective-permute-start | bytes 7077896 | tf_op jit(solution)/shard_map/ppermute | solution.py:279
  1049.9 342.2 %all-gather.26.cloned.1.call-start = ((), (), s32[]{:S(2)}) async-start(), calls=%async_computation.4 | async-start | bytes 2433024 | tf_op jit(solution)/shard_map/all_gather | solution.py:316
  1239.3 264.0 %all-gather.28.cloned.1.call-start = ((), (), s32[]{:S(2)}) async-start(), calls=%async_computation.5 | async-start | bytes 2433024 | tf_op jit(solution)/shard_map/all_gather | solution.py:316
  1312.6 75.0 %collective-permute-start.12 = (bf16[1536,768]{1,0:T(8,128)(2,1)}, bf16[1536,768]{1,0:T(8,128)(2,1)}, u32[]{:S(2)}, u32[]{:S(2)}) collective-permute-start(bf16[1536,768]{1,0:T(8,128)(2,1)} %pick.44), channel_id=1, source_target_pairs={{0,64},{64,128},{128,192},{192,0},{32,224},{96,32},{160,96},{224,1... | collective-permute-start | bytes 7077896 | tf_op jit(solution)/shard_map/ppermute | solution.py:279
  1400.7 344.1 %all-gather.30.cloned.1.call-start = ((), (), s32[]{:S(2)}) async-start(), calls=%async_computation.6 | async-start | bytes 2433024 | tf_op jit(solution)/shard_map/all_gather | solution.py:316
  1590.5 316.8 %all-gather.32.cloned.1.call-start = ((), (), s32[]{:S(2)}) async-start(), calls=%async_computation.7 | async-start | bytes 2433024 | tf_op jit(solution)/shard_map/all_gather | solution.py:316
  1663.8 76.5 %collective-permute-start.16 = (bf16[1536,768]{1,0:T(8,128)(2,1)}, bf16[1536,768]{1,0:T(8,128)(2,1)}, u32[]{:S(2)}, u32[]{:S(2)}) collective-permute-start(bf16[1536,768]{1,0:T(8,128)(2,1)} %pick.48), channel_id=1, source_target_pairs={{0,64},{64,128},{128,192},{192,0},{32,224},{96,32},{160,96},{224,1... | collective-permute-start | bytes 7077896 | tf_op jit(solution)/shard_map/ppermute | solution.py:279
  1753.4 341.1 %all-gather.34.cloned.1.call-start = ((), (), s32[]{:S(2)}) async-start(), calls=%async_computation.8 | async-start | bytes 2433024 | tf_op jit(solution)/shard_map/all_gather | solution.py:316
  1826.7 75.9 %collective-permute-start.18 = (bf16[1536,768]{1,0:T(8,128)(2,1)}, bf16[1536,768]{1,0:T(8,128)(2,1)}, u32[]{:S(2)}, u32[]{:S(2)}) collective-permute-start(bf16[1536,768]{1,0:T(8,128)(2,1)} %pick.50), channel_id=1, source_target_pairs={{0,64},{64,128},{128,192},{32,224},{96,32},{160,96},{224,160},{1,6... | collective-permute-start | bytes 7077896 | tf_op jit(solution)/shard_map/ppermute | solution.py:279
  1915.8 364.1 %all-gather.36.cloned.1.call-start = ((), (), s32[]{:S(2)}) async-start(), calls=%async_computation.9 | async-start | bytes 2433024 | tf_op jit(solution)/shard_map/all_gather | solution.py:316
  2062.4 32.1 %collective-permute-start.20 = (bf16[1536,768]{1,0:T(8,128)(2,1)}, bf16[1536,768]{1,0:T(8,128)(2,1)}, u32[]{:S(2)}, u32[]{:S(2)}) collective-permute-start(bf16[1536,768]{1,0:T(8,128)(2,1)} %pick.52), channel_id=1, source_target_pairs={{0,64},{64,128},{128,192},{192,0},{32,224},{160,96},{224,160},{1,6... | collective-permute-start | bytes 7077896 | tf_op jit(solution)/shard_map/ppermute | solution.py:279
  2103.1 339.0 %all-gather.38.cloned.1.call-start = ((), (), s32[]{:S(2)}) async-start(), calls=%async_computation.10 | async-start | bytes 2433024 | tf_op jit(solution)/shard_map/all_gather | solution.py:316
  2249.7 30.3 collective-permute-start.22
  2288.5 367.6 %all-gather.40.cloned.1.call-start = ((), (), s32[]{:S(2)}) async-start(), calls=%async_computation.11 | async-start | bytes 2433024 | tf_op jit(solution)/shard_map/all_gather | solution.py:316
  2450.7 292.3 %all-gather.42.cloned.1.call-start = ((), (), s32[]{:S(2)}) async-start(), calls=%async_computation.12 | async-start | bytes 2433024 | tf_op jit(solution)/shard_map/all_gather | solution.py:316
  2597.3 58.8 %collective-permute-start.26 = (bf16[1536,768]{1,0:T(8,128)(2,1)}, bf16[1536,768]{1,0:T(8,128)(2,1)}, u32[]{:S(2)}, u32[]{:S(2)}) collective-permute-start(bf16[1536,768]{1,0:T(8,128)(2,1)} %pick.58), channel_id=1, source_target_pairs={{0,64},{96,32},{1,65},{97,33},{2,66},{98,34},{3,67},{99,35},{4,68}... | collective-permute-start | bytes 7077896 | tf_op jit(solution)/shard_map/ppermute | solution.py:279
  2598.6 57.5 %collective-permute-start.27 = (bf16[1536,768]{1,0:T(8,128)(2,1)}, bf16[1536,768]{1,0:T(8,128)(2,1)}, u32[]{:S(2)}, u32[]{:S(2)}) collective-permute-start(bf16[1536,768]{1,0:T(8,128)(2,1)} %pick.59.lane_ref), channel_id=1, source_target_pairs={{0,32},{32,0},{64,96},{96,64},{128,160},{160,128},{192,224},{224,1... | collective-permute-start | bytes 7077896 | tf_op jit(solution)/shard_map/ppermute | solution.py:275
  2664.7 165.1 %all-gather.44.cloned.1.call-start = ((), (), s32[]{:S(2)}) async-start(), calls=%async_computation.13 | async-start | bytes 2433024 | tf_op jit(solution)/shard_map/all_gather | solution.py:316
  2751.6 165.2 %all-gather.46.cloned.1.call-start = ((), (), s32[]{:S(2)}) async-start(), calls=%async_computation.14 | async-start | bytes 2433024 | tf_op jit(solution)/shard_map/all_gather | solution.py:316
  2838.5 165.1 %all-gather.48.cloned.1.call-start = ((), (), s32[]{:S(2)}) async-start(), calls=%async_computation.15 | async-start | bytes 2433024 | tf_op jit(solution)/shard_map/all_gather | solution.py:316
  2925.3 161.6 %all-gather.50.cloned.1.call-start = ((), (), s32[]{:S(2)}) async-start(), calls=%async_computation.16 | async-start | bytes 2433024 | tf_op jit(solution)/shard_map/all_gather | solution.py:316
  (21 other events, 628.6 us)
Sparse Core Ops, SparseCore 0:
  696.2 76.4 all-gather.19
  887.1 76.3 all-gather.21
  1050.0 76.2 all-gather.23
  1239.4 76.2 all-gather.25
  1400.8 76.4 all-gather.27
  1590.6 76.4 all-gather.29
  1753.5 76.2 all-gather.31
  1916.0 77.3 all-gather.33
  2103.2 76.2 all-gather.35
  2288.7 78.2 all-gather.37
  2450.9 103.4 all-gather.39
  2664.8 74.5 all-gather.41
  2751.7 74.5 all-gather.43
  2838.6 74.5 all-gather.45
  2925.4 74.5 all-gather.47
  3012.3 74.5 all-gather.49

commit v2 on v0

v2 whole, which is shorter than its diff:
```python
import functools

import jax
import jax.numpy as jnp
import numpy as np
from jax import lax
from jax.experimental import pallas as pl
from jax.experimental.pallas import tpu as pltpu
from jax.sharding import PartitionSpec as P

VMEM_LIMIT = 62 * 1024 * 1024
HBM = pl.BlockSpec(memory_space=pltpu.HBM)
SMEM = pl.BlockSpec(memory_space=pltpu.SMEM)
VMEM = pl.BlockSpec(memory_space=pltpu.VMEM)
DIRS = (1, -1)


PACK = 64
PARTS = 2
LEAD = 7
SKIP = 5


def ring_plan(sections, layers, parts, lead, skip):
    chips = sections // 2
    items = layers * parts
    owned = [[i for i in range(items) if (i // parts) % sections // 2 == y] for y in range(chips)]
    held = [[dict.fromkeys(owned[y], 0) for y in range(chips)] for _ in DIRS]
    phases = []
    while any(len(stock) < items for lane in held for stock in lane):
        number = len(phases) + 1
        moves = []
        for lane, step in enumerate(DIRS):
            for y in range(chips):
                target = (y + step) % chips
                options = [i for i, at in held[lane][y].items() if at < number]
                options = [i for i in options if i not in held[lane][target]]
                if options and not (number >= lead + 8 and (number - lead - 7) % skip == 0):
                    moves.append((lane, y, target, min(options)))
        phases.append(moves)
        for lane, y, target, i in moves:
            held[lane][target][i] = number if number < lead else number + 1
    return phases, held


def pick_kernel(rows, places, tab_ref, *refs):
    count = len(refs) - 4
    sources, out_ref, hold_ref, in_sems, out_sems = refs[:count], *refs[count:]
    size = hold_ref.shape[0] // len(rows)
    step = size // 2

    def copies(part, view):
        for half in range(2):
            to = part * size + half * step
            yield pltpu.make_async_copy(
                view.at[pl.ds(half * step, step)],
                hold_ref.at[pl.ds(to, step)],
                in_sems.at[part * 2 + half],
            )

    def view_of(number, start):
        place = places[number]
        return sources[number].at[place + (pl.ds(start, size),)]

    used = 0
    for part, (row, choices) in enumerate(rows):
        choice = tab_ref[row]
        for number, (source, start) in enumerate(choices):

            @pl.when(choice == number)
            def _(part=part, source=source, start=start):
                for copy in copies(part, view_of(source, start)):
                    copy.start()

    for part, (row, choices) in enumerate(rows):
        for half, copy in enumerate(copies(part, view_of(*choices[0]))):
            copy.wait()
            at = pl.ds(part * size + half * step, step)
            number = part * 2 + half
            pltpu.make_async_copy(hold_ref.at[at], out_ref.at[at], out_sems.at[number]).start()
    for part in range(len(rows)):
        for half in range(2):
            at = pl.ds(part * size + half * step, step)
            number = part * 2 + half
            pltpu.make_async_copy(hold_ref.at[at], out_ref.at[at], out_sems.at[number]).wait()


def pick(tab, rows, sources, places, size, width):
    total = size * len(rows)
    return pl.pallas_call(
        functools.partial(pick_kernel, rows, places),
        out_shape=jax.ShapeDtypeStruct((total, width), jnp.bfloat16),
        in_specs=[SMEM] + [HBM] * len(sources),
        out_specs=HBM,
        scratch_shapes=[
            pltpu.VMEM((total, width), jnp.bfloat16),
            pltpu.SemaphoreType.DMA((2 * len(rows),)),
            pltpu.SemaphoreType.DMA((2 * len(rows),)),
        ],
        compiler_params=pltpu.CompilerParams(vmem_limit_bytes=VMEM_LIMIT),
        cost_estimate=pl.CostEstimate(
            flops=0, bytes_accessed=4 * total * width, transcendentals=0
        ),
        name="pick",
    )(tab, *sources)


def unpack_pairs(back):
    low = lax.broadcasted_iota(jnp.int32, (1, 1, 2 * PACK), 2) < PACK
    pairs = back.shape[0] // 2
    split = back.reshape(pairs, 2, 16, 2 * PACK)
    even, odd = split[:, 0], split[:, 1]
    turned_even = pltpu.roll(even, PACK, 2)
    turned_odd = pltpu.roll(odd, PACK, 2)
    left = jnp.where(low, even, turned_odd)
    right = jnp.where(low, turned_even, odd)
    return jnp.concatenate([left[:, 0:8], right[:, 0:8], left[:, 8:16], right[:, 8:16]], axis=1)


def turn_kernel(merge, send, *refs):
    refs = list(refs)
    h_ref = refs.pop(0)
    if merge:
        back_ref, row_ref = refs.pop(0), refs.pop(0)
    if send:
        col_ref = refs.pop(0)
    hnew_ref = refs.pop(0)
    features, tokens = h_ref.shape
    held = h_ref[...]
    if merge:
        tiles = unpack_pairs(back_ref[...].astype(jnp.float32)).astype(jnp.bfloat16)
        offset = lax.broadcasted_iota(jnp.int32, (4 * PACK, tokens), 0)
        first, second = row_ref[0:1, :] - offset, row_ref[1:2, :] - offset
        update = jnp.zeros((32, tokens), jnp.float32)
        for turn in range(tiles.shape[0] // 2):
            base = turn * 4 * PACK
            onehot = jnp.where((first == base) | (second == base), 1.0, 0.0)
            pair = jnp.concatenate([tiles[2 * turn], tiles[2 * turn + 1]], axis=1)
            update += jnp.dot(
                pair, onehot.astype(jnp.bfloat16), preferred_element_type=jnp.float32
            )
        change = update[0:features] * (1.0 / update[features:features + 1])
        held = (held.astype(jnp.float32) + change).astype(jnp.bfloat16)
    hnew_ref[...] = held
    if send:
        out_ref = refs.pop(0)
        offset = lax.broadcasted_iota(jnp.int32, (tokens, 4 * PACK), 1)
        first, second = col_ref[:, 0:1] - offset, col_ref[:, 1:2] - offset
        low = lax.broadcasted_iota(jnp.int32, (8, 2 * PACK), 1) < PACK
        for turn in range(out_ref.shape[0] // 4):
            base = turn * 4 * PACK
            onehot = jnp.where((first == base) | (second == base), 1.0, 0.0)
            found = jnp.dot(held, onehot.astype(jnp.bfloat16), preferred_element_type=jnp.float32)
            for half in range(2):
                tile = found[:, 2 * PACK * half : 2 * PACK * (half + 1)]
                top, middle, bottom = tile[0:8], tile[8:16], tile[16:24]
                even = [jnp.where(low, top, pltpu.roll(middle, PACK, 1)), bottom]
                odd = [jnp.where(low, pltpu.roll(top, PACK, 1), middle), pltpu.roll(bottom, PACK, 1)]
                number = turn * 4 + half * 2
                out_ref[number] = jnp.concatenate(even, axis=0).astype(jnp.bfloat16)
                out_ref[number + 1] = jnp.concatenate(odd, axis=0).astype(jnp.bfloat16)


def run_turn(experts, h, back, rows, cols, before, after):
    features, tokens = h.shape
    merge, send = before is not None, after is not None
    operands, specs = [h], [VMEM]
    shapes, outs = [jax.ShapeDtypeStruct(h.shape, h.dtype)], [VMEM]
    if merge:
        operands += [back, rows]
        specs += [VMEM, plane((8, tokens), before)]
    if send:
        operands += [cols]
        specs += [plane((tokens, 2), after)]
        shapes += [jax.ShapeDtypeStruct((experts, 16, 2 * PACK), jnp.bfloat16)]
        outs += [VMEM]
    return pl.pallas_call(
        functools.partial(turn_kernel, merge, send),
        out_shape=tuple(shapes),
        grid=(1,),
        in_specs=specs,
        out_specs=tuple(outs),
        compiler_params=pltpu.CompilerParams(vmem_limit_bytes=VMEM_LIMIT),
        name="turn",
    )(*operands)


def expert_kernel(
    scal_ref, blocks_ref, gain_ref, router_ref, lane_ref, other_ref, out_ref,
    win_ref, wout_ref, sems,
):
    core = scal_ref[0]

    @pl.when(core == 0)
    def _():
        pltpu.make_async_copy(lane_ref, win_ref, sems.at[0]).start()
        pltpu.make_async_copy(other_ref, wout_ref, sems.at[1]).start()

    @pl.when(core != 0)
    def _():
        pltpu.make_async_copy(other_ref, win_ref, sems.at[0]).start()
        pltpu.make_async_copy(lane_ref, wout_ref, sems.at[1]).start()

    width = win_ref.shape[1]
    groups = blocks_ref.shape[0]
    blocks = blocks_ref[...].astype(jnp.float32)
    top, bottom = blocks[:, 0:8], blocks[:, 8:16]
    parts = [top[:, None], pltpu.roll(top, PACK, 2)[:, None], bottom[:, None]]
    tall = jnp.concatenate(parts, axis=1).reshape(width, 2 * PACK)
    wide = tall.T[0:PACK]
    mean_square = jnp.mean(wide * wide, axis=1, keepdims=True)
    normed = (wide * lax.rsqrt(mean_square + 1e-06) * gain_ref[...]).astype(jnp.bfloat16)
    logit = jnp.sum(normed.astype(jnp.float32) * router_ref[...], axis=1, keepdims=True)
    gate = jax.nn.sigmoid(logit).astype(jnp.bfloat16).astype(jnp.float32)
    pltpu.make_async_copy(lane_ref, win_ref, sems.at[0]).wait()
    pre_act = lax.dot_general(
        normed, win_ref[...], (((1,), (1,)), ((), ())), preferred_element_type=jnp.float32
    )
    active = jax.nn.gelu(pre_act, approximate=True).astype(jnp.bfloat16)
    pltpu.make_async_copy(lane_ref, wout_ref, sems.at[1]).wait()
    output = jnp.dot(active, wout_ref[...], preferred_element_type=jnp.float32)
    weighted = output * gate
    spread = jnp.broadcast_to(gate, (PACK, 2 * PACK))
    zeros = jnp.zeros_like(weighted)
    tall = jnp.concatenate([weighted, zeros], axis=0).T.reshape(groups, 3, 8, 2 * PACK)
    gates = jnp.concatenate([spread, jnp.zeros_like(spread)], axis=0).T[0:8]
    gates = jnp.broadcast_to(pltpu.roll(gates, PACK, 1)[None], (groups, 8, 2 * PACK))
    low = lax.broadcasted_iota(jnp.int32, (1, 1, 2 * PACK), 2) < PACK
    first = jnp.where(low, tall[:, 0], pltpu.roll(tall[:, 1], PACK, 2))
    second = jnp.where(low, tall[:, 2], gates)
    out_ref[...] = jnp.concatenate([first, second], axis=1).astype(jnp.bfloat16)


def run_expert(layer, scal, blocks, gains, routers, lane_w, other_w):
    hidden, width = lane_w.shape
    return pl.pallas_call(
        expert_kernel,
        out_shape=jax.ShapeDtypeStruct(blocks.shape, jnp.bfloat16),
        grid=(1,),
        in_specs=[SMEM, VMEM, plane((1, width), layer), plane((1, width), layer), HBM, HBM],
        out_specs=VMEM,
        scratch_shapes=[
            pltpu.VMEM((hidden, width), jnp.bfloat16),
            pltpu.VMEM((hidden, width), jnp.bfloat16),
            pltpu.SemaphoreType.DMA((2,)),
        ],
        compiler_params=pltpu.CompilerParams(vmem_limit_bytes=VMEM_LIMIT),
        cost_estimate=pl.CostEstimate(
            flops=4 * PACK * hidden * width, bytes_accessed=4 * hidden * width, transcendentals=0
        ),
        name="expert",
    )(scal, blocks, gains, routers, lane_w, other_w)


def plane(shape, *lead):
    return pl.BlockSpec((None,) * len(lead) + shape, lambda i: lead + (0,) * len(shape))


def place_tokens(routes, experts):
    tokens = routes.shape[1]
    ids = jnp.arange(experts, dtype=jnp.int32)
    first = routes[:, :, 0:1] == ids
    second = routes[:, :, 1:2] == ids
    named = (first | second).astype(jnp.bfloat16)
    earlier = jnp.tril(jnp.ones((tokens, tokens), jnp.bfloat16), -1)
    rank = jnp.einsum("ut,lte->lue", earlier, named, preferred_element_type=jnp.float32)
    rank = rank.astype(jnp.int32) + ids * PACK
    slot_first = jnp.sum(jnp.where(first, rank, 0), axis=2)
    slot_second = jnp.sum(jnp.where(second, rank, 0), axis=2)
    cols = jnp.stack([slot_first, slot_second], axis=2)
    blank = jnp.zeros_like(slot_first)
    rows = jnp.stack([slot_first, slot_second] + [blank] * 6, axis=1)
    return cols, rows


def join(*values):
    return lax.optimization_barrier(values)


def local(inputs, routes, norm_gains, routers, expert_in, expert_out):
    sections = lax.axis_size("section")
    experts = lax.axis_size("expert")
    section_pos = lax.axis_index("section")
    repeats, _, _, hidden, width = expert_in.shape
    layers = repeats * sections
    phases, held = ring_plan(sections, layers, PARTS, LEAD, SKIP)
    size = hidden // PARTS
    scal = jnp.stack([section_pos % 2, section_pos]).astype(jnp.int32)

    buffers = {("in", r): (expert_in, (r, 0, 0)) for r in range(repeats)}
    buffers.update({("out", r): (expert_out, (r, 0, 0)) for r in range(repeats)})
    every = [(lane, y) for lane in range(2) for y in range(sections // 2)]
    table, wanted = [], []

    def source_of(lane, y, i):
        q, part = i // PARTS, i % PARTS
        if q % sections // 2 != y:
            return ("ring", held[lane][y][i]), 0
        name = ("in", "out")[lane] if q % 2 == lane else "swapped"
        return (name, q // sections), part * size

    def add_pick(by_section):
        choices = sorted(set(by_section.values()))
        table.append([choices.index(by_section.get(s, choices[0])) for s in range(sections)])
        wanted.append(choices)
        return len(table) - 1

    swap_rows = [
        [
            add_pick({2 * y + lane: ((("out", "in")[lane], r), part * size) for lane, y in every})
            for part in range(PARTS)
        ]
        for r in range(repeats)
    ]
    ring_rows = [
        [add_pick({2 * y + lane: source_of(lane, y, i) for lane, y, _, i in moves})] if moves else []
        for moves in phases
    ]
    layer_rows = [
        [
            add_pick({2 * y + lane: source_of(lane, y, q * PARTS + part) for lane, y in every})
            for part in range(PARTS)
        ]
        for q in range(layers)
    ]
    tab = jnp.asarray(np.array(table, np.int32).T)[section_pos]

    def picked(rows, tab):
        names = sorted({name for row in rows for name, _ in wanted[row]})
        found = [buffers[name] for name in names]
        plan = tuple(
            (row, tuple((names.index(name), start) for name, start in wanted[row])) for row in rows
        )
        return pick(tab, plan, [array for array, _ in found], [place for _, place in found], size, width)

    def swapped(value):
        return lax.ppermute(value, "section", [(s, s ^ 1) for s in range(sections)])

    def ring(phase, tab):
        if phase > len(phases) or not phases[phase - 1]:
            return None
        pairs = [(2 * y + lane, 2 * target + lane) for lane, y, target, _ in phases[phase - 1]]
        return lax.ppermute(picked(ring_rows[phase - 1], tab), "section", pairs)

    def arrival(q):
        parts = range(q * PARTS, (q + 1) * PARTS)
        return max(stock[i] for lane in held for stock in lane for i in parts)

    mine = lax.all_to_all(routes[:, 0], "section", split_axis=1, concat_axis=0, tiled=False)
    mine = jnp.transpose(mine, (1, 0, 2, 3)).reshape(layers, -1, 2)
    cols, rows = place_tokens(mine, experts)
    small = jnp.stack([norm_gains[:, 0], routers[:, 0, 0]])
    small = jnp.broadcast_to(small[None], (sections,) + small.shape)
    small = lax.all_to_all(small, "section", split_axis=0, concat_axis=0, tiled=True)
    small = jnp.transpose(small, (1, 2, 0, 3)).reshape(2, layers, 1, width).astype(jnp.float32)
    gains, gate_rows = small[0], small[1]
    h = jnp.transpose(inputs[0], (1, 0))

    buffers[("swapped", 0)] = (swapped(picked(swap_rows[0], tab)), ())
    later = swapped(picked(swap_rows[1], tab))
    flying = None
    for phase in range(1, LEAD):
        arrived = ring(phase, tab)
        if phase == 1:
            arrived, later, tab = join(arrived, later, tab)
            buffers[("swapped", 1)] = (later, ())
        else:
            arrived, tab = join(arrived, tab)
        buffers[("ring", phase)] = (arrived, ())
    tab, cols, rows, gains, gate_rows, h = join(tab, cols, rows, gains, gate_rows, h)

    def run_phase(phase, value, tab, flying, wish):
        value, tab = join(value, tab)
        sent = lax.all_to_all(value, "expert", split_axis=0, concat_axis=0, tiled=True)
        lane_w = other_w = None
        if wish is not None:
            lane_w = picked(layer_rows[wish], tab)
            other_w = swapped(lane_w)
        started = ring(phase, tab)
        bundle = [v for v in (sent, lane_w, other_w, tab, flying) if v is not None]
        bundle = list(join(*bundle))
        sent = bundle.pop(0)
        if wish is not None:
            lane_w, other_w = bundle.pop(0), bundle.pop(0)
        tab = bundle.pop(0)
        if flying is not None:
            buffers[("ring", phase)] = (bundle.pop(0), ())
        return sent, tab, started, lane_w, other_w

    back = None
    for q in range(layers):
        first, second = LEAD + 2 * q, LEAD + 2 * q + 1
        h, blocks = run_turn(
            experts, h, back, rows, cols, q - 1 if q else None, q
        )
        wish = q if arrival(q) < first else None
        blocks, tab, flying, lane_w, other_w = run_phase(first, blocks, tab, flying, wish)
        if wish is None:
            lane_w = picked(layer_rows[q], tab)
            other_w = swapped(lane_w)
        back = run_expert(q, scal, blocks, gains, gate_rows, lane_w, other_w)
        back, tab, flying, _, _ = run_phase(second, back, tab, flying, None)

    (h,) = run_turn(experts, h, back, rows, cols, layers - 1, None)
    return jnp.transpose(h, (1, 0))[None]


def solution(mesh):
    return jax.shard_map(
        local,
        mesh=mesh,
        in_specs=(
            P("section", None, "expert"),
            P(None, "section", None, None, None),
            P(None, "section", None),
            P(None, "section", "expert", None),
            P(None, "section", "expert", None, None),
            P(None, "section", "expert", None, None),
        ),
        out_specs=P("section", None, "expert"),
        check_vma=False,
    )
```

time: 1800 us -> 936 us (0.52)
  local copies, waits for them, and re-layouts: 557 us -> 20.9 us
  starting transfers between devices: 443 us -> 127 us
  Pallas kernels: 0 us -> 278 us
  blocking collectives: 0 us -> 265 us
  other arithmetic: 245 us -> 1.48 us
  waiting for transfers between devices: 451 us -> 228 us
  matrix products: 85.5 us -> 0.89 us
    gather x92 -> x0, local copies, waits for them, and re-layouts: 314 us -> none  [the longest x23 156 us: combine(): weights = gate_grid.reshape(-1)[flat_index].astype(jnp.float32)]
    all_to_all x69 -> x16, starting transfers between devices: 379 us -> 78.5 us  [the longest x14 63 us: run_phase(): lax.all_to_all(value, 'expert', split_axis=0, concat_axis=0, tiled=True)]
    pallas_call x0 -> x79, Pallas kernels: none -> 278 us  [the longest x46 138 us: pick(): pl.pallas_call(functools.partial(pick_kernel, rows, places), out_shape=ja...]
    all_to_all x0 -> x18, blocking collectives: none -> 265 us  [run_phase(): lax.all_to_all(value, 'expert', split_axis=0, concat_axis=0, tiled=True)]
    all_to_all x69 -> x16, waiting for transfers between devices: 344 us -> 133 us  [the longest x14 124 us: run_phase(): lax.all_to_all(value, 'expert', split_axis=0, concat_axis=0, tiled=True)]
    another operation x46 -> x4, other arithmetic: 208 us -> 1.44 us  [the longest x1 0.82 us: place_tokens(): rows = jnp.stack([slot_first, slot_second] + [blank] * 6, axis=1)]
    scatter x23 -> x0, local copies, waits for them, and re-layouts: 99.3 us -> none  [place_rows(): slot_table = jnp.full((experts * capacity,), -1, jnp.int32).at[flat_ids *...]
    dot_general x46 -> x1, matrix products: 85.5 us -> 0.89 us  [place_tokens(): jnp.einsum('ut,lte->lue', earlier, named, preferred_element_type=jnp.floa...]
  transfers between devices with their start and end apart: 115 -> 62, of which waited for: 92 -> 30; matrix products, arithmetic and copies ran while one was open for 23% -> 1% of each run, Pallas kernels for 0% -> 14%
where the time goes in v2:
time: 936 us; the launch traced here: 923 us
  Pallas kernels  278 us (30%)
  blocking collectives  265 us (28%)
  waiting for transfers between devices  228 us (24%)
  starting transfers between devices  127 us (14%)
  local copies, waits for them, and re-layouts  20.9 us (2%)
    all_to_all x18, blocking collectives, run_phase(): lax.all_to_all(value, 'expert', split_axis=0, concat_axis=0, tiled=True)  265 us
    pallas_call x46, Pallas kernels, pick(): pl.pallas_call(functools.partial(pick_kernel, rows, places), out_shape=ja...  138 us
    all_to_all x14, waiting for transfers between devices, run_phase(): lax.all_to_all(value, 'expert', split_axis=0, concat_axis=0, tiled=True)  124 us
    ppermute x28, waiting for transfers between devices, ring(): return lax.ppermute(picked(ring_rows[phase - 1], tab), 'section', pairs)  93.1 us
    pallas_call x16, Pallas kernels, run_expert(): pl.pallas_call(expert_kernel, out_shape=jax.ShapeDtypeStruct(blocks.shape...  79.7 us
    all_to_all x14, starting transfers between devices, run_phase(): lax.all_to_all(value, 'expert', split_axis=0, concat_axis=0, tiled=True)  63 us
    pallas_call x17, Pallas kernels, run_turn(): pl.pallas_call(functools.partial(turn_kernel, merge, send), out_shape=tup...  60.4 us
    ppermute x28, starting transfers between devices, ring(): return lax.ppermute(picked(ring_rows[phase - 1], tab), 'section', pairs)  42.5 us
  transfers between devices with their start and end apart: 62, of which 30 were waited for; matrix products, arithmetic and copies ran while one was open for 1% of the time, Pallas kernels for 14%

profile of v2, /device:TPU:8, one launch (start us, length us, event | category | flops | bytes accessed | tf_op | source)
XLA Modules:
  0.0 923.2 jit_solution(220417674883166598)
XLA Ops:
  13.8 15.0 %collective-permute-done.1.refs_1_.refs_0_ = bf16[768,768]{1,0:T(8,128)(2,1)S(1)} collective-permute-done((bf16[768,768]{1,0:T(8,128)(2,1)}, bf16[768,768]{1,0:T(8,128)(2,1)S(1)}, u32[]{:S(2)}, u32[]{:S(2)}) %collective-permute-start.1) | collective-permute-done | bytes 1179680 | tf_op jit(solution)/shard_map/ppermute | solution.py:343
  34.1 16.2 %collective-permute-done.3.refs_1_.refs_2_ = bf16[768,768]{1,0:T(8,128)(2,1)S(1)} collective-permute-done((bf16[768,768]{1,0:T(8,128)(2,1)}, bf16[768,768]{1,0:T(8,128)(2,1)S(1)}, u32[]{:S(2)}, u32[]{:S(2)}) %collective-permute-start.3) | collective-permute-done | bytes 1179680 | tf_op jit(solution)/shard_map/ppermute | solution.py:343
  54.5 17.4 %collective-permute-done.4.refs_2_.refs_3_.refs_1_ = bf16[768,768]{1,0:T(8,128)(2,1)S(1)} collective-permute-done((bf16[768,768]{1,0:T(8,128)(2,1)}, bf16[768,768]{1,0:T(8,128)(2,1)S(1)}, u32[]{:S(2)}, u32[]{:S(2)}) %collective-permute-start.4) | collective-permute-done | bytes 1179680 | tf_op jit(solution)/shard_map/ppermute | solution.py:343
  75.8 17.6 %collective-permute-done.5.refs_2_.refs_4_.refs_3_ = bf16[768,768]{1,0:T(8,128)(2,1)S(1)} collective-permute-done((bf16[768,768]{1,0:T(8,128)(2,1)}, bf16[768,768]{1,0:T(8,128)(2,1)S(1)}, u32[]{:S(2)}, u32[]{:S(2)}) %collective-permute-start.5) | collective-permute-done | bytes 1179680 | tf_op jit(solution)/shard_map/ppermute | solution.py:343
  152.6 10.0 %all-to-all-start.2 = ((bf16[32,16,128]{2,1,0:T(8,128)(2,1)}), bf16[32,16,128]{2,1,0:T(8,128)(2,1)S(1)}, u32[]{:S(2)}, u32[]{:S(2)}) async-start(bf16[32,16,128]{2,1,0:T(8,128)(2,1)} %get-tuple-element.245), calls=%async_computation.2 | async-start | bytes 262144 | tf_op jit(solution)/shard_map/all_to_all | solution.py:374
  163.3 9.7 %all-to-all-done.2.blocks_ref = bf16[32,16,128]{2,1,0:T(8,128)(2,1)S(1)} async-done(((bf16[32,16,128]{2,1,0:T(8,128)(2,1)}), bf16[32,16,128]{2,1,0:T(8,128)(2,1)S(1)}, u32[]{:S(2)}, u32[]{:S(2)}) %all-to-all-start.2) | async-done | bytes 131104 | tf_op jit(solution)/shard_map/all_to_all | solution.py:374
  183.4 11.0 %all-to-all-done.3.refs_1_ = bf16[32,16,128]{2,1,0:T(8,128)(2,1)S(1)} async-done(((bf16[32,16,128]{2,1,0:T(8,128)(2,1)}), bf16[32,16,128]{2,1,0:T(8,128)(2,1)S(1)}, u32[]{:S(2)}, u32[]{:S(2)}) %all-to-all-start.3) | async-done | bytes 131104 | tf_op jit(solution)/shard_map/all_to_all | solution.py:374
  210.7 14.8 %all_to_all.180.blocks_ref = bf16[32,16,128]{2,1,0:T(8,128)(2,1)} all-to-all(bf16[32,16,128]{2,1,0:T(8,128)(2,1)S(1)} %copy-done.38), channel_id=1, replica_groups=mesh['section'=8,'expert'=32] {'expert'}, dimensions={0} | all-to-all | bytes 262144 | tf_op jit(solution)/shard_map/all_to_all | solution.py:374
  234.5 10.3 %all-to-all-done.5.refs_1_ = bf16[32,16,128]{2,1,0:T(8,128)(2,1)S(1)} async-done(((bf16[32,16,128]{2,1,0:T(8,128)(2,1)}), bf16[32,16,128]{2,1,0:T(8,128)(2,1)S(1)}, u32[]{:S(2)}, u32[]{:S(2)}) %all-to-all-start.5) | async-done | bytes 131104 | tf_op jit(solution)/shard_map/all_to_all | solution.py:374
  284.4 10.4 %all-to-all-done.7.refs_1_ = bf16[32,16,128]{2,1,0:T(8,128)(2,1)S(1)} async-done(((bf16[32,16,128]{2,1,0:T(8,128)(2,1)}), bf16[32,16,128]{2,1,0:T(8,128)(2,1)S(1)}, u32[]{:S(2)}, u32[]{:S(2)}) %all-to-all-start.7) | async-done | bytes 131104 | tf_op jit(solution)/shard_map/all_to_all | solution.py:374
  299.2 14.9 %all_to_all.181.blocks_ref = bf16[32,16,128]{2,1,0:T(8,128)(2,1)} all-to-all(bf16[32,16,128]{2,1,0:T(8,128)(2,1)} %get-tuple-element.289), channel_id=1, replica_groups=mesh['section'=8,'expert'=32] {'expert'}, dimensions={0} | all-to-all | bytes 262144 | tf_op jit(solution)/shard_map/all_to_all | solution.py:374
  382.2 10.7 %all-to-all-done.11.refs_1_ = bf16[32,16,128]{2,1,0:T(8,128)(2,1)S(1)} async-done(((bf16[32,16,128]{2,1,0:T(8,128)(2,1)}), bf16[32,16,128]{2,1,0:T(8,128)(2,1)S(1)}, u32[]{:S(2)}, u32[]{:S(2)}) %all-to-all-start.11) | async-done | bytes 131104 | tf_op jit(solution)/shard_map/all_to_all | solution.py:374
  397.3 14.9 %all_to_all.182.blocks_ref = bf16[32,16,128]{2,1,0:T(8,128)(2,1)} all-to-all(bf16[32,16,128]{2,1,0:T(8,128)(2,1)} %get-tuple-element.315), channel_id=1, replica_groups=mesh['section'=8,'expert'=32] {'expert'}, dimensions={0} | all-to-all | bytes 262144 | tf_op jit(solution)/shard_map/all_to_all | solution.py:374
  453.2 14.7 %all_to_all.183.blocks_ref = bf16[32,16,128]{2,1,0:T(8,128)(2,1)} all-to-all(bf16[32,16,128]{2,1,0:T(8,128)(2,1)S(1)} %copy-done.40), channel_id=1, replica_groups=mesh['section'=8,'expert'=32] {'expert'}, dimensions={0} | all-to-all | bytes 262144 | tf_op jit(solution)/shard_map/all_to_all | solution.py:374
  473.8 15.0 %all_to_all.184.refs_1_ = bf16[32,16,128]{2,1,0:T(8,128)(2,1)} all-to-all(bf16[32,16,128]{2,1,0:T(8,128)(2,1)} %expert.22), channel_id=1, replica_groups=mesh['section'=8,'expert'=32] {'expert'}, dimensions={0} | all-to-all | bytes 262144 | tf_op jit(solution)/shard_map/all_to_all | solution.py:374
  509.6 14.9 %all_to_all.185.blocks_ref = bf16[32,16,128]{2,1,0:T(8,128)(2,1)} all-to-all(bf16[32,16,128]{2,1,0:T(8,128)(2,1)S(1)} %copy-done.34), channel_id=1, replica_groups=mesh['section'=8,'expert'=32] {'expert'}, dimensions={0} | all-to-all | bytes 262144 | tf_op jit(solution)/shard_map/all_to_all | solution.py:374
  533.4 10.3 %all-to-all-done.17.refs_1_ = bf16[32,16,128]{2,1,0:T(8,128)(2,1)S(1)} async-done(((bf16[32,16,128]{2,1,0:T(8,128)(2,1)}), bf16[32,16,128]{2,1,0:T(8,128)(2,1)S(1)}, u32[]{:S(2)}, u32[]{:S(2)}) %all-to-all-start.17) | async-done | bytes 131104 | tf_op jit(solution)/shard_map/all_to_all | solution.py:374
  561.6 14.1 %all_to_all.186.blocks_ref = bf16[32,16,128]{2,1,0:T(8,128)(2,1)} all-to-all(bf16[32,16,128]{2,1,0:T(8,128)(2,1)S(1)} %copy-done.37), channel_id=1, replica_groups=mesh['section'=8,'expert'=32] {'expert'}, dimensions={0} | all-to-all | bytes 262144 | tf_op jit(solution)/shard_map/all_to_all | solution.py:374
  585.5 9.7 %all-to-all-done.19.refs_1_ = bf16[32,16,128]{2,1,0:T(8,128)(2,1)S(1)} async-done(((bf16[32,16,128]{2,1,0:T(8,128)(2,1)}), bf16[32,16,128]{2,1,0:T(8,128)(2,1)S(1)}, u32[]{:S(2)}, u32[]{:S(2)}) %all-to-all-start.19) | async-done | bytes 131104 | tf_op jit(solution)/shard_map/all_to_all | solution.py:374
  610.2 14.3 %all_to_all.187.blocks_ref = bf16[32,16,128]{2,1,0:T(8,128)(2,1)} all-to-all(bf16[32,16,128]{2,1,0:T(8,128)(2,1)S(1)} %copy-done.42), channel_id=1, replica_groups=mesh['section'=8,'expert'=32] {'expert'}, dimensions={0} | all-to-all | bytes 262144 | tf_op jit(solution)/shard_map/all_to_all | solution.py:374
  634.2 10.5 %all-to-all-done.21.refs_1_ = bf16[32,16,128]{2,1,0:T(8,128)(2,1)S(1)} async-done(((bf16[32,16,128]{2,1,0:T(8,128)(2,1)}), bf16[32,16,128]{2,1,0:T(8,128)(2,1)S(1)}, u32[]{:S(2)}, u32[]{:S(2)}) %all-to-all-start.21) | async-done | bytes 131104 | tf_op jit(solution)/shard_map/all_to_all | solution.py:374
  661.9 14.6 %all_to_all.188.blocks_ref = bf16[32,16,128]{2,1,0:T(8,128)(2,1)} all-to-all(bf16[32,16,128]{2,1,0:T(8,128)(2,1)S(1)} %copy-done.39), channel_id=1, replica_groups=mesh['section'=8,'expert'=32] {'expert'}, dimensions={0} | all-to-all | bytes 262144 | tf_op jit(solution)/shard_map/all_to_all | solution.py:374
  685.5 10.4 %all-to-all-done.23.refs_1_ = bf16[32,16,128]{2,1,0:T(8,128)(2,1)S(1)} async-done(((bf16[32,16,128]{2,1,0:T(8,128)(2,1)}), bf16[32,16,128]{2,1,0:T(8,128)(2,1)S(1)}, u32[]{:S(2)}, u32[]{:S(2)}) %all-to-all-start.23) | async-done | bytes 131104 | tf_op jit(solution)/shard_map/all_to_all | solution.py:374
  707.2 14.7 %all_to_all.189.blocks_ref = bf16[32,16,128]{2,1,0:T(8,128)(2,1)} all-to-all(bf16[32,16,128]{2,1,0:T(8,128)(2,1)S(1)} %copy-done.43), channel_id=1, replica_groups=mesh['section'=8,'expert'=32] {'expert'}, dimensions={0} | all-to-all | bytes 262144 | tf_op jit(solution)/shard_map/all_to_all | solution.py:374
  727.0 15.0 %all_to_all.190.refs_1_ = bf16[32,16,128]{2,1,0:T(8,128)(2,1)} all-to-all(bf16[32,16,128]{2,1,0:T(8,128)(2,1)} %expert.27), channel_id=1, replica_groups=mesh['section'=8,'expert'=32] {'expert'}, dimensions={0} | all-to-all | bytes 262144 | tf_op jit(solution)/shard_map/all_to_all | solution.py:374
  758.8 14.0 %all_to_all.191.blocks_ref = bf16[32,16,128]{2,1,0:T(8,128)(2,1)} all-to-all(bf16[32,16,128]{2,1,0:T(8,128)(2,1)S(1)} %copy-done.36), channel_id=1, replica_groups=mesh['section'=8,'expert'=32] {'expert'}, dimensions={0} | all-to-all | bytes 262144 | tf_op jit(solution)/shard_map/all_to_all | solution.py:374
  802.0 14.4 %all_to_all.192.blocks_ref = bf16[32,16,128]{2,1,0:T(8,128)(2,1)} all-to-all(bf16[32,16,128]{2,1,0:T(8,128)(2,1)S(1)} %copy-done.44), channel_id=1, replica_groups=mesh['section'=8,'expert'=32] {'expert'}, dimensions={0} | all-to-all | bytes 262144 | tf_op jit(solution)/shard_map/all_to_all | solution.py:374
  821.4 15.2 %all_to_all.193.refs_1_ = bf16[32,16,128]{2,1,0:T(8,128)(2,1)} all-to-all(bf16[32,16,128]{2,1,0:T(8,128)(2,1)} %expert.29), channel_id=1, replica_groups=mesh['section'=8,'expert'=32] {'expert'}, dimensions={0} | all-to-all | bytes 262144 | tf_op jit(solution)/shard_map/all_to_all | solution.py:374
  843.8 14.8 %all_to_all.194.blocks_ref = bf16[32,16,128]{2,1,0:T(8,128)(2,1)} all-to-all(bf16[32,16,128]{2,1,0:T(8,128)(2,1)S(1)} %copy-done.41), channel_id=1, replica_groups=mesh['section'=8,'expert'=32] {'expert'}, dimensions={0} | all-to-all | bytes 262144 | tf_op jit(solution)/shard_map/all_to_all | solution.py:374
  863.5 14.9 %all_to_all.195.refs_1_ = bf16[32,16,128]{2,1,0:T(8,128)(2,1)} all-to-all(bf16[32,16,128]{2,1,0:T(8,128)(2,1)} %expert.30), channel_id=1, replica_groups=mesh['section'=8,'expert'=32] {'expert'}, dimensions={0} | all-to-all | bytes 262144 | tf_op jit(solution)/shard_map/all_to_all | solution.py:374
  885.6 14.8 %all_to_all.196.blocks_ref = bf16[32,16,128]{2,1,0:T(8,128)(2,1)} all-to-all(bf16[32,16,128]{2,1,0:T(8,128)(2,1)S(1)} %copy-done.35), channel_id=1, replica_groups=mesh['section'=8,'expert'=32] {'expert'}, dimensions={0} | all-to-all | bytes 262144 | tf_op jit(solution)/shard_map/all_to_all | solution.py:374
  905.3 14.9 %all_to_all.197.refs_1_ = bf16[32,16,128]{2,1,0:T(8,128)(2,1)} all-to-all(bf16[32,16,128]{2,1,0:T(8,128)(2,1)} %expert.31), channel_id=1, replica_groups=mesh['section'=8,'expert'=32] {'expert'}, dimensions={0} | all-to-all | bytes 262144 | tf_op jit(solution)/shard_map/all_to_all | solution.py:374
  (309 shorter events, 487.2 us)
Async XLA Ops:
  97.2 18.0 %collective-permute-start.6 = (bf16[768,768]{1,0:T(8,128)(2,1)}, bf16[768,768]{1,0:T(8,128)(2,1)S(1)}, u32[]{:S(2)}, u32[]{:S(2)}) collective-permute-start(bf16[768,768]{1,0:T(8,128)(2,1)} %pick.52), channel_id=1, source_target_pairs={{0,64},{64,128},{128,192},{192,0},{32,224},{96,32},{160,96},{224,1... | collective-permute-start | bytes 3538952 | tf_op jit(solution)/shard_map/ppermute | solution.py:343
  98.0 21.1 %all-to-all-start.1 = ((bf16[8,2,2,768]{3,1,2,0:T(2,128)(2,1)}), bf16[8,2,2,768]{3,1,2,0:T(2,128)(2,1)S(1)}, u32[]{:S(2)}, u32[]{:S(2)}) async-start(bf16[8,2,2,768]{3,1,2,0:T(2,128)(2,1)} %broadcast_in_dim.27), calls=%async_computation.1 | async-start | bytes 98304 | tf_op jit(solution)/shard_map/all_to_all | solution.py:354
  119.0 20.2 %collective-permute-start.7 = (bf16[768,768]{1,0:T(8,128)(2,1)}, bf16[768,768]{1,0:T(8,128)(2,1)S(1)}, u32[]{:S(2)}, u32[]{:S(2)}) collective-permute-start(bf16[768,768]{1,0:T(8,128)(2,1)} %pick.53), channel_id=1, source_target_pairs={{0,64},{64,128},{128,192},{192,0},{32,224},{96,32},{160,96},{224,1... | collective-permute-start | bytes 3538952 | tf_op jit(solution)/shard_map/ppermute | solution.py:343
  119.1 18.3 %all-to-all-start = ((s32[1,2,8,512,2]{3,4,1,0,2:T(2,128)}), s32[1,2,8,512,2]{3,4,1,0,2:T(2,128)S(1)}, u32[]{:S(2)}, u32[]{:S(2)}) async-start(s32[1,2,8,512,2]{3,4,1,0,2:T(2,128)} %bitcast.43), calls=%async_computation | async-start | bytes 131072 | tf_op jit(solution)/shard_map/all_to_all | solution.py:349
  148.0 25.0 %collective-permute-start.8 = (bf16[1536,768]{1,0:T(8,128)(2,1)}, bf16[1536,768]{1,0:T(8,128)(2,1)}, u32[]{:S(2)}, u32[]{:S(2)}) collective-permute-start(bf16[1536,768]{1,0:T(8,128)(2,1)} %pick.54.lane_ref), channel_id=1, source_target_pairs={{0,32},{32,0},{64,96},{96,64},{128,160},{160,128},{192,224},{224,1... | collective-permute-start | bytes 7077896 | tf_op jit(solution)/shard_map/ppermute | solution.py:337
  150.9 32.4 %collective-permute-start.9 = (bf16[768,768]{1,0:T(8,128)(2,1)}, bf16[768,768]{1,0:T(8,128)(2,1)S(1)}, u32[]{:S(2)}, u32[]{:S(2)}) collective-permute-start(bf16[768,768]{1,0:T(8,128)(2,1)} %pick.55), channel_id=1, source_target_pairs={{0,64},{64,128},{128,192},{192,0},{32,224},{96,32},{160,96},{224,1... | collective-permute-start | bytes 3538952 | tf_op jit(solution)/shard_map/ppermute | solution.py:343
  152.6 20.3 %all-to-all-start.2 = ((bf16[32,16,128]{2,1,0:T(8,128)(2,1)}), bf16[32,16,128]{2,1,0:T(8,128)(2,1)S(1)}, u32[]{:S(2)}, u32[]{:S(2)}) async-start(bf16[32,16,128]{2,1,0:T(8,128)(2,1)} %get-tuple-element.245), calls=%async_computation.2 | async-start | bytes 262144 | tf_op jit(solution)/shard_map/all_to_all | solution.py:374
  202.0 23.5 %collective-permute-start.10 = (bf16[1536,768]{1,0:T(8,128)(2,1)}, bf16[1536,768]{1,0:T(8,128)(2,1)}, u32[]{:S(2)}, u32[]{:S(2)}) collective-permute-start(bf16[1536,768]{1,0:T(8,128)(2,1)} %pick.56.lane_ref), channel_id=1, source_target_pairs={{0,32},{32,0},{64,96},{96,64},{128,160},{160,128},{192,224},{224,1... | collective-permute-start | bytes 7077896 | tf_op jit(solution)/shard_map/ppermute | solution.py:337
  205.0 20.6 %collective-permute-start.11 = (bf16[768,768]{1,0:T(8,128)(2,1)}, bf16[768,768]{1,0:T(8,128)(2,1)S(1)}, u32[]{:S(2)}, u32[]{:S(2)}) collective-permute-start(bf16[768,768]{1,0:T(8,128)(2,1)} %pick.57), channel_id=1, source_target_pairs={{0,64},{64,128},{128,192},{192,0},{32,224},{96,32},{160,96},{224,1... | collective-permute-start | bytes 3538952 | tf_op jit(solution)/shard_map/ppermute | solution.py:343
  207.9 26.6 %collective-permute-start.12 = (bf16[768,768]{1,0:T(8,128)(2,1)}, bf16[768,768]{1,0:T(8,128)(2,1)}, u32[]{:S(2)}, u32[]{:S(2)}) collective-permute-start(bf16[768,768]{1,0:T(8,128)(2,1)} %pick.58), channel_id=1, source_target_pairs={{0,64},{64,128},{128,192},{192,0},{32,224},{96,32},{160,96},{224,1... | collective-permute-start | bytes 3538952 | tf_op jit(solution)/shard_map/ppermute | solution.py:343
  252.4 19.5 %collective-permute-start.13 = (bf16[1536,768]{1,0:T(8,128)(2,1)}, bf16[1536,768]{1,0:T(8,128)(2,1)}, u32[]{:S(2)}, u32[]{:S(2)}) collective-permute-start(bf16[1536,768]{1,0:T(8,128)(2,1)} %pick.59.lane_ref), channel_id=1, source_target_pairs={{0,32},{32,0},{64,96},{96,64},{128,160},{160,128},{192,224},{224,1... | collective-permute-start | bytes 7077896 | tf_op jit(solution)/shard_map/ppermute | solution.py:337
  262.1 22.4 %collective-permute-start.15 = (bf16[768,768]{1,0:T(8,128)(2,1)}, bf16[768,768]{1,0:T(8,128)(2,1)S(1)}, u32[]{:S(2)}, u32[]{:S(2)}) collective-permute-start(bf16[768,768]{1,0:T(8,128)(2,1)} %pick.61), channel_id=1, source_target_pairs={{0,64},{64,128},{128,192},{192,0},{32,224},{96,32},{160,96},{224,1... | collective-permute-start | bytes 3538952 | tf_op jit(solution)/shard_map/ppermute | solution.py:343
  279.6 34.5 %collective-permute-start.16 = (bf16[768,768]{1,0:T(8,128)(2,1)}, bf16[768,768]{1,0:T(8,128)(2,1)}, u32[]{:S(2)}, u32[]{:S(2)}) collective-permute-start(bf16[768,768]{1,0:T(8,128)(2,1)} %pick.62), channel_id=1, source_target_pairs={{0,64},{64,128},{128,192},{192,0},{32,224},{96,32},{160,96},{224,1... | collective-permute-start | bytes 3538952 | tf_op jit(solution)/shard_map/ppermute | solution.py:343
  349.6 19.4 %collective-permute-start.19 = (bf16[1536,768]{1,0:T(8,128)(2,1)}, bf16[1536,768]{1,0:T(8,128)(2,1)}, u32[]{:S(2)}, u32[]{:S(2)}) collective-permute-start(bf16[1536,768]{1,0:T(8,128)(2,1)} %pick.65.lane_ref), channel_id=1, source_target_pairs={{0,32},{32,0},{64,96},{96,64},{128,160},{160,128},{192,224},{224,1... | collective-permute-start | bytes 7077896 | tf_op jit(solution)/shard_map/ppermute | solution.py:337
  360.1 22.1 %collective-permute-start.21 = (bf16[768,768]{1,0:T(8,128)(2,1)}, bf16[768,768]{1,0:T(8,128)(2,1)}, u32[]{:S(2)}, u32[]{:S(2)}) collective-permute-start(bf16[768,768]{1,0:T(8,128)(2,1)} %pick.67), channel_id=1, source_target_pairs={{0,64},{64,128},{128,192},{192,0},{32,224},{96,32},{160,96},{224,1... | collective-permute-start | bytes 3538952 | tf_op jit(solution)/shard_map/ppermute | solution.py:343
  377.0 35.2 %collective-permute-start.22 = (bf16[768,768]{1,0:T(8,128)(2,1)}, bf16[768,768]{1,0:T(8,128)(2,1)S(1)}, u32[]{:S(2)}, u32[]{:S(2)}) collective-permute-start(bf16[768,768]{1,0:T(8,128)(2,1)} %pick.68), channel_id=1, source_target_pairs={{0,64},{64,128},{128,192},{192,0},{32,224},{96,32},{160,96},{224,1... | collective-permute-start | bytes 3538952 | tf_op jit(solution)/shard_map/ppermute | solution.py:343
  449.2 19.5 %collective-permute-start.25 = (bf16[1536,768]{1,0:T(8,128)(2,1)}, bf16[1536,768]{1,0:T(8,128)(2,1)}, u32[]{:S(2)}, u32[]{:S(2)}) collective-permute-start(bf16[1536,768]{1,0:T(8,128)(2,1)} %pick.71.lane_ref), channel_id=1, source_target_pairs={{0,32},{32,0},{64,96},{96,64},{128,160},{160,128},{192,224},{224,1... | collective-permute-start | bytes 7077896 | tf_op jit(solution)/shard_map/ppermute | solution.py:337
  495.8 28.6 %collective-permute-start.27 = (bf16[1536,768]{1,0:T(8,128)(2,1)}, bf16[1536,768]{1,0:T(8,128)(2,1)}, u32[]{:S(2)}, u32[]{:S(2)}) collective-permute-start(bf16[1536,768]{1,0:T(8,128)(2,1)} %pick.73.lane_ref), channel_id=1, source_target_pairs={{0,32},{32,0},{64,96},{96,64},{128,160},{160,128},{192,224},{224,1... | collective-permute-start | bytes 7077896 | tf_op jit(solution)/shard_map/ppermute | solution.py:337
  498.8 25.7 %collective-permute-start.28 = (bf16[768,768]{1,0:T(8,128)(2,1)}, bf16[768,768]{1,0:T(8,128)(2,1)S(1)}, u32[]{:S(2)}, u32[]{:S(2)}) collective-permute-start(bf16[768,768]{1,0:T(8,128)(2,1)} %pick.74), channel_id=1, source_target_pairs={{0,64},{64,128},{128,192},{32,224},{96,32},{160,96},{224,160},{1,6... | collective-permute-start | bytes 3538952 | tf_op jit(solution)/shard_map/ppermute | solution.py:343
  505.3 28.2 %collective-permute-start.29 = (bf16[768,768]{1,0:T(8,128)(2,1)}, bf16[768,768]{1,0:T(8,128)(2,1)}, u32[]{:S(2)}, u32[]{:S(2)}) collective-permute-start(bf16[768,768]{1,0:T(8,128)(2,1)} %pick.75), channel_id=1, source_target_pairs={{0,64},{64,128},{128,192},{32,224},{96,32},{160,96},{224,160},{1,6... | collective-permute-start | bytes 3538952 | tf_op jit(solution)/shard_map/ppermute | solution.py:343
  551.3 24.4 %collective-permute-start.30 = (bf16[1536,768]{1,0:T(8,128)(2,1)}, bf16[1536,768]{1,0:T(8,128)(2,1)}, u32[]{:S(2)}, u32[]{:S(2)}) collective-permute-start(bf16[1536,768]{1,0:T(8,128)(2,1)} %pick.76.lane_ref), channel_id=1, source_target_pairs={{0,32},{32,0},{64,96},{96,64},{128,160},{160,128},{192,224},{224,1... | collective-permute-start | bytes 7077896 | tf_op jit(solution)/shard_map/ppermute | solution.py:337
  554.3 21.4 %collective-permute-start.31 = (bf16[768,768]{1,0:T(8,128)(2,1)}, bf16[768,768]{1,0:T(8,128)(2,1)S(1)}, u32[]{:S(2)}, u32[]{:S(2)}) collective-permute-start(bf16[768,768]{1,0:T(8,128)(2,1)} %pick.77), channel_id=1, source_target_pairs={{0,64},{64,128},{128,192},{192,0},{32,224},{160,96},{224,160},{1,6... | collective-permute-start | bytes 3538952 | tf_op jit(solution)/shard_map/ppermute | solution.py:343
  559.6 25.8 %collective-permute-start.32 = (bf16[768,768]{1,0:T(8,128)(2,1)}, bf16[768,768]{1,0:T(8,128)(2,1)}, u32[]{:S(2)}, u32[]{:S(2)}) collective-permute-start(bf16[768,768]{1,0:T(8,128)(2,1)} %pick.78), channel_id=1, source_target_pairs={{0,64},{64,128},{128,192},{192,0},{32,224},{160,96},{224,160},{1,6... | collective-permute-start | bytes 3538952 | tf_op jit(solution)/shard_map/ppermute | solution.py:343
  602.8 21.8 %collective-permute-start.33 = (bf16[1536,768]{1,0:T(8,128)(2,1)}, bf16[1536,768]{1,0:T(8,128)(2,1)}, u32[]{:S(2)}, u32[]{:S(2)}) collective-permute-start(bf16[1536,768]{1,0:T(8,128)(2,1)} %pick.79.lane_ref), channel_id=1, source_target_pairs={{0,32},{32,0},{64,96},{96,64},{128,160},{160,128},{192,224},{224,1... | collective-permute-start | bytes 7077896 | tf_op jit(solution)/shard_map/ppermute | solution.py:337
  605.7 28.6 %collective-permute-start.34 = (bf16[768,768]{1,0:T(8,128)(2,1)}, bf16[768,768]{1,0:T(8,128)(2,1)S(1)}, u32[]{:S(2)}, u32[]{:S(2)}) collective-permute-start(bf16[768,768]{1,0:T(8,128)(2,1)} %pick.80), channel_id=1, source_target_pairs={{64,128},{128,192},{192,0},{32,224},{96,32},{224,160},{65,129},{12... | collective-permute-start | bytes 3538952 | tf_op jit(solution)/shard_map/ppermute | solution.py:343
  652.3 24.2 %collective-permute-start.35 = (bf16[1536,768]{1,0:T(8,128)(2,1)}, bf16[1536,768]{1,0:T(8,128)(2,1)}, u32[]{:S(2)}, u32[]{:S(2)}) collective-permute-start(bf16[1536,768]{1,0:T(8,128)(2,1)} %pick.81.lane_ref), channel_id=1, source_target_pairs={{0,32},{32,0},{64,96},{96,64},{128,160},{160,128},{192,224},{224,1... | collective-permute-start | bytes 7077896 | tf_op jit(solution)/shard_map/ppermute | solution.py:337
  655.2 21.3 %collective-permute-start.36 = (bf16[768,768]{1,0:T(8,128)(2,1)}, bf16[768,768]{1,0:T(8,128)(2,1)S(1)}, u32[]{:S(2)}, u32[]{:S(2)}) collective-permute-start(bf16[768,768]{1,0:T(8,128)(2,1)} %pick.82), channel_id=1, source_target_pairs={{64,128},{128,192},{192,0},{32,224},{96,32},{224,160},{65,129},{12... | collective-permute-start | bytes 3538952 | tf_op jit(solution)/shard_map/ppermute | solution.py:343
  660.2 25.3 %collective-permute-start.37 = (bf16[768,768]{1,0:T(8,128)(2,1)}, bf16[768,768]{1,0:T(8,128)(2,1)}, u32[]{:S(2)}, u32[]{:S(2)}) collective-permute-start(bf16[768,768]{1,0:T(8,128)(2,1)} %pick.83), channel_id=1, source_target_pairs={{192,0},{160,96},{193,1},{161,97},{194,2},{162,98},{195,3},{163,99... | collective-permute-start | bytes 3538952 | tf_op jit(solution)/shard_map/ppermute | solution.py:343
  703.5 18.4 %collective-permute-start.38 = (bf16[1536,768]{1,0:T(8,128)(2,1)}, bf16[1536,768]{1,0:T(8,128)(2,1)}, u32[]{:S(2)}, u32[]{:S(2)}) collective-permute-start(bf16[1536,768]{1,0:T(8,128)(2,1)} %pick.84.lane_ref), channel_id=1, source_target_pairs={{0,32},{32,0},{64,96},{96,64},{128,160},{160,128},{192,224},{224,1... | collective-permute-start | bytes 7077896 | tf_op jit(solution)/shard_map/ppermute | solution.py:337
  748.9 23.8 %collective-permute-start.40 = (bf16[1536,768]{1,0:T(8,128)(2,1)}, bf16[1536,768]{1,0:T(8,128)(2,1)}, u32[]{:S(2)}, u32[]{:S(2)}) collective-permute-start(bf16[1536,768]{1,0:T(8,128)(2,1)} %pick.86.lane_ref), channel_id=1, source_target_pairs={{0,32},{32,0},{64,96},{96,64},{128,160},{160,128},{192,224},{224,1... | collective-permute-start | bytes 7077896 | tf_op jit(solution)/shard_map/ppermute | solution.py:337
  753.2 19.5 %collective-permute-start.41 = (bf16[768,768]{1,0:T(8,128)(2,1)}, bf16[768,768]{1,0:T(8,128)(2,1)S(1)}, u32[]{:S(2)}, u32[]{:S(2)}) collective-permute-start(bf16[768,768]{1,0:T(8,128)(2,1)} %pick.87), channel_id=1, source_target_pairs={{0,64},{96,32},{1,65},{97,33},{2,66},{98,34},{3,67},{99,35},{4,68}... | collective-permute-start | bytes 3538952 | tf_op jit(solution)/shard_map/ppermute | solution.py:343
  757.5 26.9 %collective-permute-start.42 = (bf16[768,768]{1,0:T(8,128)(2,1)}, bf16[768,768]{1,0:T(8,128)(2,1)}, u32[]{:S(2)}, u32[]{:S(2)}) collective-permute-start(bf16[768,768]{1,0:T(8,128)(2,1)} %pick.88), channel_id=1, source_target_pairs={{0,64},{96,32},{1,65},{97,33},{2,66},{98,34},{3,67},{99,35},{4,68}... | collective-permute-start | bytes 3538952 | tf_op jit(solution)/shard_map/ppermute | solution.py:343
  (78 other events, 688.4 us)

commit v3 on v2

v3 whole, which is shorter than its diff:
```python
import functools

import jax
import jax.numpy as jnp
import numpy as np
from jax import lax
from jax.experimental import pallas as pl
from jax.experimental.pallas import tpu as pltpu
from jax.sharding import PartitionSpec as P

VMEM_LIMIT = 62 * 1024 * 1024
HBM = pl.BlockSpec(memory_space=pltpu.HBM)
SMEM = pl.BlockSpec(memory_space=pltpu.SMEM)
VMEM = pl.BlockSpec(memory_space=pltpu.VMEM)
DIRS = (1, -1)


PACK = 64
SLOTS = 48
ROWS = 10
PARTS = 2
LEAD = 8


def ring_plan(sections, layers, parts):
    chips = sections // 2
    items = layers * parts
    owned = [[i for i in range(items) if (i // parts) % sections // 2 == y] for y in range(chips)]
    held = [[dict.fromkeys(owned[y], 0) for y in range(chips)] for _ in DIRS]
    phases = []
    while any(len(stock) < items for lane in held for stock in lane):
        number = len(phases) + 1
        moves = []
        for lane, step in enumerate(DIRS):
            for y in range(chips):
                target = (y + step) % chips
                options = [i for i, at in held[lane][y].items() if at < number]
                options = [i for i in options if i not in held[lane][target]]
                if options:
                    moves.append((lane, y, target, min(options)))
        phases.append(moves)
        for lane, y, target, i in moves:
            held[lane][target][i] = number + 1
    return phases, held


class Side:
    def __init__(self, tab, jobs, size, width):
        self.jobs, self.size, self.width = jobs, size, width
        found = {name: place for job in jobs for name, place in job["sources"].items()}
        self.names = sorted(found)
        self.places = [found[name][1] for name in self.names]
        self.operands = [tab] + [found[name][0] for name in self.names] if jobs else []
        self.in_specs = [SMEM] + [HBM] * len(self.names) if jobs else []
        self.shapes, self.out_specs, self.scratch = [], [], []
        for job in jobs:
            shape = (size * len(job["rows"]), width)
            self.shapes.append(jax.ShapeDtypeStruct(shape, jnp.bfloat16))
            self.out_specs.append(HBM)
            self.scratch.append(pltpu.VMEM(shape, jnp.bfloat16))
            self.scratch.append(pltpu.SemaphoreType.DMA((len(job["rows"]),)))
            self.scratch.append(pltpu.SemaphoreType.DMA((len(job["rows"]),)))

    def bind(self, inputs, outputs, scratch):
        self.inputs, self.outputs, self.holds = inputs, outputs, scratch

    def view(self, name, start):
        number = self.names.index(name)
        place = self.places[number] + (pl.ds(start, self.size),)
        return self.inputs[1 + number].at[place]

    def parts(self):
        for number, job in enumerate(self.jobs):
            hold, in_sems, out_sems = self.holds[3 * number : 3 * number + 3]
            for part, (row, choices) in enumerate(job["rows"]):
                at = pl.ds(part * self.size, self.size)
                target = self.outputs[number].at[at]
                yield row, choices, hold.at[at], target, in_sems.at[part], out_sems.at[part]

    def begin(self):
        for row, choices, hold, _, in_sem, _ in self.parts():
            choice = self.inputs[0][row]
            for number, (name, start) in enumerate(choices):

                @pl.when(choice == number)
                def _(name=name, start=start, hold=hold, in_sem=in_sem):
                    pltpu.make_async_copy(self.view(name, start), hold, in_sem).start()

    def middle(self):
        for _, choices, hold, target, in_sem, out_sem in self.parts():
            pltpu.make_async_copy(self.view(*choices[0]), hold, in_sem).wait()
            pltpu.make_async_copy(hold, target, out_sem).start()

    def finish(self):
        for _, _, hold, target, _, out_sem in self.parts():
            pltpu.make_async_copy(hold, target, out_sem).wait()


def call_with_side(kernel, side, operands, in_specs, shapes, out_specs, scratch, **options):
    n_in, n_side = len(operands), len(side.operands)
    n_out, n_scratch = len(shapes), len(scratch)

    def body(*refs):
        refs = list(refs)

        def take(count):
            taken = refs[:count]
            del refs[:count]
            return taken

        ins, side_ins = take(n_in), take(n_side)
        outs, side_outs = take(n_out), take(len(side.shapes))
        own = take(n_scratch)
        side.bind(side_ins, side_outs, refs)
        kernel(side, *ins, *outs, *own)

    return pl.pallas_call(
        body,
        out_shape=tuple(shapes) + tuple(side.shapes),
        grid=(1,),
        in_specs=list(in_specs) + side.in_specs,
        out_specs=tuple(out_specs) + tuple(side.out_specs),
        scratch_shapes=list(scratch) + side.scratch,
        compiler_params=pltpu.CompilerParams(vmem_limit_bytes=VMEM_LIMIT),
        **options,
    )(*operands, *side.operands)


def copy_kernel(side):
    side.begin()
    side.middle()
    side.finish()


LANES = 128


def turned(value, lanes):
    return pltpu.roll(value, lanes % LANES, value.ndim - 1)


def lanes_of(value):
    return lax.broadcasted_iota(jnp.int32, (1,) * (value.ndim - 1) + (LANES,), value.ndim - 1)


def fold_tail(third, at):
    axis = third.ndim - 1
    spread = pltpu.roll(turned(third, -at - 32), 0, axis, stride=16, stride_axis=axis - 1)
    place = lax.broadcasted_iota(jnp.int32, third.shape, axis) // 16
    own = place == lax.broadcasted_iota(jnp.int32, third.shape, axis - 1)
    return jnp.sum(jnp.where(own, spread, 0.0), axis=axis - 1, keepdims=True)


def unfold_tail(row, at):
    value = jnp.broadcast_to(turned(row, at + 32), row.shape[:-2] + (8, LANES))
    number = lax.broadcasted_iota(jnp.int32, value.shape, value.ndim - 2)
    for step in (1, 2, 4):
        value = jnp.where((number & step) != 0, turned(value, -16 * step), value)
    return value


def pack(first, second, third, at, gates=None):
    lanes = lanes_of(first)
    top = jnp.where(
        lanes < SLOTS,
        turned(first, -at),
        jnp.where(lanes < 2 * SLOTS, turned(second, SLOTS - at), turned(third, 2 * SLOTS - at)),
    )
    tail = fold_tail(third, at)
    axis = first.ndim - 2
    number = lax.broadcasted_iota(jnp.int32, top.shape, axis)
    last = jnp.broadcast_to(tail, top.shape)
    if gates is not None:
        last = jnp.where(number == 0, last, gates)
    return jnp.concatenate([top, last], axis=axis)


def unpack(blocks, at):
    top, last = blocks[..., 0:8, :], blocks[..., 8:16, :]
    lanes = lanes_of(blocks)
    third = jnp.where(
        lanes - at < 32, turned(top, at - 2 * SLOTS), unfold_tail(last[..., 0:1, :], at)
    )
    return turned(top, at), turned(top, at - SLOTS), third, turned(last, at)


def unpack_pairs(back):
    pairs = back.shape[0] // 2
    split = back.reshape(pairs, 2, 16, LANES)
    low = lanes_of(back) < PACK
    both = zip(unpack(split[:, 0], 0), unpack(split[:, 1], PACK))
    groups = [jnp.where(low, even, odd) for even, odd in both]
    gates = jnp.broadcast_to(groups[3][:, 1:2], groups[0].shape)
    return jnp.concatenate(groups[0:3] + [gates], axis=1)


def send_blocks(value):
    count = value.shape[0]
    packed = value[:, 0:ROWS].reshape(count * ROWS // 2, 2, LANES)
    sent = lax.all_to_all(packed, "expert", split_axis=0, concat_axis=0, tiled=True)
    return jnp.pad(sent.reshape(count, ROWS, LANES), ((0, 0), (0, 16 - ROWS), (0, 0)))


def turn_kernel(merge, send, side, *refs):
    side.begin()
    refs = list(refs)
    h_ref = refs.pop(0)
    if merge:
        back_ref, row_ref = refs.pop(0), refs.pop(0)
    if send:
        next_ref = refs.pop(0)
    hnew_ref = refs.pop(0)
    features, tokens = h_ref.shape
    held = h_ref[...]
    if merge:
        tiles = unpack_pairs(back_ref[...].astype(jnp.float32)).astype(jnp.bfloat16)
        offset = lax.broadcasted_iota(jnp.int32, (4 * PACK, tokens), 0)
        first, second = row_ref[0:1, :] - offset, row_ref[1:2, :] - offset
        update = jnp.zeros((32, tokens), jnp.float32)
        for turn in range(tiles.shape[0] // 2):
            base = turn * 4 * PACK
            onehot = jnp.where((first == base) | (second == base), 1.0, 0.0)
            pair = jnp.concatenate([tiles[2 * turn], tiles[2 * turn + 1]], axis=1)
            update += jnp.dot(
                pair, onehot.astype(jnp.bfloat16), preferred_element_type=jnp.float32
            )
        change = update[0:features] * (1.0 / update[features:features + 1])
        held = (held.astype(jnp.float32) + change).astype(jnp.bfloat16)
    hnew_ref[...] = held
    side.middle()
    if send:
        out_ref = refs.pop(0)
        offset = lax.broadcasted_iota(jnp.int32, (tokens, 4 * PACK), 1)
        col = next_ref[...].astype(jnp.float32).T.astype(jnp.int32)
        first, second = col[:, 0:1] - offset, col[:, 1:2] - offset
        for turn in range(out_ref.shape[0] // 4):
            base = turn * 4 * PACK
            onehot = jnp.where((first == base) | (second == base), 1.0, 0.0)
            found = jnp.dot(held, onehot.astype(jnp.bfloat16), preferred_element_type=jnp.float32)
            for half in range(2):
                tile = found[:, LANES * half : LANES * (half + 1)]
                groups = tile[0:8], tile[8:16], tile[16:24]
                number = turn * 4 + half * 2
                out_ref[number] = pack(*groups, 0).astype(jnp.bfloat16)
                out_ref[number + 1] = pack(*groups, PACK).astype(jnp.bfloat16)
    side.finish()


def run_turn(side, experts, h, back, rows, before, after):
    features, tokens = h.shape
    merge, send = before is not None, after is not None
    operands, specs = [h], [VMEM]
    shapes, outs = [jax.ShapeDtypeStruct(h.shape, h.dtype)], [VMEM]
    if merge:
        operands += [back, rows]
        specs += [VMEM, plane((8, tokens), before)]
    if send:
        operands += [rows]
        specs += [plane((8, tokens), after)]
        shapes += [jax.ShapeDtypeStruct((experts, 16, LANES), jnp.bfloat16)]
        outs += [VMEM]
    return call_with_side(
        functools.partial(turn_kernel, merge, send), side, operands, specs, shapes, outs, [],
        name="turn",
    )


def expert_kernel(
    side, scal_ref, blocks_ref, gain_ref, router_ref, lane_ref, other_ref, out_ref,
    win_ref, wout_ref, sems,
):
    core = scal_ref[0]

    @pl.when(core == 0)
    def _():
        pltpu.make_async_copy(lane_ref, win_ref, sems.at[0]).start()
        pltpu.make_async_copy(other_ref, wout_ref, sems.at[1]).start()

    @pl.when(core != 0)
    def _():
        pltpu.make_async_copy(other_ref, win_ref, sems.at[0]).start()
        pltpu.make_async_copy(lane_ref, wout_ref, sems.at[1]).start()

    side.begin()
    width = win_ref.shape[1]
    groups = blocks_ref.shape[0]
    blocks = blocks_ref[...].astype(jnp.float32)
    parts = [group[:, None] for group in unpack(blocks, 0)[0:3]]
    tall = jnp.concatenate(parts, axis=1).reshape(width, LANES)
    wide = tall.T[0:PACK]
    mean_square = jnp.mean(wide * wide, axis=1, keepdims=True)
    normed = (wide * lax.rsqrt(mean_square + 1e-06) * gain_ref[...]).astype(jnp.bfloat16)
    logit = jnp.sum(normed.astype(jnp.float32) * router_ref[...], axis=1, keepdims=True)
    gate = jax.nn.sigmoid(logit).astype(jnp.bfloat16).astype(jnp.float32)
    pltpu.make_async_copy(lane_ref, win_ref, sems.at[0]).wait()
    pre_act = lax.dot_general(
        normed, win_ref[...], (((1,), (1,)), ((), ())), preferred_element_type=jnp.float32
    )
    side.middle()
    active = jax.nn.gelu(pre_act, approximate=True).astype(jnp.bfloat16)
    pltpu.make_async_copy(lane_ref, wout_ref, sems.at[1]).wait()
    output = jnp.dot(active, wout_ref[...], preferred_element_type=jnp.float32)
    weighted = output * gate
    spread = jnp.broadcast_to(gate, (PACK, LANES))
    zeros = jnp.zeros_like(weighted)
    tall = jnp.concatenate([weighted, zeros], axis=0).T.reshape(groups, 3, 8, LANES)
    gates = jnp.concatenate([spread, jnp.zeros_like(spread)], axis=0).T[0:8]
    gates = jnp.broadcast_to(gates[None], (groups, 8, LANES))
    out_ref[...] = pack(tall[:, 0], tall[:, 1], tall[:, 2], 0, gates).astype(jnp.bfloat16)
    side.finish()


def run_expert(side, layer, scal, blocks, gains, routers, lane_w, other_w):
    hidden, width = lane_w.shape
    return call_with_side(
        expert_kernel,
        side,
        [scal, blocks, gains, routers, lane_w, other_w],
        [SMEM, VMEM, plane((1, width), layer), plane((1, width), layer), HBM, HBM],
        [jax.ShapeDtypeStruct(blocks.shape, jnp.bfloat16)],
        [VMEM],
        [
            pltpu.VMEM((hidden, width), jnp.bfloat16),
            pltpu.VMEM((hidden, width), jnp.bfloat16),
            pltpu.SemaphoreType.DMA((2,)),
        ],
        cost_estimate=pl.CostEstimate(
            flops=4 * PACK * hidden * width, bytes_accessed=4 * hidden * width, transcendentals=0
        ),
        name="expert",
    )


def plane(shape, *lead):
    return pl.BlockSpec((None,) * len(lead) + shape, lambda i: lead + (0,) * len(shape))


def place_tokens(routes, experts):
    tokens = routes.shape[1]
    ids = jnp.arange(experts, dtype=jnp.int32)
    first = routes[:, :, 0:1] == ids
    second = routes[:, :, 1:2] == ids
    named = (first | second).astype(jnp.bfloat16)
    earlier = jnp.tril(jnp.ones((tokens, tokens), jnp.bfloat16), -1)
    rank = jnp.einsum("ut,lte->lue", earlier, named, preferred_element_type=jnp.float32)
    rank = rank.astype(jnp.int32) + ids * PACK
    slot_first = jnp.sum(jnp.where(first, rank, 0), axis=2)
    slot_second = jnp.sum(jnp.where(second, rank, 0), axis=2)
    blank = jnp.zeros_like(slot_first)
    return jnp.stack([slot_first, slot_second] + [blank] * 6, axis=1)


def join(*values):
    return lax.optimization_barrier(values)


def local(inputs, routes, norm_gains, routers, expert_in, expert_out):
    sections = lax.axis_size("section")
    experts = lax.axis_size("expert")
    section_pos = lax.axis_index("section")
    repeats, _, _, hidden, width = expert_in.shape
    layers = repeats * sections
    phases, held = ring_plan(sections, layers, PARTS)
    size = hidden // PARTS
    scal = jnp.stack([section_pos % 2, section_pos]).astype(jnp.int32)

    buffers = {("in", r): (expert_in, (r, 0, 0)) for r in range(repeats)}
    buffers.update({("out", r): (expert_out, (r, 0, 0)) for r in range(repeats)})
    every = [(lane, y) for lane in range(2) for y in range(sections // 2)]
    table, wanted = [], []

    def source_of(lane, y, i):
        q, part = i // PARTS, i % PARTS
        if q % sections // 2 != y:
            return ("ring", held[lane][y][i]), 0
        name = ("in", "out")[lane] if q % 2 == lane else "swapped"
        return (name, q // sections), part * size

    def add_pick(by_section):
        choices = sorted(set(by_section.values()))
        table.append([choices.index(by_section.get(s, choices[0])) for s in range(sections)])
        wanted.append(choices)
        return len(table) - 1

    swap_rows = [
        [
            add_pick({2 * y + lane: ((("out", "in")[lane], r), part * size) for lane, y in every})
            for part in range(PARTS)
        ]
        for r in range(repeats)
    ]
    ring_rows = [
        [add_pick({2 * y + lane: source_of(lane, y, i) for lane, y, _, i in moves})] if moves else []
        for moves in phases
    ]
    layer_rows = [
        [
            add_pick({2 * y + lane: source_of(lane, y, q * PARTS + part) for lane, y in every})
            for part in range(PARTS)
        ]
        for q in range(layers)
    ]
    tab = jnp.asarray(np.array(table, np.int32).T)[section_pos]

    def job(rows):
        names = sorted({name for row in rows for name, _ in wanted[row]})
        return {
            "sources": {name: buffers[name] for name in names},
            "rows": [(row, wanted[row]) for row in rows],
        }

    def side(*rows):
        return Side(tab, [job(some) for some in rows if some], size, width)

    def picked(rows):
        (value,) = call_with_side(copy_kernel, side(rows), [], [], [], [], [], name="pick")
        return value

    def swapped(value):
        return lax.ppermute(value, "section", [(s, s ^ 1) for s in range(sections)])

    def ring_row(phase):
        return ring_rows[phase - 1] if phase <= len(phases) else []

    def ring(phase, value):
        pairs = [(2 * y + lane, 2 * target + lane) for lane, y, target, _ in phases[phase - 1]]
        return lax.ppermute(value, "section", pairs)

    def arrival(q):
        parts = range(q * PARTS, (q + 1) * PARTS)
        return max(stock[i] for lane in held for stock in lane for i in parts)

    mine = lax.all_to_all(routes[:, 0], "section", split_axis=1, concat_axis=0, tiled=False)
    mine = jnp.transpose(mine, (1, 0, 2, 3)).reshape(layers, -1, 2)
    rows = place_tokens(mine, experts)
    small = jnp.stack([norm_gains[:, 0], routers[:, 0, 0]])
    small = jnp.broadcast_to(small[None], (sections,) + small.shape)
    small = lax.all_to_all(small, "section", split_axis=0, concat_axis=0, tiled=True)
    small = jnp.transpose(small, (1, 2, 0, 3)).reshape(2, layers, 1, width).astype(jnp.float32)
    gains, gate_rows = small[0], small[1]
    h = jnp.transpose(inputs[0], (1, 0))

    buffers[("swapped", 0)] = (swapped(picked(swap_rows[0])), ())
    later = swapped(picked(swap_rows[1]))
    flying = None
    for phase in range(1, LEAD):
        started = ring(phase, picked(ring_row(phase)))
        if flying is not None:
            flying, tab = join(flying, tab)
            buffers[("ring", phase)] = (flying, ())
        if phase == 2:
            later, tab = join(later, tab)
            buffers[("swapped", 1)] = (later, ())
        flying = started
    tab, rows, gains, gate_rows, h = join(tab, rows, gains, gate_rows, h)

    def wish_of(phase):
        for q in range(layers):
            first = LEAD + 2 * q
            if phase == first - 1 and arrival(q) < first - 1:
                return q
            if phase == first and first - 1 <= arrival(q) < first:
                return q
        return None

    def sides(phase):
        wish = wish_of(phase)
        return wish, side([] if wish is None else layer_rows[wish], ring_row(phase))

    ready = {}

    def run_phase(phase, wish, value, flying, extra):
        extra = list(extra)
        bundle = [send_blocks(value)]
        if wish is not None:
            lane_w = extra.pop(0)
            bundle += [lane_w, swapped(lane_w)]
        started = ring(phase, extra.pop(0)) if extra else None
        if flying is not None:
            bundle.append(flying)
        bundle = list(join(*bundle))
        if flying is not None:
            buffers[("ring", phase)] = (bundle.pop(), ())
        if wish is not None:
            ready[wish] = (bundle[1], bundle[2])
        return bundle[0], started

    back = None
    for q in range(layers):
        first = LEAD + 2 * q
        wish, beside = sides(first)
        before = q - 1 if q else None
        h, blocks, *extra = run_turn(beside, experts, h, back, rows, before, q)
        blocks, flying = run_phase(first, wish, blocks, flying, extra)
        if q not in ready:
            lane_w = picked(layer_rows[q])
            ready[q] = (lane_w, swapped(lane_w))
        wish, beside = sides(first + 1)
        back, *extra = run_expert(beside, q, scal, blocks, gains, gate_rows, *ready.pop(q))
        back, flying = run_phase(first + 1, wish, back, flying, extra)

    (h,) = run_turn(side(), experts, h, back, rows, layers - 1, None)
    return jnp.transpose(h, (1, 0))[None]


def solution(mesh):
    return jax.shard_map(
        local,
        mesh=mesh,
        in_specs=(
            P("section", None, "expert"),
            P(None, "section", None, None, None),
            P(None, "section", None),
            P(None, "section", "expert", None),
            P(None, "section", "expert", None, None),
            P(None, "section", "expert", None, None),
        ),
        out_specs=P("section", None, "expert"),
        check_vma=False,
    )
```

time: 936 us -> 835 us (0.89)
  waiting for transfers between devices: 228 us -> 53.5 us
  blocking collectives: 265 us -> 416 us
  Pallas kernels: 278 us -> 199 us
  local copies, waits for them, and re-layouts: 20.9 us -> 73.4 us
  starting transfers between devices: 127 us -> 77.6 us
    all_to_all x18 -> x31, blocking collectives: 265 us -> 416 us  [send_blocks(): lax.all_to_all(packed, 'expert', split_axis=0, concat_axis=0, tiled=True)]
    all_to_all x14 -> x1, waiting for transfers between devices: 124 us -> 9.66 us  [send_blocks(): lax.all_to_all(packed, 'expert', split_axis=0, concat_axis=0, tiled=True)]
    pallas_call x79 -> x42, Pallas kernels: 278 us -> 199 us  [call_with_side(): pl.pallas_call(body, out_shape=tuple(shapes) + tuple(side.shapes), grid=(...]
    ppermute x28, waiting for transfers between devices: 93.1 us -> 30.1 us  [ring(): return lax.ppermute(value, 'section', pairs)]
    all_to_all x14 -> x1, starting transfers between devices: 63 us -> 11.5 us  [send_blocks(): lax.all_to_all(packed, 'expert', split_axis=0, concat_axis=0, tiled=True)]
    reshape x0 -> x64, local copies, waits for them, and re-layouts: none -> 30.9 us  [the longest x32 29.9 us: send_blocks(): packed = value[:, 0:ROWS].reshape(count * ROWS // 2, 2, LANES)]
    pad x0 -> x32, local copies, waits for them, and re-layouts: none -> 21.8 us  [send_blocks(): jnp.pad(sent.reshape(count, ROWS, LANES), ((0, 0), (0, 16 - ROWS), (0, 0)))]
  transfers between devices with their start and end apart: 62 -> 49, of which waited for: 30 -> 9; matrix products, arithmetic and copies ran while one was open for 1% -> 6% of each run, Pallas kernels for 14% -> 9%
where the time goes in v3:
time: 835 us; the launch traced here: 823 us
  blocking collectives  416 us (50%)
  Pallas kernels  199 us (24%)
  starting transfers between devices  77.6 us (9%)
  local copies, waits for them, and re-layouts  73.4 us (9%)
  waiting for transfers between devices  53.5 us (6%)
    all_to_all x31, blocking collectives, send_blocks(): lax.all_to_all(packed, 'expert', split_axis=0, concat_axis=0, tiled=True)  416 us
    pallas_call x42, Pallas kernels, call_with_side(): pl.pallas_call(body, out_shape=tuple(shapes) + tuple(side.shapes), grid=(...  199 us
    ppermute x28, starting transfers between devices, ring(): return lax.ppermute(value, 'section', pairs)  50.8 us
    ppermute x28, waiting for transfers between devices, ring(): return lax.ppermute(value, 'section', pairs)  30.1 us
    reshape x32, local copies, waits for them, and re-layouts, send_blocks(): packed = value[:, 0:ROWS].reshape(count * ROWS // 2, 2, LANES)  29.9 us
    pad x32, local copies, waits for them, and re-layouts, send_blocks(): jnp.pad(sent.reshape(count, ROWS, LANES), ((0, 0), (0, 16 - ROWS), (0, 0)))  21.8 us
    unnamed x43, local copies, waits for them, and re-layouts  17.2 us
  transfers between devices with their start and end apart: 49, of which 9 were waited for; matrix products, arithmetic and copies ran while one was open for 6% of the time, Pallas kernels for 9%

profile of v3, /device:TPU:8, one launch (start us, length us, event | category | flops | bytes accessed | tf_op | source)
XLA Modules:
  0.0 822.8 jit_solution(17026040111809095443)
XLA Ops:
  80.8 12.8 %all-to-all-done = s32[1,2,8,512,2]{3,4,1,0,2:T(2,128)S(1)} async-done(((s32[1,2,8,512,2]{3,4,1,0,2:T(2,128)}), s32[1,2,8,512,2]{3,4,1,0,2:T(2,128)S(1)}, u32[]{:S(2)}, u32[]{:S(2)}) %all-to-all-start) | async-done | bytes 65568 | tf_op jit(solution)/shard_map/all_to_all | solution.py:433
  138.4 13.3 %all_to_all.180 = bf16[160,2,128]{2,1,0:T(2,128)(2,1)S(1)} all-to-all(bf16[160,2,128]{2,1,0:T(2,128)(2,1)S(1)} %reshape.222), channel_id=1, replica_groups=mesh['section'=8,'expert'=32] {'expert'}, dimensions={0} | all-to-all | bytes 163840 | tf_op jit(solution)/shard_map/all_to_all | solution.py:200
  160.6 13.3 %all_to_all.181 = bf16[160,2,128]{2,1,0:T(2,128)(2,1)S(1)} all-to-all(bf16[160,2,128]{2,1,0:T(2,128)(2,1)S(1)} %reshape.224), channel_id=1, replica_groups=mesh['section'=8,'expert'=32] {'expert'}, dimensions={0} | all-to-all | bytes 163840 | tf_op jit(solution)/shard_map/all_to_all | solution.py:200
  186.1 13.8 %all_to_all.182 = bf16[160,2,128]{2,1,0:T(2,128)(2,1)S(1)} all-to-all(bf16[160,2,128]{2,1,0:T(2,128)(2,1)S(1)} %reshape.226), channel_id=1, replica_groups=mesh['section'=8,'expert'=32] {'expert'}, dimensions={0} | all-to-all | bytes 163840 | tf_op jit(solution)/shard_map/all_to_all | solution.py:200
  209.5 13.3 %all_to_all.183 = bf16[160,2,128]{2,1,0:T(2,128)(2,1)S(1)} all-to-all(bf16[160,2,128]{2,1,0:T(2,128)(2,1)S(1)} %reshape.228), channel_id=1, replica_groups=mesh['section'=8,'expert'=32] {'expert'}, dimensions={0} | all-to-all | bytes 163840 | tf_op jit(solution)/shard_map/all_to_all | solution.py:200
  229.8 13.3 %all_to_all.184 = bf16[160,2,128]{2,1,0:T(2,128)(2,1)S(1)} all-to-all(bf16[160,2,128]{2,1,0:T(2,128)(2,1)S(1)} %reshape.230), channel_id=1, replica_groups=mesh['section'=8,'expert'=32] {'expert'}, dimensions={0} | all-to-all | bytes 163840 | tf_op jit(solution)/shard_map/all_to_all | solution.py:200
  251.7 13.3 %all_to_all.185 = bf16[160,2,128]{2,1,0:T(2,128)(2,1)S(1)} all-to-all(bf16[160,2,128]{2,1,0:T(2,128)(2,1)S(1)} %reshape.232), channel_id=1, replica_groups=mesh['section'=8,'expert'=32] {'expert'}, dimensions={0} | all-to-all | bytes 163840 | tf_op jit(solution)/shard_map/all_to_all | solution.py:200
  278.3 13.3 %all_to_all.186 = bf16[160,2,128]{2,1,0:T(2,128)(2,1)S(1)} all-to-all(bf16[160,2,128]{2,1,0:T(2,128)(2,1)S(1)} %reshape.234), channel_id=1, replica_groups=mesh['section'=8,'expert'=32] {'expert'}, dimensions={0} | all-to-all | bytes 163840 | tf_op jit(solution)/shard_map/all_to_all | solution.py:200
  299.9 13.3 %all_to_all.187 = bf16[160,2,128]{2,1,0:T(2,128)(2,1)S(1)} all-to-all(bf16[160,2,128]{2,1,0:T(2,128)(2,1)S(1)} %reshape.236), channel_id=1, replica_groups=mesh['section'=8,'expert'=32] {'expert'}, dimensions={0} | all-to-all | bytes 163840 | tf_op jit(solution)/shard_map/all_to_all | solution.py:200
  320.4 13.3 %all_to_all.188 = bf16[160,2,128]{2,1,0:T(2,128)(2,1)S(1)} all-to-all(bf16[160,2,128]{2,1,0:T(2,128)(2,1)S(1)} %reshape.238), channel_id=1, replica_groups=mesh['section'=8,'expert'=32] {'expert'}, dimensions={0} | all-to-all | bytes 163840 | tf_op jit(solution)/shard_map/all_to_all | solution.py:200
  343.5 13.4 %all_to_all.189 = bf16[160,2,128]{2,1,0:T(2,128)(2,1)S(1)} all-to-all(bf16[160,2,128]{2,1,0:T(2,128)(2,1)S(1)} %reshape.240), channel_id=1, replica_groups=mesh['section'=8,'expert'=32] {'expert'}, dimensions={0} | all-to-all | bytes 163840 | tf_op jit(solution)/shard_map/all_to_all | solution.py:200
  371.2 13.3 %all_to_all.190 = bf16[160,2,128]{2,1,0:T(2,128)(2,1)S(1)} all-to-all(bf16[160,2,128]{2,1,0:T(2,128)(2,1)S(1)} %reshape.242), channel_id=1, replica_groups=mesh['section'=8,'expert'=32] {'expert'}, dimensions={0} | all-to-all | bytes 163840 | tf_op jit(solution)/shard_map/all_to_all | solution.py:200
  391.5 13.4 %all_to_all.191 = bf16[160,2,128]{2,1,0:T(2,128)(2,1)S(1)} all-to-all(bf16[160,2,128]{2,1,0:T(2,128)(2,1)S(1)} %reshape.244), channel_id=1, replica_groups=mesh['section'=8,'expert'=32] {'expert'}, dimensions={0} | all-to-all | bytes 163840 | tf_op jit(solution)/shard_map/all_to_all | solution.py:200
  418.8 13.2 %all_to_all.192 = bf16[160,2,128]{2,1,0:T(2,128)(2,1)S(1)} all-to-all(bf16[160,2,128]{2,1,0:T(2,128)(2,1)S(1)} %reshape.246), channel_id=1, replica_groups=mesh['section'=8,'expert'=32] {'expert'}, dimensions={0} | all-to-all | bytes 163840 | tf_op jit(solution)/shard_map/all_to_all | solution.py:200
  438.9 13.4 %all_to_all.193 = bf16[160,2,128]{2,1,0:T(2,128)(2,1)S(1)} all-to-all(bf16[160,2,128]{2,1,0:T(2,128)(2,1)S(1)} %reshape.248), channel_id=1, replica_groups=mesh['section'=8,'expert'=32] {'expert'}, dimensions={0} | all-to-all | bytes 163840 | tf_op jit(solution)/shard_map/all_to_all | solution.py:200
  468.6 14.0 %all_to_all.194 = bf16[160,2,128]{2,1,0:T(2,128)(2,1)S(1)} all-to-all(bf16[160,2,128]{2,1,0:T(2,128)(2,1)S(1)} %reshape.250), channel_id=1, replica_groups=mesh['section'=8,'expert'=32] {'expert'}, dimensions={0} | all-to-all | bytes 163840 | tf_op jit(solution)/shard_map/all_to_all | solution.py:200
  489.6 13.2 %all_to_all.195 = bf16[160,2,128]{2,1,0:T(2,128)(2,1)S(1)} all-to-all(bf16[160,2,128]{2,1,0:T(2,128)(2,1)S(1)} %reshape.252), channel_id=1, replica_groups=mesh['section'=8,'expert'=32] {'expert'}, dimensions={0} | all-to-all | bytes 163840 | tf_op jit(solution)/shard_map/all_to_all | solution.py:200
  515.5 13.3 %all_to_all.196 = bf16[160,2,128]{2,1,0:T(2,128)(2,1)S(1)} all-to-all(bf16[160,2,128]{2,1,0:T(2,128)(2,1)S(1)} %reshape.254), channel_id=1, replica_groups=mesh['section'=8,'expert'=32] {'expert'}, dimensions={0} | all-to-all | bytes 163840 | tf_op jit(solution)/shard_map/all_to_all | solution.py:200
  535.7 13.3 %all_to_all.197 = bf16[160,2,128]{2,1,0:T(2,128)(2,1)S(1)} all-to-all(bf16[160,2,128]{2,1,0:T(2,128)(2,1)S(1)} %reshape.256), channel_id=1, replica_groups=mesh['section'=8,'expert'=32] {'expert'}, dimensions={0} | all-to-all | bytes 163840 | tf_op jit(solution)/shard_map/all_to_all | solution.py:200
  559.2 13.5 %all_to_all.198 = bf16[160,2,128]{2,1,0:T(2,128)(2,1)S(1)} all-to-all(bf16[160,2,128]{2,1,0:T(2,128)(2,1)S(1)} %reshape.258), channel_id=1, replica_groups=mesh['section'=8,'expert'=32] {'expert'}, dimensions={0} | all-to-all | bytes 163840 | tf_op jit(solution)/shard_map/all_to_all | solution.py:200
  579.7 13.8 %all_to_all.199 = bf16[160,2,128]{2,1,0:T(2,128)(2,1)S(1)} all-to-all(bf16[160,2,128]{2,1,0:T(2,128)(2,1)S(1)} %reshape.260), channel_id=1, replica_groups=mesh['section'=8,'expert'=32] {'expert'}, dimensions={0} | all-to-all | bytes 163840 | tf_op jit(solution)/shard_map/all_to_all | solution.py:200
  602.5 13.4 %all_to_all.200 = bf16[160,2,128]{2,1,0:T(2,128)(2,1)S(1)} all-to-all(bf16[160,2,128]{2,1,0:T(2,128)(2,1)S(1)} %reshape.262), channel_id=1, replica_groups=mesh['section'=8,'expert'=32] {'expert'}, dimensions={0} | all-to-all | bytes 163840 | tf_op jit(solution)/shard_map/all_to_all | solution.py:200
  623.9 13.3 %all_to_all.201 = bf16[160,2,128]{2,1,0:T(2,128)(2,1)S(1)} all-to-all(bf16[160,2,128]{2,1,0:T(2,128)(2,1)S(1)} %reshape.264), channel_id=1, replica_groups=mesh['section'=8,'expert'=32] {'expert'}, dimensions={0} | all-to-all | bytes 163840 | tf_op jit(solution)/shard_map/all_to_all | solution.py:200
  645.4 13.7 %all_to_all.202 = bf16[160,2,128]{2,1,0:T(2,128)(2,1)S(1)} all-to-all(bf16[160,2,128]{2,1,0:T(2,128)(2,1)S(1)} %reshape.266), channel_id=1, replica_groups=mesh['section'=8,'expert'=32] {'expert'}, dimensions={0} | all-to-all | bytes 163840 | tf_op jit(solution)/shard_map/all_to_all | solution.py:200
  664.4 13.3 %all_to_all.203 = bf16[160,2,128]{2,1,0:T(2,128)(2,1)S(1)} all-to-all(bf16[160,2,128]{2,1,0:T(2,128)(2,1)S(1)} %reshape.268), channel_id=1, replica_groups=mesh['section'=8,'expert'=32] {'expert'}, dimensions={0} | all-to-all | bytes 163840 | tf_op jit(solution)/shard_map/all_to_all | solution.py:200
  685.9 13.5 %all_to_all.204 = bf16[160,2,128]{2,1,0:T(2,128)(2,1)S(1)} all-to-all(bf16[160,2,128]{2,1,0:T(2,128)(2,1)S(1)} %reshape.270), channel_id=1, replica_groups=mesh['section'=8,'expert'=32] {'expert'}, dimensions={0} | all-to-all | bytes 163840 | tf_op jit(solution)/shard_map/all_to_all | solution.py:200
  704.8 13.3 %all_to_all.205 = bf16[160,2,128]{2,1,0:T(2,128)(2,1)S(1)} all-to-all(bf16[160,2,128]{2,1,0:T(2,128)(2,1)S(1)} %reshape.272), channel_id=1, replica_groups=mesh['section'=8,'expert'=32] {'expert'}, dimensions={0} | all-to-all | bytes 163840 | tf_op jit(solution)/shard_map/all_to_all | solution.py:200
  726.2 13.5 %all_to_all.206 = bf16[160,2,128]{2,1,0:T(2,128)(2,1)S(1)} all-to-all(bf16[160,2,128]{2,1,0:T(2,128)(2,1)S(1)} %reshape.274), channel_id=1, replica_groups=mesh['section'=8,'expert'=32] {'expert'}, dimensions={0} | all-to-all | bytes 163840 | tf_op jit(solution)/shard_map/all_to_all | solution.py:200
  745.0 13.6 %all_to_all.207 = bf16[160,2,128]{2,1,0:T(2,128)(2,1)S(1)} all-to-all(bf16[160,2,128]{2,1,0:T(2,128)(2,1)S(1)} %reshape.276), channel_id=1, replica_groups=mesh['section'=8,'expert'=32] {'expert'}, dimensions={0} | all-to-all | bytes 163840 | tf_op jit(solution)/shard_map/all_to_all | solution.py:200
  766.8 13.5 %all_to_all.208 = bf16[160,2,128]{2,1,0:T(2,128)(2,1)S(1)} all-to-all(bf16[160,2,128]{2,1,0:T(2,128)(2,1)S(1)} %reshape.278), channel_id=1, replica_groups=mesh['section'=8,'expert'=32] {'expert'}, dimensions={0} | all-to-all | bytes 163840 | tf_op jit(solution)/shard_map/all_to_all | solution.py:200
  785.7 13.3 %all_to_all.209 = bf16[160,2,128]{2,1,0:T(2,128)(2,1)S(1)} all-to-all(bf16[160,2,128]{2,1,0:T(2,128)(2,1)S(1)} %reshape.280), channel_id=1, replica_groups=mesh['section'=8,'expert'=32] {'expert'}, dimensions={0} | all-to-all | bytes 163840 | tf_op jit(solution)/shard_map/all_to_all | solution.py:200
  805.7 13.3 %all_to_all.210 = bf16[160,2,128]{2,1,0:T(2,128)(2,1)S(1)} all-to-all(bf16[160,2,128]{2,1,0:T(2,128)(2,1)S(1)} %reshape.282), channel_id=1, replica_groups=mesh['section'=8,'expert'=32] {'expert'}, dimensions={0} | all-to-all | bytes 163840 | tf_op jit(solution)/shard_map/all_to_all | solution.py:200
  (299 shorter events, 392.9 us)
Async XLA Ops:
  8.2 21.2 %collective-permute-start.2 = (bf16[1536,768]{1,0:T(8,128)(2,1)}, bf16[1536,768]{1,0:T(8,128)(2,1)}, u32[]{:S(2)}, u32[]{:S(2)}) collective-permute-start(bf16[1536,768]{1,0:T(8,128)(2,1)} %pick.11), channel_id=1, source_target_pairs={{0,32},{32,0},{64,96},{96,64},{128,160},{160,128},{192,224},{224,1... | collective-permute-start | bytes 7077896 | tf_op jit(solution)/shard_map/ppermute | solution.py:420
  17.4 24.7 %collective-permute-start.1 = (bf16[768,768]{1,0:T(8,128)(2,1)}, bf16[768,768]{1,0:T(8,128)(2,1)}, u32[]{:S(2)}, u32[]{:S(2)}) collective-permute-start(bf16[768,768]{1,0:T(8,128)(2,1)} %pick.10), channel_id=1, source_target_pairs={{0,64},{64,128},{128,192},{192,0},{32,224},{96,32},{160,96},{224,1... | collective-permute-start | bytes 3538952 | tf_op jit(solution)/shard_map/ppermute | solution.py:427
  33.5 21.1 %collective-permute-start.5 = (bf16[768,768]{1,0:T(8,128)(2,1)}, bf16[768,768]{1,0:T(8,128)(2,1)S(1)}, u32[]{:S(2)}, u32[]{:S(2)}) collective-permute-start(bf16[768,768]{1,0:T(8,128)(2,1)} %pick.14), channel_id=1, source_target_pairs={{0,64},{64,128},{128,192},{192,0},{32,224},{96,32},{160,96},{224,1... | collective-permute-start | bytes 3538952 | tf_op jit(solution)/shard_map/ppermute | solution.py:427
  45.2 22.5 %collective-permute-start.4 = (bf16[768,768]{1,0:T(8,128)(2,1)}, bf16[768,768]{1,0:T(8,128)(2,1)}, u32[]{:S(2)}, u32[]{:S(2)}) collective-permute-start(bf16[768,768]{1,0:T(8,128)(2,1)} %pick.13), channel_id=1, source_target_pairs={{0,64},{64,128},{128,192},{192,0},{32,224},{96,32},{160,96},{224,1... | collective-permute-start | bytes 3538952 | tf_op jit(solution)/shard_map/ppermute | solution.py:427
  47.3 25.6 %all-to-all-start.1 = ((bf16[8,2,2,768]{3,1,2,0:T(2,128)(2,1)}), bf16[8,2,2,768]{3,1,2,0:T(2,128)(2,1)S(1)}, u32[]{:S(2)}, u32[]{:S(2)}) async-start(bf16[8,2,2,768]{3,1,2,0:T(2,128)(2,1)} %broadcast_in_dim.27), calls=%async_computation.1 | async-start | bytes 98304 | tf_op jit(solution)/shard_map/all_to_all | solution.py:438
  58.8 36.7 %collective-permute-start.7 = (bf16[768,768]{1,0:T(8,128)(2,1)}, bf16[768,768]{1,0:T(8,128)(2,1)S(1)}, u32[]{:S(2)}, u32[]{:S(2)}) collective-permute-start(bf16[768,768]{1,0:T(8,128)(2,1)} %pick.16), channel_id=1, source_target_pairs={{0,64},{64,128},{128,192},{192,0},{32,224},{96,32},{160,96},{224,1... | collective-permute-start | bytes 3538952 | tf_op jit(solution)/shard_map/ppermute | solution.py:427
  70.7 24.8 %collective-permute-start.6 = (bf16[768,768]{1,0:T(8,128)(2,1)}, bf16[768,768]{1,0:T(8,128)(2,1)}, u32[]{:S(2)}, u32[]{:S(2)}) collective-permute-start(bf16[768,768]{1,0:T(8,128)(2,1)} %pick.15), channel_id=1, source_target_pairs={{0,64},{64,128},{128,192},{192,0},{32,224},{96,32},{160,96},{224,1... | collective-permute-start | bytes 3538952 | tf_op jit(solution)/shard_map/ppermute | solution.py:427
  73.0 20.7 %all-to-all-start = ((s32[1,2,8,512,2]{3,4,1,0,2:T(2,128)}), s32[1,2,8,512,2]{3,4,1,0,2:T(2,128)S(1)}, u32[]{:S(2)}, u32[]{:S(2)}) async-start(s32[1,2,8,512,2]{3,4,1,0,2:T(2,128)} %bitcast.40), calls=%async_computation | async-start | bytes 131072 | tf_op jit(solution)/shard_map/all_to_all | solution.py:433
  101.4 29.6 %collective-permute-start.8 = (bf16[1536,768]{1,0:T(8,128)(2,1)}, bf16[1536,768]{1,0:T(8,128)(2,1)}, u32[]{:S(2)}, u32[]{:S(2)}) collective-permute-start(bf16[1536,768]{1,0:T(8,128)(2,1)} %get-tuple-element.210.refs_4_), channel_id=1, source_target_pairs={{0,32},{32,0},{64,96},{96,64},{128,160},{160,128},{192,224},{224,1... | collective-permute-start | bytes 7077896 | tf_op jit(solution)/shard_map/ppermute | solution.py:420
  104.7 26.3 %collective-permute-start.9 = (bf16[768,768]{1,0:T(8,128)(2,1)}, bf16[768,768]{1,0:T(8,128)(2,1)S(1)}, u32[]{:S(2)}, u32[]{:S(2)}) collective-permute-start(bf16[768,768]{1,0:T(8,128)(2,1)} %pick.17), channel_id=1, source_target_pairs={{0,64},{64,128},{128,192},{192,0},{32,224},{96,32},{160,96},{224,1... | collective-permute-start | bytes 3538952 | tf_op jit(solution)/shard_map/ppermute | solution.py:427
  106.2 46.1 %collective-permute-start.10 = (bf16[768,768]{1,0:T(8,128)(2,1)}, bf16[768,768]{1,0:T(8,128)(2,1)}, u32[]{:S(2)}, u32[]{:S(2)}) collective-permute-start(bf16[768,768]{1,0:T(8,128)(2,1)} %get-tuple-element.215), channel_id=1, source_target_pairs={{0,64},{64,128},{128,192},{192,0},{32,224},{96,32},{160,96},{224,1... | collective-permute-start | bytes 3538952 | tf_op jit(solution)/shard_map/ppermute | solution.py:427
  108.5 21.8 %all-to-all-start.2 = ((bf16[160,2,128]{2,1,0:T(2,128)(2,1)}), bf16[160,2,128]{2,1,0:T(2,128)(2,1)S(1)}, u32[]{:S(2)}, u32[]{:S(2)}) async-start(bf16[160,2,128]{2,1,0:T(2,128)(2,1)} %reshape.220), calls=%async_computation.2 | async-start | bytes 163840 | tf_op jit(solution)/shard_map/all_to_all | solution.py:200
  182.4 18.2 %collective-permute-start.13 = (bf16[1536,768]{1,0:T(8,128)(2,1)}, bf16[1536,768]{1,0:T(8,128)(2,1)}, u32[]{:S(2)}, u32[]{:S(2)}) collective-permute-start(bf16[1536,768]{1,0:T(8,128)(2,1)} %get-tuple-element.235.refs_4_), channel_id=1, source_target_pairs={{0,32},{32,0},{64,96},{96,64},{128,160},{160,128},{192,224},{224,1... | collective-permute-start | bytes 7077896 | tf_op jit(solution)/shard_map/ppermute | solution.py:420
  184.0 39.5 %collective-permute-start.15 = (bf16[768,768]{1,0:T(8,128)(2,1)}, bf16[768,768]{1,0:T(8,128)(2,1)}, u32[]{:S(2)}, u32[]{:S(2)}) collective-permute-start(bf16[768,768]{1,0:T(8,128)(2,1)} %get-tuple-element.233), channel_id=1, source_target_pairs={{0,64},{64,128},{128,192},{192,0},{32,224},{96,32},{160,96},{224,1... | collective-permute-start | bytes 3538952 | tf_op jit(solution)/shard_map/ppermute | solution.py:427
  205.9 37.9 %collective-permute-start.16 = (bf16[768,768]{1,0:T(8,128)(2,1)}, bf16[768,768]{1,0:T(8,128)(2,1)S(1)}, u32[]{:S(2)}, u32[]{:S(2)}) collective-permute-start(bf16[768,768]{1,0:T(8,128)(2,1)} %get-tuple-element.239), channel_id=1, source_target_pairs={{0,64},{64,128},{128,192},{192,0},{32,224},{96,32},{160,96},{224,1... | collective-permute-start | bytes 3538952 | tf_op jit(solution)/shard_map/ppermute | solution.py:427
  275.5 38.4 %collective-permute-start.21 = (bf16[768,768]{1,0:T(8,128)(2,1)}, bf16[768,768]{1,0:T(8,128)(2,1)}, u32[]{:S(2)}, u32[]{:S(2)}) collective-permute-start(bf16[768,768]{1,0:T(8,128)(2,1)} %get-tuple-element.257), channel_id=1, source_target_pairs={{0,64},{64,128},{128,192},{192,0},{32,224},{96,32},{160,96},{224,1... | collective-permute-start | bytes 3538952 | tf_op jit(solution)/shard_map/ppermute | solution.py:427
  297.6 36.8 %collective-permute-start.22 = (bf16[768,768]{1,0:T(8,128)(2,1)}, bf16[768,768]{1,0:T(8,128)(2,1)S(1)}, u32[]{:S(2)}, u32[]{:S(2)}) collective-permute-start(bf16[768,768]{1,0:T(8,128)(2,1)} %get-tuple-element.263), channel_id=1, source_target_pairs={{0,64},{64,128},{128,192},{192,0},{32,224},{96,32},{160,96},{224,1... | collective-permute-start | bytes 3538952 | tf_op jit(solution)/shard_map/ppermute | solution.py:427
  365.7 19.5 %collective-permute-start.25 = (bf16[1536,768]{1,0:T(8,128)(2,1)}, bf16[1536,768]{1,0:T(8,128)(2,1)}, u32[]{:S(2)}, u32[]{:S(2)}) collective-permute-start(bf16[1536,768]{1,0:T(8,128)(2,1)} %get-tuple-element.283.refs_4_), channel_id=1, source_target_pairs={{0,32},{32,0},{64,96},{96,64},{128,160},{160,128},{192,224},{224,1... | collective-permute-start | bytes 7077896 | tf_op jit(solution)/shard_map/ppermute | solution.py:420
  366.0 19.2 %collective-permute-start.26 = (bf16[768,768]{1,0:T(8,128)(2,1)}, bf16[768,768]{1,0:T(8,128)(2,1)S(1)}, u32[]{:S(2)}, u32[]{:S(2)}) collective-permute-start(bf16[768,768]{1,0:T(8,128)(2,1)} %get-tuple-element.276), channel_id=1, source_target_pairs={{0,64},{64,128},{128,192},{192,0},{32,224},{96,32},{160,96},{224,1... | collective-permute-start | bytes 3538952 | tf_op jit(solution)/shard_map/ppermute | solution.py:427
  367.5 38.1 %collective-permute-start.27 = (bf16[768,768]{1,0:T(8,128)(2,1)}, bf16[768,768]{1,0:T(8,128)(2,1)}, u32[]{:S(2)}, u32[]{:S(2)}) collective-permute-start(bf16[768,768]{1,0:T(8,128)(2,1)} %get-tuple-element.281), channel_id=1, source_target_pairs={{0,64},{64,128},{128,192},{32,224},{96,32},{160,96},{224,160},{1,6... | collective-permute-start | bytes 3538952 | tf_op jit(solution)/shard_map/ppermute | solution.py:427
  412.0 20.7 %collective-permute-start.28 = (bf16[1536,768]{1,0:T(8,128)(2,1)}, bf16[1536,768]{1,0:T(8,128)(2,1)}, u32[]{:S(2)}, u32[]{:S(2)}) collective-permute-start(bf16[1536,768]{1,0:T(8,128)(2,1)} %get-tuple-element.295.refs_4_), channel_id=1, source_target_pairs={{0,32},{32,0},{64,96},{96,64},{128,160},{160,128},{192,224},{224,1... | collective-permute-start | bytes 7077896 | tf_op jit(solution)/shard_map/ppermute | solution.py:420
  412.1 20.6 %collective-permute-start.29 = (bf16[768,768]{1,0:T(8,128)(2,1)}, bf16[768,768]{1,0:T(8,128)(2,1)S(1)}, u32[]{:S(2)}, u32[]{:S(2)}) collective-permute-start(bf16[768,768]{1,0:T(8,128)(2,1)} %get-tuple-element.288), channel_id=1, source_target_pairs={{0,64},{64,128},{128,192},{32,224},{96,32},{160,96},{224,160},{1,6... | collective-permute-start | bytes 3538952 | tf_op jit(solution)/shard_map/ppermute | solution.py:427
  415.9 37.1 %collective-permute-start.30 = (bf16[768,768]{1,0:T(8,128)(2,1)}, bf16[768,768]{1,0:T(8,128)(2,1)}, u32[]{:S(2)}, u32[]{:S(2)}) collective-permute-start(bf16[768,768]{1,0:T(8,128)(2,1)} %get-tuple-element.293), channel_id=1, source_target_pairs={{0,64},{64,128},{128,192},{192,0},{32,224},{160,96},{224,160},{1,6... | collective-permute-start | bytes 3538952 | tf_op jit(solution)/shard_map/ppermute | solution.py:427
  459.8 23.6 %collective-permute-start.31 = (bf16[1536,768]{1,0:T(8,128)(2,1)}, bf16[1536,768]{1,0:T(8,128)(2,1)}, u32[]{:S(2)}, u32[]{:S(2)}) collective-permute-start(bf16[1536,768]{1,0:T(8,128)(2,1)} %get-tuple-element.307.refs_4_), channel_id=1, source_target_pairs={{0,32},{32,0},{64,96},{96,64},{128,160},{160,128},{192,224},{224,1... | collective-permute-start | bytes 7077896 | tf_op jit(solution)/shard_map/ppermute | solution.py:420
  459.9 23.5 %collective-permute-start.32 = (bf16[768,768]{1,0:T(8,128)(2,1)}, bf16[768,768]{1,0:T(8,128)(2,1)S(1)}, u32[]{:S(2)}, u32[]{:S(2)}) collective-permute-start(bf16[768,768]{1,0:T(8,128)(2,1)} %get-tuple-element.300), channel_id=1, source_target_pairs={{0,64},{64,128},{128,192},{192,0},{32,224},{160,96},{224,160},{1,6... | collective-permute-start | bytes 3538952 | tf_op jit(solution)/shard_map/ppermute | solution.py:427
  462.3 41.3 %collective-permute-start.33 = (bf16[768,768]{1,0:T(8,128)(2,1)}, bf16[768,768]{1,0:T(8,128)(2,1)}, u32[]{:S(2)}, u32[]{:S(2)}) collective-permute-start(bf16[768,768]{1,0:T(8,128)(2,1)} %get-tuple-element.305), channel_id=1, source_target_pairs={{64,128},{128,192},{192,0},{32,224},{96,32},{224,160},{65,129},{12... | collective-permute-start | bytes 3538952 | tf_op jit(solution)/shard_map/ppermute | solution.py:427
  509.9 19.6 %collective-permute-start.34 = (bf16[1536,768]{1,0:T(8,128)(2,1)}, bf16[1536,768]{1,0:T(8,128)(2,1)}, u32[]{:S(2)}, u32[]{:S(2)}) collective-permute-start(bf16[1536,768]{1,0:T(8,128)(2,1)} %get-tuple-element.319.refs_4_), channel_id=1, source_target_pairs={{0,32},{32,0},{64,96},{96,64},{128,160},{160,128},{192,224},{224,1... | collective-permute-start | bytes 7077896 | tf_op jit(solution)/shard_map/ppermute | solution.py:420
  510.0 19.5 %collective-permute-start.35 = (bf16[768,768]{1,0:T(8,128)(2,1)}, bf16[768,768]{1,0:T(8,128)(2,1)S(1)}, u32[]{:S(2)}, u32[]{:S(2)}) collective-permute-start(bf16[768,768]{1,0:T(8,128)(2,1)} %get-tuple-element.312), channel_id=1, source_target_pairs={{64,128},{128,192},{192,0},{32,224},{96,32},{224,160},{65,129},{12... | collective-permute-start | bytes 3538952 | tf_op jit(solution)/shard_map/ppermute | solution.py:427
  512.8 37.0 %collective-permute-start.36 = (bf16[768,768]{1,0:T(8,128)(2,1)}, bf16[768,768]{1,0:T(8,128)(2,1)}, u32[]{:S(2)}, u32[]{:S(2)}) collective-permute-start(bf16[768,768]{1,0:T(8,128)(2,1)} %get-tuple-element.317), channel_id=1, source_target_pairs={{192,0},{160,96},{193,1},{161,97},{194,2},{162,98},{195,3},{163,99... | collective-permute-start | bytes 3538952 | tf_op jit(solution)/shard_map/ppermute | solution.py:427
  556.9 37.2 %collective-permute-start.39 = (bf16[768,768]{1,0:T(8,128)(2,1)}, bf16[768,768]{1,0:T(8,128)(2,1)}, u32[]{:S(2)}, u32[]{:S(2)}) collective-permute-start(bf16[768,768]{1,0:T(8,128)(2,1)} %get-tuple-element.329), channel_id=1, source_target_pairs={{0,64},{96,32},{1,65},{97,33},{2,66},{98,34},{3,67},{99,35},{4,68}... | collective-permute-start | bytes 3538952 | tf_op jit(solution)/shard_map/ppermute | solution.py:427
  600.2 18.9 %collective-permute-start.40 = (bf16[1536,768]{1,0:T(8,128)(2,1)}, bf16[1536,768]{1,0:T(8,128)(2,1)}, u32[]{:S(2)}, u32[]{:S(2)}) collective-permute-start(bf16[1536,768]{1,0:T(8,128)(2,1)} %get-tuple-element.339.refs_4_), channel_id=1, source_target_pairs={{0,32},{32,0},{64,96},{96,64},{128,160},{160,128},{192,224},{224,1... | collective-permute-start | bytes 7077896 | tf_op jit(solution)/shard_map/ppermute | solution.py:420
  600.3 18.8 %collective-permute-start.41 = (bf16[768,768]{1,0:T(8,128)(2,1)}, bf16[768,768]{1,0:T(8,128)(2,1)S(1)}, u32[]{:S(2)}, u32[]{:S(2)}) collective-permute-start(bf16[768,768]{1,0:T(8,128)(2,1)} %get-tuple-element.335), channel_id=1, source_target_pairs={{0,64},{96,32},{1,65},{97,33},{2,66},{98,34},{3,67},{99,35},{4,68}... | collective-permute-start | bytes 3538952 | tf_op jit(solution)/shard_map/ppermute | solution.py:427
  (38 other events, 359.7 us)

commit v4 on v2

v4 whole, which is shorter than its diff:
```python
import functools

import jax
import jax.numpy as jnp
import numpy as np
from jax import lax
from jax.experimental import pallas as pl
from jax.experimental.pallas import tpu as pltpu
from jax.sharding import PartitionSpec as P

VMEM_LIMIT = 62 * 1024 * 1024
HBM = pl.BlockSpec(memory_space=pltpu.HBM)
SMEM = pl.BlockSpec(memory_space=pltpu.SMEM)
VMEM = pl.BlockSpec(memory_space=pltpu.VMEM)
DIRS = (1, -1)


PACK = 64
SLOTS = 48
ROWS = 10
PARTS = 2
LEAD = 6


def ring_plan(sections, layers, parts, lead):
    chips = sections // 2
    items = layers * parts
    held = [
        [
            {i: (0, 0, 0) for i in range(items) if (i // parts) % sections // 2 == y}
            for y in range(chips)
        ]
        for _ in DIRS
    ]
    steps = []
    while any(len(stock) < items for lane in held for stock in lane):
        number = len(steps) + 1
        moves = []
        for lane, step in enumerate(DIRS):
            for y in range(chips):
                target = (y + step) % chips
                there = held[lane][target]
                options = sorted(i for i, at in held[lane][y].items() if at[0] < number and i not in there)
                for place, i in enumerate(options[: 1 if number <= lead else parts]):
                    moves.append((lane, y, target, i, place))
        steps.append(moves)
        for lane, _, target, i, place in moves:
            held[lane][target][i] = (number + (number < lead), number, place)
    return steps, held


def pick_kernel(rows, places, tab_ref, *refs):
    count = len(places)
    sources, (out_ref, hold_ref, in_sems, out_sems) = refs[:count], refs[count:]
    size = hold_ref.shape[0] // len(rows)

    def view(number, start):
        return sources[number].at[places[number] + (pl.ds(start, size),)]

    def part_of(ref, part):
        return ref.at[pl.ds(part * size, size)]

    for part, (row, choices) in enumerate(rows):
        choice = tab_ref[row]
        for number, (source, start) in enumerate(choices):

            @pl.when(choice == number)
            def _(part=part, source=source, start=start):
                pltpu.make_async_copy(
                    view(source, start), part_of(hold_ref, part), in_sems.at[part]
                ).start()

    def leave(part):
        return pltpu.make_async_copy(
            part_of(hold_ref, part), part_of(out_ref, part), out_sems.at[part]
        )

    for part, (_, choices) in enumerate(rows):
        pltpu.make_async_copy(
            view(*choices[0]), part_of(hold_ref, part), in_sems.at[part]
        ).wait()
        leave(part).start()
    for part in range(len(rows)):
        leave(part).wait()


def pick(tab, rows, sources, places, size, width):
    shape = (size * len(rows), width)
    return pl.pallas_call(
        functools.partial(pick_kernel, rows, places),
        out_shape=jax.ShapeDtypeStruct(shape, jnp.bfloat16),
        in_specs=[SMEM] + [HBM] * len(sources),
        out_specs=HBM,
        scratch_shapes=[
            pltpu.VMEM(shape, jnp.bfloat16),
            pltpu.SemaphoreType.DMA((len(rows),)),
            pltpu.SemaphoreType.DMA((len(rows),)),
        ],
        compiler_params=pltpu.CompilerParams(vmem_limit_bytes=VMEM_LIMIT),
        cost_estimate=pl.CostEstimate(
            flops=0, bytes_accessed=4 * shape[0] * width, transcendentals=0
        ),
        name="pick",
    )(tab, *sources)


LANES = 128


def turned(value, lanes):
    return pltpu.roll(value, lanes % LANES, value.ndim - 1)


def lanes_of(value):
    return lax.broadcasted_iota(jnp.int32, (1,) * (value.ndim - 1) + (LANES,), value.ndim - 1)


def fold_tail(third, at):
    axis = third.ndim - 1
    spread = pltpu.roll(turned(third, -at - 32), 0, axis, stride=16, stride_axis=axis - 1)
    place = lax.broadcasted_iota(jnp.int32, third.shape, axis) // 16
    own = place == lax.broadcasted_iota(jnp.int32, third.shape, axis - 1)
    return jnp.sum(jnp.where(own, spread, 0.0), axis=axis - 1, keepdims=True)


def unfold_tail(row, at):
    value = jnp.broadcast_to(turned(row, at + 32), row.shape[:-2] + (8, LANES))
    number = lax.broadcasted_iota(jnp.int32, value.shape, value.ndim - 2)
    for step in (1, 2, 4):
        value = jnp.where((number & step) != 0, turned(value, -16 * step), value)
    return value


def pack(first, second, third, at, gates=None):
    lanes = lanes_of(first)
    top = jnp.where(
        lanes < SLOTS,
        turned(first, -at),
        jnp.where(lanes < 2 * SLOTS, turned(second, SLOTS - at), turned(third, 2 * SLOTS - at)),
    )
    tail = fold_tail(third, at)
    axis = first.ndim - 2
    number = lax.broadcasted_iota(jnp.int32, top.shape, axis)
    last = jnp.broadcast_to(tail, top.shape)
    if gates is not None:
        last = jnp.where(number == 0, last, gates)
    return jnp.concatenate([top, last], axis=axis)


def unpack(blocks, at):
    top, last = blocks[..., 0:8, :], blocks[..., 8:16, :]
    lanes = lanes_of(blocks)
    third = jnp.where(
        lanes - at < 32, turned(top, at - 2 * SLOTS), unfold_tail(last[..., 0:1, :], at)
    )
    return turned(top, at), turned(top, at - SLOTS), third, turned(last, at)


def unpack_pairs(back):
    pairs = back.shape[0] // 2
    split = back.reshape(pairs, 2, 16, LANES)
    low = lanes_of(back) < PACK
    both = zip(unpack(split[:, 0], 0), unpack(split[:, 1], PACK))
    groups = [jnp.where(low, even, odd) for even, odd in both]
    gates = jnp.broadcast_to(groups[3][:, 1:2], groups[0].shape)
    return jnp.concatenate(groups[0:3] + [gates], axis=1)


TILES = ROWS // 2


def load_blocks(ref, wide_ref):
    for number in range(wide_ref.shape[0]):
        block = ref[TILES * number : TILES * (number + 1)].reshape(ROWS, LANES)
        wide_ref[number, 0:ROWS] = block.astype(jnp.float32)
    return wide_ref[...]


def store_block(ref, number, block):
    rows = block.astype(jnp.bfloat16).reshape(8, 2, LANES)
    ref[TILES * number : TILES * (number + 1)] = rows[0:TILES]


def send_blocks(value):
    return lax.all_to_all(value, "expert", split_axis=0, concat_axis=0, tiled=True)


def turn_kernel(merge, send, *refs):
    refs = list(refs)
    h_ref = refs.pop(0)
    if merge:
        back_ref, row_ref = refs.pop(0), refs.pop(0)
    if send:
        next_ref = refs.pop(0)
    hnew_ref = refs.pop(0)
    features, tokens = h_ref.shape
    held = h_ref[...]
    if merge:
        tiles = unpack_pairs(load_blocks(back_ref, refs.pop())).astype(jnp.bfloat16)
        offset = lax.broadcasted_iota(jnp.int32, (4 * PACK, tokens), 0)
        first, second = row_ref[0:1, :] - offset, row_ref[1:2, :] - offset
        update = jnp.zeros((32, tokens), jnp.float32)
        for turn in range(tiles.shape[0] // 2):
            base = turn * 4 * PACK
            onehot = jnp.where((first == base) | (second == base), 1.0, 0.0)
            pair = jnp.concatenate([tiles[2 * turn], tiles[2 * turn + 1]], axis=1)
            update += jnp.dot(
                pair, onehot.astype(jnp.bfloat16), preferred_element_type=jnp.float32
            )
        change = update[0:features] * (1.0 / update[features:features + 1])
        held = (held.astype(jnp.float32) + change).astype(jnp.bfloat16)
    hnew_ref[...] = held
    if send:
        out_ref = refs.pop(0)
        offset = lax.broadcasted_iota(jnp.int32, (tokens, 4 * PACK), 1)
        col = next_ref[...].astype(jnp.float32).T.astype(jnp.int32)
        first, second = col[:, 0:1] - offset, col[:, 1:2] - offset
        for turn in range(out_ref.shape[0] // TILES // 4):
            base = turn * 4 * PACK
            onehot = jnp.where((first == base) | (second == base), 1.0, 0.0)
            found = jnp.dot(held, onehot.astype(jnp.bfloat16), preferred_element_type=jnp.float32)
            for half in range(2):
                tile = found[:, LANES * half : LANES * (half + 1)]
                groups = tile[0:8], tile[8:16], tile[16:24]
                number = turn * 4 + half * 2
                store_block(out_ref, number, pack(*groups, 0))
                store_block(out_ref, number + 1, pack(*groups, PACK))


def run_turn(experts, h, back, rows, before, after):
    features, tokens = h.shape
    merge, send = before is not None, after is not None
    operands, specs, scratch = [h], [VMEM], []
    shapes, outs = [jax.ShapeDtypeStruct(h.shape, h.dtype)], [VMEM]
    if merge:
        operands += [back, rows]
        specs += [VMEM, plane((8, tokens), before)]
        scratch += [pltpu.VMEM((experts, 16, LANES), jnp.float32)]
    if send:
        operands += [rows]
        specs += [plane((8, tokens), after)]
        shapes += [jax.ShapeDtypeStruct((experts * TILES, 2, LANES), jnp.bfloat16)]
        outs += [VMEM]
    return pl.pallas_call(
        functools.partial(turn_kernel, merge, send),
        out_shape=tuple(shapes),
        grid=(1,),
        in_specs=specs,
        out_specs=tuple(outs),
        scratch_shapes=scratch,
        compiler_params=pltpu.CompilerParams(vmem_limit_bytes=VMEM_LIMIT),
        name="turn",
    )(*operands)


def expert_kernel(
    scal_ref, blocks_ref, gain_ref, router_ref, lane_ref, other_ref, out_ref,
    win_ref, wout_ref, wide_ref, sems,
):
    core = scal_ref[0]

    @pl.when(core == 0)
    def _():
        pltpu.make_async_copy(lane_ref, win_ref, sems.at[0]).start()
        pltpu.make_async_copy(other_ref, wout_ref, sems.at[1]).start()

    @pl.when(core != 0)
    def _():
        pltpu.make_async_copy(other_ref, win_ref, sems.at[0]).start()
        pltpu.make_async_copy(lane_ref, wout_ref, sems.at[1]).start()

    width = win_ref.shape[1]
    groups = wide_ref.shape[0]
    blocks = load_blocks(blocks_ref, wide_ref)
    parts = [group[:, None] for group in unpack(blocks, 0)[0:3]]
    tall = jnp.concatenate(parts, axis=1).reshape(width, LANES)
    wide = tall.T[0:PACK]
    mean_square = jnp.mean(wide * wide, axis=1, keepdims=True)
    normed = (wide * lax.rsqrt(mean_square + 1e-06) * gain_ref[...]).astype(jnp.bfloat16)
    logit = jnp.sum(normed.astype(jnp.float32) * router_ref[...], axis=1, keepdims=True)
    gate = jax.nn.sigmoid(logit).astype(jnp.bfloat16).astype(jnp.float32)
    pltpu.make_async_copy(lane_ref, win_ref, sems.at[0]).wait()
    pre_act = lax.dot_general(
        normed, win_ref[...], (((1,), (1,)), ((), ())), preferred_element_type=jnp.float32
    )
    active = jax.nn.gelu(pre_act, approximate=True).astype(jnp.bfloat16)
    pltpu.make_async_copy(lane_ref, wout_ref, sems.at[1]).wait()
    output = jnp.dot(active, wout_ref[...], preferred_element_type=jnp.float32)
    weighted = output * gate
    spread = jnp.broadcast_to(gate, (PACK, LANES))
    zeros = jnp.zeros_like(weighted)
    tall = jnp.concatenate([weighted, zeros], axis=0).T.reshape(groups, 3, 8, LANES)
    gates = jnp.concatenate([spread, jnp.zeros_like(spread)], axis=0).T[0:8]
    gates = jnp.broadcast_to(gates[None], (groups, 8, LANES))
    packed = pack(tall[:, 0], tall[:, 1], tall[:, 2], 0, gates)
    for number in range(groups):
        store_block(out_ref, number, packed[number])


def run_expert(layer, scal, blocks, gains, routers, lane_w, other_w):
    hidden, width = lane_w.shape
    return pl.pallas_call(
        expert_kernel,
        out_shape=jax.ShapeDtypeStruct(blocks.shape, jnp.bfloat16),
        grid=(1,),
        in_specs=[SMEM, VMEM, plane((1, width), layer), plane((1, width), layer), HBM, HBM],
        out_specs=VMEM,
        scratch_shapes=[
            pltpu.VMEM((hidden, width), jnp.bfloat16),
            pltpu.VMEM((hidden, width), jnp.bfloat16),
            pltpu.VMEM((blocks.shape[0] // TILES, 16, LANES), jnp.float32),
            pltpu.SemaphoreType.DMA((2,)),
        ],
        compiler_params=pltpu.CompilerParams(vmem_limit_bytes=VMEM_LIMIT),
        cost_estimate=pl.CostEstimate(
            flops=4 * PACK * hidden * width, bytes_accessed=4 * hidden * width, transcendentals=0
        ),
        name="expert",
    )(scal, blocks, gains, routers, lane_w, other_w)


def plane(shape, *lead):
    return pl.BlockSpec((None,) * len(lead) + shape, lambda i: lead + (0,) * len(shape))


def place_tokens(routes, experts):
    tokens = routes.shape[1]
    ids = jnp.arange(experts, dtype=jnp.int32)
    first = routes[:, :, 0:1] == ids
    second = routes[:, :, 1:2] == ids
    named = (first | second).astype(jnp.bfloat16)
    earlier = jnp.tril(jnp.ones((tokens, tokens), jnp.bfloat16), -1)
    rank = jnp.einsum("ut,lte->lue", earlier, named, preferred_element_type=jnp.float32)
    rank = rank.astype(jnp.int32) + ids * PACK
    slot_first = jnp.sum(jnp.where(first, rank, 0), axis=2)
    slot_second = jnp.sum(jnp.where(second, rank, 0), axis=2)
    blank = jnp.zeros_like(slot_first)
    return jnp.stack([slot_first, slot_second] + [blank] * 6, axis=1)


def join(*values):
    return lax.optimization_barrier(values)


def local(inputs, routes, norm_gains, routers, expert_in, expert_out):
    sections = lax.axis_size("section")
    experts = lax.axis_size("expert")
    section_pos = lax.axis_index("section")
    repeats, _, _, hidden, width = expert_in.shape
    layers = repeats * sections
    steps, held = ring_plan(sections, layers, PARTS, LEAD)
    size = hidden // PARTS
    scal = jnp.stack([section_pos % 2, section_pos]).astype(jnp.int32)

    buffers = {("in", r): (expert_in, (r, 0, 0)) for r in range(repeats)}
    buffers.update({("out", r): (expert_out, (r, 0, 0)) for r in range(repeats)})
    every = [(lane, y) for lane in range(2) for y in range(sections // 2)]
    table, wanted = [], []

    def source_of(lane, y, i):
        q, part = i // PARTS, i % PARTS
        if q % sections // 2 != y:
            _, number, place = held[lane][y][i]
            return ("ring", number), place * size
        name = ("in", "out")[lane] if q % 2 == lane else "swapped"
        return (name, q // sections), part * size

    def add_pick(by_section):
        choices = sorted(set(by_section.values()))
        table.append([choices.index(by_section.get(s, choices[0])) for s in range(sections)])
        wanted.append(choices)
        return len(table) - 1

    swap_rows = [
        [
            add_pick({2 * y + lane: ((("out", "in")[lane], r), part * size) for lane, y in every})
            for part in range(PARTS)
        ]
        for r in range(repeats)
    ]
    ring_rows = [
        [
            add_pick({2 * y + lane: source_of(lane, y, i) for lane, y, _, i, at in moves if at == place})
            for place in sorted({move[4] for move in moves})
        ]
        for moves in steps
    ]
    layer_rows = [
        [
            add_pick({2 * y + lane: source_of(lane, y, q * PARTS + part) for lane, y in every})
            for part in range(PARTS)
        ]
        for q in range(layers)
    ]
    tab = jnp.asarray(np.array(table, np.int32).T)[section_pos]

    def picked(rows, tab):
        names = sorted({name for row in rows for name, _ in wanted[row]})
        found = [buffers[name] for name in names]
        plan = tuple(
            (row, tuple((names.index(name), start) for name, start in wanted[row])) for row in rows
        )
        places = [place for _, place in found]
        return pick(tab, plan, [array for array, _ in found], places, size, width)

    def swapped(value):
        return lax.ppermute(value, "section", [(s, s ^ 1) for s in range(sections)])

    def ring(number, tab):
        if number > len(steps):
            return None
        moves = steps[number - 1]
        pairs = sorted({(2 * y + lane, 2 * target + lane) for lane, y, target, _, _ in moves})
        return lax.ppermute(picked(ring_rows[number - 1], tab), "section", pairs)

    def arrival(q):
        parts = range(q * PARTS, (q + 1) * PARTS)
        return max(stock[i][0] for lane in held for stock in lane for i in parts)

    mine = lax.all_to_all(routes[:, 0], "section", split_axis=1, concat_axis=0, tiled=False)
    mine = jnp.transpose(mine, (1, 0, 2, 3)).reshape(layers, -1, 2)
    rows = place_tokens(mine, experts)
    small = jnp.stack([norm_gains[:, 0], routers[:, 0, 0]])
    small = jnp.broadcast_to(small[None], (sections,) + small.shape)
    small = lax.all_to_all(small, "section", split_axis=0, concat_axis=0, tiled=True)
    small = jnp.transpose(small, (1, 2, 0, 3)).reshape(2, layers, 1, width).astype(jnp.float32)
    gains, gate_rows = small[0], small[1]
    h = jnp.transpose(inputs[0], (1, 0))

    buffers[("swapped", 0)] = (swapped(picked(swap_rows[0], tab)), ())
    later = swapped(picked(swap_rows[1], tab))
    flying = None
    for number in range(1, LEAD + 1):
        started = ring(number, tab)
        if flying is not None:
            flying, tab = join(flying, tab)
            buffers[("ring", number - 1)] = (flying, ())
        if number == 2:
            later, tab = join(later, tab)
            buffers[("swapped", 1)] = (later, ())
        flying = started
    flying, tab, rows, gains, gate_rows, h = join(flying, tab, rows, gains, gate_rows, h)
    buffers[("ring", LEAD)] = (flying, ())

    back = coming = None
    for q in range(layers):
        h, blocks = run_turn(experts, h, back, rows, q - 1 if q else None, q)
        blocks, tab = join(blocks, tab)
        sent = send_blocks(blocks)
        flying = ring(LEAD + 1 + q, tab)
        if coming is None:
            lane_w = picked(layer_rows[q], tab)
            coming = (lane_w, swapped(lane_w))
        blocks, lane_w, other_w, tab = join(sent, *coming, tab)
        back = run_expert(q, scal, blocks, gains, gate_rows, lane_w, other_w)
        back, tab = join(back, tab)
        sent = send_blocks(back)
        coming = None
        if q + 1 < layers and arrival(q + 1) < LEAD + 1 + q:
            lane_w = picked(layer_rows[q + 1], tab)
            coming = (lane_w, swapped(lane_w))
        if flying is None:
            back, tab = join(sent, tab)
        else:
            back, flying, tab = join(sent, flying, tab)
            buffers[("ring", LEAD + 1 + q)] = (flying, ())

    (h,) = run_turn(experts, h, back, rows, layers - 1, None)
    return jnp.transpose(h, (1, 0))[None]


def solution(mesh):
    return jax.shard_map(
        local,
        mesh=mesh,
        in_specs=(
            P("section", None, "expert"),
            P(None, "section", None, None, None),
            P(None, "section", None),
            P(None, "section", "expert", None),
            P(None, "section", "expert", None, None),
            P(None, "section", "expert", None, None),
        ),
        out_specs=P("section", None, "expert"),
        check_vma=False,
    )
```

time: 936 us -> 848 us (0.906)
  blocking collectives: 265 us -> 205 us
  waiting for transfers between devices: 228 us -> 195 us
  starting transfers between devices: 127 us -> 152 us
  Pallas kernels: 278 us -> 260 us
    all_to_all x18 -> x14, blocking collectives: 265 us -> 205 us  [send_blocks(): lax.all_to_all(value, 'expert', split_axis=0, concat_axis=0, tiled=True)]
    all_to_all x14 -> x18, starting transfers between devices: 63 us -> 107 us  [send_blocks(): lax.all_to_all(value, 'expert', split_axis=0, concat_axis=0, tiled=True)]
    all_to_all x14 -> x18, waiting for transfers between devices: 124 us -> 93.2 us  [send_blocks(): lax.all_to_all(value, 'expert', split_axis=0, concat_axis=0, tiled=True)]
    pallas_call x46 -> x35, Pallas kernels: 138 us -> 118 us  [pick(): pl.pallas_call(functools.partial(pick_kernel, rows, places), out_shape=ja...]
    ppermute x28 -> x17, starting transfers between devices: 42.5 us -> 29 us  [ring(): return lax.ppermute(picked(ring_rows[number - 1], tab), 'section', pairs)]
    ppermute x28 -> x17, waiting for transfers between devices: 93.1 us -> 88.5 us  [ring(): return lax.ppermute(picked(ring_rows[number - 1], tab), 'section', pairs)]
  transfers between devices with their start and end apart: 62 -> 55, of which waited for: 30 -> 32; matrix products, arithmetic and copies ran while one was open for 1% -> 1% of each run, Pallas kernels for 14% -> 22%
where the time goes in v4:
time: 848 us; the launch traced here: 834 us
  Pallas kernels  260 us (31%)
  blocking collectives  205 us (24%)
  waiting for transfers between devices  195 us (23%)
  starting transfers between devices  152 us (18%)
  local copies, waits for them, and re-layouts  17.6 us (2%)
    all_to_all x14, blocking collectives, send_blocks(): lax.all_to_all(value, 'expert', split_axis=0, concat_axis=0, tiled=True)  205 us
    pallas_call x35, Pallas kernels, pick(): pl.pallas_call(functools.partial(pick_kernel, rows, places), out_shape=ja...  118 us
    all_to_all x18, starting transfers between devices, send_blocks(): lax.all_to_all(value, 'expert', split_axis=0, concat_axis=0, tiled=True)  107 us
    all_to_all x18, waiting for transfers between devices, send_blocks(): lax.all_to_all(value, 'expert', split_axis=0, concat_axis=0, tiled=True)  93.2 us
    ppermute x17, waiting for transfers between devices, ring(): return lax.ppermute(picked(ring_rows[number - 1], tab), 'section', pairs)  88.5 us
    pallas_call x16, Pallas kernels, run_expert(): pl.pallas_call(expert_kernel, out_shape=jax.ShapeDtypeStruct(blocks.shape...  80 us
    pallas_call x17, Pallas kernels, run_turn(): pl.pallas_call(functools.partial(turn_kernel, merge, send), out_shape=tup...  62.2 us
    ppermute x17, starting transfers between devices, ring(): return lax.ppermute(picked(ring_rows[number - 1], tab), 'section', pairs)  29 us
  transfers between devices with their start and end apart: 55, of which 32 were waited for; matrix products, arithmetic and copies ran while one was open for 1% of the time, Pallas kernels for 22%

profile of v4, /device:TPU:8, one launch (start us, length us, event | category | flops | bytes accessed | tf_op | source)
XLA Modules:
  0.0 834.2 jit_solution(7822369397794007240)
XLA Ops:
  18.7 10.7 %collective-permute-done.3.refs_1_.refs_0_ = bf16[768,768]{1,0:T(8,128)(2,1)S(1)} collective-permute-done((bf16[768,768]{1,0:T(8,128)(2,1)}, bf16[768,768]{1,0:T(8,128)(2,1)S(1)}, u32[]{:S(2)}, u32[]{:S(2)}) %collective-permute-start.3) | collective-permute-done | bytes 1179680 | tf_op jit(solution)/shard_map/ppermute | solution.py:414
  60.3 7.4 collective-permute-done.4.refs_1_.refs_4_.refs_3_.refs_2_
  80.8 12.8 %all-to-all-done = s32[1,2,8,512,2]{3,4,1,0,2:T(2,128)S(1)} async-done(((s32[1,2,8,512,2]{3,4,1,0,2:T(2,128)}), s32[1,2,8,512,2]{3,4,1,0,2:T(2,128)S(1)}, u32[]{:S(2)}, u32[]{:S(2)}) %all-to-all-start) | async-done | bytes 65568 | tf_op jit(solution)/shard_map/all_to_all | solution.py:420
  106.9 11.3 %all-to-all-start.2 = ((bf16[160,2,128]{2,1,0:T(2,128)(2,1)}), bf16[160,2,128]{2,1,0:T(2,128)(2,1)S(1)}, u32[]{:S(2)}, u32[]{:S(2)}) async-start(bf16[160,2,128]{2,1,0:T(2,128)(2,1)} %get-tuple-element.233), calls=%async_computation.2 | async-start | bytes 163840 | tf_op jit(solution)/shard_map/all_to_all | solution.py:185
  118.8 9.5 %all-to-all-done.2.blocks_ref = bf16[160,2,128]{2,1,0:T(2,128)(2,1)S(1)} async-done(((bf16[160,2,128]{2,1,0:T(2,128)(2,1)}), bf16[160,2,128]{2,1,0:T(2,128)(2,1)S(1)}, u32[]{:S(2)}, u32[]{:S(2)}) %all-to-all-start.2) | async-done | bytes 81952 | tf_op jit(solution)/shard_map/all_to_all | solution.py:185
  138.3 10.3 %all-to-all-done.3.refs_1_ = bf16[160,2,128]{2,1,0:T(2,128)(2,1)S(1)} async-done(((bf16[160,2,128]{2,1,0:T(2,128)(2,1)}), bf16[160,2,128]{2,1,0:T(2,128)(2,1)S(1)}, u32[]{:S(2)}, u32[]{:S(2)}) %all-to-all-start.3) | async-done | bytes 81952 | tf_op jit(solution)/shard_map/all_to_all | solution.py:185
  161.2 13.8 %all_to_all.180.blocks_ref = bf16[160,2,128]{2,1,0:T(2,128)(2,1)} all-to-all(bf16[160,2,128]{2,1,0:T(2,128)(2,1)S(1)} %copy-done.25), channel_id=1, replica_groups=mesh['section'=8,'expert'=32] {'expert'}, dimensions={0} | all-to-all | bytes 163840 | tf_op jit(solution)/shard_map/all_to_all | solution.py:185
  189.3 8.7 %all-to-all-done.5.refs_1_ = bf16[160,2,128]{2,1,0:T(2,128)(2,1)S(1)} async-done(((bf16[160,2,128]{2,1,0:T(2,128)(2,1)}), bf16[160,2,128]{2,1,0:T(2,128)(2,1)S(1)}, u32[]{:S(2)}, u32[]{:S(2)}) %all-to-all-start.5) | async-done | bytes 81952 | tf_op jit(solution)/shard_map/all_to_all | solution.py:185
  208.3 13.8 %all_to_all.181.blocks_ref = bf16[160,2,128]{2,1,0:T(2,128)(2,1)} all-to-all(bf16[160,2,128]{2,1,0:T(2,128)(2,1)S(1)} %copy-done.27), channel_id=1, replica_groups=mesh['section'=8,'expert'=32] {'expert'}, dimensions={0} | all-to-all | bytes 163840 | tf_op jit(solution)/shard_map/all_to_all | solution.py:185
  253.3 13.7 %all_to_all.182.blocks_ref = bf16[160,2,128]{2,1,0:T(2,128)(2,1)} all-to-all(bf16[160,2,128]{2,1,0:T(2,128)(2,1)S(1)} %copy-done.26), channel_id=1, replica_groups=mesh['section'=8,'expert'=32] {'expert'}, dimensions={0} | all-to-all | bytes 163840 | tf_op jit(solution)/shard_map/all_to_all | solution.py:185
  282.0 7.9 all-to-all-done.9.refs_1_
  299.8 13.7 %all_to_all.183.blocks_ref = bf16[160,2,128]{2,1,0:T(2,128)(2,1)} all-to-all(bf16[160,2,128]{2,1,0:T(2,128)(2,1)S(1)} %copy-done.28), channel_id=1, replica_groups=mesh['section'=8,'expert'=32] {'expert'}, dimensions={0} | all-to-all | bytes 163840 | tf_op jit(solution)/shard_map/all_to_all | solution.py:185
  368.0 9.1 %collective-permute-done.19.refs_3_.refs_1_.refs_4_.refs_2_ = bf16[1536,768]{1,0:T(8,128)(2,1)} collective-permute-done((bf16[1536,768]{1,0:T(8,128)(2,1)}, bf16[1536,768]{1,0:T(8,128)(2,1)}, u32[]{:S(2)}, u32[]{:S(2)}) %collective-permute-start.19) | collective-permute-done | bytes 2359328 | tf_op jit(solution)/shard_map/ppermute | solution.py:414
  382.9 8.4 %all-to-all-start.14 = ((bf16[160,2,128]{2,1,0:T(2,128)(2,1)}), bf16[160,2,128]{2,1,0:T(2,128)(2,1)S(1)}, u32[]{:S(2)}, u32[]{:S(2)}) async-start(bf16[160,2,128]{2,1,0:T(2,128)(2,1)} %get-tuple-element.315), calls=%async_computation.14 | async-start | bytes 163840 | tf_op jit(solution)/shard_map/all_to_all | solution.py:185
  416.3 9.5 %collective-permute-done.21.refs_2_.refs_1_.refs_4_.refs_3_ = bf16[1536,768]{1,0:T(8,128)(2,1)} collective-permute-done((bf16[1536,768]{1,0:T(8,128)(2,1)}, bf16[1536,768]{1,0:T(8,128)(2,1)}, u32[]{:S(2)}, u32[]{:S(2)}) %collective-permute-start.21) | collective-permute-done | bytes 2359328 | tf_op jit(solution)/shard_map/ppermute | solution.py:414
  430.9 9.1 %all-to-all-start.16 = ((bf16[160,2,128]{2,1,0:T(2,128)(2,1)}), bf16[160,2,128]{2,1,0:T(2,128)(2,1)S(1)}, u32[]{:S(2)}, u32[]{:S(2)}) async-start(bf16[160,2,128]{2,1,0:T(2,128)(2,1)} %get-tuple-element.328), calls=%async_computation.16 | async-start | bytes 163840 | tf_op jit(solution)/shard_map/all_to_all | solution.py:185
  464.9 9.7 %collective-permute-done.23.refs_2_.refs_4_.refs_3_.refs_5_ = bf16[1536,768]{1,0:T(8,128)(2,1)} collective-permute-done((bf16[1536,768]{1,0:T(8,128)(2,1)}, bf16[1536,768]{1,0:T(8,128)(2,1)}, u32[]{:S(2)}, u32[]{:S(2)}) %collective-permute-start.23) | collective-permute-done | bytes 2359328 | tf_op jit(solution)/shard_map/ppermute | solution.py:414
  479.5 9.3 %all-to-all-start.18 = ((bf16[160,2,128]{2,1,0:T(2,128)(2,1)}), bf16[160,2,128]{2,1,0:T(2,128)(2,1)S(1)}, u32[]{:S(2)}, u32[]{:S(2)}) async-start(bf16[160,2,128]{2,1,0:T(2,128)(2,1)} %get-tuple-element.341), calls=%async_computation.18 | async-start | bytes 163840 | tf_op jit(solution)/shard_map/all_to_all | solution.py:185
  508.1 7.3 all-to-all-start.19
  559.9 10.2 %all-to-all-done.21.refs_1_ = bf16[160,2,128]{2,1,0:T(2,128)(2,1)S(1)} async-done(((bf16[160,2,128]{2,1,0:T(2,128)(2,1)}), bf16[160,2,128]{2,1,0:T(2,128)(2,1)S(1)}, u32[]{:S(2)}, u32[]{:S(2)}) %all-to-all-start.21) | async-done | bytes 81952 | tf_op jit(solution)/shard_map/all_to_all | solution.py:185
  598.9 7.8 all-to-all-start.23
  606.7 15.1 %collective-permute-done.29.refs_5_ = bf16[1536,768]{1,0:T(8,128)(2,1)} collective-permute-done((bf16[1536,768]{1,0:T(8,128)(2,1)}, bf16[1536,768]{1,0:T(8,128)(2,1)}, u32[]{:S(2)}, u32[]{:S(2)}) %collective-permute-start.29) | collective-permute-done | bytes 2359328 | tf_op jit(solution)/shard_map/ppermute | solution.py:414
  626.2 20.0 %all_to_all.184.blocks_ref = bf16[160,2,128]{2,1,0:T(2,128)(2,1)} all-to-all(bf16[160,2,128]{2,1,0:T(2,128)(2,1)} %get-tuple-element.380), channel_id=1, replica_groups=mesh['section'=8,'expert'=32] {'expert'}, dimensions={0} | all-to-all | bytes 163840 | tf_op jit(solution)/shard_map/all_to_all | solution.py:185
  654.9 14.1 %all_to_all.185.refs_1_ = bf16[160,2,128]{2,1,0:T(2,128)(2,1)} all-to-all(bf16[160,2,128]{2,1,0:T(2,128)(2,1)S(1)} %copy-done.23), channel_id=1, replica_groups=mesh['section'=8,'expert'=32] {'expert'}, dimensions={0} | all-to-all | bytes 163840 | tf_op jit(solution)/shard_map/all_to_all | solution.py:185
  672.8 14.6 %all_to_all.186.blocks_ref = bf16[160,2,128]{2,1,0:T(2,128)(2,1)} all-to-all(bf16[160,2,128]{2,1,0:T(2,128)(2,1)} %get-tuple-element.392), channel_id=1, replica_groups=mesh['section'=8,'expert'=32] {'expert'}, dimensions={0} | all-to-all | bytes 163840 | tf_op jit(solution)/shard_map/all_to_all | solution.py:185
  696.1 14.1 %all_to_all.187.refs_1_ = bf16[160,2,128]{2,1,0:T(2,128)(2,1)} all-to-all(bf16[160,2,128]{2,1,0:T(2,128)(2,1)S(1)} %copy-done.24), channel_id=1, replica_groups=mesh['section'=8,'expert'=32] {'expert'}, dimensions={0} | all-to-all | bytes 163840 | tf_op jit(solution)/shard_map/all_to_all | solution.py:185
  714.0 14.9 %all_to_all.188.blocks_ref = bf16[160,2,128]{2,1,0:T(2,128)(2,1)} all-to-all(bf16[160,2,128]{2,1,0:T(2,128)(2,1)} %get-tuple-element.404), channel_id=1, replica_groups=mesh['section'=8,'expert'=32] {'expert'}, dimensions={0} | all-to-all | bytes 163840 | tf_op jit(solution)/shard_map/all_to_all | solution.py:185
  737.7 14.1 %all_to_all.189.refs_1_ = bf16[160,2,128]{2,1,0:T(2,128)(2,1)} all-to-all(bf16[160,2,128]{2,1,0:T(2,128)(2,1)S(1)} %copy-done.22), channel_id=1, replica_groups=mesh['section'=8,'expert'=32] {'expert'}, dimensions={0} | all-to-all | bytes 163840 | tf_op jit(solution)/shard_map/all_to_all | solution.py:185
  755.6 14.7 %all_to_all.190.blocks_ref = bf16[160,2,128]{2,1,0:T(2,128)(2,1)} all-to-all(bf16[160,2,128]{2,1,0:T(2,128)(2,1)} %get-tuple-element.417), channel_id=1, replica_groups=mesh['section'=8,'expert'=32] {'expert'}, dimensions={0} | all-to-all | bytes 163840 | tf_op jit(solution)/shard_map/all_to_all | solution.py:185
  778.9 14.1 %all_to_all.191.refs_1_ = bf16[160,2,128]{2,1,0:T(2,128)(2,1)} all-to-all(bf16[160,2,128]{2,1,0:T(2,128)(2,1)S(1)} %copy-done.21), channel_id=1, replica_groups=mesh['section'=8,'expert'=32] {'expert'}, dimensions={0} | all-to-all | bytes 163840 | tf_op jit(solution)/shard_map/all_to_all | solution.py:185
  796.8 14.7 %all_to_all.192.blocks_ref = bf16[160,2,128]{2,1,0:T(2,128)(2,1)} all-to-all(bf16[160,2,128]{2,1,0:T(2,128)(2,1)} %get-tuple-element.427), channel_id=1, replica_groups=mesh['section'=8,'expert'=32] {'expert'}, dimensions={0} | all-to-all | bytes 163840 | tf_op jit(solution)/shard_map/all_to_all | solution.py:185
  816.5 14.7 %all_to_all.193.refs_1_ = bf16[160,2,128]{2,1,0:T(2,128)(2,1)} all-to-all(bf16[160,2,128]{2,1,0:T(2,128)(2,1)} %expert.31), channel_id=1, replica_groups=mesh['section'=8,'expert'=32] {'expert'}, dimensions={0} | all-to-all | bytes 163840 | tf_op jit(solution)/shard_map/all_to_all | solution.py:185
  (246 shorter events, 453.9 us)
Async XLA Ops:
  8.2 21.2 %collective-permute-start.2 = (bf16[1536,768]{1,0:T(8,128)(2,1)}, bf16[1536,768]{1,0:T(8,128)(2,1)}, u32[]{:S(2)}, u32[]{:S(2)}) collective-permute-start(bf16[1536,768]{1,0:T(8,128)(2,1)} %pick.37), channel_id=1, source_target_pairs={{0,32},{32,0},{64,96},{96,64},{128,160},{160,128},{192,224},{224,1... | collective-permute-start | bytes 7077896 | tf_op jit(solution)/shard_map/ppermute | solution.py:407
  17.4 24.8 %collective-permute-start.1 = (bf16[768,768]{1,0:T(8,128)(2,1)}, bf16[768,768]{1,0:T(8,128)(2,1)}, u32[]{:S(2)}, u32[]{:S(2)}) collective-permute-start(bf16[768,768]{1,0:T(8,128)(2,1)} %pick.36), channel_id=1, source_target_pairs={{0,64},{32,224},{64,128},{96,32},{128,192},{160,96},{192,0},{224,1... | collective-permute-start | bytes 3538952 | tf_op jit(solution)/shard_map/ppermute | solution.py:414
  33.5 21.2 %collective-permute-start.5 = (bf16[768,768]{1,0:T(8,128)(2,1)}, bf16[768,768]{1,0:T(8,128)(2,1)S(1)}, u32[]{:S(2)}, u32[]{:S(2)}) collective-permute-start(bf16[768,768]{1,0:T(8,128)(2,1)} %pick.40), channel_id=1, source_target_pairs={{0,64},{32,224},{64,128},{96,32},{128,192},{160,96},{192,0},{224,1... | collective-permute-start | bytes 3538952 | tf_op jit(solution)/shard_map/ppermute | solution.py:414
  45.2 22.6 %collective-permute-start.4 = (bf16[768,768]{1,0:T(8,128)(2,1)}, bf16[768,768]{1,0:T(8,128)(2,1)}, u32[]{:S(2)}, u32[]{:S(2)}) collective-permute-start(bf16[768,768]{1,0:T(8,128)(2,1)} %pick.39), channel_id=1, source_target_pairs={{0,64},{32,224},{64,128},{96,32},{128,192},{160,96},{192,0},{224,1... | collective-permute-start | bytes 3538952 | tf_op jit(solution)/shard_map/ppermute | solution.py:414
  47.3 25.7 %all-to-all-start.1 = ((bf16[8,2,2,768]{3,1,2,0:T(2,128)(2,1)}), bf16[8,2,2,768]{3,1,2,0:T(2,128)(2,1)S(1)}, u32[]{:S(2)}, u32[]{:S(2)}) async-start(bf16[8,2,2,768]{3,1,2,0:T(2,128)(2,1)} %broadcast_in_dim.27), calls=%async_computation.1 | async-start | bytes 98304 | tf_op jit(solution)/shard_map/all_to_all | solution.py:425
  58.8 36.7 %collective-permute-start.7 = (bf16[768,768]{1,0:T(8,128)(2,1)}, bf16[768,768]{1,0:T(8,128)(2,1)S(1)}, u32[]{:S(2)}, u32[]{:S(2)}) collective-permute-start(bf16[768,768]{1,0:T(8,128)(2,1)} %pick.42), channel_id=1, source_target_pairs={{0,64},{32,224},{64,128},{96,32},{128,192},{160,96},{192,0},{224,1... | collective-permute-start | bytes 3538952 | tf_op jit(solution)/shard_map/ppermute | solution.py:414
  70.7 24.8 %collective-permute-start.6 = (bf16[768,768]{1,0:T(8,128)(2,1)}, bf16[768,768]{1,0:T(8,128)(2,1)}, u32[]{:S(2)}, u32[]{:S(2)}) collective-permute-start(bf16[768,768]{1,0:T(8,128)(2,1)} %pick.41), channel_id=1, source_target_pairs={{0,64},{32,224},{64,128},{96,32},{128,192},{160,96},{192,0},{224,1... | collective-permute-start | bytes 3538952 | tf_op jit(solution)/shard_map/ppermute | solution.py:414
  101.7 26.6 %collective-permute-start.8 = (bf16[1536,768]{1,0:T(8,128)(2,1)}, bf16[1536,768]{1,0:T(8,128)(2,1)}, u32[]{:S(2)}, u32[]{:S(2)}) collective-permute-start(bf16[1536,768]{1,0:T(8,128)(2,1)} %pick.43.lane_ref), channel_id=1, source_target_pairs={{0,32},{32,0},{64,96},{96,64},{128,160},{160,128},{192,224},{224,1... | collective-permute-start | bytes 7077896 | tf_op jit(solution)/shard_map/ppermute | solution.py:407
  105.2 33.1 %collective-permute-start.9 = (bf16[1536,768]{1,0:T(8,128)(2,1)}, bf16[1536,768]{1,0:T(8,128)(2,1)}, u32[]{:S(2)}, u32[]{:S(2)}) collective-permute-start(bf16[1536,768]{1,0:T(8,128)(2,1)} %pick.44), channel_id=1, source_target_pairs={{0,64},{32,224},{64,128},{96,32},{128,192},{160,96},{192,0},{224,1... | collective-permute-start | bytes 7077896 | tf_op jit(solution)/shard_map/ppermute | solution.py:414
  106.9 21.4 %all-to-all-start.2 = ((bf16[160,2,128]{2,1,0:T(2,128)(2,1)}), bf16[160,2,128]{2,1,0:T(2,128)(2,1)S(1)}, u32[]{:S(2)}, u32[]{:S(2)}) async-start(bf16[160,2,128]{2,1,0:T(2,128)(2,1)} %get-tuple-element.233), calls=%async_computation.2 | async-start | bytes 163840 | tf_op jit(solution)/shard_map/all_to_all | solution.py:185
  160.0 29.2 %collective-permute-start.11 = (bf16[1536,768]{1,0:T(8,128)(2,1)}, bf16[1536,768]{1,0:T(8,128)(2,1)}, u32[]{:S(2)}, u32[]{:S(2)}) collective-permute-start(bf16[1536,768]{1,0:T(8,128)(2,1)} %pick.46), channel_id=1, source_target_pairs={{0,64},{32,224},{64,128},{96,32},{128,192},{160,96},{192,0},{224,1... | collective-permute-start | bytes 7077896 | tf_op jit(solution)/shard_map/ppermute | solution.py:414
  183.5 38.5 %collective-permute-start.12 = (bf16[1536,768]{1,0:T(8,128)(2,1)}, bf16[1536,768]{1,0:T(8,128)(2,1)}, u32[]{:S(2)}, u32[]{:S(2)}) collective-permute-start(bf16[1536,768]{1,0:T(8,128)(2,1)} %pick.47.lane_ref), channel_id=1, source_target_pairs={{0,32},{32,0},{64,96},{96,64},{128,160},{160,128},{192,224},{224,1... | collective-permute-start | bytes 7077896 | tf_op jit(solution)/shard_map/ppermute | solution.py:407
  205.9 29.2 %collective-permute-start.13 = (bf16[1536,768]{1,0:T(8,128)(2,1)}, bf16[1536,768]{1,0:T(8,128)(2,1)}, u32[]{:S(2)}, u32[]{:S(2)}) collective-permute-start(bf16[1536,768]{1,0:T(8,128)(2,1)} %pick.48), channel_id=1, source_target_pairs={{0,64},{32,224},{64,128},{96,32},{128,192},{160,96},{192,0},{224,1... | collective-permute-start | bytes 7077896 | tf_op jit(solution)/shard_map/ppermute | solution.py:414
  252.8 29.2 %collective-permute-start.15 = (bf16[1536,768]{1,0:T(8,128)(2,1)}, bf16[1536,768]{1,0:T(8,128)(2,1)}, u32[]{:S(2)}, u32[]{:S(2)}) collective-permute-start(bf16[1536,768]{1,0:T(8,128)(2,1)} %pick.50), channel_id=1, source_target_pairs={{0,64},{32,224},{64,128},{96,32},{128,192},{160,96},{192,0},{224,1... | collective-permute-start | bytes 7077896 | tf_op jit(solution)/shard_map/ppermute | solution.py:414
  275.4 38.0 %collective-permute-start.16 = (bf16[1536,768]{1,0:T(8,128)(2,1)}, bf16[1536,768]{1,0:T(8,128)(2,1)}, u32[]{:S(2)}, u32[]{:S(2)}) collective-permute-start(bf16[1536,768]{1,0:T(8,128)(2,1)} %pick.51.lane_ref), channel_id=1, source_target_pairs={{0,32},{32,0},{64,96},{96,64},{128,160},{160,128},{192,224},{224,1... | collective-permute-start | bytes 7077896 | tf_op jit(solution)/shard_map/ppermute | solution.py:407
  297.9 29.3 %collective-permute-start.17 = (bf16[1536,768]{1,0:T(8,128)(2,1)}, bf16[1536,768]{1,0:T(8,128)(2,1)}, u32[]{:S(2)}, u32[]{:S(2)}) collective-permute-start(bf16[1536,768]{1,0:T(8,128)(2,1)} %pick.52), channel_id=1, source_target_pairs={{0,64},{32,224},{64,128},{96,32},{128,192},{160,96},{192,0},{224,1... | collective-permute-start | bytes 7077896 | tf_op jit(solution)/shard_map/ppermute | solution.py:414
  347.8 29.2 %collective-permute-start.19 = (bf16[1536,768]{1,0:T(8,128)(2,1)}, bf16[1536,768]{1,0:T(8,128)(2,1)}, u32[]{:S(2)}, u32[]{:S(2)}) collective-permute-start(bf16[1536,768]{1,0:T(8,128)(2,1)} %pick.54), channel_id=1, source_target_pairs={{0,64},{32,224},{64,128},{96,32},{128,192},{160,96},{192,0},{224,1... | collective-permute-start | bytes 7077896 | tf_op jit(solution)/shard_map/ppermute | solution.py:414
  364.0 37.4 %collective-permute-start.20 = (bf16[1536,768]{1,0:T(8,128)(2,1)}, bf16[1536,768]{1,0:T(8,128)(2,1)}, u32[]{:S(2)}, u32[]{:S(2)}) collective-permute-start(bf16[1536,768]{1,0:T(8,128)(2,1)} %pick.55.lane_ref), channel_id=1, source_target_pairs={{0,32},{32,0},{64,96},{96,64},{128,160},{160,128},{192,224},{224,1... | collective-permute-start | bytes 7077896 | tf_op jit(solution)/shard_map/ppermute | solution.py:407
  394.8 31.1 %collective-permute-start.21 = (bf16[1536,768]{1,0:T(8,128)(2,1)}, bf16[1536,768]{1,0:T(8,128)(2,1)}, u32[]{:S(2)}, u32[]{:S(2)}) collective-permute-start(bf16[1536,768]{1,0:T(8,128)(2,1)} %pick.56), channel_id=1, source_target_pairs={{0,64},{32,224},{64,128},{96,32},{128,192},{160,96},{224,160},{1,6... | collective-permute-start | bytes 7077896 | tf_op jit(solution)/shard_map/ppermute | solution.py:414
  410.4 39.7 %collective-permute-start.22 = (bf16[1536,768]{1,0:T(8,128)(2,1)}, bf16[1536,768]{1,0:T(8,128)(2,1)}, u32[]{:S(2)}, u32[]{:S(2)}) collective-permute-start(bf16[1536,768]{1,0:T(8,128)(2,1)} %pick.57.lane_ref), channel_id=1, source_target_pairs={{0,32},{32,0},{64,96},{96,64},{128,160},{160,128},{192,224},{224,1... | collective-permute-start | bytes 7077896 | tf_op jit(solution)/shard_map/ppermute | solution.py:407
  443.5 31.1 %collective-permute-start.23 = (bf16[1536,768]{1,0:T(8,128)(2,1)}, bf16[1536,768]{1,0:T(8,128)(2,1)}, u32[]{:S(2)}, u32[]{:S(2)}) collective-permute-start(bf16[1536,768]{1,0:T(8,128)(2,1)} %pick.58), channel_id=1, source_target_pairs={{0,64},{32,224},{64,128},{128,192},{160,96},{192,0},{224,160},{1,6... | collective-permute-start | bytes 7077896 | tf_op jit(solution)/shard_map/ppermute | solution.py:414
  459.2 39.7 %collective-permute-start.24 = (bf16[1536,768]{1,0:T(8,128)(2,1)}, bf16[1536,768]{1,0:T(8,128)(2,1)}, u32[]{:S(2)}, u32[]{:S(2)}) collective-permute-start(bf16[1536,768]{1,0:T(8,128)(2,1)} %pick.59.lane_ref), channel_id=1, source_target_pairs={{0,32},{32,0},{64,96},{96,64},{128,160},{160,128},{192,224},{224,1... | collective-permute-start | bytes 7077896 | tf_op jit(solution)/shard_map/ppermute | solution.py:407
  492.2 29.0 %collective-permute-start.25 = (bf16[1536,768]{1,0:T(8,128)(2,1)}, bf16[1536,768]{1,0:T(8,128)(2,1)}, u32[]{:S(2)}, u32[]{:S(2)}) collective-permute-start(bf16[1536,768]{1,0:T(8,128)(2,1)} %pick.60), channel_id=1, source_target_pairs={{32,224},{64,128},{96,32},{128,192},{192,0},{224,160},{33,225},{65... | collective-permute-start | bytes 7077896 | tf_op jit(solution)/shard_map/ppermute | solution.py:414
  508.0 37.5 %collective-permute-start.26 = (bf16[1536,768]{1,0:T(8,128)(2,1)}, bf16[1536,768]{1,0:T(8,128)(2,1)}, u32[]{:S(2)}, u32[]{:S(2)}) collective-permute-start(bf16[1536,768]{1,0:T(8,128)(2,1)} %pick.61.lane_ref), channel_id=1, source_target_pairs={{0,32},{32,0},{64,96},{96,64},{128,160},{160,128},{192,224},{224,1... | collective-permute-start | bytes 7077896 | tf_op jit(solution)/shard_map/ppermute | solution.py:407
  554.6 33.9 %collective-permute-start.28 = (bf16[1536,768]{1,0:T(8,128)(2,1)}, bf16[1536,768]{1,0:T(8,128)(2,1)}, u32[]{:S(2)}, u32[]{:S(2)}) collective-permute-start(bf16[1536,768]{1,0:T(8,128)(2,1)} %pick.63.lane_ref), channel_id=1, source_target_pairs={{0,32},{32,0},{64,96},{96,64},{128,160},{160,128},{192,224},{224,1... | collective-permute-start | bytes 7077896 | tf_op jit(solution)/shard_map/ppermute | solution.py:407
  581.7 40.1 %collective-permute-start.29 = (bf16[1536,768]{1,0:T(8,128)(2,1)}, bf16[1536,768]{1,0:T(8,128)(2,1)}, u32[]{:S(2)}, u32[]{:S(2)}) collective-permute-start(bf16[1536,768]{1,0:T(8,128)(2,1)} %pick.64), channel_id=1, source_target_pairs={{0,64},{96,32},{1,65},{97,33},{2,66},{98,34},{3,67},{99,35},{4,68}... | collective-permute-start | bytes 7077896 | tf_op jit(solution)/shard_map/ppermute | solution.py:414
  597.6 48.6 %collective-permute-start.30 = (bf16[1536,768]{1,0:T(8,128)(2,1)}, bf16[1536,768]{1,0:T(8,128)(2,1)}, u32[]{:S(2)}, u32[]{:S(2)}) collective-permute-start(bf16[1536,768]{1,0:T(8,128)(2,1)} %pick.65.lane_ref), channel_id=1, source_target_pairs={{0,32},{32,0},{64,96},{96,64},{128,160},{160,128},{192,224},{224,1... | collective-permute-start | bytes 7077896 | tf_op jit(solution)/shard_map/ppermute | solution.py:407
  598.9 22.9 %all-to-all-start.23 = ((bf16[160,2,128]{2,1,0:T(2,128)(2,1)}), bf16[160,2,128]{2,1,0:T(2,128)(2,1)S(1)}, u32[]{:S(2)}, u32[]{:S(2)}) async-start(bf16[160,2,128]{2,1,0:T(2,128)(2,1)} %expert.26), calls=%async_computation.23 | async-start | bytes 163840 | tf_op jit(solution)/shard_map/all_to_all | solution.py:185
  654.8 32.6 %collective-permute-start.31 = (bf16[1536,768]{1,0:T(8,128)(2,1)}, bf16[1536,768]{1,0:T(8,128)(2,1)}, u32[]{:S(2)}, u32[]{:S(2)}) collective-permute-start(bf16[1536,768]{1,0:T(8,128)(2,1)} %pick.66.lane_ref), channel_id=1, source_target_pairs={{0,32},{32,0},{64,96},{96,64},{128,160},{160,128},{192,224},{224,1... | collective-permute-start | bytes 7077896 | tf_op jit(solution)/shard_map/ppermute | solution.py:407
  696.0 32.9 %collective-permute-start.32 = (bf16[1536,768]{1,0:T(8,128)(2,1)}, bf16[1536,768]{1,0:T(8,128)(2,1)}, u32[]{:S(2)}, u32[]{:S(2)}) collective-permute-start(bf16[1536,768]{1,0:T(8,128)(2,1)} %pick.67.lane_ref), channel_id=1, source_target_pairs={{0,32},{32,0},{64,96},{96,64},{128,160},{160,128},{192,224},{224,1... | collective-permute-start | bytes 7077896 | tf_op jit(solution)/shard_map/ppermute | solution.py:407
  737.5 32.7 %collective-permute-start.33 = (bf16[1536,768]{1,0:T(8,128)(2,1)}, bf16[1536,768]{1,0:T(8,128)(2,1)}, u32[]{:S(2)}, u32[]{:S(2)}) collective-permute-start(bf16[1536,768]{1,0:T(8,128)(2,1)} %pick.68.lane_ref), channel_id=1, source_target_pairs={{0,32},{32,0},{64,96},{96,64},{128,160},{160,128},{192,224},{224,1... | collective-permute-start | bytes 7077896 | tf_op jit(solution)/shard_map/ppermute | solution.py:407
  778.8 32.7 %collective-permute-start.34 = (bf16[1536,768]{1,0:T(8,128)(2,1)}, bf16[1536,768]{1,0:T(8,128)(2,1)}, u32[]{:S(2)}, u32[]{:S(2)}) collective-permute-start(bf16[1536,768]{1,0:T(8,128)(2,1)} %pick.69.lane_ref), channel_id=1, source_target_pairs={{0,32},{32,0},{64,96},{96,64},{128,160},{160,128},{192,224},{224,1... | collective-permute-start | bytes 7077896 | tf_op jit(solution)/shard_map/ppermute | solution.py:407
  (55 other events, 456.8 us)

commit v5 on v4

v5 whole, which is shorter than its diff:
```python
import functools

import jax
import jax.numpy as jnp
import numpy as np
from jax import lax
from jax.experimental import pallas as pl
from jax.experimental.pallas import tpu as pltpu
from jax.sharding import PartitionSpec as P

VMEM_LIMIT = 64400 * 1024
HBM = pl.BlockSpec(memory_space=pltpu.HBM)
SMEM = pl.BlockSpec(memory_space=pltpu.SMEM)
VMEM = pl.BlockSpec(memory_space=pltpu.VMEM)
DIRS = (1, -1)


PACK = 64
SLOTS = 48
ROWS = 10
PARTS = 2
UNROLL = 2
AHEAD = (64, 20, 1, 3, 1, 5, 6, 4, 4, 2, 4, 3, 6, 3, 2, 5)
AHEAD_A_HOP = (13.5, 49, 3.5, 0.5, 3.5, 0.5, 1.5, 0.5, 0.5, 0.5, 0.5, 0.5, 0.5, 1, 1, 0.5)
LEAD = 8


def ring_plan(sections, layers, parts, lead):
    chips = sections // 2
    items = layers * parts

    def earliest(i, lane, target):
        hops = ((i // parts) % sections // 2 - target) * DIRS[lane] % chips
        return lead + i // parts - AHEAD[i // parts] - AHEAD_A_HOP[i // parts] * hops

    held = [
        [
            {i: (0, 0, 0) for i in range(items) if (i // parts) % sections // 2 == y}
            for y in range(chips)
        ]
        for _ in DIRS
    ]
    steps = []
    while any(len(stock) < items for lane in held for stock in lane):
        number = len(steps) + 1
        moves = []
        for lane, step in enumerate(DIRS):
            for y in range(chips):
                target = (y + step) % chips
                there = held[lane][target]
                options = [i for i, at in held[lane][y].items() if at[0] < number and i not in there]
                options = sorted(i for i in options if number >= earliest(i, lane, target))
                for place, i in enumerate(options[: 1 if number <= lead else parts]):
                    moves.append((lane, y, target, i, place))
        steps.append(moves)
        for lane, _, target, i, place in moves:
            held[lane][target][i] = (number + (number < lead), number, place)
    return steps, held


class Reads:
    def __init__(self, rows, places, size, tab_ref, sources, hold_ref, sems):
        self.rows, self.places, self.size = rows, places, size
        self.tab_ref, self.sources = tab_ref, sources
        self.hold_ref, self.sems = hold_ref, sems

    def part_of(self, ref, part):
        return ref.at[pl.ds(pl.multiple_of(part * self.size, self.size), self.size)]

    def copy(self, part, choice):
        number, start = choice
        view = self.sources[number].at[self.places[number] + (pl.ds(start, self.size),)]
        return pltpu.make_async_copy(view, self.part_of(self.hold_ref, part), self.sems.at[part])

    def start(self):
        for part, (row, choices) in enumerate(self.rows):
            wish = self.tab_ref[row]
            for number, choice in enumerate(choices):

                @pl.when(wish == number)
                def _(part=part, choice=choice):
                    self.copy(part, choice).start()

    def wait(self, part):
        to = self.part_of(self.hold_ref, part)
        pltpu.make_async_copy(to, to, self.sems.at[part]).wait()

    def forward(self, out_ref, sems):
        for part in range(len(self.rows)):
            self.wait(part)
            self.leave(part, out_ref, sems).start()

    def finish(self, out_ref, sems):
        for part in range(len(self.rows)):
            self.leave(part, out_ref, sems).wait()

    def leave(self, part, out_ref, sems):
        return pltpu.make_async_copy(
            self.part_of(self.hold_ref, part), self.part_of(out_ref, part), sems.at[part]
        )


def pick_kernel(rows, places, size, tab_ref, *refs):
    count = len(places)
    sources, (out_ref, hold_ref, in_sems, out_sems) = refs[:count], refs[count:]
    reads = Reads(rows, places, size, tab_ref, sources, hold_ref, in_sems)
    reads.start()
    reads.forward(out_ref, out_sems)
    reads.finish(out_ref, out_sems)


def pick(tab, rows, sources, places, size, width):
    shape = (size * len(rows), width)
    return pl.pallas_call(
        functools.partial(pick_kernel, rows, places, size),
        out_shape=jax.ShapeDtypeStruct(shape, jnp.bfloat16),
        in_specs=[SMEM] + [HBM] * len(sources),
        out_specs=HBM,
        scratch_shapes=[
            pltpu.VMEM(shape, jnp.bfloat16),
            pltpu.SemaphoreType.DMA((len(rows),)),
            pltpu.SemaphoreType.DMA((len(rows),)),
        ],
        compiler_params=pltpu.CompilerParams(vmem_limit_bytes=VMEM_LIMIT),
        cost_estimate=pl.CostEstimate(
            flops=0, bytes_accessed=4 * shape[0] * width, transcendentals=0
        ),
        name="pick",
    )(tab, *sources)


LANES = 128


def turned(value, lanes):
    return pltpu.roll(value, lanes % LANES, value.ndim - 1)


def lanes_of(value):
    return lax.broadcasted_iota(jnp.int32, (1,) * (value.ndim - 1) + (LANES,), value.ndim - 1)


def fold_tail(third, at):
    axis = third.ndim - 1
    spread = pltpu.roll(turned(third, -at - 32), 0, axis, stride=16, stride_axis=axis - 1)
    place = lax.broadcasted_iota(jnp.int32, third.shape, axis) // 16
    own = place == lax.broadcasted_iota(jnp.int32, third.shape, axis - 1)
    return jnp.sum(jnp.where(own, spread, 0.0), axis=axis - 1, keepdims=True)


def unfold_tail(row, at):
    value = jnp.broadcast_to(turned(row, at + 32), row.shape[:-2] + (8, LANES))
    number = lax.broadcasted_iota(jnp.int32, value.shape, value.ndim - 2)
    for step in (1, 2, 4):
        value = jnp.where((number & step) != 0, turned(value, -16 * step), value)
    return value


def pack(first, second, third, at, gates=None):
    lanes = lanes_of(first)
    top = jnp.where(
        lanes < SLOTS,
        turned(first, -at),
        jnp.where(lanes < 2 * SLOTS, turned(second, SLOTS - at), turned(third, 2 * SLOTS - at)),
    )
    tail = fold_tail(third, at)
    axis = first.ndim - 2
    number = lax.broadcasted_iota(jnp.int32, top.shape, axis)
    last = jnp.broadcast_to(tail, top.shape)
    if gates is not None:
        last = jnp.where(number == 0, last, gates)
    return jnp.concatenate([top, last], axis=axis)


def unpack(blocks, at):
    top, last = blocks[..., 0:8, :], blocks[..., 8:16, :]
    lanes = lanes_of(blocks)
    third = jnp.where(
        lanes - at < 32, turned(top, at - 2 * SLOTS), unfold_tail(last[..., 0:1, :], at)
    )
    return turned(top, at), turned(top, at - SLOTS), third, turned(last, at)


def unpack_pairs(back):
    pairs = back.shape[0] // 2
    split = back.reshape(pairs, 2, 16, LANES)
    low = lanes_of(back) < PACK
    both = zip(unpack(split[:, 0], 0), unpack(split[:, 1], PACK))
    groups = [jnp.where(low, even, odd) for even, odd in both]
    gates = jnp.broadcast_to(groups[3][:, 1:2], groups[0].shape)
    return jnp.concatenate(groups[0:3] + [gates], axis=1)


TILES = ROWS // 2


def load_blocks(ref, wide_ref):
    @pl.loop(0, wide_ref.shape[0], step=8)
    def _(begin):
        for more in range(8):
            block = ref[pl.ds(TILES * (begin + more), TILES)].reshape(ROWS, LANES)
            wide_ref[begin + more, 0:ROWS] = block.astype(jnp.float32)

    return wide_ref[...]


def store_block(ref, number, block):
    rows = block.astype(jnp.bfloat16).reshape(8, 2, LANES)
    ref[pl.ds(TILES * number, TILES)] = rows[0:TILES]


def send_blocks(value):
    return lax.all_to_all(value, "expert", split_axis=0, concat_axis=0, tiled=True)


def turn_kernel(merge, send, side, *refs):
    refs = list(refs)
    h_ref = refs.pop(0)
    if merge:
        back_ref, row_ref = refs.pop(0), refs.pop(0)
    if send:
        next_ref = refs.pop(0)
    if side:
        (rows, places, size), count = side, len(side[1])
        out_sems, in_sems, hold_ref = refs.pop(), refs.pop(), refs.pop()
        tab_ref, sources = refs.pop(0), refs[:count]
        del refs[:count]
        reads = Reads(rows, places, size, tab_ref, sources, hold_ref, in_sems)
        reads.start()
    if merge:
        tiles_ref, update_ref, wide_ref = refs.pop(), refs.pop(), refs.pop()
    hnew_ref = refs.pop(0)
    features, tokens = h_ref.shape
    held = h_ref[...]
    if merge:
        tiles = unpack_pairs(load_blocks(back_ref, wide_ref)).astype(jnp.bfloat16)
        offset = lax.broadcasted_iota(jnp.int32, (4 * PACK, tokens), 0)
        first, second = row_ref[0:1, :] - offset, row_ref[1:2, :] - offset
        tiles_ref[...] = tiles
        update_ref[...] = jnp.zeros_like(update_ref)

        @pl.loop(0, tiles.shape[0] // 2, step=4)
        def _(begin):
            update = update_ref[...]
            for more in range(4):
                turn = begin + more
                base = turn * 4 * PACK
                onehot = jnp.where((first == base) | (second == base), 1.0, 0.0)
                pair = jnp.concatenate([tiles_ref[2 * turn], tiles_ref[2 * turn + 1]], axis=1)
                update += jnp.dot(
                    pair, onehot.astype(jnp.bfloat16), preferred_element_type=jnp.float32
                )
            update_ref[...] = update

        update = update_ref[...]
        change = update[0:features] * (1.0 / update[features:features + 1])
        held = (held.astype(jnp.float32) + change).astype(jnp.bfloat16)
    hnew_ref[...] = held
    if send:
        out_ref = refs.pop(0)
    if side:
        side_ref = refs.pop(0)
        reads.forward(side_ref, out_sems)
    if send:
        offset = lax.broadcasted_iota(jnp.int32, (tokens, 4 * PACK), 1)
        col = next_ref[...].astype(jnp.float32).T.astype(jnp.int32)
        first, second = col[:, 0:1] - offset, col[:, 1:2] - offset
        @pl.loop(0, out_ref.shape[0] // TILES // 4, step=UNROLL)
        def _(begin):
            for more in range(UNROLL):
                turn = begin + more
                base = turn * 4 * PACK
                onehot = jnp.where((first == base) | (second == base), 1.0, 0.0)
                found = jnp.dot(held, onehot.astype(jnp.bfloat16), preferred_element_type=jnp.float32)
                for half in range(2):
                    tile = found[:, LANES * half : LANES * (half + 1)]
                    groups = tile[0:8], tile[8:16], tile[16:24]
                    number = turn * 4 + half * 2
                    store_block(out_ref, number, pack(*groups, 0))
                    store_block(out_ref, number + 1, pack(*groups, PACK))
    if side:
        reads.finish(side_ref, out_sems)


def run_turn(experts, h, back, rows, before, after, side=None):
    features, tokens = h.shape
    merge, send = before is not None, after is not None
    operands, specs, scratch = [h], [VMEM], []
    shapes, outs = [jax.ShapeDtypeStruct(h.shape, h.dtype)], [VMEM]
    if merge:
        operands += [back, rows]
        specs += [VMEM, plane((8, tokens), before)]
        scratch += [
            pltpu.VMEM((experts, 16, LANES), jnp.float32),
            pltpu.VMEM((32, tokens), jnp.float32),
            pltpu.VMEM((experts // 2, 32, LANES), jnp.bfloat16),
        ]
    if send:
        operands += [rows]
        specs += [plane((8, tokens), after)]
        shapes += [jax.ShapeDtypeStruct((experts * TILES, 2, LANES), jnp.bfloat16)]
        outs += [VMEM]
    plan = None
    if side is not None:
        tab, picks, sources, places, size, width = side
        plan = (picks, places, size)
        operands += [tab] + sources
        specs += [SMEM] + [HBM] * len(sources)
        shape = (size * len(picks), width)
        shapes += [jax.ShapeDtypeStruct(shape, jnp.bfloat16)]
        outs += [HBM]
        scratch += [
            pltpu.VMEM(shape, jnp.bfloat16),
            pltpu.SemaphoreType.DMA((len(picks),)),
            pltpu.SemaphoreType.DMA((len(picks),)),
        ]
    return pl.pallas_call(
        functools.partial(turn_kernel, merge, send, plan),
        out_shape=tuple(shapes),
        grid=(1,),
        in_specs=specs,
        out_specs=tuple(outs),
        scratch_shapes=scratch,
        compiler_params=pltpu.CompilerParams(vmem_limit_bytes=VMEM_LIMIT),
        name="turn",
    )(*operands)


def expert_kernel(in_rows, out_rows, places, size, blocks_ref, gain_ref, router_ref, tab_ref, *refs):
    sources, refs = refs[: len(places)], refs[len(places) :]
    out_ref, win_ref, wout_ref, wide_ref, sum_ref, in_sems, out_sems = refs
    in_reads = Reads(in_rows, places, size, tab_ref, sources, win_ref, in_sems)
    out_reads = Reads(out_rows, places, size, tab_ref, sources, wout_ref, out_sems)
    in_reads.start()
    out_reads.start()
    width = win_ref.shape[1]
    groups = wide_ref.shape[0]
    blocks = load_blocks(blocks_ref, wide_ref)
    parts = [group[:, None] for group in unpack(blocks, 0)[0:3]]
    tall = jnp.concatenate(parts, axis=1).reshape(width, LANES)
    wide = tall.T[0:PACK]
    mean_square = jnp.mean(wide * wide, axis=1, keepdims=True)
    normed = (wide * lax.rsqrt(mean_square + 1e-06) * gain_ref[...]).astype(jnp.bfloat16)
    logit = jnp.sum(normed.astype(jnp.float32) * router_ref[...], axis=1, keepdims=True)
    gate = jax.nn.sigmoid(logit).astype(jnp.bfloat16).astype(jnp.float32)
    sum_ref[...] = jnp.zeros_like(sum_ref)

    @pl.loop(0, len(in_rows))
    def _(part):
        some = pl.ds(pl.multiple_of(part * size, size), size)
        in_reads.wait(part)
        pre_act = lax.dot_general(
            normed, win_ref[some], (((1,), (1,)), ((), ())), preferred_element_type=jnp.float32
        )
        active = jax.nn.gelu(pre_act, approximate=True).astype(jnp.bfloat16)
        out_reads.wait(part)
        sum_ref[...] += jnp.dot(active, wout_ref[some], preferred_element_type=jnp.float32)

    output = sum_ref[...]
    weighted = output * gate
    spread = jnp.broadcast_to(gate, (PACK, LANES))
    zeros = jnp.zeros_like(weighted)
    tall = jnp.concatenate([weighted, zeros], axis=0).T.reshape(groups, 3, 8, LANES)
    gates = jnp.concatenate([spread, jnp.zeros_like(spread)], axis=0).T[0:8]
    gates = jnp.broadcast_to(gates[None], (groups, 8, LANES))
    packed = pack(tall[:, 0], tall[:, 1], tall[:, 2], 0, gates)
    wide_ref[...] = packed

    @pl.loop(0, groups, step=8)
    def _(begin):
        for more in range(8):
            store_block(out_ref, begin + more, wide_ref[begin + more])


def run_expert(layer, blocks, gains, routers, weights):
    tab, (in_rows, out_rows), sources, places, size, width = weights
    hidden = size * len(in_rows)
    return pl.pallas_call(
        functools.partial(expert_kernel, in_rows, out_rows, places, size),
        out_shape=jax.ShapeDtypeStruct(blocks.shape, jnp.bfloat16),
        grid=(1,),
        in_specs=[VMEM, plane((1, width), layer), plane((1, width), layer), SMEM]
        + [HBM] * len(sources),
        out_specs=VMEM,
        scratch_shapes=[
            pltpu.VMEM((hidden, width), jnp.bfloat16),
            pltpu.VMEM((hidden, width), jnp.bfloat16),
            pltpu.VMEM((blocks.shape[0] // TILES, 16, LANES), jnp.float32),
            pltpu.VMEM((PACK, width), jnp.float32),
            pltpu.SemaphoreType.DMA((len(in_rows),)),
            pltpu.SemaphoreType.DMA((len(out_rows),)),
        ],
        compiler_params=pltpu.CompilerParams(vmem_limit_bytes=VMEM_LIMIT),
        cost_estimate=pl.CostEstimate(
            flops=4 * PACK * hidden * width, bytes_accessed=4 * hidden * width, transcendentals=0
        ),
        name="expert",
    )(blocks, gains, routers, tab, *sources)


def plane(shape, *lead):
    return pl.BlockSpec((None,) * len(lead) + shape, lambda i: lead + (0,) * len(shape))


def place_tokens(routes, experts):
    tokens = routes.shape[1]
    ids = jnp.arange(experts, dtype=jnp.int32)
    first = routes[:, :, 0:1] == ids
    second = routes[:, :, 1:2] == ids
    named = (first | second).astype(jnp.bfloat16)
    earlier = jnp.tril(jnp.ones((tokens, tokens), jnp.bfloat16), -1)
    rank = jnp.einsum("ut,lte->lue", earlier, named, preferred_element_type=jnp.float32)
    rank = rank.astype(jnp.int32) + ids * PACK
    slot_first = jnp.sum(jnp.where(first, rank, 0), axis=2)
    slot_second = jnp.sum(jnp.where(second, rank, 0), axis=2)
    blank = jnp.zeros_like(slot_first)
    return jnp.stack([slot_first, slot_second] + [blank] * 6, axis=1)


def join(*values):
    return lax.optimization_barrier(values)


def local(inputs, routes, norm_gains, routers, expert_in, expert_out):
    sections = lax.axis_size("section")
    experts = lax.axis_size("expert")
    section_pos = lax.axis_index("section")
    repeats, _, _, hidden, width = expert_in.shape
    layers = repeats * sections
    steps, held = ring_plan(sections, layers, PARTS, LEAD)
    size = hidden // PARTS

    buffers = {("in", r): (expert_in, (r, 0, 0)) for r in range(repeats)}
    buffers.update({("out", r): (expert_out, (r, 0, 0)) for r in range(repeats)})
    every = [(lane, y) for lane in range(2) for y in range(sections // 2)]
    table, wanted = [], []

    def source_of(lane, y, i):
        q, part = i // PARTS, i % PARTS
        if q % sections // 2 != y:
            _, number, place = held[lane][y][i]
            return ("ring", number), place * size
        name = ("in", "out")[lane] if q % 2 == lane else "swapped"
        return (name, q // sections), part * size

    def other_of(lane, y, i):
        q, part = i // PARTS, i % PARTS
        if q % sections // 2 != y:
            _, number, place = held[1 - lane][y][i]
            return ("turned", number), place * size
        name = ("out", "in")[lane] if q % 2 == lane else "given"
        return (name, q // sections), part * size

    def add_pick(by_section):
        choices = sorted(set(by_section.values()))
        table.append([choices.index(by_section.get(s, choices[0])) for s in range(sections)])
        wanted.append(choices)
        return len(table) - 1

    swap_rows = [
        [
            add_pick({2 * y + lane: ((("out", "in")[lane], r), part * size) for lane, y in every})
            for part in range(PARTS)
        ]
        for r in range(repeats)
    ]
    ring_rows = [
        [
            add_pick({2 * y + lane: source_of(lane, y, i) for lane, y, _, i, at in moves if at == place})
            for place in sorted({move[4] for move in moves})
        ]
        for moves in steps
    ]
    give_rows = [
        [
            add_pick({2 * y + lane: ((("in", "out")[lane], r), part * size) for lane, y in every})
            for part in range(PARTS)
        ]
        for r in range(repeats)
    ]

    def matrix_rows(q, kind):
        found = []
        for part in range(PARTS):
            i = q * PARTS + part
            by_section = {
                2 * y + lane: (source_of if lane == kind else other_of)(lane, y, i)
                for lane, y in every
            }
            found.append(add_pick(by_section))
        return found

    layer_rows = [(matrix_rows(q, 0), matrix_rows(q, 1)) for q in range(layers)]
    tab = jnp.asarray(np.array(table, np.int32).T)[section_pos]

    def plan_of(groups, tab):
        names = sorted({name for rows in groups for row in rows for name, _ in wanted[row]})
        found = [buffers[name] for name in names]
        plans = [
            tuple(
                (row, tuple((names.index(name), start) for name, start in wanted[row]))
                for row in rows
            )
            for rows in groups
        ]
        arrays, places = [array for array, _ in found], [place for _, place in found]
        return tab, plans, arrays, places, size, width

    def picked(rows, tab):
        tab, (plan,), arrays, places, size, width = plan_of([rows], tab)
        return pick(tab, plan, arrays, places, size, width)

    def swapped(value):
        return lax.ppermute(value, "section", [(s, s ^ 1) for s in range(sections)])

    def ring(number, value):
        moves = steps[number - 1]
        pairs = sorted({(2 * y + lane, 2 * target + lane) for lane, y, target, _, _ in moves})
        return lax.ppermute(value, "section", pairs)

    def arrived(number, value):
        buffers[("ring", number)] = (value, ())

    def turned_over(number):
        return swapped(buffers[("ring", number)][0])

    over_at = {q: [] for q in range(layers)}
    for number in range(LEAD - 1, len(steps) + 1):
        users = [
            i // PARTS for lane in held for stock in lane for i, at in stock.items() if at[1] == number
        ]
        over_at[max(min(users), number + 1 - LEAD, 1)].append(number)
    first_later = min(
        number
        for number, rows in enumerate(ring_rows, 1)
        for row in rows
        if ("swapped", 1) in {name for name, _ in wanted[row]}
    )
    own_at = {max(first_later - 1 - LEAD, 1): ("swapped", swap_rows), sections - 1: ("given", give_rows)}

    mine = lax.all_to_all(routes[:, 0], "section", split_axis=1, concat_axis=0, tiled=False)
    mine = jnp.transpose(mine, (1, 0, 2, 3)).reshape(layers, -1, 2)
    rows = place_tokens(mine, experts)
    small = jnp.stack([norm_gains[:, 0], routers[:, 0, 0]])
    small = jnp.broadcast_to(small[None], (sections,) + small.shape)
    small = lax.all_to_all(small, "section", split_axis=0, concat_axis=0, tiled=True)
    small = jnp.transpose(small, (1, 2, 0, 3)).reshape(2, layers, 1, width).astype(jnp.float32)
    gains, gate_rows = small[0], small[1]
    h = jnp.transpose(inputs[0], (1, 0))

    buffers[("swapped", 0)] = (swapped(picked(swap_rows[0], tab)), ())
    flying = waiting = None
    for number in range(1, LEAD + 1):
        started = ring(number, picked(ring_rows[number - 1], tab))
        if number == 1:
            given = swapped(picked(give_rows[0], tab))
        if number == 2:
            given, tab, rows, gains, gate_rows, h = join(given, tab, rows, gains, gate_rows, h)
            buffers[("given", 0)] = (given, ())
        if number == 3:
            h, blocks = run_turn(experts, h, None, rows, None, 0)
            blocks, tab = join(blocks, tab)
            blocks = send_blocks(blocks)
        if waiting is not None:
            waiting, tab = join(waiting, tab)
            buffers[("turned", number - 2)] = (waiting, ())
        if flying is not None and number < LEAD:
            flying, tab = join(flying, tab)
            arrived(number - 1, flying)
            waiting = turned_over(number - 1)
        if number == 5:
            blocks, tab = join(blocks, tab)
        if number < LEAD:
            flying = started
    under_way = [flying, started]

    for q in range(layers):
        number = LEAD + q
        if q:
            side = None
            if number <= len(steps):
                tab, (plan,), *place = plan_of([ring_rows[number - 1]], tab)
                side = (tab, plan, *place)
            h, blocks, *extra = run_turn(experts, h, back, rows, q - 1, q, side)
            blocks, tab = join(blocks, tab)
            sent = send_blocks(blocks)
            under_way = [ring(number, extra[0])] if extra else []
            swaps = {("turned", n): turned_over(n) for n in over_at[q]}
            if q in own_at:
                name, some = own_at[q]
                swaps[(name, 1)] = swapped(picked(some[1], tab))
            blocks, tab, *values = join(sent, tab, *swaps.values())
            buffers.update({name: (value, ()) for name, value in zip(swaps, values)})
        back = run_expert(q, blocks, gains, gate_rows, plan_of(layer_rows[q], tab))
        back, tab, *under_way = join(send_blocks(back), tab, *under_way)
        for back_by, value in enumerate(reversed(under_way)):
            arrived(number - back_by, value)

    (h,) = run_turn(experts, h, back, rows, layers - 1, None)
    return jnp.transpose(h, (1, 0))[None]


def solution(mesh):
    return jax.shard_map(
        local,
        mesh=mesh,
        in_specs=(
            P("section", None, "expert"),
            P(None, "section", None, None, None),
            P(None, "section", None),
            P(None, "section", "expert", None),
            P(None, "section", "expert", None, None),
            P(None, "section", "expert", None, None),
        ),
        out_specs=P("section", None, "expert"),
        check_vma=False,
    )
```

time: 848 us -> 857 us (1.011)
  waiting for transfers between devices: 195 us -> 276 us
  Pallas kernels: 260 us -> 209 us
  blocking collectives: 205 us -> 170 us
  starting transfers between devices: 152 us -> 168 us
    all_to_all x18 -> x21, waiting for transfers between devices: 93.2 us -> 178 us  [send_blocks(): lax.all_to_all(value, 'expert', split_axis=0, concat_axis=0, tiled=True)]
    pallas_call x68 -> x45, Pallas kernels: 260 us -> 209 us  [the longest x17 89.7 us: run_turn(): pl.pallas_call(functools.partial(turn_kernel, merge, send, plan), out_sha...]
    ppermute x17 -> x22, starting transfers between devices: 29 us -> 69.6 us  [ring(): return lax.ppermute(value, 'section', pairs)]
    all_to_all x14 -> x11, blocking collectives: 205 us -> 170 us  [send_blocks(): lax.all_to_all(value, 'expert', split_axis=0, concat_axis=0, tiled=True)]
    all_to_all x18 -> x21, starting transfers between devices: 107 us -> 84 us  [send_blocks(): lax.all_to_all(value, 'expert', split_axis=0, concat_axis=0, tiled=True)]
    ppermute x17 -> x22, waiting for transfers between devices: 88.5 us -> 89.9 us  [ring(): return lax.ppermute(value, 'section', pairs)]
  transfers between devices with their start and end apart: 55 -> 71, of which waited for: 32 -> 32; matrix products, arithmetic and copies ran while one was open for 1% -> 1% of each run, Pallas kernels for 22% -> 18%
where the time goes in v5:
time: 857 us; the launch traced here: 843 us
  waiting for transfers between devices  276 us (32%)
  Pallas kernels  209 us (24%)
  blocking collectives  170 us (20%)
  starting transfers between devices  168 us (20%)
  local copies, waits for them, and re-layouts  17.2 us (2%)
    all_to_all x21, waiting for transfers between devices, send_blocks(): lax.all_to_all(value, 'expert', split_axis=0, concat_axis=0, tiled=True)  178 us
    all_to_all x11, blocking collectives, send_blocks(): lax.all_to_all(value, 'expert', split_axis=0, concat_axis=0, tiled=True)  170 us
    ppermute x22, waiting for transfers between devices, ring(): return lax.ppermute(value, 'section', pairs)  89.9 us
    pallas_call x17, Pallas kernels, run_turn(): pl.pallas_call(functools.partial(turn_kernel, merge, send, plan), out_sha...  89.7 us
    all_to_all x21, starting transfers between devices, send_blocks(): lax.all_to_all(value, 'expert', split_axis=0, concat_axis=0, tiled=True)  84 us
    pallas_call x16, Pallas kernels, run_expert(): pl.pallas_call(functools.partial(expert_kernel, in_rows, out_rows, places...  82.1 us
    ppermute x22, starting transfers between devices, ring(): return lax.ppermute(value, 'section', pairs)  69.6 us
    pallas_call x12, Pallas kernels, pick(): pl.pallas_call(functools.partial(pick_kernel, rows, places, size), out_sh...  37.5 us
  transfers between devices with their start and end apart: 71, of which 32 were waited for; matrix products, arithmetic and copies ran while one was open for 1% of the time, Pallas kernels for 18%

profile of v5, /device:TPU:8, one launch (start us, length us, event | category | flops | bytes accessed | tf_op | source)
XLA Modules:
  0.0 843.1 jit_solution(13287533144630215539)
XLA Ops:
  28.3 8.5 %all-to-all-done = s32[1,2,8,512,2]{3,4,1,0,2:T(2,128)S(1)} async-done(((s32[1,2,8,512,2]{3,4,1,0,2:T(2,128)}), s32[1,2,8,512,2]{3,4,1,0,2:T(2,128)S(1)}, u32[]{:S(2)}, u32[]{:S(2)}) %all-to-all-start) | async-done | bytes 65568 | tf_op jit(solution)/shard_map/all_to_all | solution.py:541
  48.8 11.4 %collective-permute-done.3.refs_2_.refs_0_.refs_1_.refs_4_ = bf16[768,768]{1,0:T(8,128)(2,1)} collective-permute-done((bf16[768,768]{1,0:T(8,128)(2,1)}, bf16[768,768]{1,0:T(8,128)(2,1)}, u32[]{:S(2)}, u32[]{:S(2)}) %collective-permute-start.3) | collective-permute-done | bytes 1179680 | tf_op jit(solution)/shard_map/ppermute | solution.py:519
  66.5 15.1 %collective-permute-done.6.refs_1_.refs_2_.refs_5_.refs_3_ = bf16[768,768]{1,0:T(8,128)(2,1)} collective-permute-done((bf16[768,768]{1,0:T(8,128)(2,1)}, bf16[768,768]{1,0:T(8,128)(2,1)}, u32[]{:S(2)}, u32[]{:S(2)}) %collective-permute-start.6) | collective-permute-done | bytes 1179680 | tf_op jit(solution)/shard_map/ppermute | solution.py:519
  88.1 15.1 %collective-permute-done.5.refs_2_.refs_6_.refs_1_.refs_4_.refs_5_ = bf16[768,768]{1,0:T(8,128)(2,1)} collective-permute-done((bf16[768,768]{1,0:T(8,128)(2,1)}, bf16[768,768]{1,0:T(8,128)(2,1)}, u32[]{:S(2)}, u32[]{:S(2)}) %collective-permute-start.5) | collective-permute-done | bytes 1179680 | tf_op jit(solution)/shard_map/ppermute | solution.py:519
  110.6 20.7 %all_to_all.180.blocks_ref = bf16[160,2,128]{2,1,0:T(2,128)(2,1)} all-to-all(bf16[160,2,128]{2,1,0:T(2,128)(2,1)S(1)} %copy-done.21), channel_id=1, replica_groups=mesh['section'=8,'expert'=32] {'expert'}, dimensions={0} | all-to-all | bytes 163840 | tf_op jit(solution)/shard_map/all_to_all | solution.py:213
  139.0 13.0 %collective-permute-done.9.refs_8_.refs_3_.refs_6_ = bf16[768,768]{1,0:T(8,128)(2,1)} collective-permute-done((bf16[768,768]{1,0:T(8,128)(2,1)}, bf16[768,768]{1,0:T(8,128)(2,1)}, u32[]{:S(2)}, u32[]{:S(2)}) %collective-permute-start.9) | collective-permute-done | bytes 1179680 | tf_op jit(solution)/shard_map/ppermute | solution.py:519
  174.6 11.5 %collective-permute-done.15.refs_9_.refs_8_.refs_10_.refs_4_.refs_7_.refs_3_ = bf16[768,768]{1,0:T(8,128)(2,1)} collective-permute-done((bf16[768,768]{1,0:T(8,128)(2,1)}, bf16[768,768]{1,0:T(8,128)(2,1)}, u32[]{:S(2)}, u32[]{:S(2)}) %collective-permute-start.15) | collective-permute-done | bytes 1179680 | tf_op jit(solution)/shard_map/ppermute | solution.py:519
  194.3 16.4 %all_to_all.181.blocks_ref = bf16[160,2,128]{2,1,0:T(2,128)(2,1)} all-to-all(bf16[160,2,128]{2,1,0:T(2,128)(2,1)} %get-tuple-element.252), channel_id=1, replica_groups=mesh['section'=8,'expert'=32] {'expert'}, dimensions={0} | all-to-all | bytes 163840 | tf_op jit(solution)/shard_map/all_to_all | solution.py:213
  215.7 14.6 %all_to_all.182.refs_1_ = bf16[160,2,128]{2,1,0:T(2,128)(2,1)} all-to-all(bf16[160,2,128]{2,1,0:T(2,128)(2,1)} %expert.17), channel_id=1, replica_groups=mesh['section'=8,'expert'=32] {'expert'}, dimensions={0} | all-to-all | bytes 163840 | tf_op jit(solution)/shard_map/all_to_all | solution.py:213
  241.2 14.6 %all_to_all.183.blocks_ref = bf16[160,2,128]{2,1,0:T(2,128)(2,1)} all-to-all(bf16[160,2,128]{2,1,0:T(2,128)(2,1)} %get-tuple-element.264), channel_id=1, replica_groups=mesh['section'=8,'expert'=32] {'expert'}, dimensions={0} | all-to-all | bytes 163840 | tf_op jit(solution)/shard_map/all_to_all | solution.py:213
  265.2 10.0 %all-to-all-done.7.refs_1_ = bf16[160,2,128]{2,1,0:T(2,128)(2,1)S(1)} async-done(((bf16[160,2,128]{2,1,0:T(2,128)(2,1)}), bf16[160,2,128]{2,1,0:T(2,128)(2,1)S(1)}, u32[]{:S(2)}, u32[]{:S(2)}) %all-to-all-start.7) | async-done | bytes 81952 | tf_op jit(solution)/shard_map/all_to_all | solution.py:213
  293.1 10.1 %all-to-all-done.8.blocks_ref = bf16[160,2,128]{2,1,0:T(2,128)(2,1)S(1)} async-done(((bf16[160,2,128]{2,1,0:T(2,128)(2,1)}), bf16[160,2,128]{2,1,0:T(2,128)(2,1)S(1)}, u32[]{:S(2)}, u32[]{:S(2)}) %all-to-all-start.8) | async-done | bytes 81952 | tf_op jit(solution)/shard_map/all_to_all | solution.py:213
  331.5 14.6 %all_to_all.184.blocks_ref = bf16[160,2,128]{2,1,0:T(2,128)(2,1)} all-to-all(bf16[160,2,128]{2,1,0:T(2,128)(2,1)} %get-tuple-element.287), channel_id=1, replica_groups=mesh['section'=8,'expert'=32] {'expert'}, dimensions={0} | all-to-all | bytes 163840 | tf_op jit(solution)/shard_map/all_to_all | solution.py:213
  355.2 10.0 %all-to-all-done.11.refs_1_ = bf16[160,2,128]{2,1,0:T(2,128)(2,1)S(1)} async-done(((bf16[160,2,128]{2,1,0:T(2,128)(2,1)}), bf16[160,2,128]{2,1,0:T(2,128)(2,1)S(1)}, u32[]{:S(2)}, u32[]{:S(2)}) %all-to-all-start.11) | async-done | bytes 81952 | tf_op jit(solution)/shard_map/all_to_all | solution.py:213
  377.1 10.1 %all-to-all-done.12.blocks_ref = bf16[160,2,128]{2,1,0:T(2,128)(2,1)S(1)} async-done(((bf16[160,2,128]{2,1,0:T(2,128)(2,1)}), bf16[160,2,128]{2,1,0:T(2,128)(2,1)S(1)}, u32[]{:S(2)}, u32[]{:S(2)}) %all-to-all-start.12) | async-done | bytes 81952 | tf_op jit(solution)/shard_map/all_to_all | solution.py:213
  419.5 14.6 %all_to_all.185.blocks_ref = bf16[160,2,128]{2,1,0:T(2,128)(2,1)} all-to-all(bf16[160,2,128]{2,1,0:T(2,128)(2,1)} %get-tuple-element.309), channel_id=1, replica_groups=mesh['section'=8,'expert'=32] {'expert'}, dimensions={0} | all-to-all | bytes 163840 | tf_op jit(solution)/shard_map/all_to_all | solution.py:213
  443.5 9.6 %all-to-all-done.15.refs_1_ = bf16[160,2,128]{2,1,0:T(2,128)(2,1)S(1)} async-done(((bf16[160,2,128]{2,1,0:T(2,128)(2,1)}), bf16[160,2,128]{2,1,0:T(2,128)(2,1)S(1)}, u32[]{:S(2)}, u32[]{:S(2)}) %all-to-all-start.15) | async-done | bytes 81952 | tf_op jit(solution)/shard_map/all_to_all | solution.py:213
  470.5 10.1 %all-to-all-done.16.blocks_ref = bf16[160,2,128]{2,1,0:T(2,128)(2,1)S(1)} async-done(((bf16[160,2,128]{2,1,0:T(2,128)(2,1)}), bf16[160,2,128]{2,1,0:T(2,128)(2,1)S(1)}, u32[]{:S(2)}, u32[]{:S(2)}) %all-to-all-start.16) | async-done | bytes 81952 | tf_op jit(solution)/shard_map/all_to_all | solution.py:213
  509.3 14.6 %all_to_all.186.blocks_ref = bf16[160,2,128]{2,1,0:T(2,128)(2,1)} all-to-all(bf16[160,2,128]{2,1,0:T(2,128)(2,1)} %get-tuple-element.331), channel_id=1, replica_groups=mesh['section'=8,'expert'=32] {'expert'}, dimensions={0} | all-to-all | bytes 163840 | tf_op jit(solution)/shard_map/all_to_all | solution.py:213
  532.9 10.0 %all-to-all-done.19.refs_1_ = bf16[160,2,128]{2,1,0:T(2,128)(2,1)S(1)} async-done(((bf16[160,2,128]{2,1,0:T(2,128)(2,1)}), bf16[160,2,128]{2,1,0:T(2,128)(2,1)S(1)}, u32[]{:S(2)}, u32[]{:S(2)}) %all-to-all-start.19) | async-done | bytes 81952 | tf_op jit(solution)/shard_map/all_to_all | solution.py:213
  554.4 10.1 %all-to-all-done.20.blocks_ref = bf16[160,2,128]{2,1,0:T(2,128)(2,1)S(1)} async-done(((bf16[160,2,128]{2,1,0:T(2,128)(2,1)}), bf16[160,2,128]{2,1,0:T(2,128)(2,1)S(1)}, u32[]{:S(2)}, u32[]{:S(2)}) %all-to-all-start.20) | async-done | bytes 81952 | tf_op jit(solution)/shard_map/all_to_all | solution.py:213
  592.3 14.8 %all_to_all.187.blocks_ref = bf16[160,2,128]{2,1,0:T(2,128)(2,1)} all-to-all(bf16[160,2,128]{2,1,0:T(2,128)(2,1)} %get-tuple-element.354), channel_id=1, replica_groups=mesh['section'=8,'expert'=32] {'expert'}, dimensions={0} | all-to-all | bytes 163840 | tf_op jit(solution)/shard_map/all_to_all | solution.py:213
  616.4 10.0 %all-to-all-done.23.refs_1_ = bf16[160,2,128]{2,1,0:T(2,128)(2,1)S(1)} async-done(((bf16[160,2,128]{2,1,0:T(2,128)(2,1)}), bf16[160,2,128]{2,1,0:T(2,128)(2,1)S(1)}, u32[]{:S(2)}, u32[]{:S(2)}) %all-to-all-start.23) | async-done | bytes 81952 | tf_op jit(solution)/shard_map/all_to_all | solution.py:213
  642.7 10.1 %all-to-all-done.24.blocks_ref = bf16[160,2,128]{2,1,0:T(2,128)(2,1)S(1)} async-done(((bf16[160,2,128]{2,1,0:T(2,128)(2,1)}), bf16[160,2,128]{2,1,0:T(2,128)(2,1)S(1)}, u32[]{:S(2)}, u32[]{:S(2)}) %all-to-all-start.24) | async-done | bytes 81952 | tf_op jit(solution)/shard_map/all_to_all | solution.py:213
  664.0 8.7 %all-to-all-done.25.refs_1_ = bf16[160,2,128]{2,1,0:T(2,128)(2,1)S(1)} async-done(((bf16[160,2,128]{2,1,0:T(2,128)(2,1)}), bf16[160,2,128]{2,1,0:T(2,128)(2,1)S(1)}, u32[]{:S(2)}, u32[]{:S(2)}) %all-to-all-start.25) | async-done | bytes 81952 | tf_op jit(solution)/shard_map/all_to_all | solution.py:213
  680.2 14.9 %all_to_all.188.blocks_ref = bf16[160,2,128]{2,1,0:T(2,128)(2,1)} all-to-all(bf16[160,2,128]{2,1,0:T(2,128)(2,1)} %get-tuple-element.376), channel_id=1, replica_groups=mesh['section'=8,'expert'=32] {'expert'}, dimensions={0} | all-to-all | bytes 163840 | tf_op jit(solution)/shard_map/all_to_all | solution.py:213
  704.0 10.0 %all-to-all-done.27.refs_1_ = bf16[160,2,128]{2,1,0:T(2,128)(2,1)S(1)} async-done(((bf16[160,2,128]{2,1,0:T(2,128)(2,1)}), bf16[160,2,128]{2,1,0:T(2,128)(2,1)S(1)}, u32[]{:S(2)}, u32[]{:S(2)}) %all-to-all-start.27) | async-done | bytes 81952 | tf_op jit(solution)/shard_map/all_to_all | solution.py:213
  725.4 10.1 %all-to-all-done.28.blocks_ref = bf16[160,2,128]{2,1,0:T(2,128)(2,1)S(1)} async-done(((bf16[160,2,128]{2,1,0:T(2,128)(2,1)}), bf16[160,2,128]{2,1,0:T(2,128)(2,1)S(1)}, u32[]{:S(2)}, u32[]{:S(2)}) %all-to-all-start.28) | async-done | bytes 81952 | tf_op jit(solution)/shard_map/all_to_all | solution.py:213
  765.1 15.1 %all_to_all.189.blocks_ref = bf16[160,2,128]{2,1,0:T(2,128)(2,1)} all-to-all(bf16[160,2,128]{2,1,0:T(2,128)(2,1)} %get-tuple-element.398), channel_id=1, replica_groups=mesh['section'=8,'expert'=32] {'expert'}, dimensions={0} | all-to-all | bytes 163840 | tf_op jit(solution)/shard_map/all_to_all | solution.py:213
  789.2 10.0 %all-to-all-done.31.refs_1_ = bf16[160,2,128]{2,1,0:T(2,128)(2,1)S(1)} async-done(((bf16[160,2,128]{2,1,0:T(2,128)(2,1)}), bf16[160,2,128]{2,1,0:T(2,128)(2,1)S(1)}, u32[]{:S(2)}, u32[]{:S(2)}) %all-to-all-start.31) | async-done | bytes 81952 | tf_op jit(solution)/shard_map/all_to_all | solution.py:213
  809.3 10.1 %all-to-all-done.32.blocks_ref = bf16[160,2,128]{2,1,0:T(2,128)(2,1)S(1)} async-done(((bf16[160,2,128]{2,1,0:T(2,128)(2,1)}), bf16[160,2,128]{2,1,0:T(2,128)(2,1)S(1)}, u32[]{:S(2)}, u32[]{:S(2)}) %all-to-all-start.32) | async-done | bytes 81952 | tf_op jit(solution)/shard_map/all_to_all | solution.py:213
  825.0 14.6 %all_to_all.190.refs_1_ = bf16[160,2,128]{2,1,0:T(2,128)(2,1)} all-to-all(bf16[160,2,128]{2,1,0:T(2,128)(2,1)} %expert.31), channel_id=1, replica_groups=mesh['section'=8,'expert'=32] {'expert'}, dimensions={0} | all-to-all | bytes 163840 | tf_op jit(solution)/shard_map/all_to_all | solution.py:213
  (237 shorter events, 448.8 us)
Async XLA Ops:
  8.1 30.5 %collective-permute-start = (bf16[1536,768]{1,0:T(8,128)(2,1)}, bf16[1536,768]{1,0:T(8,128)(2,1)}, u32[]{:S(2)}, u32[]{:S(2)}) collective-permute-start(bf16[1536,768]{1,0:T(8,128)(2,1)} %pick.12), channel_id=1, source_target_pairs={{0,32},{32,0},{64,96},{96,64},{128,160},{160,128},{192,224},{224,1... | collective-permute-start | bytes 7077896 | tf_op jit(solution)/shard_map/ppermute | solution.py:514
  17.9 20.7 %collective-permute-start.2 = (bf16[768,768]{1,0:T(8,128)(2,1)}, bf16[768,768]{1,0:T(8,128)(2,1)}, u32[]{:S(2)}, u32[]{:S(2)}) collective-permute-start(bf16[768,768]{1,0:T(8,128)(2,1)} %pick.14), channel_id=1, source_target_pairs={{0,64},{32,224},{64,128},{96,32},{128,192},{160,96},{1,65},{33,225... | collective-permute-start | bytes 3538952 | tf_op jit(solution)/shard_map/ppermute | solution.py:519
  103.2 28.2 %collective-permute-start.11 = (bf16[768,768]{1,0:T(8,128)(2,1)}, bf16[768,768]{1,0:T(8,128)(2,1)}, u32[]{:S(2)}, u32[]{:S(2)}) collective-permute-start(bf16[768,768]{1,0:T(8,128)(2,1)} %collective-permute-done.5.refs_2_.refs_6_.refs_1_.refs_4_.refs_5_), channel_id=1, source_target_pairs={{0,32},{32,0},{64,96},{96,64},{128,160},{160,128},{192,224},{224,1... | collective-permute-start | bytes 3538952 | tf_op jit(solution)/shard_map/ppermute | solution.py:514
  106.2 25.2 %collective-permute-start.10 = (bf16[768,768]{1,0:T(8,128)(2,1)}, bf16[768,768]{1,0:T(8,128)(2,1)}, u32[]{:S(2)}, u32[]{:S(2)}) collective-permute-start(bf16[768,768]{1,0:T(8,128)(2,1)} %pick.19), channel_id=1, source_target_pairs={{32,224},{64,128},{96,32},{128,192},{160,96},{192,0},{224,160},{33... | collective-permute-start | bytes 3538952 | tf_op jit(solution)/shard_map/ppermute | solution.py:519
  155.2 19.4 %collective-permute-start.14 = (bf16[768,768]{1,0:T(8,128)(2,1)}, bf16[768,768]{1,0:T(8,128)(2,1)}, u32[]{:S(2)}, u32[]{:S(2)}) collective-permute-start(bf16[768,768]{1,0:T(8,128)(2,1)} %pick.20), channel_id=1, source_target_pairs={{64,128},{96,32},{128,192},{160,96},{192,0},{224,160},{65,129},{97... | collective-permute-start | bytes 3538952 | tf_op jit(solution)/shard_map/ppermute | solution.py:519
  163.4 22.7 %collective-permute-start.15 = (bf16[768,768]{1,0:T(8,128)(2,1)}, bf16[768,768]{1,0:T(8,128)(2,1)}, u32[]{:S(2)}, u32[]{:S(2)}) collective-permute-start(bf16[768,768]{1,0:T(8,128)(2,1)} %pick.21), channel_id=1, source_target_pairs={{0,64},{32,224},{64,128},{96,32},{128,192},{160,96},{192,0},{224,1... | collective-permute-start | bytes 3538952 | tf_op jit(solution)/shard_map/ppermute | solution.py:519
  192.2 38.1 %collective-permute-start.18 = (bf16[1536,768]{1,0:T(8,128)(2,1)}, bf16[1536,768]{1,0:T(8,128)(2,1)}, u32[]{:S(2)}, u32[]{:S(2)}) collective-permute-start(bf16[1536,768]{1,0:T(8,128)(2,1)} %get-tuple-element.258), channel_id=1, source_target_pairs={{0,64},{32,224},{128,192},{160,96},{192,0},{224,160},{1,65},{33,22... | collective-permute-start | bytes 7077896 | tf_op jit(solution)/shard_map/ppermute | solution.py:519
  236.2 38.9 %collective-permute-start.19 = (bf16[1536,768]{1,0:T(8,128)(2,1)}, bf16[1536,768]{1,0:T(8,128)(2,1)}, u32[]{:S(2)}, u32[]{:S(2)}) collective-permute-start(bf16[1536,768]{1,0:T(8,128)(2,1)} %get-tuple-element.268), channel_id=1, source_target_pairs={{0,64},{32,224},{64,128},{96,32},{128,192},{160,96},{192,0},{224,1... | collective-permute-start | bytes 7077896 | tf_op jit(solution)/shard_map/ppermute | solution.py:519
  265.1 28.0 %collective-permute-start.20 = (bf16[1536,768]{1,0:T(8,128)(2,1)}, bf16[1536,768]{1,0:T(8,128)(2,1)}, u32[]{:S(2)}, u32[]{:S(2)}) collective-permute-start(bf16[1536,768]{1,0:T(8,128)(2,1)} %collective-permute-done.18.refs_6_.refs_5_.refs_8_.refs_3_.refs_4_), channel_id=1, source_target_pairs={{0,32},{32,0},{64,96},{96,64},{128,160},{160,128},{192,224},{224,1... | collective-permute-start | bytes 7077896 | tf_op jit(solution)/shard_map/ppermute | solution.py:514
  285.3 31.0 %collective-permute-start.23 = (bf16[1536,768]{1,0:T(8,128)(2,1)}, bf16[1536,768]{1,0:T(8,128)(2,1)}, u32[]{:S(2)}, u32[]{:S(2)}) collective-permute-start(bf16[1536,768]{1,0:T(8,128)(2,1)} %get-tuple-element.280), channel_id=1, source_target_pairs={{0,64},{32,224},{64,128},{96,32},{192,0},{224,160},{1,65},{33,225}... | collective-permute-start | bytes 7077896 | tf_op jit(solution)/shard_map/ppermute | solution.py:519
  329.6 35.6 %collective-permute-start.24 = (bf16[1536,768]{1,0:T(8,128)(2,1)}, bf16[1536,768]{1,0:T(8,128)(2,1)}, u32[]{:S(2)}, u32[]{:S(2)}) collective-permute-start(bf16[1536,768]{1,0:T(8,128)(2,1)} %get-tuple-element.291), channel_id=1, source_target_pairs={{0,64},{32,224},{64,128},{160,96},{192,0},{1,65},{33,225},{65,129}... | collective-permute-start | bytes 7077896 | tf_op jit(solution)/shard_map/ppermute | solution.py:519
  355.1 22.0 %collective-permute-start.25 = (bf16[1536,768]{1,0:T(8,128)(2,1)}, bf16[1536,768]{1,0:T(8,128)(2,1)}, u32[]{:S(2)}, u32[]{:S(2)}) collective-permute-start(bf16[1536,768]{1,0:T(8,128)(2,1)} %collective-permute-done.23.refs_5_.refs_6_.refs_3_), channel_id=1, source_target_pairs={{0,32},{32,0},{64,96},{96,64},{128,160},{160,128},{192,224},{224,1... | collective-permute-start | bytes 7077896 | tf_op jit(solution)/shard_map/ppermute | solution.py:514
  365.1 22.1 %collective-permute-start.26 = (bf16[1536,768]{1,0:T(8,128)(2,1)}, bf16[1536,768]{1,0:T(8,128)(2,1)}, u32[]{:S(2)}, u32[]{:S(2)}) collective-permute-start(bf16[1536,768]{1,0:T(8,128)(2,1)} %collective-permute-done.24.refs_6_.refs_4_), channel_id=1, source_target_pairs={{0,32},{32,0},{64,96},{96,64},{128,160},{160,128},{192,224},{224,1... | collective-permute-start | bytes 7077896 | tf_op jit(solution)/shard_map/ppermute | solution.py:514
  371.3 31.1 %collective-permute-start.27 = (bf16[1536,768]{1,0:T(8,128)(2,1)}, bf16[1536,768]{1,0:T(8,128)(2,1)}, u32[]{:S(2)}, u32[]{:S(2)}) collective-permute-start(bf16[1536,768]{1,0:T(8,128)(2,1)} %get-tuple-element.303), channel_id=1, source_target_pairs={{0,64},{64,128},{96,32},{128,192},{160,96},{224,160},{1,65},{65,12... | collective-permute-start | bytes 7077896 | tf_op jit(solution)/shard_map/ppermute | solution.py:519
  413.6 39.5 %collective-permute-start.28 = (bf16[1536,768]{1,0:T(8,128)(2,1)}, bf16[1536,768]{1,0:T(8,128)(2,1)}, u32[]{:S(2)}, u32[]{:S(2)}) collective-permute-start(bf16[1536,768]{1,0:T(8,128)(2,1)} %get-tuple-element.313), channel_id=1, source_target_pairs={{0,64},{32,224},{64,128},{96,32},{128,192},{160,96},{1,65},{33,225... | collective-permute-start | bytes 7077896 | tf_op jit(solution)/shard_map/ppermute | solution.py:519
  443.0 27.4 %collective-permute-start.29 = (bf16[1536,768]{1,0:T(8,128)(2,1)}, bf16[1536,768]{1,0:T(8,128)(2,1)}, u32[]{:S(2)}, u32[]{:S(2)}) collective-permute-start(bf16[1536,768]{1,0:T(8,128)(2,1)} %collective-permute-done.27.refs_6_.refs_5_.refs_3_), channel_id=1, source_target_pairs={{0,32},{32,0},{64,96},{96,64},{128,160},{160,128},{192,224},{224,1... | collective-permute-start | bytes 7077896 | tf_op jit(solution)/shard_map/ppermute | solution.py:514
  463.2 28.6 %collective-permute-start.32 = (bf16[1536,768]{1,0:T(8,128)(2,1)}, bf16[1536,768]{1,0:T(8,128)(2,1)}, u32[]{:S(2)}, u32[]{:S(2)}) collective-permute-start(bf16[1536,768]{1,0:T(8,128)(2,1)} %get-tuple-element.325), channel_id=1, source_target_pairs={{32,224},{64,128},{96,32},{128,192},{160,96},{192,0},{224,160},{33... | collective-permute-start | bytes 7077896 | tf_op jit(solution)/shard_map/ppermute | solution.py:519
  506.5 36.4 %collective-permute-start.33 = (bf16[1536,768]{1,0:T(8,128)(2,1)}, bf16[1536,768]{1,0:T(8,128)(2,1)}, u32[]{:S(2)}, u32[]{:S(2)}) collective-permute-start(bf16[1536,768]{1,0:T(8,128)(2,1)} %get-tuple-element.336), channel_id=1, source_target_pairs={{32,224},{64,128},{96,32},{128,192},{160,96},{192,0},{224,160},{33... | collective-permute-start | bytes 7077896 | tf_op jit(solution)/shard_map/ppermute | solution.py:519
  532.8 21.6 %collective-permute-start.34 = (bf16[1536,768]{1,0:T(8,128)(2,1)}, bf16[1536,768]{1,0:T(8,128)(2,1)}, u32[]{:S(2)}, u32[]{:S(2)}) collective-permute-start(bf16[1536,768]{1,0:T(8,128)(2,1)} %collective-permute-done.32.refs_6_.refs_4_.refs_5_.refs_3_), channel_id=1, source_target_pairs={{0,32},{32,0},{64,96},{96,64},{128,160},{160,128},{192,224},{224,1... | collective-permute-start | bytes 7077896 | tf_op jit(solution)/shard_map/ppermute | solution.py:514
  542.9 21.6 %collective-permute-start.35 = (bf16[1536,768]{1,0:T(8,128)(2,1)}, bf16[1536,768]{1,0:T(8,128)(2,1)}, u32[]{:S(2)}, u32[]{:S(2)}) collective-permute-start(bf16[1536,768]{1,0:T(8,128)(2,1)} %collective-permute-done.33.refs_7_.refs_5_.refs_6_.refs_4_), channel_id=1, source_target_pairs={{0,32},{32,0},{64,96},{96,64},{128,160},{160,128},{192,224},{224,1... | collective-permute-start | bytes 7077896 | tf_op jit(solution)/shard_map/ppermute | solution.py:514
  549.0 31.1 %collective-permute-start.36 = (bf16[1536,768]{1,0:T(8,128)(2,1)}, bf16[1536,768]{1,0:T(8,128)(2,1)}, u32[]{:S(2)}, u32[]{:S(2)}) collective-permute-start(bf16[1536,768]{1,0:T(8,128)(2,1)} %get-tuple-element.348), channel_id=1, source_target_pairs={{0,64},{32,224},{96,32},{128,192},{192,0},{224,160},{1,65},{33,225... | collective-permute-start | bytes 7077896 | tf_op jit(solution)/shard_map/ppermute | solution.py:519
  591.0 35.5 %collective-permute-start.37 = (bf16[1536,768]{1,0:T(8,128)(2,1)}, bf16[1536,768]{1,0:T(8,128)(2,1)}, u32[]{:S(2)}, u32[]{:S(2)}) collective-permute-start(bf16[1536,768]{1,0:T(8,128)(2,1)} %get-tuple-element.358), channel_id=1, source_target_pairs={{0,64},{32,224},{128,192},{192,0},{224,160},{1,65},{33,225},{129,1... | collective-permute-start | bytes 7077896 | tf_op jit(solution)/shard_map/ppermute | solution.py:519
  616.3 26.3 %collective-permute-start.38 = (bf16[1536,768]{1,0:T(8,128)(2,1)}, bf16[1536,768]{1,0:T(8,128)(2,1)}, u32[]{:S(2)}, u32[]{:S(2)}) collective-permute-start(bf16[1536,768]{1,0:T(8,128)(2,1)} %collective-permute-done.36.refs_5_.refs_6_.refs_4_.refs_3_), channel_id=1, source_target_pairs={{0,32},{32,0},{64,96},{96,64},{128,160},{160,128},{192,224},{224,1... | collective-permute-start | bytes 7077896 | tf_op jit(solution)/shard_map/ppermute | solution.py:514
  626.5 26.3 %collective-permute-start.39 = (bf16[1536,768]{1,0:T(8,128)(2,1)}, bf16[1536,768]{1,0:T(8,128)(2,1)}, u32[]{:S(2)}, u32[]{:S(2)}) collective-permute-start(bf16[1536,768]{1,0:T(8,128)(2,1)} %collective-permute-done.37.refs_6_.refs_5_.refs_4_), channel_id=1, source_target_pairs={{0,32},{32,0},{64,96},{96,64},{128,160},{160,128},{192,224},{224,1... | collective-permute-start | bytes 7077896 | tf_op jit(solution)/shard_map/ppermute | solution.py:514
  632.6 31.3 %collective-permute-start.40 = (bf16[1536,768]{1,0:T(8,128)(2,1)}, bf16[1536,768]{1,0:T(8,128)(2,1)}, u32[]{:S(2)}, u32[]{:S(2)}) collective-permute-start(bf16[1536,768]{1,0:T(8,128)(2,1)} %get-tuple-element.370), channel_id=1, source_target_pairs={{64,128},{160,96},{192,0},{224,160},{65,129},{161,97},{193,1},{225... | collective-permute-start | bytes 7077896 | tf_op jit(solution)/shard_map/ppermute | solution.py:519
  678.9 35.2 %collective-permute-start.41 = (bf16[1536,768]{1,0:T(8,128)(2,1)}, bf16[1536,768]{1,0:T(8,128)(2,1)}, u32[]{:S(2)}, u32[]{:S(2)}) collective-permute-start(bf16[1536,768]{1,0:T(8,128)(2,1)} %get-tuple-element.380), channel_id=1, source_target_pairs={{0,64},{96,32},{160,96},{192,0},{1,65},{97,33},{161,97},{193,1},{2... | collective-permute-start | bytes 7077896 | tf_op jit(solution)/shard_map/ppermute | solution.py:519
  703.9 21.4 %collective-permute-start.42 = (bf16[1536,768]{1,0:T(8,128)(2,1)}, bf16[1536,768]{1,0:T(8,128)(2,1)}, u32[]{:S(2)}, u32[]{:S(2)}) collective-permute-start(bf16[1536,768]{1,0:T(8,128)(2,1)} %collective-permute-done.40.refs_5_.refs_6_.refs_3_), channel_id=1, source_target_pairs={{0,32},{32,0},{64,96},{96,64},{128,160},{160,128},{192,224},{224,1... | collective-permute-start | bytes 7077896 | tf_op jit(solution)/shard_map/ppermute | solution.py:514
  714.0 21.4 %collective-permute-start.43 = (bf16[1536,768]{1,0:T(8,128)(2,1)}, bf16[1536,768]{1,0:T(8,128)(2,1)}, u32[]{:S(2)}, u32[]{:S(2)}) collective-permute-start(bf16[1536,768]{1,0:T(8,128)(2,1)} %collective-permute-done.41.refs_5_.refs_7_.refs_6_.refs_4_), channel_id=1, source_target_pairs={{0,32},{32,0},{64,96},{96,64},{128,160},{160,128},{192,224},{224,1... | collective-permute-start | bytes 7077896 | tf_op jit(solution)/shard_map/ppermute | solution.py:514
  720.2 31.1 %collective-permute-start.44 = (bf16[1536,768]{1,0:T(8,128)(2,1)}, bf16[1536,768]{1,0:T(8,128)(2,1)}, u32[]{:S(2)}, u32[]{:S(2)}) collective-permute-start(bf16[1536,768]{1,0:T(8,128)(2,1)} %get-tuple-element.392), channel_id=1, source_target_pairs={{0,64},{96,32},{1,65},{97,33},{2,66},{98,34},{3,67},{99,35},{4,68}... | collective-permute-start | bytes 7077896 | tf_op jit(solution)/shard_map/ppermute | solution.py:519
  761.2 38.0 %collective-permute-start.45 = (bf16[1536,768]{1,0:T(8,128)(2,1)}, bf16[1536,768]{1,0:T(8,128)(2,1)}, u32[]{:S(2)}, u32[]{:S(2)}) collective-permute-start(bf16[1536,768]{1,0:T(8,128)(2,1)} %get-tuple-element.402), channel_id=1, source_target_pairs={{64,128},{65,129},{66,130},{67,131},{68,132},{69,133},{70,134},{71... | collective-permute-start | bytes 7077896 | tf_op jit(solution)/shard_map/ppermute | solution.py:519
  789.1 20.2 %collective-permute-start.46 = (bf16[1536,768]{1,0:T(8,128)(2,1)}, bf16[1536,768]{1,0:T(8,128)(2,1)}, u32[]{:S(2)}, u32[]{:S(2)}) collective-permute-start(bf16[1536,768]{1,0:T(8,128)(2,1)} %collective-permute-done.44.refs_5_), channel_id=1, source_target_pairs={{0,32},{32,0},{64,96},{96,64},{128,160},{160,128},{192,224},{224,1... | collective-permute-start | bytes 7077896 | tf_op jit(solution)/shard_map/ppermute | solution.py:514
  799.2 20.2 %collective-permute-start.47 = (bf16[1536,768]{1,0:T(8,128)(2,1)}, bf16[1536,768]{1,0:T(8,128)(2,1)}, u32[]{:S(2)}, u32[]{:S(2)}) collective-permute-start(bf16[1536,768]{1,0:T(8,128)(2,1)} %collective-permute-done.45.refs_6_), channel_id=1, source_target_pairs={{0,32},{32,0},{64,96},{96,64},{128,160},{160,128},{192,224},{224,1... | collective-permute-start | bytes 7077896 | tf_op jit(solution)/shard_map/ppermute | solution.py:514
  (64 other events, 612.1 us)

commit v6 on v4

--- a/solution.py
+++ b/solution.py
@@ -8,7 +8,7 @@
 from jax.experimental.pallas import tpu as pltpu
 from jax.sharding import PartitionSpec as P
 
-VMEM_LIMIT = 62 * 1024 * 1024
+VMEM_LIMIT = 64400 * 1024
 HBM = pl.BlockSpec(memory_space=pltpu.HBM)
 SMEM = pl.BlockSpec(memory_space=pltpu.SMEM)
 VMEM = pl.BlockSpec(memory_space=pltpu.VMEM)
@@ -49,59 +49,112 @@
     return steps, held
 
 
-def pick_kernel(rows, places, tab_ref, *refs):
-    count = len(places)
-    sources, (out_ref, hold_ref, in_sems, out_sems) = refs[:count], refs[count:]
-    size = hold_ref.shape[0] // len(rows)
-
-    def view(number, start):
-        return sources[number].at[places[number] + (pl.ds(start, size),)]
-
-    def part_of(ref, part):
-        return ref.at[pl.ds(part * size, size)]
-
-    for part, (row, choices) in enumerate(rows):
-        choice = tab_ref[row]
-        for number, (source, start) in enumerate(choices):
-
-            @pl.when(choice == number)
-            def _(part=part, source=source, start=start):
-                pltpu.make_async_copy(
-                    view(source, start), part_of(hold_ref, part), in_sems.at[part]
-                ).start()
-
-    def leave(part):
+class Reads:
+    def __init__(self, rows, places, size, tab_ref, sources, hold_ref, sems):
+        self.rows, self.places, self.size = rows, places, size
+        self.tab_ref, self.sources = tab_ref, sources
+        self.hold_ref, self.sems = hold_ref, sems
+
+    def part_of(self, ref, part):
+        return ref.at[pl.ds(pl.multiple_of(part * self.size, self.size), self.size)]
+
+    def copy(self, part, choice):
+        number, start = choice
+        view = self.sources[number].at[self.places[number] + (pl.ds(start, self.size),)]
+        return pltpu.make_async_copy(view, self.part_of(self.hold_ref, part), self.sems.at[part])
+
+    def start(self):
+        for part, (row, choices) in enumerate(self.rows):
+            wish = self.tab_ref[row]
+            for number, choice in enumerate(choices):
+
+                @pl.when(wish == number)
+                def _(part=part, choice=choice):
+                    self.copy(part, choice).start()
+
+    def wait(self, part):
+        to = self.part_of(self.hold_ref, part)
+        pltpu.make_async_copy(to, to, self.sems.at[part]).wait()
+
+    def forward(self, out_ref, sems):
+        for part in range(len(self.rows)):
+            self.wait(part)
+            self.leave(part, out_ref, sems).start()
+
+    def finish(self, out_ref, sems):
+        for part in range(len(self.rows)):
+            self.leave(part, out_ref, sems).wait()
+
+    def leave(self, part, out_ref, sems):
         return pltpu.make_async_copy(
-            part_of(hold_ref, part), part_of(out_ref, part), out_sems.at[part]
+            self.part_of(self.hold_ref, part), self.part_of(out_ref, part), sems.at[part]
         )
 
-    for part, (_, choices) in enumerate(rows):
-        pltpu.make_async_copy(
-            view(*choices[0]), part_of(hold_ref, part), in_sems.at[part]
-        ).wait()
-        leave(part).start()
-    for part in range(len(rows)):
-        leave(part).wait()
-
-
-def pick(tab, rows, sources, places, size, width):
-    shape = (size * len(rows), width)
+
+class Side:
+    def __init__(self, side):
+        self.tab, self.jobs, arrays, self.places, self.size, width = side
+        self.operands = [self.tab] + arrays
+        self.in_specs = [SMEM] + [HBM] * len(arrays)
+        shapes = [(self.size * len(rows), width) for rows in self.jobs]
+        self.out_shapes = [jax.ShapeDtypeStruct(shape, jnp.bfloat16) for shape in shapes]
+        self.out_specs = [HBM] * len(self.jobs)
+        self.scratch = []
+        for rows, shape in zip(self.jobs, shapes):
+            self.scratch += [pltpu.VMEM(shape, jnp.bfloat16)]
+            self.scratch += [pltpu.SemaphoreType.DMA((len(rows),))] * 2
+
+    def bind(self, inputs, outputs, scratch):
+        self.outputs = outputs
+        self.reads = [
+            Reads(rows, self.places, self.size, inputs[0], inputs[1:], hold_ref, in_sems)
+            for rows, hold_ref, in_sems in zip(self.jobs, scratch[0::3], scratch[1::3])
+        ]
+        self.out_sems = scratch[2::3]
+
+    def start(self):
+        for reads in self.reads:
+            reads.start()
+
+    def forward(self):
+        for reads, out_ref, sems in zip(self.reads, self.outputs, self.out_sems):
+            reads.forward(out_ref, sems)
+
+    def finish(self):
+        for reads, out_ref, sems in zip(self.reads, self.outputs, self.out_sems):
+            reads.finish(out_ref, sems)
+
+
+def call_with_side(kernel, side, operands, in_specs, shapes, out_specs, scratch, **options):
+    beside = Side(side)
+    counts = [len(operands), len(beside.operands), len(shapes), len(beside.out_shapes), len(scratch)]
+
+    def body(*refs):
+        cuts = np.cumsum(counts)
+        groups = [refs[end - count : end] for count, end in zip(counts, cuts)]
+        beside.bind(groups[1], groups[3], refs[cuts[-1] :])
+        kernel(beside, *groups[0], *groups[2], *groups[4])
+
     return pl.pallas_call(
-        functools.partial(pick_kernel, rows, places),
-        out_shape=jax.ShapeDtypeStruct(shape, jnp.bfloat16),
-        in_specs=[SMEM] + [HBM] * len(sources),
-        out_specs=HBM,
-        scratch_shapes=[
-            pltpu.VMEM(shape, jnp.bfloat16),
-            pltpu.SemaphoreType.DMA((len(rows),)),
-            pltpu.SemaphoreType.DMA((len(rows),)),
-        ],
+        body,
+        out_shape=tuple(shapes) + tuple(beside.out_shapes),
+        grid=(1,),
+        in_specs=list(in_specs) + beside.in_specs,
+        out_specs=tuple(out_specs) + tuple(beside.out_specs),
+        scratch_shapes=list(scratch) + beside.scratch,
         compiler_params=pltpu.CompilerParams(vmem_limit_bytes=VMEM_LIMIT),
-        cost_estimate=pl.CostEstimate(
-            flops=0, bytes_accessed=4 * shape[0] * width, transcendentals=0
-        ),
-        name="pick",
-    )(tab, *sources)
+        **options,
+    )(*operands, *beside.operands)
+
+
+def copy_kernel(side):
+    side.start()
+    side.forward()
+    side.finish()
+
+
+def pick(side):
+    return call_with_side(copy_kernel, side, [], [], [], [], [], name="pick")[0]
 
 
 LANES = 128
@@ -185,7 +238,8 @@
     return lax.all_to_all(value, "expert", split_axis=0, concat_axis=0, tiled=True)
 
 
-def turn_kernel(merge, send, *refs):
+def turn_kernel(merge, send, side, *refs):
+    side.start()
     refs = list(refs)
     h_ref = refs.pop(0)
     if merge:
@@ -210,6 +264,7 @@
         change = update[0:features] * (1.0 / update[features:features + 1])
         held = (held.astype(jnp.float32) + change).astype(jnp.bfloat16)
     hnew_ref[...] = held
+    side.forward()
     if send:
         out_ref = refs.pop(0)
         offset = lax.broadcasted_iota(jnp.int32, (tokens, 4 * PACK), 1)
@@ -225,9 +280,10 @@
                 number = turn * 4 + half * 2
                 store_block(out_ref, number, pack(*groups, 0))
                 store_block(out_ref, number + 1, pack(*groups, PACK))
-
-
-def run_turn(experts, h, back, rows, before, after):
+    side.finish()
+
+
+def run_turn(side, experts, h, back, rows, before, after):
     features, tokens = h.shape
     merge, send = before is not None, after is not None
     operands, specs, scratch = [h], [VMEM], []
@@ -241,20 +297,14 @@
         specs += [plane((8, tokens), after)]
         shapes += [jax.ShapeDtypeStruct((experts * TILES, 2, LANES), jnp.bfloat16)]
         outs += [VMEM]
-    return pl.pallas_call(
-        functools.partial(turn_kernel, merge, send),
-        out_shape=tuple(shapes),
-        grid=(1,),
-        in_specs=specs,
-        out_specs=tuple(outs),
-        scratch_shapes=scratch,
-        compiler_params=pltpu.CompilerParams(vmem_limit_bytes=VMEM_LIMIT),
+    return call_with_side(
+        functools.partial(turn_kernel, merge, send), side, operands, specs, shapes, outs, scratch,
         name="turn",
-    )(*operands)
+    )
 
 
 def expert_kernel(
-    scal_ref, blocks_ref, gain_ref, router_ref, lane_ref, other_ref, out_ref,
+    side, scal_ref, blocks_ref, gain_ref, router_ref, lane_ref, other_ref, out_ref,
     win_ref, wout_ref, wide_ref, sems,
 ):
     core = scal_ref[0]
@@ -269,6 +319,7 @@
         pltpu.make_async_copy(other_ref, win_ref, sems.at[0]).start()
         pltpu.make_async_copy(lane_ref, wout_ref, sems.at[1]).start()
 
+    side.start()
     width = win_ref.shape[1]
     groups = wide_ref.shape[0]
     blocks = load_blocks(blocks_ref, wide_ref)
@@ -283,6 +334,7 @@
     pre_act = lax.dot_general(
         normed, win_ref[...], (((1,), (1,)), ((), ())), preferred_element_type=jnp.float32
     )
+    side.forward()
     active = jax.nn.gelu(pre_act, approximate=True).astype(jnp.bfloat16)
     pltpu.make_async_copy(lane_ref, wout_ref, sems.at[1]).wait()
     output = jnp.dot(active, wout_ref[...], preferred_element_type=jnp.float32)
@@ -295,28 +347,29 @@
     packed = pack(tall[:, 0], tall[:, 1], tall[:, 2], 0, gates)
     for number in range(groups):
         store_block(out_ref, number, packed[number])
-
-
-def run_expert(layer, scal, blocks, gains, routers, lane_w, other_w):
+    side.finish()
+
+
+def run_expert(side, layer, scal, blocks, gains, routers, lane_w, other_w):
     hidden, width = lane_w.shape
-    return pl.pallas_call(
+    return call_with_side(
         expert_kernel,
-        out_shape=jax.ShapeDtypeStruct(blocks.shape, jnp.bfloat16),
-        grid=(1,),
-        in_specs=[SMEM, VMEM, plane((1, width), layer), plane((1, width), layer), HBM, HBM],
-        out_specs=VMEM,
-        scratch_shapes=[
+        side,
+        [scal, blocks, gains, routers, lane_w, other_w],
+        [SMEM, VMEM, plane((1, width), layer), plane((1, width), layer), HBM, HBM],
+        [jax.ShapeDtypeStruct(blocks.shape, jnp.bfloat16)],
+        [VMEM],
+        [
             pltpu.VMEM((hidden, width), jnp.bfloat16),
             pltpu.VMEM((hidden, width), jnp.bfloat16),
             pltpu.VMEM((blocks.shape[0] // TILES, 16, LANES), jnp.float32),
             pltpu.SemaphoreType.DMA((2,)),
         ],
-        compiler_params=pltpu.CompilerParams(vmem_limit_bytes=VMEM_LIMIT),
         cost_estimate=pl.CostEstimate(
             flops=4 * PACK * hidden * width, bytes_accessed=4 * hidden * width, transcendentals=0
         ),
         name="expert",
-    )(scal, blocks, gains, routers, lane_w, other_w)
+    )
 
 
 def plane(shape, *lead):
@@ -394,24 +447,28 @@
     ]
     tab = jnp.asarray(np.array(table, np.int32).T)[section_pos]
 
+    def side_of(tab, *jobs):
+        names = sorted({name for rows in jobs for row in rows for name, _ in wanted[row]})
+        found = [buffers[name] for name in names]
+        plans = [
+            tuple(
+                (row, tuple((names.index(name), start) for name, start in wanted[row]))
+                for row in rows
+            )
+            for rows in jobs
+        ]
+        return tab, plans, [array for array, _ in found], [at for _, at in found], size, width
+
     def picked(rows, tab):
-        names = sorted({name for row in rows for name, _ in wanted[row]})
-        found = [buffers[name] for name in names]
-        plan = tuple(
-            (row, tuple((names.index(name), start) for name, start in wanted[row])) for row in rows
-        )
-        places = [place for _, place in found]
-        return pick(tab, plan, [array for array, _ in found], places, size, width)
+        return pick(side_of(tab, rows))
 
     def swapped(value):
         return lax.ppermute(value, "section", [(s, s ^ 1) for s in range(sections)])
 
-    def ring(number, tab):
-        if number > len(steps):
-            return None
+    def ring(number, value):
         moves = steps[number - 1]
         pairs = sorted({(2 * y + lane, 2 * target + lane) for lane, y, target, _, _ in moves})
-        return lax.ppermute(picked(ring_rows[number - 1], tab), "section", pairs)
+        return lax.ppermute(value, "section", pairs)
 
     def arrival(q):
         parts = range(q * PARTS, (q + 1) * PARTS)
@@ -431,41 +488,48 @@
     later = swapped(picked(swap_rows[1], tab))
     flying = None
     for number in range(1, LEAD + 1):
-        started = ring(number, tab)
+        started = ring(number, picked(ring_rows[number - 1], tab))
+        if number == LEAD:
+            h, tab = join(h, tab)
+            h, blocks = run_turn(side_of(tab), experts, h, None, rows, None, 0)
+            blocks, tab = join(send_blocks(blocks), tab)
         if flying is not None:
             flying, tab = join(flying, tab)
             buffers[("ring", number - 1)] = (flying, ())
         if number == 2:
-            later, tab = join(later, tab)
+            later, tab, rows, gains, gate_rows, h = join(later, tab, rows, gains, gate_rows, h)
             buffers[("swapped", 1)] = (later, ())
         flying = started
-    flying, tab, rows, gains, gate_rows, h = join(flying, tab, rows, gains, gate_rows, h)
+    flying, tab, blocks = join(flying, tab, blocks)
     buffers[("ring", LEAD)] = (flying, ())
-
-    back = coming = None
+    lane_w = picked(layer_rows[0], tab)
+    coming = (lane_w, swapped(lane_w))
+    flying = ring(LEAD + 1, picked(ring_rows[LEAD], tab))
+    blocks, tab, *coming = join(blocks, tab, *coming)
+
     for q in range(layers):
-        h, blocks = run_turn(experts, h, back, rows, q - 1 if q else None, q)
-        blocks, tab = join(blocks, tab)
-        sent = send_blocks(blocks)
-        flying = ring(LEAD + 1 + q, tab)
-        if coming is None:
-            lane_w = picked(layer_rows[q], tab)
-            coming = (lane_w, swapped(lane_w))
-        blocks, lane_w, other_w, tab = join(sent, *coming, tab)
-        back = run_expert(q, scal, blocks, gains, gate_rows, lane_w, other_w)
-        back, tab = join(back, tab)
-        sent = send_blocks(back)
-        coming = None
-        if q + 1 < layers and arrival(q + 1) < LEAD + 1 + q:
-            lane_w = picked(layer_rows[q + 1], tab)
-            coming = (lane_w, swapped(lane_w))
+        number = LEAD + 1 + q
+        if q:
+            jobs = ([ring_rows[number - 1]] if number <= len(steps) else []) + (
+                [] if coming else [layer_rows[q]]
+            )
+            h, blocks, *extra = run_turn(side_of(tab, *jobs), experts, h, back, rows, q - 1, q)
+            flying = ring(number, extra.pop(0)) if number <= len(steps) else None
+            if not coming:
+                coming = (extra[0], swapped(extra[0]))
+            blocks, tab, *coming = join(send_blocks(blocks), tab, *coming)
+        jobs = [layer_rows[q + 1]] if q + 1 < layers and arrival(q + 1) < number else []
+        back, *extra = run_expert(
+            side_of(tab, *jobs), q, scal, blocks, gains, gate_rows, *coming
+        )
+        coming = (extra[0], swapped(extra[0])) if jobs else None
         if flying is None:
-            back, tab = join(sent, tab)
+            back, tab = join(send_blocks(back), tab)
         else:
-            back, flying, tab = join(sent, flying, tab)
-            buffers[("ring", LEAD + 1 + q)] = (flying, ())
-
-    (h,) = run_turn(experts, h, back, rows, layers - 1, None)
+            back, tab, flying = join(send_blocks(back), tab, flying)
+            buffers[("ring", number)] = (flying, ())
+
+    (h,) = run_turn(side_of(tab), experts, h, back, rows, layers - 1, None)
     return jnp.transpose(h, (1, 0))[None]
 
 

time: 848 us -> 822 us (0.969)
  Pallas kernels: 260 us -> 205 us
  blocking collectives: 205 us -> 238 us
  starting transfers between devices: 152 us -> 137 us
  waiting for transfers between devices: 195 us -> 210 us
    pallas_call x68 -> x43, Pallas kernels: 260 us -> 205 us  [call_with_side(): pl.pallas_call(body, out_shape=tuple(shapes) + tuple(beside.out_shapes),...]
    all_to_all x14 -> x15, blocking collectives: 205 us -> 238 us  [send_blocks(): lax.all_to_all(value, 'expert', split_axis=0, concat_axis=0, tiled=True)]
    all_to_all x18 -> x17, starting transfers between devices: 107 us -> 92.4 us  [send_blocks(): lax.all_to_all(value, 'expert', split_axis=0, concat_axis=0, tiled=True)]
    ppermute x17, waiting for transfers between devices: 88.5 us -> 99.6 us  [ring(): return lax.ppermute(value, 'section', pairs)]
    all_to_all x18 -> x17, waiting for transfers between devices: 93.2 us -> 92.8 us  [send_blocks(): lax.all_to_all(value, 'expert', split_axis=0, concat_axis=0, tiled=True)]
  transfers between devices with their start and end apart: 55 -> 54, of which waited for: 32 -> 28; matrix products, arithmetic and copies ran while one was open for 1% -> 1% of each run, Pallas kernels for 22% -> 18%
where the time goes in v6:
time: 822 us; the launch traced here: 809 us
  blocking collectives  238 us (29%)
  waiting for transfers between devices  210 us (26%)
  Pallas kernels  205 us (25%)
  starting transfers between devices  137 us (17%)
  local copies, waits for them, and re-layouts  14.9 us (2%)
    all_to_all x15, blocking collectives, send_blocks(): lax.all_to_all(value, 'expert', split_axis=0, concat_axis=0, tiled=True)  238 us
    pallas_call x43, Pallas kernels, call_with_side(): pl.pallas_call(body, out_shape=tuple(shapes) + tuple(beside.out_shapes),...  205 us
    ppermute x17, waiting for transfers between devices, ring(): return lax.ppermute(value, 'section', pairs)  99.6 us
    all_to_all x17, waiting for transfers between devices, send_blocks(): lax.all_to_all(value, 'expert', split_axis=0, concat_axis=0, tiled=True)  92.8 us
    all_to_all x17, starting transfers between devices, send_blocks(): lax.all_to_all(value, 'expert', split_axis=0, concat_axis=0, tiled=True)  92.4 us
    ppermute x17, starting transfers between devices, ring(): return lax.ppermute(value, 'section', pairs)  31 us
    all_to_all x1, waiting for transfers between devices, local(): lax.all_to_all(routes[:, 0], 'section', split_axis=1, concat_axis=0, tile...  17.5 us
  transfers between devices with their start and end apart: 54, of which 28 were waited for; matrix products, arithmetic and copies ran while one was open for 1% of the time, Pallas kernels for 18%

profile of v6, /device:TPU:8, one launch (start us, length us, event | category | flops | bytes accessed | tf_op | source)
XLA Modules:
  0.0 808.7 jit_solution(16101219707099261944)
XLA Ops:
  30.1 17.5 %all-to-all-done = s32[1,2,8,512,2]{3,4,1,0,2:T(2,128)S(1)} async-done(((s32[1,2,8,512,2]{3,4,1,0,2:T(2,128)}), s32[1,2,8,512,2]{3,4,1,0,2:T(2,128)S(1)}, u32[]{:S(2)}, u32[]{:S(2)}) %all-to-all-start) | async-done | bytes 65568 | tf_op jit(solution)/shard_map/all_to_all | solution.py:477
  58.8 11.0 %collective-permute-done.5.refs_2_.refs_4_.refs_3_.refs_9_.refs_10_.refs_8_.refs_7_ = bf16[768,768]{1,0:T(8,128)(2,1)} collective-permute-done((bf16[768,768]{1,0:T(8,128)(2,1)}, bf16[768,768]{1,0:T(8,128)(2,1)}, u32[]{:S(2)}, u32[]{:S(2)}) %collective-permute-start.5) | collective-permute-done | bytes 1179680 | tf_op jit(solution)/shard_map/ppermute | solution.py:471
  72.8 9.7 %collective-permute-done.4.refs_2_.refs_5_.refs_4_.refs_10_.refs_11_.refs_9_.refs_8_ = bf16[768,768]{1,0:T(8,128)(2,1)} collective-permute-done((bf16[768,768]{1,0:T(8,128)(2,1)}, bf16[768,768]{1,0:T(8,128)(2,1)}, u32[]{:S(2)}, u32[]{:S(2)}) %collective-permute-start.4) | collective-permute-done | bytes 1179680 | tf_op jit(solution)/shard_map/ppermute | solution.py:471
  90.7 20.9 %all_to_all.180.refs_1_ = bf16[160,2,128]{2,1,0:T(2,128)(2,1)} all-to-all(bf16[160,2,128]{2,1,0:T(2,128)(2,1)} %get-tuple-element.218), channel_id=1, replica_groups=mesh['section'=8,'expert'=32] {'expert'}, dimensions={0} | all-to-all | bytes 163840 | tf_op jit(solution)/shard_map/all_to_all | solution.py:238
  127.8 9.4 %all-to-all-start.3 = ((bf16[160,2,128]{2,1,0:T(2,128)(2,1)}), bf16[160,2,128]{2,1,0:T(2,128)(2,1)S(1)}, u32[]{:S(2)}, u32[]{:S(2)}) async-start(bf16[160,2,128]{2,1,0:T(2,128)(2,1)} %expert.16), calls=%async_computation.3 | async-start | bytes 163840 | tf_op jit(solution)/shard_map/all_to_all | solution.py:238
  137.2 13.0 %collective-permute-done.9.refs_13_.refs_14_.refs_7_.refs_10_.refs_9_.refs_8_ = bf16[1536,768]{1,0:T(8,128)(2,1)} collective-permute-done((bf16[1536,768]{1,0:T(8,128)(2,1)}, bf16[1536,768]{1,0:T(8,128)(2,1)}, u32[]{:S(2)}, u32[]{:S(2)}) %collective-permute-start.9) | collective-permute-done | bytes 2359328 | tf_op jit(solution)/shard_map/ppermute | solution.py:471
  158.5 19.8 %all_to_all.181.refs_1_ = bf16[160,2,128]{2,1,0:T(2,128)(2,1)} all-to-all(bf16[160,2,128]{2,1,0:T(2,128)(2,1)} %get-tuple-element.237), channel_id=1, replica_groups=mesh['section'=8,'expert'=32] {'expert'}, dimensions={0} | all-to-all | bytes 163840 | tf_op jit(solution)/shard_map/all_to_all | solution.py:238
  190.5 10.1 %all-to-all-done.5.refs_1_ = bf16[160,2,128]{2,1,0:T(2,128)(2,1)S(1)} async-done(((bf16[160,2,128]{2,1,0:T(2,128)(2,1)}), bf16[160,2,128]{2,1,0:T(2,128)(2,1)S(1)}, u32[]{:S(2)}, u32[]{:S(2)}) %all-to-all-start.5) | async-done | bytes 81952 | tf_op jit(solution)/shard_map/all_to_all | solution.py:238
  208.2 14.5 %all_to_all.182.refs_1_ = bf16[160,2,128]{2,1,0:T(2,128)(2,1)} all-to-all(bf16[160,2,128]{2,1,0:T(2,128)(2,1)} %get-tuple-element.249), channel_id=1, replica_groups=mesh['section'=8,'expert'=32] {'expert'}, dimensions={0} | all-to-all | bytes 163840 | tf_op jit(solution)/shard_map/all_to_all | solution.py:238
  252.6 14.4 %all_to_all.183.refs_1_ = bf16[160,2,128]{2,1,0:T(2,128)(2,1)} all-to-all(bf16[160,2,128]{2,1,0:T(2,128)(2,1)} %get-tuple-element.260), channel_id=1, replica_groups=mesh['section'=8,'expert'=32] {'expert'}, dimensions={0} | all-to-all | bytes 163840 | tf_op jit(solution)/shard_map/all_to_all | solution.py:238
  279.3 8.2 %all-to-all-done.9.refs_1_ = bf16[160,2,128]{2,1,0:T(2,128)(2,1)S(1)} async-done(((bf16[160,2,128]{2,1,0:T(2,128)(2,1)}), bf16[160,2,128]{2,1,0:T(2,128)(2,1)S(1)}, u32[]{:S(2)}, u32[]{:S(2)}) %all-to-all-start.9) | async-done | bytes 81952 | tf_op jit(solution)/shard_map/all_to_all | solution.py:238
  294.5 14.6 %all_to_all.184.refs_1_ = bf16[160,2,128]{2,1,0:T(2,128)(2,1)} all-to-all(bf16[160,2,128]{2,1,0:T(2,128)(2,1)} %get-tuple-element.272), channel_id=1, replica_groups=mesh['section'=8,'expert'=32] {'expert'}, dimensions={0} | all-to-all | bytes 163840 | tf_op jit(solution)/shard_map/all_to_all | solution.py:238
  340.4 9.7 %all-to-all-done.12.refs_1_ = bf16[160,2,128]{2,1,0:T(2,128)(2,1)S(1)} async-done(((bf16[160,2,128]{2,1,0:T(2,128)(2,1)}), bf16[160,2,128]{2,1,0:T(2,128)(2,1)S(1)}, u32[]{:S(2)}, u32[]{:S(2)}) %all-to-all-start.12) | async-done | bytes 81952 | tf_op jit(solution)/shard_map/all_to_all | solution.py:238
  360.7 8.2 %collective-permute-done.19.refs_8_.refs_6_.refs_11_.refs_10_.refs_9_ = bf16[1536,768]{1,0:T(8,128)(2,1)} collective-permute-done((bf16[1536,768]{1,0:T(8,128)(2,1)}, bf16[1536,768]{1,0:T(8,128)(2,1)}, u32[]{:S(2)}, u32[]{:S(2)}) %collective-permute-start.19) | collective-permute-done | bytes 2359328 | tf_op jit(solution)/shard_map/ppermute | solution.py:471
  405.7 10.1 %collective-permute-done.21.refs_7_.refs_6_.refs_11_.refs_10_.refs_9_ = bf16[1536,768]{1,0:T(8,128)(2,1)} collective-permute-done((bf16[1536,768]{1,0:T(8,128)(2,1)}, bf16[1536,768]{1,0:T(8,128)(2,1)}, u32[]{:S(2)}, u32[]{:S(2)}) %collective-permute-start.21) | collective-permute-done | bytes 2359328 | tf_op jit(solution)/shard_map/ppermute | solution.py:471
  422.4 9.4 %all-to-all-start.16 = ((bf16[160,2,128]{2,1,0:T(2,128)(2,1)}), bf16[160,2,128]{2,1,0:T(2,128)(2,1)S(1)}, u32[]{:S(2)}, u32[]{:S(2)}) async-start(bf16[160,2,128]{2,1,0:T(2,128)(2,1)} %get-tuple-element.307), calls=%async_computation.16 | async-start | bytes 163840 | tf_op jit(solution)/shard_map/all_to_all | solution.py:238
  452.5 10.3 %collective-permute-done.23.refs_7_.refs_11_.refs_10_.refs_12_.refs_9_ = bf16[1536,768]{1,0:T(8,128)(2,1)} collective-permute-done((bf16[1536,768]{1,0:T(8,128)(2,1)}, bf16[1536,768]{1,0:T(8,128)(2,1)}, u32[]{:S(2)}, u32[]{:S(2)}) %collective-permute-start.23) | collective-permute-done | bytes 2359328 | tf_op jit(solution)/shard_map/ppermute | solution.py:471
  469.2 9.6 %all-to-all-start.18 = ((bf16[160,2,128]{2,1,0:T(2,128)(2,1)}), bf16[160,2,128]{2,1,0:T(2,128)(2,1)S(1)}, u32[]{:S(2)}, u32[]{:S(2)}) async-start(bf16[160,2,128]{2,1,0:T(2,128)(2,1)} %get-tuple-element.319), calls=%async_computation.18 | async-start | bytes 163840 | tf_op jit(solution)/shard_map/all_to_all | solution.py:238
  499.9 8.2 %collective-permute-done.25.refs_5_.refs_11_.refs_10_.refs_12_ = bf16[1536,768]{1,0:T(8,128)(2,1)} collective-permute-done((bf16[1536,768]{1,0:T(8,128)(2,1)}, bf16[1536,768]{1,0:T(8,128)(2,1)}, u32[]{:S(2)}, u32[]{:S(2)}) %collective-permute-start.25) | collective-permute-done | bytes 2359328 | tf_op jit(solution)/shard_map/ppermute | solution.py:471
  543.9 10.5 %all-to-all-done.21.refs_1_ = bf16[160,2,128]{2,1,0:T(2,128)(2,1)S(1)} async-done(((bf16[160,2,128]{2,1,0:T(2,128)(2,1)}), bf16[160,2,128]{2,1,0:T(2,128)(2,1)S(1)}, u32[]{:S(2)}, u32[]{:S(2)}) %all-to-all-start.21) | async-done | bytes 81952 | tf_op jit(solution)/shard_map/all_to_all | solution.py:238
  564.8 9.2 %all-to-all-done.22.refs_1_ = bf16[160,2,128]{2,1,0:T(2,128)(2,1)S(1)} async-done(((bf16[160,2,128]{2,1,0:T(2,128)(2,1)}), bf16[160,2,128]{2,1,0:T(2,128)(2,1)S(1)}, u32[]{:S(2)}, u32[]{:S(2)}) %all-to-all-start.22) | async-done | bytes 81952 | tf_op jit(solution)/shard_map/all_to_all | solution.py:238
  586.1 16.6 %collective-permute-done.29.refs_12_ = bf16[1536,768]{1,0:T(8,128)(2,1)} collective-permute-done((bf16[1536,768]{1,0:T(8,128)(2,1)}, bf16[1536,768]{1,0:T(8,128)(2,1)}, u32[]{:S(2)}, u32[]{:S(2)}) %collective-permute-start.29) | collective-permute-done | bytes 2359328 | tf_op jit(solution)/shard_map/ppermute | solution.py:471
  607.1 20.0 %all_to_all.185.refs_1_ = bf16[160,2,128]{2,1,0:T(2,128)(2,1)} all-to-all(bf16[160,2,128]{2,1,0:T(2,128)(2,1)} %get-tuple-element.354), channel_id=1, replica_groups=mesh['section'=8,'expert'=32] {'expert'}, dimensions={0} | all-to-all | bytes 163840 | tf_op jit(solution)/shard_map/all_to_all | solution.py:238
  633.1 15.0 %all_to_all.186.refs_1_ = bf16[160,2,128]{2,1,0:T(2,128)(2,1)} all-to-all(bf16[160,2,128]{2,1,0:T(2,128)(2,1)} %get-tuple-element.360), channel_id=1, replica_groups=mesh['section'=8,'expert'=32] {'expert'}, dimensions={0} | all-to-all | bytes 163840 | tf_op jit(solution)/shard_map/all_to_all | solution.py:238
  651.9 14.7 %all_to_all.187.refs_1_ = bf16[160,2,128]{2,1,0:T(2,128)(2,1)} all-to-all(bf16[160,2,128]{2,1,0:T(2,128)(2,1)} %get-tuple-element.364), channel_id=1, replica_groups=mesh['section'=8,'expert'=32] {'expert'}, dimensions={0} | all-to-all | bytes 163840 | tf_op jit(solution)/shard_map/all_to_all | solution.py:238
  672.7 15.2 %all_to_all.188.refs_1_ = bf16[160,2,128]{2,1,0:T(2,128)(2,1)} all-to-all(bf16[160,2,128]{2,1,0:T(2,128)(2,1)} %get-tuple-element.371), channel_id=1, replica_groups=mesh['section'=8,'expert'=32] {'expert'}, dimensions={0} | all-to-all | bytes 163840 | tf_op jit(solution)/shard_map/all_to_all | solution.py:238
  691.8 14.7 %all_to_all.189.refs_1_ = bf16[160,2,128]{2,1,0:T(2,128)(2,1)} all-to-all(bf16[160,2,128]{2,1,0:T(2,128)(2,1)} %get-tuple-element.375), channel_id=1, replica_groups=mesh['section'=8,'expert'=32] {'expert'}, dimensions={0} | all-to-all | bytes 163840 | tf_op jit(solution)/shard_map/all_to_all | solution.py:238
  712.6 15.0 %all_to_all.190.refs_1_ = bf16[160,2,128]{2,1,0:T(2,128)(2,1)} all-to-all(bf16[160,2,128]{2,1,0:T(2,128)(2,1)} %get-tuple-element.381), channel_id=1, replica_groups=mesh['section'=8,'expert'=32] {'expert'}, dimensions={0} | all-to-all | bytes 163840 | tf_op jit(solution)/shard_map/all_to_all | solution.py:238
  731.4 14.7 %all_to_all.191.refs_1_ = bf16[160,2,128]{2,1,0:T(2,128)(2,1)} all-to-all(bf16[160,2,128]{2,1,0:T(2,128)(2,1)} %get-tuple-element.385), channel_id=1, replica_groups=mesh['section'=8,'expert'=32] {'expert'}, dimensions={0} | all-to-all | bytes 163840 | tf_op jit(solution)/shard_map/all_to_all | solution.py:238
  752.2 15.3 %all_to_all.192.refs_1_ = bf16[160,2,128]{2,1,0:T(2,128)(2,1)} all-to-all(bf16[160,2,128]{2,1,0:T(2,128)(2,1)} %get-tuple-element.391), channel_id=1, replica_groups=mesh['section'=8,'expert'=32] {'expert'}, dimensions={0} | all-to-all | bytes 163840 | tf_op jit(solution)/shard_map/all_to_all | solution.py:238
  771.3 14.7 %all_to_all.193.refs_1_ = bf16[160,2,128]{2,1,0:T(2,128)(2,1)} all-to-all(bf16[160,2,128]{2,1,0:T(2,128)(2,1)} %get-tuple-element.395), channel_id=1, replica_groups=mesh['section'=8,'expert'=32] {'expert'}, dimensions={0} | all-to-all | bytes 163840 | tf_op jit(solution)/shard_map/all_to_all | solution.py:238
  791.0 14.7 %all_to_all.194.refs_1_ = bf16[160,2,128]{2,1,0:T(2,128)(2,1)} all-to-all(bf16[160,2,128]{2,1,0:T(2,128)(2,1)} %expert.31), channel_id=1, replica_groups=mesh['section'=8,'expert'=32] {'expert'}, dimensions={0} | all-to-all | bytes 163840 | tf_op jit(solution)/shard_map/all_to_all | solution.py:238
  (196 shorter events, 388.6 us)
Async XLA Ops:
  8.2 41.2 %collective-permute-start = (bf16[1536,768]{1,0:T(8,128)(2,1)}, bf16[1536,768]{1,0:T(8,128)(2,1)}, u32[]{:S(2)}, u32[]{:S(2)}) collective-permute-start(bf16[1536,768]{1,0:T(8,128)(2,1)} %pick.10), channel_id=1, source_target_pairs={{0,32},{32,0},{64,96},{96,64},{128,160},{160,128},{192,224},{224,1... | collective-permute-start | bytes 7077896 | tf_op jit(solution)/shard_map/ppermute | solution.py:466
  17.9 31.5 %collective-permute-start.2 = (bf16[768,768]{1,0:T(8,128)(2,1)}, bf16[768,768]{1,0:T(8,128)(2,1)}, u32[]{:S(2)}, u32[]{:S(2)}) collective-permute-start(bf16[768,768]{1,0:T(8,128)(2,1)} %pick.12), channel_id=1, source_target_pairs={{0,64},{32,224},{64,128},{96,32},{128,192},{160,96},{192,0},{224,1... | collective-permute-start | bytes 3538952 | tf_op jit(solution)/shard_map/ppermute | solution.py:471
  22.5 31.6 %collective-permute-start.3 = (bf16[768,768]{1,0:T(8,128)(2,1)}, bf16[768,768]{1,0:T(8,128)(2,1)}, u32[]{:S(2)}, u32[]{:S(2)}) collective-permute-start(bf16[768,768]{1,0:T(8,128)(2,1)} %pick.13), channel_id=1, source_target_pairs={{0,64},{32,224},{64,128},{96,32},{128,192},{160,96},{192,0},{224,1... | collective-permute-start | bytes 3538952 | tf_op jit(solution)/shard_map/ppermute | solution.py:471
  24.6 23.0 %all-to-all-start = ((s32[1,2,8,512,2]{3,4,1,0,2:T(2,128)}), s32[1,2,8,512,2]{3,4,1,0,2:T(2,128)S(1)}, u32[]{:S(2)}, u32[]{:S(2)}) async-start(s32[1,2,8,512,2]{3,4,1,0,2:T(2,128)} %bitcast.40), calls=%async_computation | async-start | bytes 131072 | tf_op jit(solution)/shard_map/all_to_all | solution.py:477
  57.1 25.3 %collective-permute-start.4 = (bf16[768,768]{1,0:T(8,128)(2,1)}, bf16[768,768]{1,0:T(8,128)(2,1)}, u32[]{:S(2)}, u32[]{:S(2)}) collective-permute-start(bf16[768,768]{1,0:T(8,128)(2,1)} %pick.14), channel_id=1, source_target_pairs={{0,64},{32,224},{64,128},{96,32},{128,192},{160,96},{192,0},{224,1... | collective-permute-start | bytes 3538952 | tf_op jit(solution)/shard_map/ppermute | solution.py:471
  82.5 29.2 %collective-permute-start.7 = (bf16[768,768]{1,0:T(8,128)(2,1)}, bf16[768,768]{1,0:T(8,128)(2,1)}, u32[]{:S(2)}, u32[]{:S(2)}) collective-permute-start(bf16[768,768]{1,0:T(8,128)(2,1)} %pick.17), channel_id=1, source_target_pairs={{0,64},{32,224},{64,128},{96,32},{128,192},{160,96},{192,0},{224,1... | collective-permute-start | bytes 3538952 | tf_op jit(solution)/shard_map/ppermute | solution.py:471
  86.3 26.6 %collective-permute-start.6 = (bf16[768,768]{1,0:T(8,128)(2,1)}, bf16[768,768]{1,0:T(8,128)(2,1)}, u32[]{:S(2)}, u32[]{:S(2)}) collective-permute-start(bf16[768,768]{1,0:T(8,128)(2,1)} %pick.16), channel_id=1, source_target_pairs={{0,64},{32,224},{64,128},{96,32},{128,192},{160,96},{192,0},{224,1... | collective-permute-start | bytes 3538952 | tf_op jit(solution)/shard_map/ppermute | solution.py:471
  119.7 30.4 %collective-permute-start.9 = (bf16[1536,768]{1,0:T(8,128)(2,1)}, bf16[1536,768]{1,0:T(8,128)(2,1)}, u32[]{:S(2)}, u32[]{:S(2)}) collective-permute-start(bf16[1536,768]{1,0:T(8,128)(2,1)} %pick.19), channel_id=1, source_target_pairs={{0,64},{32,224},{64,128},{96,32},{128,192},{160,96},{192,0},{224,1... | collective-permute-start | bytes 7077896 | tf_op jit(solution)/shard_map/ppermute | solution.py:471
  127.8 22.3 %all-to-all-start.3 = ((bf16[160,2,128]{2,1,0:T(2,128)(2,1)}), bf16[160,2,128]{2,1,0:T(2,128)(2,1)S(1)}, u32[]{:S(2)}, u32[]{:S(2)}) async-start(bf16[160,2,128]{2,1,0:T(2,128)(2,1)} %expert.16), calls=%async_computation.3 | async-start | bytes 163840 | tf_op jit(solution)/shard_map/all_to_all | solution.py:238
  157.1 21.2 %collective-permute-start.10 = (bf16[1536,768]{1,0:T(8,128)(2,1)}, bf16[1536,768]{1,0:T(8,128)(2,1)}, u32[]{:S(2)}, u32[]{:S(2)}) collective-permute-start(bf16[1536,768]{1,0:T(8,128)(2,1)} %get-tuple-element.240.refs_4_), channel_id=1, source_target_pairs={{0,32},{32,0},{64,96},{96,64},{128,160},{160,128},{192,224},{224,1... | collective-permute-start | bytes 7077896 | tf_op jit(solution)/shard_map/ppermute | solution.py:466
  157.2 33.3 %collective-permute-start.11 = (bf16[1536,768]{1,0:T(8,128)(2,1)}, bf16[1536,768]{1,0:T(8,128)(2,1)}, u32[]{:S(2)}, u32[]{:S(2)}) collective-permute-start(bf16[1536,768]{1,0:T(8,128)(2,1)} %get-tuple-element.244), channel_id=1, source_target_pairs={{0,64},{32,224},{64,128},{96,32},{128,192},{160,96},{192,0},{224,1... | collective-permute-start | bytes 7077896 | tf_op jit(solution)/shard_map/ppermute | solution.py:471
  184.6 38.1 %collective-permute-start.12 = (bf16[1536,768]{1,0:T(8,128)(2,1)}, bf16[1536,768]{1,0:T(8,128)(2,1)}, u32[]{:S(2)}, u32[]{:S(2)}) collective-permute-start(bf16[1536,768]{1,0:T(8,128)(2,1)} %get-tuple-element.252.refs_4_), channel_id=1, source_target_pairs={{0,32},{32,0},{64,96},{96,64},{128,160},{160,128},{192,224},{224,1... | collective-permute-start | bytes 7077896 | tf_op jit(solution)/shard_map/ppermute | solution.py:466
  207.1 29.2 %collective-permute-start.13 = (bf16[1536,768]{1,0:T(8,128)(2,1)}, bf16[1536,768]{1,0:T(8,128)(2,1)}, u32[]{:S(2)}, u32[]{:S(2)}) collective-permute-start(bf16[1536,768]{1,0:T(8,128)(2,1)} %get-tuple-element.255), channel_id=1, source_target_pairs={{0,64},{32,224},{64,128},{96,32},{128,192},{160,96},{192,0},{224,1... | collective-permute-start | bytes 7077896 | tf_op jit(solution)/shard_map/ppermute | solution.py:471
  249.2 30.1 %collective-permute-start.15 = (bf16[1536,768]{1,0:T(8,128)(2,1)}, bf16[1536,768]{1,0:T(8,128)(2,1)}, u32[]{:S(2)}, u32[]{:S(2)}) collective-permute-start(bf16[1536,768]{1,0:T(8,128)(2,1)} %get-tuple-element.267), channel_id=1, source_target_pairs={{0,64},{32,224},{64,128},{96,32},{128,192},{160,96},{192,0},{224,1... | collective-permute-start | bytes 7077896 | tf_op jit(solution)/shard_map/ppermute | solution.py:471
  273.1 36.0 %collective-permute-start.16 = (bf16[1536,768]{1,0:T(8,128)(2,1)}, bf16[1536,768]{1,0:T(8,128)(2,1)}, u32[]{:S(2)}, u32[]{:S(2)}) collective-permute-start(bf16[1536,768]{1,0:T(8,128)(2,1)} %get-tuple-element.275.refs_4_), channel_id=1, source_target_pairs={{0,32},{32,0},{64,96},{96,64},{128,160},{160,128},{192,224},{224,1... | collective-permute-start | bytes 7077896 | tf_op jit(solution)/shard_map/ppermute | solution.py:466
  293.7 29.2 %collective-permute-start.17 = (bf16[1536,768]{1,0:T(8,128)(2,1)}, bf16[1536,768]{1,0:T(8,128)(2,1)}, u32[]{:S(2)}, u32[]{:S(2)}) collective-permute-start(bf16[1536,768]{1,0:T(8,128)(2,1)} %get-tuple-element.278), channel_id=1, source_target_pairs={{0,64},{32,224},{64,128},{96,32},{128,192},{160,96},{192,0},{224,1... | collective-permute-start | bytes 7077896 | tf_op jit(solution)/shard_map/ppermute | solution.py:471
  339.6 29.2 %collective-permute-start.19 = (bf16[1536,768]{1,0:T(8,128)(2,1)}, bf16[1536,768]{1,0:T(8,128)(2,1)}, u32[]{:S(2)}, u32[]{:S(2)}) collective-permute-start(bf16[1536,768]{1,0:T(8,128)(2,1)} %get-tuple-element.290), channel_id=1, source_target_pairs={{0,64},{32,224},{64,128},{96,32},{128,192},{160,96},{192,0},{224,1... | collective-permute-start | bytes 7077896 | tf_op jit(solution)/shard_map/ppermute | solution.py:471
  356.7 38.2 %collective-permute-start.20 = (bf16[1536,768]{1,0:T(8,128)(2,1)}, bf16[1536,768]{1,0:T(8,128)(2,1)}, u32[]{:S(2)}, u32[]{:S(2)}) collective-permute-start(bf16[1536,768]{1,0:T(8,128)(2,1)} %get-tuple-element.298.refs_4_), channel_id=1, source_target_pairs={{0,32},{32,0},{64,96},{96,64},{128,160},{160,128},{192,224},{224,1... | collective-permute-start | bytes 7077896 | tf_op jit(solution)/shard_map/ppermute | solution.py:466
  384.8 31.1 %collective-permute-start.21 = (bf16[1536,768]{1,0:T(8,128)(2,1)}, bf16[1536,768]{1,0:T(8,128)(2,1)}, u32[]{:S(2)}, u32[]{:S(2)}) collective-permute-start(bf16[1536,768]{1,0:T(8,128)(2,1)} %get-tuple-element.302), channel_id=1, source_target_pairs={{0,64},{32,224},{64,128},{96,32},{128,192},{160,96},{224,160},{1,6... | collective-permute-start | bytes 7077896 | tf_op jit(solution)/shard_map/ppermute | solution.py:471
  401.6 40.4 %collective-permute-start.22 = (bf16[1536,768]{1,0:T(8,128)(2,1)}, bf16[1536,768]{1,0:T(8,128)(2,1)}, u32[]{:S(2)}, u32[]{:S(2)}) collective-permute-start(bf16[1536,768]{1,0:T(8,128)(2,1)} %get-tuple-element.310.refs_4_), channel_id=1, source_target_pairs={{0,32},{32,0},{64,96},{96,64},{128,160},{160,128},{192,224},{224,1... | collective-permute-start | bytes 7077896 | tf_op jit(solution)/shard_map/ppermute | solution.py:466
  431.8 31.1 %collective-permute-start.23 = (bf16[1536,768]{1,0:T(8,128)(2,1)}, bf16[1536,768]{1,0:T(8,128)(2,1)}, u32[]{:S(2)}, u32[]{:S(2)}) collective-permute-start(bf16[1536,768]{1,0:T(8,128)(2,1)} %get-tuple-element.314), channel_id=1, source_target_pairs={{0,64},{32,224},{64,128},{128,192},{160,96},{192,0},{224,160},{1,6... | collective-permute-start | bytes 7077896 | tf_op jit(solution)/shard_map/ppermute | solution.py:471
  448.6 40.3 %collective-permute-start.24 = (bf16[1536,768]{1,0:T(8,128)(2,1)}, bf16[1536,768]{1,0:T(8,128)(2,1)}, u32[]{:S(2)}, u32[]{:S(2)}) collective-permute-start(bf16[1536,768]{1,0:T(8,128)(2,1)} %get-tuple-element.322.refs_4_), channel_id=1, source_target_pairs={{0,32},{32,0},{64,96},{96,64},{128,160},{160,128},{192,224},{224,1... | collective-permute-start | bytes 7077896 | tf_op jit(solution)/shard_map/ppermute | solution.py:466
  478.8 29.3 %collective-permute-start.25 = (bf16[1536,768]{1,0:T(8,128)(2,1)}, bf16[1536,768]{1,0:T(8,128)(2,1)}, u32[]{:S(2)}, u32[]{:S(2)}) collective-permute-start(bf16[1536,768]{1,0:T(8,128)(2,1)} %get-tuple-element.326), channel_id=1, source_target_pairs={{32,224},{64,128},{96,32},{128,192},{192,0},{224,160},{33,225},{65... | collective-permute-start | bytes 7077896 | tf_op jit(solution)/shard_map/ppermute | solution.py:471
  495.5 37.7 %collective-permute-start.26 = (bf16[1536,768]{1,0:T(8,128)(2,1)}, bf16[1536,768]{1,0:T(8,128)(2,1)}, u32[]{:S(2)}, u32[]{:S(2)}) collective-permute-start(bf16[1536,768]{1,0:T(8,128)(2,1)} %get-tuple-element.334.refs_4_), channel_id=1, source_target_pairs={{0,32},{32,0},{64,96},{96,64},{128,160},{160,128},{192,224},{224,1... | collective-permute-start | bytes 7077896 | tf_op jit(solution)/shard_map/ppermute | solution.py:466
  539.9 34.1 %collective-permute-start.28 = (bf16[1536,768]{1,0:T(8,128)(2,1)}, bf16[1536,768]{1,0:T(8,128)(2,1)}, u32[]{:S(2)}, u32[]{:S(2)}) collective-permute-start(bf16[1536,768]{1,0:T(8,128)(2,1)} %get-tuple-element.346.refs_4_), channel_id=1, source_target_pairs={{0,32},{32,0},{64,96},{96,64},{128,160},{160,128},{192,224},{224,1... | collective-permute-start | bytes 7077896 | tf_op jit(solution)/shard_map/ppermute | solution.py:466
  563.5 39.2 %collective-permute-start.29 = (bf16[1536,768]{1,0:T(8,128)(2,1)}, bf16[1536,768]{1,0:T(8,128)(2,1)}, u32[]{:S(2)}, u32[]{:S(2)}) collective-permute-start(bf16[1536,768]{1,0:T(8,128)(2,1)} %get-tuple-element.350), channel_id=1, source_target_pairs={{0,64},{96,32},{1,65},{97,33},{2,66},{98,34},{3,67},{99,35},{4,68}... | collective-permute-start | bytes 7077896 | tf_op jit(solution)/shard_map/ppermute | solution.py:471
  580.5 46.5 %collective-permute-start.30 = (bf16[1536,768]{1,0:T(8,128)(2,1)}, bf16[1536,768]{1,0:T(8,128)(2,1)}, u32[]{:S(2)}, u32[]{:S(2)}) collective-permute-start(bf16[1536,768]{1,0:T(8,128)(2,1)} %get-tuple-element.357.refs_4_), channel_id=1, source_target_pairs={{0,32},{32,0},{64,96},{96,64},{128,160},{160,128},{192,224},{224,1... | collective-permute-start | bytes 7077896 | tf_op jit(solution)/shard_map/ppermute | solution.py:466
  580.7 21.9 %all-to-all-start.23 = ((bf16[160,2,128]{2,1,0:T(2,128)(2,1)}), bf16[160,2,128]{2,1,0:T(2,128)(2,1)S(1)}, u32[]{:S(2)}, u32[]{:S(2)}) async-start(bf16[160,2,128]{2,1,0:T(2,128)(2,1)} %get-tuple-element.349), calls=%async_computation.23 | async-start | bytes 163840 | tf_op jit(solution)/shard_map/all_to_all | solution.py:238
  633.0 33.6 %collective-permute-start.31 = (bf16[1536,768]{1,0:T(8,128)(2,1)}, bf16[1536,768]{1,0:T(8,128)(2,1)}, u32[]{:S(2)}, u32[]{:S(2)}) collective-permute-start(bf16[1536,768]{1,0:T(8,128)(2,1)} %get-tuple-element.367.refs_4_), channel_id=1, source_target_pairs={{0,32},{32,0},{64,96},{96,64},{128,160},{160,128},{192,224},{224,1... | collective-permute-start | bytes 7077896 | tf_op jit(solution)/shard_map/ppermute | solution.py:466
  672.6 33.8 %collective-permute-start.32 = (bf16[1536,768]{1,0:T(8,128)(2,1)}, bf16[1536,768]{1,0:T(8,128)(2,1)}, u32[]{:S(2)}, u32[]{:S(2)}) collective-permute-start(bf16[1536,768]{1,0:T(8,128)(2,1)} %get-tuple-element.378.refs_4_), channel_id=1, source_target_pairs={{0,32},{32,0},{64,96},{96,64},{128,160},{160,128},{192,224},{224,1... | collective-permute-start | bytes 7077896 | tf_op jit(solution)/shard_map/ppermute | solution.py:466
  712.5 33.6 %collective-permute-start.33 = (bf16[1536,768]{1,0:T(8,128)(2,1)}, bf16[1536,768]{1,0:T(8,128)(2,1)}, u32[]{:S(2)}, u32[]{:S(2)}) collective-permute-start(bf16[1536,768]{1,0:T(8,128)(2,1)} %get-tuple-element.388.refs_4_), channel_id=1, source_target_pairs={{0,32},{32,0},{64,96},{96,64},{128,160},{160,128},{192,224},{224,1... | collective-permute-start | bytes 7077896 | tf_op jit(solution)/shard_map/ppermute | solution.py:466
  752.1 33.9 %collective-permute-start.34 = (bf16[1536,768]{1,0:T(8,128)(2,1)}, bf16[1536,768]{1,0:T(8,128)(2,1)}, u32[]{:S(2)}, u32[]{:S(2)}) collective-permute-start(bf16[1536,768]{1,0:T(8,128)(2,1)} %get-tuple-element.398.refs_4_), channel_id=1, source_target_pairs={{0,32},{32,0},{64,96},{96,64},{128,160},{160,128},{192,224},{224,1... | collective-permute-start | bytes 7077896 | tf_op jit(solution)/shard_map/ppermute | solution.py:466
  (42 other events, 359.8 us)

commit v7 on v6

--- a/solution.py
+++ b/solution.py
@@ -17,6 +17,7 @@
 
 PACK = 64
 SLOTS = 48
+FAST = 8
 ROWS = 10
 PARTS = 2
 LEAD = 6
@@ -234,8 +235,24 @@
     ref[TILES * number : TILES * (number + 1)] = rows[0:TILES]
 
 
+def place_of(expert, experts):
+    return expert % FAST * (experts // FAST) + expert // FAST
+
+
 def send_blocks(value):
-    return lax.all_to_all(value, "expert", split_axis=0, concat_axis=0, tiled=True)
+    experts = lax.axis_size("expert")
+    slow = experts // FAST
+    along_z = [[x * FAST + z for z in range(FAST)] for x in range(slow)]
+    along_x = [[x * FAST + z for x in range(slow)] for z in range(FAST)]
+
+    def exchange(some, groups):
+        return lax.all_to_all(
+            some, "expert", split_axis=0, concat_axis=0, axis_index_groups=groups, tiled=True
+        )
+
+    half = exchange(value, along_z).reshape(FAST, slow, TILES, 2, LANES)
+    half = jnp.transpose(half, (1, 0, 2, 3, 4)).reshape(value.shape)
+    return exchange(half, along_x)
 
 
 def turn_kernel(merge, send, side, *refs):
@@ -270,7 +287,8 @@
         offset = lax.broadcasted_iota(jnp.int32, (tokens, 4 * PACK), 1)
         col = next_ref[...].astype(jnp.float32).T.astype(jnp.int32)
         first, second = col[:, 0:1] - offset, col[:, 1:2] - offset
-        for turn in range(out_ref.shape[0] // TILES // 4):
+        experts = out_ref.shape[0] // TILES
+        for turn in range(experts // 4):
             base = turn * 4 * PACK
             onehot = jnp.where((first == base) | (second == base), 1.0, 0.0)
             found = jnp.dot(held, onehot.astype(jnp.bfloat16), preferred_element_type=jnp.float32)
@@ -278,8 +296,9 @@
                 tile = found[:, LANES * half : LANES * (half + 1)]
                 groups = tile[0:8], tile[8:16], tile[16:24]
                 number = turn * 4 + half * 2
-                store_block(out_ref, number, pack(*groups, 0))
-                store_block(out_ref, number + 1, pack(*groups, PACK))
+                places = [place_of(e, experts) for e in (number, number + 1)]
+                store_block(out_ref, places[0], pack(*groups, 0))
+                store_block(out_ref, places[1], pack(*groups, PACK))
     side.finish()
 
 
@@ -346,7 +365,7 @@
     gates = jnp.broadcast_to(gates[None], (groups, 8, LANES))
     packed = pack(tall[:, 0], tall[:, 1], tall[:, 2], 0, gates)
     for number in range(groups):
-        store_block(out_ref, number, packed[number])
+        store_block(out_ref, place_of(number, groups), packed[number])
     side.finish()
 
 
@@ -475,17 +494,19 @@
         return max(stock[i][0] for lane in held for stock in lane for i in parts)
 
     mine = lax.all_to_all(routes[:, 0], "section", split_axis=1, concat_axis=0, tiled=False)
-    mine = jnp.transpose(mine, (1, 0, 2, 3)).reshape(layers, -1, 2)
-    rows = place_tokens(mine, experts)
     small = jnp.stack([norm_gains[:, 0], routers[:, 0, 0]])
     small = jnp.broadcast_to(small[None], (sections,) + small.shape)
     small = lax.all_to_all(small, "section", split_axis=0, concat_axis=0, tiled=True)
+    h = jnp.transpose(inputs[0], (1, 0))
+
+    mine_first = swapped(picked(swap_rows[0], tab))
+    mine_first, tab, mine, small = join(mine_first, tab, mine, small)
+    buffers[("swapped", 0)] = (mine_first, ())
+    later = swapped(picked(swap_rows[1], tab))
+    mine = jnp.transpose(mine, (1, 0, 2, 3)).reshape(layers, -1, 2)
+    rows = place_tokens(mine, experts)
     small = jnp.transpose(small, (1, 2, 0, 3)).reshape(2, layers, 1, width).astype(jnp.float32)
     gains, gate_rows = small[0], small[1]
-    h = jnp.transpose(inputs[0], (1, 0))
-
-    buffers[("swapped", 0)] = (swapped(picked(swap_rows[0], tab)), ())
-    later = swapped(picked(swap_rows[1], tab))
     flying = None
     for number in range(1, LEAD + 1):
         started = ring(number, picked(ring_rows[number - 1], tab))

time: 822 us -> 983 us (1.20)
  blocking collectives: 238 us -> 539 us
  waiting for transfers between devices: 210 us -> 122 us
  starting transfers between devices: 137 us -> 83.9 us
    all_to_all x15 -> x51, blocking collectives: 238 us -> 539 us  [exchange(): lax.all_to_all(some, 'expert', split_axis=0, concat_axis=0, axis_index_gr...]
    ppermute x17, waiting for transfers between devices: 99.6 us -> 44 us  [ring(): return lax.ppermute(value, 'section', pairs)]
    all_to_all x17 -> x13, starting transfers between devices: 92.4 us -> 44.6 us  [exchange(): lax.all_to_all(some, 'expert', split_axis=0, concat_axis=0, axis_index_gr...]
    all_to_all x17 -> x13, waiting for transfers between devices: 92.8 us -> 70.1 us  [exchange(): lax.all_to_all(some, 'expert', split_axis=0, concat_axis=0, axis_index_gr...]
    all_to_all x1, waiting for transfers between devices: 17.5 us -> 4.15 us  [local(): lax.all_to_all(routes[:, 0], 'section', split_axis=1, concat_axis=0, tile...]
  transfers between devices with their start and end apart: 54 -> 50, of which waited for: 28 -> 20; matrix products, arithmetic and copies ran while one was open for 1% -> 1% of each run, Pallas kernels for 18% -> 15%
where the time goes in v7:
time: 983 us; the launch traced here: 968 us
  blocking collectives  539 us (55%)
  Pallas kernels  204 us (21%)
  waiting for transfers between devices  122 us (12%)
  starting transfers between devices  83.9 us (9%)
  local copies, waits for them, and re-layouts  14.8 us (2%)
    all_to_all x51, blocking collectives, exchange(): lax.all_to_all(some, 'expert', split_axis=0, concat_axis=0, axis_index_gr...  539 us
    pallas_call x43, Pallas kernels, call_with_side(): pl.pallas_call(body, out_shape=tuple(shapes) + tuple(beside.out_shapes),...  204 us
    all_to_all x13, waiting for transfers between devices, exchange(): lax.all_to_all(some, 'expert', split_axis=0, concat_axis=0, axis_index_gr...  70.1 us
    all_to_all x13, starting transfers between devices, exchange(): lax.all_to_all(some, 'expert', split_axis=0, concat_axis=0, axis_index_gr...  44.6 us
    ppermute x17, waiting for transfers between devices, ring(): return lax.ppermute(value, 'section', pairs)  44 us
    ppermute x17, starting transfers between devices, ring(): return lax.ppermute(value, 'section', pairs)  27.3 us
  transfers between devices with their start and end apart: 50, of which 20 were waited for; matrix products, arithmetic and copies ran while one was open for 1% of the time, Pallas kernels for 15%

profile of v7, /device:TPU:8, one launch (start us, length us, event | category | flops | bytes accessed | tf_op | source)
XLA Modules:
  0.0 967.6 jit_solution(9287934795296521821)
XLA Ops:
  39.5 11.2 %collective-permute-done.2.refs_2_.refs_1_.refs_7_.refs_8_ = bf16[768,768]{1,0:T(8,128)(2,1)} collective-permute-done((bf16[768,768]{1,0:T(8,128)(2,1)}, bf16[768,768]{1,0:T(8,128)(2,1)}, u32[]{:S(2)}, u32[]{:S(2)}) %collective-permute-start.2) | collective-permute-done | bytes 1179680 | tf_op jit(solution)/shard_map/ppermute | solution.py:490
  54.2 9.1 collective-permute-done.3.refs_2_.refs_1_.refs_3_.refs_8_.refs_9_
  66.8 9.1 collective-permute-done.5.refs_2_.refs_4_.refs_3_.refs_9_.refs_10_.refs_8_.refs_7_
  79.4 9.1 collective-permute-done.4.refs_2_.refs_5_.refs_4_.refs_10_.refs_11_.refs_9_.refs_8_
  94.9 16.7 %all_to_all.340 = bf16[160,2,128]{2,1,0:T(2,128)(2,1)S(1)} all-to-all(bf16[160,2,128]{2,1,0:T(2,128)(2,1)} %get-tuple-element.226), channel_id=1, replica_groups={{0,1,2,3,4,5,6,7},{8,9,10,11,12,13,14,15},{16,17,18,19,20,21,22,23},{24..., dimensions={0} | all-to-all | bytes 163840 | tf_op jit(solution)/shard_map/all_to_all | solution.py:249
  111.7 9.9 %all_to_all.341.refs_1_ = bf16[160,2,128]{2,1,0:T(2,128)(2,1)} all-to-all(bf16[160,2,128]{2,1,0:T(2,128)(2,1)S(1)} %bitcast.207), channel_id=1, replica_groups={{0,8,16,24},{1,9,17,25},{2,10,18,26},{3,11,19,27},{4,12,20,28},{5,13,21..., dimensions={0} | all-to-all | bytes 163840 | tf_op jit(solution)/shard_map/all_to_all | solution.py:249
  135.6 12.6 %all_to_all.342 = bf16[160,2,128]{2,1,0:T(2,128)(2,1)S(1)} all-to-all(bf16[160,2,128]{2,1,0:T(2,128)(2,1)} %expert.16), channel_id=1, replica_groups={{0,1,2,3,4,5,6,7},{8,9,10,11,12,13,14,15},{16,17,18,19,20,21,22,23},{24..., dimensions={0} | all-to-all | bytes 163840 | tf_op jit(solution)/shard_map/all_to_all | solution.py:249
  167.6 12.6 %all_to_all.343 = bf16[160,2,128]{2,1,0:T(2,128)(2,1)S(1)} all-to-all(bf16[160,2,128]{2,1,0:T(2,128)(2,1)} %get-tuple-element.245), channel_id=1, replica_groups={{0,1,2,3,4,5,6,7},{8,9,10,11,12,13,14,15},{16,17,18,19,20,21,22,23},{24..., dimensions={0} | all-to-all | bytes 163840 | tf_op jit(solution)/shard_map/all_to_all | solution.py:249
  195.5 12.2 %all_to_all.345 = bf16[160,2,128]{2,1,0:T(2,128)(2,1)S(1)} all-to-all(bf16[160,2,128]{2,1,0:T(2,128)(2,1)} %get-tuple-element.251), channel_id=1, replica_groups={{0,1,2,3,4,5,6,7},{8,9,10,11,12,13,14,15},{16,17,18,19,20,21,22,23},{24..., dimensions={0} | all-to-all | bytes 163840 | tf_op jit(solution)/shard_map/all_to_all | solution.py:249
  225.5 11.8 %all_to_all.346 = bf16[160,2,128]{2,1,0:T(2,128)(2,1)S(1)} all-to-all(bf16[160,2,128]{2,1,0:T(2,128)(2,1)} %get-tuple-element.257), channel_id=1, replica_groups={{0,1,2,3,4,5,6,7},{8,9,10,11,12,13,14,15},{16,17,18,19,20,21,22,23},{24..., dimensions={0} | all-to-all | bytes 163840 | tf_op jit(solution)/shard_map/all_to_all | solution.py:249
  251.1 11.8 %all_to_all.348 = bf16[160,2,128]{2,1,0:T(2,128)(2,1)S(1)} all-to-all(bf16[160,2,128]{2,1,0:T(2,128)(2,1)} %expert.18), channel_id=1, replica_groups={{0,1,2,3,4,5,6,7},{8,9,10,11,12,13,14,15},{16,17,18,19,20,21,22,23},{24..., dimensions={0} | all-to-all | bytes 163840 | tf_op jit(solution)/shard_map/all_to_all | solution.py:249
  280.8 11.8 %all_to_all.349 = bf16[160,2,128]{2,1,0:T(2,128)(2,1)S(1)} all-to-all(bf16[160,2,128]{2,1,0:T(2,128)(2,1)} %get-tuple-element.268), channel_id=1, replica_groups={{0,1,2,3,4,5,6,7},{8,9,10,11,12,13,14,15},{16,17,18,19,20,21,22,23},{24..., dimensions={0} | all-to-all | bytes 163840 | tf_op jit(solution)/shard_map/all_to_all | solution.py:249
  307.5 12.2 %all_to_all.351 = bf16[160,2,128]{2,1,0:T(2,128)(2,1)S(1)} all-to-all(bf16[160,2,128]{2,1,0:T(2,128)(2,1)} %get-tuple-element.274), channel_id=1, replica_groups={{0,1,2,3,4,5,6,7},{8,9,10,11,12,13,14,15},{16,17,18,19,20,21,22,23},{24..., dimensions={0} | all-to-all | bytes 163840 | tf_op jit(solution)/shard_map/all_to_all | solution.py:249
  336.8 11.8 %all_to_all.352 = bf16[160,2,128]{2,1,0:T(2,128)(2,1)S(1)} all-to-all(bf16[160,2,128]{2,1,0:T(2,128)(2,1)} %get-tuple-element.280), channel_id=1, replica_groups={{0,1,2,3,4,5,6,7},{8,9,10,11,12,13,14,15},{16,17,18,19,20,21,22,23},{24..., dimensions={0} | all-to-all | bytes 163840 | tf_op jit(solution)/shard_map/all_to_all | solution.py:249
  362.5 11.8 %all_to_all.354 = bf16[160,2,128]{2,1,0:T(2,128)(2,1)S(1)} all-to-all(bf16[160,2,128]{2,1,0:T(2,128)(2,1)} %expert.20), channel_id=1, replica_groups={{0,1,2,3,4,5,6,7},{8,9,10,11,12,13,14,15},{16,17,18,19,20,21,22,23},{24..., dimensions={0} | all-to-all | bytes 163840 | tf_op jit(solution)/shard_map/all_to_all | solution.py:249
  418.9 12.2 %all_to_all.356 = bf16[160,2,128]{2,1,0:T(2,128)(2,1)S(1)} all-to-all(bf16[160,2,128]{2,1,0:T(2,128)(2,1)} %get-tuple-element.297), channel_id=1, replica_groups={{0,1,2,3,4,5,6,7},{8,9,10,11,12,13,14,15},{16,17,18,19,20,21,22,23},{24..., dimensions={0} | all-to-all | bytes 163840 | tf_op jit(solution)/shard_map/all_to_all | solution.py:249
  473.7 12.2 %all_to_all.358 = bf16[160,2,128]{2,1,0:T(2,128)(2,1)S(1)} all-to-all(bf16[160,2,128]{2,1,0:T(2,128)(2,1)} %get-tuple-element.309), channel_id=1, replica_groups={{0,1,2,3,4,5,6,7},{8,9,10,11,12,13,14,15},{16,17,18,19,20,21,22,23},{24..., dimensions={0} | all-to-all | bytes 163840 | tf_op jit(solution)/shard_map/all_to_all | solution.py:249
  528.7 12.2 %all_to_all.360 = bf16[160,2,128]{2,1,0:T(2,128)(2,1)S(1)} all-to-all(bf16[160,2,128]{2,1,0:T(2,128)(2,1)} %get-tuple-element.321), channel_id=1, replica_groups={{0,1,2,3,4,5,6,7},{8,9,10,11,12,13,14,15},{16,17,18,19,20,21,22,23},{24..., dimensions={0} | all-to-all | bytes 163840 | tf_op jit(solution)/shard_map/all_to_all | solution.py:249
  582.0 12.2 %all_to_all.363 = bf16[160,2,128]{2,1,0:T(2,128)(2,1)S(1)} all-to-all(bf16[160,2,128]{2,1,0:T(2,128)(2,1)} %get-tuple-element.333), channel_id=1, replica_groups={{0,1,2,3,4,5,6,7},{8,9,10,11,12,13,14,15},{16,17,18,19,20,21,22,23},{24..., dimensions={0} | all-to-all | bytes 163840 | tf_op jit(solution)/shard_map/all_to_all | solution.py:249
  620.0 8.8 all_to_all.365.refs_1_
  634.8 12.2 %all_to_all.366 = bf16[160,2,128]{2,1,0:T(2,128)(2,1)S(1)} all-to-all(bf16[160,2,128]{2,1,0:T(2,128)(2,1)} %get-tuple-element.345), channel_id=1, replica_groups={{0,1,2,3,4,5,6,7},{8,9,10,11,12,13,14,15},{16,17,18,19,20,21,22,23},{24..., dimensions={0} | all-to-all | bytes 163840 | tf_op jit(solution)/shard_map/all_to_all | solution.py:249
  687.1 12.2 %all_to_all.369 = bf16[160,2,128]{2,1,0:T(2,128)(2,1)S(1)} all-to-all(bf16[160,2,128]{2,1,0:T(2,128)(2,1)} %get-tuple-element.357), channel_id=1, replica_groups={{0,1,2,3,4,5,6,7},{8,9,10,11,12,13,14,15},{16,17,18,19,20,21,22,23},{24..., dimensions={0} | all-to-all | bytes 163840 | tf_op jit(solution)/shard_map/all_to_all | solution.py:249
  712.0 11.8 %all_to_all.371 = bf16[160,2,128]{2,1,0:T(2,128)(2,1)S(1)} all-to-all(bf16[160,2,128]{2,1,0:T(2,128)(2,1)} %get-tuple-element.362), channel_id=1, replica_groups={{0,1,2,3,4,5,6,7},{8,9,10,11,12,13,14,15},{16,17,18,19,20,21,22,23},{24..., dimensions={0} | all-to-all | bytes 163840 | tf_op jit(solution)/shard_map/all_to_all | solution.py:249
  738.8 12.2 %all_to_all.373 = bf16[160,2,128]{2,1,0:T(2,128)(2,1)S(1)} all-to-all(bf16[160,2,128]{2,1,0:T(2,128)(2,1)} %get-tuple-element.368), channel_id=1, replica_groups={{0,1,2,3,4,5,6,7},{8,9,10,11,12,13,14,15},{16,17,18,19,20,21,22,23},{24..., dimensions={0} | all-to-all | bytes 163840 | tf_op jit(solution)/shard_map/all_to_all | solution.py:249
  763.6 11.8 %all_to_all.375 = bf16[160,2,128]{2,1,0:T(2,128)(2,1)S(1)} all-to-all(bf16[160,2,128]{2,1,0:T(2,128)(2,1)} %get-tuple-element.372), channel_id=1, replica_groups={{0,1,2,3,4,5,6,7},{8,9,10,11,12,13,14,15},{16,17,18,19,20,21,22,23},{24..., dimensions={0} | all-to-all | bytes 163840 | tf_op jit(solution)/shard_map/all_to_all | solution.py:249
  790.4 12.2 %all_to_all.377 = bf16[160,2,128]{2,1,0:T(2,128)(2,1)S(1)} all-to-all(bf16[160,2,128]{2,1,0:T(2,128)(2,1)} %get-tuple-element.379), channel_id=1, replica_groups={{0,1,2,3,4,5,6,7},{8,9,10,11,12,13,14,15},{16,17,18,19,20,21,22,23},{24..., dimensions={0} | all-to-all | bytes 163840 | tf_op jit(solution)/shard_map/all_to_all | solution.py:249
  815.2 11.8 %all_to_all.379 = bf16[160,2,128]{2,1,0:T(2,128)(2,1)S(1)} all-to-all(bf16[160,2,128]{2,1,0:T(2,128)(2,1)} %get-tuple-element.383), channel_id=1, replica_groups={{0,1,2,3,4,5,6,7},{8,9,10,11,12,13,14,15},{16,17,18,19,20,21,22,23},{24..., dimensions={0} | all-to-all | bytes 163840 | tf_op jit(solution)/shard_map/all_to_all | solution.py:249
  842.0 12.2 %all_to_all.381 = bf16[160,2,128]{2,1,0:T(2,128)(2,1)S(1)} all-to-all(bf16[160,2,128]{2,1,0:T(2,128)(2,1)} %get-tuple-element.389), channel_id=1, replica_groups={{0,1,2,3,4,5,6,7},{8,9,10,11,12,13,14,15},{16,17,18,19,20,21,22,23},{24..., dimensions={0} | all-to-all | bytes 163840 | tf_op jit(solution)/shard_map/all_to_all | solution.py:249
  866.8 12.0 %all_to_all.383 = bf16[160,2,128]{2,1,0:T(2,128)(2,1)S(1)} all-to-all(bf16[160,2,128]{2,1,0:T(2,128)(2,1)} %get-tuple-element.393), channel_id=1, replica_groups={{0,1,2,3,4,5,6,7},{8,9,10,11,12,13,14,15},{16,17,18,19,20,21,22,23},{24..., dimensions={0} | all-to-all | bytes 163840 | tf_op jit(solution)/shard_map/all_to_all | solution.py:249
  893.7 12.2 %all_to_all.385 = bf16[160,2,128]{2,1,0:T(2,128)(2,1)S(1)} all-to-all(bf16[160,2,128]{2,1,0:T(2,128)(2,1)} %get-tuple-element.399), channel_id=1, replica_groups={{0,1,2,3,4,5,6,7},{8,9,10,11,12,13,14,15},{16,17,18,19,20,21,22,23},{24..., dimensions={0} | all-to-all | bytes 163840 | tf_op jit(solution)/shard_map/all_to_all | solution.py:249
  918.5 11.8 %all_to_all.387 = bf16[160,2,128]{2,1,0:T(2,128)(2,1)S(1)} all-to-all(bf16[160,2,128]{2,1,0:T(2,128)(2,1)} %get-tuple-element.403), channel_id=1, replica_groups={{0,1,2,3,4,5,6,7},{8,9,10,11,12,13,14,15},{16,17,18,19,20,21,22,23},{24..., dimensions={0} | all-to-all | bytes 163840 | tf_op jit(solution)/shard_map/all_to_all | solution.py:249
  944.1 11.8 %all_to_all.389 = bf16[160,2,128]{2,1,0:T(2,128)(2,1)S(1)} all-to-all(bf16[160,2,128]{2,1,0:T(2,128)(2,1)} %expert.31), channel_id=1, replica_groups={{0,1,2,3,4,5,6,7},{8,9,10,11,12,13,14,15},{16,17,18,19,20,21,22,23},{24..., dimensions={0} | all-to-all | bytes 163840 | tf_op jit(solution)/shard_map/all_to_all | solution.py:249
  (236 shorter events, 590.6 us)
Async XLA Ops:
  28.0 22.7 %collective-permute-start.1 = (bf16[1536,768]{1,0:T(8,128)(2,1)}, bf16[1536,768]{1,0:T(8,128)(2,1)}, u32[]{:S(2)}, u32[]{:S(2)}) collective-permute-start(bf16[1536,768]{1,0:T(8,128)(2,1)} %pick.11), channel_id=1, source_target_pairs={{0,32},{32,0},{64,96},{96,64},{128,160},{160,128},{192,224},{224,1... | collective-permute-start | bytes 7077896 | tf_op jit(solution)/shard_map/ppermute | solution.py:485
  34.6 28.7 %collective-permute-start.3 = (bf16[768,768]{1,0:T(8,128)(2,1)}, bf16[768,768]{1,0:T(8,128)(2,1)}, u32[]{:S(2)}, u32[]{:S(2)}) collective-permute-start(bf16[768,768]{1,0:T(8,128)(2,1)} %pick.13), channel_id=1, source_target_pairs={{0,64},{32,224},{64,128},{96,32},{128,192},{160,96},{192,0},{224,1... | collective-permute-start | bytes 3538952 | tf_op jit(solution)/shard_map/ppermute | solution.py:490
  53.7 22.3 %collective-permute-start.5 = (bf16[768,768]{1,0:T(8,128)(2,1)}, bf16[768,768]{1,0:T(8,128)(2,1)}, u32[]{:S(2)}, u32[]{:S(2)}) collective-permute-start(bf16[768,768]{1,0:T(8,128)(2,1)} %pick.15), channel_id=1, source_target_pairs={{0,64},{32,224},{64,128},{96,32},{128,192},{160,96},{192,0},{224,1... | collective-permute-start | bytes 3538952 | tf_op jit(solution)/shard_map/ppermute | solution.py:490
  66.3 22.3 %collective-permute-start.4 = (bf16[768,768]{1,0:T(8,128)(2,1)}, bf16[768,768]{1,0:T(8,128)(2,1)}, u32[]{:S(2)}, u32[]{:S(2)}) collective-permute-start(bf16[768,768]{1,0:T(8,128)(2,1)} %pick.14), channel_id=1, source_target_pairs={{0,64},{32,224},{64,128},{96,32},{128,192},{160,96},{192,0},{224,1... | collective-permute-start | bytes 3538952 | tf_op jit(solution)/shard_map/ppermute | solution.py:490
  78.9 42.6 %collective-permute-start.7 = (bf16[768,768]{1,0:T(8,128)(2,1)}, bf16[768,768]{1,0:T(8,128)(2,1)}, u32[]{:S(2)}, u32[]{:S(2)}) collective-permute-start(bf16[768,768]{1,0:T(8,128)(2,1)} %pick.17), channel_id=1, source_target_pairs={{0,64},{32,224},{64,128},{96,32},{128,192},{160,96},{192,0},{224,1... | collective-permute-start | bytes 3538952 | tf_op jit(solution)/shard_map/ppermute | solution.py:490
  91.6 30.0 %collective-permute-start.6 = (bf16[768,768]{1,0:T(8,128)(2,1)}, bf16[768,768]{1,0:T(8,128)(2,1)}, u32[]{:S(2)}, u32[]{:S(2)}) collective-permute-start(bf16[768,768]{1,0:T(8,128)(2,1)} %pick.16), channel_id=1, source_target_pairs={{0,64},{32,224},{64,128},{96,32},{128,192},{160,96},{192,0},{224,1... | collective-permute-start | bytes 3538952 | tf_op jit(solution)/shard_map/ppermute | solution.py:490
  128.4 29.4 %collective-permute-start.9 = (bf16[1536,768]{1,0:T(8,128)(2,1)}, bf16[1536,768]{1,0:T(8,128)(2,1)}, u32[]{:S(2)}, u32[]{:S(2)}) collective-permute-start(bf16[1536,768]{1,0:T(8,128)(2,1)} %pick.19), channel_id=1, source_target_pairs={{0,64},{32,224},{64,128},{96,32},{128,192},{160,96},{192,0},{224,1... | collective-permute-start | bytes 7077896 | tf_op jit(solution)/shard_map/ppermute | solution.py:490
  164.9 24.1 %collective-permute-start.10 = (bf16[1536,768]{1,0:T(8,128)(2,1)}, bf16[1536,768]{1,0:T(8,128)(2,1)}, u32[]{:S(2)}, u32[]{:S(2)}) collective-permute-start(bf16[1536,768]{1,0:T(8,128)(2,1)} %get-tuple-element.248.refs_4_), channel_id=1, source_target_pairs={{0,32},{32,0},{64,96},{96,64},{128,160},{160,128},{192,224},{224,1... | collective-permute-start | bytes 7077896 | tf_op jit(solution)/shard_map/ppermute | solution.py:485
  165.1 46.6 %collective-permute-start.11 = (bf16[1536,768]{1,0:T(8,128)(2,1)}, bf16[1536,768]{1,0:T(8,128)(2,1)}, u32[]{:S(2)}, u32[]{:S(2)}) collective-permute-start(bf16[1536,768]{1,0:T(8,128)(2,1)} %get-tuple-element.252), channel_id=1, source_target_pairs={{0,64},{32,224},{64,128},{96,32},{128,192},{160,96},{192,0},{224,1... | collective-permute-start | bytes 7077896 | tf_op jit(solution)/shard_map/ppermute | solution.py:490
  195.4 50.7 %collective-permute-start.12 = (bf16[1536,768]{1,0:T(8,128)(2,1)}, bf16[1536,768]{1,0:T(8,128)(2,1)}, u32[]{:S(2)}, u32[]{:S(2)}) collective-permute-start(bf16[1536,768]{1,0:T(8,128)(2,1)} %get-tuple-element.260.refs_4_), channel_id=1, source_target_pairs={{0,32},{32,0},{64,96},{96,64},{128,160},{160,128},{192,224},{224,1... | collective-permute-start | bytes 7077896 | tf_op jit(solution)/shard_map/ppermute | solution.py:485
  223.9 43.2 %collective-permute-start.13 = (bf16[1536,768]{1,0:T(8,128)(2,1)}, bf16[1536,768]{1,0:T(8,128)(2,1)}, u32[]{:S(2)}, u32[]{:S(2)}) collective-permute-start(bf16[1536,768]{1,0:T(8,128)(2,1)} %get-tuple-element.263), channel_id=1, source_target_pairs={{0,64},{32,224},{64,128},{96,32},{128,192},{160,96},{192,0},{224,1... | collective-permute-start | bytes 7077896 | tf_op jit(solution)/shard_map/ppermute | solution.py:490
  279.9 21.6 %collective-permute-start.14 = (bf16[1536,768]{1,0:T(8,128)(2,1)}, bf16[1536,768]{1,0:T(8,128)(2,1)}, u32[]{:S(2)}, u32[]{:S(2)}) collective-permute-start(bf16[1536,768]{1,0:T(8,128)(2,1)} %get-tuple-element.271.refs_4_), channel_id=1, source_target_pairs={{0,32},{32,0},{64,96},{96,64},{128,160},{160,128},{192,224},{224,1... | collective-permute-start | bytes 7077896 | tf_op jit(solution)/shard_map/ppermute | solution.py:485
  280.0 43.7 %collective-permute-start.15 = (bf16[1536,768]{1,0:T(8,128)(2,1)}, bf16[1536,768]{1,0:T(8,128)(2,1)}, u32[]{:S(2)}, u32[]{:S(2)}) collective-permute-start(bf16[1536,768]{1,0:T(8,128)(2,1)} %get-tuple-element.275), channel_id=1, source_target_pairs={{0,64},{32,224},{64,128},{96,32},{128,192},{160,96},{192,0},{224,1... | collective-permute-start | bytes 7077896 | tf_op jit(solution)/shard_map/ppermute | solution.py:490
  307.4 50.1 %collective-permute-start.16 = (bf16[1536,768]{1,0:T(8,128)(2,1)}, bf16[1536,768]{1,0:T(8,128)(2,1)}, u32[]{:S(2)}, u32[]{:S(2)}) collective-permute-start(bf16[1536,768]{1,0:T(8,128)(2,1)} %get-tuple-element.283.refs_4_), channel_id=1, source_target_pairs={{0,32},{32,0},{64,96},{96,64},{128,160},{160,128},{192,224},{224,1... | collective-permute-start | bytes 7077896 | tf_op jit(solution)/shard_map/ppermute | solution.py:485
  335.5 43.2 %collective-permute-start.17 = (bf16[1536,768]{1,0:T(8,128)(2,1)}, bf16[1536,768]{1,0:T(8,128)(2,1)}, u32[]{:S(2)}, u32[]{:S(2)}) collective-permute-start(bf16[1536,768]{1,0:T(8,128)(2,1)} %get-tuple-element.286), channel_id=1, source_target_pairs={{0,64},{32,224},{64,128},{96,32},{128,192},{160,96},{192,0},{224,1... | collective-permute-start | bytes 7077896 | tf_op jit(solution)/shard_map/ppermute | solution.py:490
  391.7 21.2 %collective-permute-start.18 = (bf16[1536,768]{1,0:T(8,128)(2,1)}, bf16[1536,768]{1,0:T(8,128)(2,1)}, u32[]{:S(2)}, u32[]{:S(2)}) collective-permute-start(bf16[1536,768]{1,0:T(8,128)(2,1)} %get-tuple-element.294.refs_4_), channel_id=1, source_target_pairs={{0,32},{32,0},{64,96},{96,64},{128,160},{160,128},{192,224},{224,1... | collective-permute-start | bytes 7077896 | tf_op jit(solution)/shard_map/ppermute | solution.py:485
  395.2 39.9 %collective-permute-start.19 = (bf16[1536,768]{1,0:T(8,128)(2,1)}, bf16[1536,768]{1,0:T(8,128)(2,1)}, u32[]{:S(2)}, u32[]{:S(2)}) collective-permute-start(bf16[1536,768]{1,0:T(8,128)(2,1)} %get-tuple-element.298), channel_id=1, source_target_pairs={{0,64},{32,224},{64,128},{96,32},{128,192},{160,96},{192,0},{224,1... | collective-permute-start | bytes 7077896 | tf_op jit(solution)/shard_map/ppermute | solution.py:490
  418.8 48.8 %collective-permute-start.20 = (bf16[1536,768]{1,0:T(8,128)(2,1)}, bf16[1536,768]{1,0:T(8,128)(2,1)}, u32[]{:S(2)}, u32[]{:S(2)}) collective-permute-start(bf16[1536,768]{1,0:T(8,128)(2,1)} %get-tuple-element.306.refs_4_), channel_id=1, source_target_pairs={{0,32},{32,0},{64,96},{96,64},{128,160},{160,128},{192,224},{224,1... | collective-permute-start | bytes 7077896 | tf_op jit(solution)/shard_map/ppermute | solution.py:485
  450.3 39.8 %collective-permute-start.21 = (bf16[1536,768]{1,0:T(8,128)(2,1)}, bf16[1536,768]{1,0:T(8,128)(2,1)}, u32[]{:S(2)}, u32[]{:S(2)}) collective-permute-start(bf16[1536,768]{1,0:T(8,128)(2,1)} %get-tuple-element.310), channel_id=1, source_target_pairs={{0,64},{32,224},{64,128},{96,32},{128,192},{160,96},{224,160},{1,6... | collective-permute-start | bytes 7077896 | tf_op jit(solution)/shard_map/ppermute | solution.py:490
  473.6 49.0 %collective-permute-start.22 = (bf16[1536,768]{1,0:T(8,128)(2,1)}, bf16[1536,768]{1,0:T(8,128)(2,1)}, u32[]{:S(2)}, u32[]{:S(2)}) collective-permute-start(bf16[1536,768]{1,0:T(8,128)(2,1)} %get-tuple-element.318.refs_4_), channel_id=1, source_target_pairs={{0,32},{32,0},{64,96},{96,64},{128,160},{160,128},{192,224},{224,1... | collective-permute-start | bytes 7077896 | tf_op jit(solution)/shard_map/ppermute | solution.py:485
  505.3 44.4 %collective-permute-start.23 = (bf16[1536,768]{1,0:T(8,128)(2,1)}, bf16[1536,768]{1,0:T(8,128)(2,1)}, u32[]{:S(2)}, u32[]{:S(2)}) collective-permute-start(bf16[1536,768]{1,0:T(8,128)(2,1)} %get-tuple-element.322), channel_id=1, source_target_pairs={{0,64},{32,224},{64,128},{128,192},{160,96},{192,0},{224,160},{1,6... | collective-permute-start | bytes 7077896 | tf_op jit(solution)/shard_map/ppermute | solution.py:490
  528.6 47.3 %collective-permute-start.24 = (bf16[1536,768]{1,0:T(8,128)(2,1)}, bf16[1536,768]{1,0:T(8,128)(2,1)}, u32[]{:S(2)}, u32[]{:S(2)}) collective-permute-start(bf16[1536,768]{1,0:T(8,128)(2,1)} %get-tuple-element.330.refs_4_), channel_id=1, source_target_pairs={{0,32},{32,0},{64,96},{96,64},{128,160},{160,128},{192,224},{224,1... | collective-permute-start | bytes 7077896 | tf_op jit(solution)/shard_map/ppermute | solution.py:485
  558.6 44.4 %collective-permute-start.25 = (bf16[1536,768]{1,0:T(8,128)(2,1)}, bf16[1536,768]{1,0:T(8,128)(2,1)}, u32[]{:S(2)}, u32[]{:S(2)}) collective-permute-start(bf16[1536,768]{1,0:T(8,128)(2,1)} %get-tuple-element.334), channel_id=1, source_target_pairs={{32,224},{64,128},{96,32},{128,192},{192,0},{224,160},{33,225},{65... | collective-permute-start | bytes 7077896 | tf_op jit(solution)/shard_map/ppermute | solution.py:490
  581.9 46.8 %collective-permute-start.26 = (bf16[1536,768]{1,0:T(8,128)(2,1)}, bf16[1536,768]{1,0:T(8,128)(2,1)}, u32[]{:S(2)}, u32[]{:S(2)}) collective-permute-start(bf16[1536,768]{1,0:T(8,128)(2,1)} %get-tuple-element.342.refs_4_), channel_id=1, source_target_pairs={{0,32},{32,0},{64,96},{96,64},{128,160},{160,128},{192,224},{224,1... | collective-permute-start | bytes 7077896 | tf_op jit(solution)/shard_map/ppermute | solution.py:485
  611.4 44.4 %collective-permute-start.27 = (bf16[1536,768]{1,0:T(8,128)(2,1)}, bf16[1536,768]{1,0:T(8,128)(2,1)}, u32[]{:S(2)}, u32[]{:S(2)}) collective-permute-start(bf16[1536,768]{1,0:T(8,128)(2,1)} %get-tuple-element.346), channel_id=1, source_target_pairs={{160,96},{192,0},{161,97},{193,1},{162,98},{194,2},{163,99},{195,3... | collective-permute-start | bytes 7077896 | tf_op jit(solution)/shard_map/ppermute | solution.py:490
  634.7 46.4 %collective-permute-start.28 = (bf16[1536,768]{1,0:T(8,128)(2,1)}, bf16[1536,768]{1,0:T(8,128)(2,1)}, u32[]{:S(2)}, u32[]{:S(2)}) collective-permute-start(bf16[1536,768]{1,0:T(8,128)(2,1)} %get-tuple-element.354.refs_4_), channel_id=1, source_target_pairs={{0,32},{32,0},{64,96},{96,64},{128,160},{160,128},{192,224},{224,1... | collective-permute-start | bytes 7077896 | tf_op jit(solution)/shard_map/ppermute | solution.py:485
  663.8 44.4 %collective-permute-start.29 = (bf16[1536,768]{1,0:T(8,128)(2,1)}, bf16[1536,768]{1,0:T(8,128)(2,1)}, u32[]{:S(2)}, u32[]{:S(2)}) collective-permute-start(bf16[1536,768]{1,0:T(8,128)(2,1)} %get-tuple-element.358), channel_id=1, source_target_pairs={{0,64},{96,32},{1,65},{97,33},{2,66},{98,34},{3,67},{99,35},{4,68}... | collective-permute-start | bytes 7077896 | tf_op jit(solution)/shard_map/ppermute | solution.py:490
  687.0 45.6 %collective-permute-start.30 = (bf16[1536,768]{1,0:T(8,128)(2,1)}, bf16[1536,768]{1,0:T(8,128)(2,1)}, u32[]{:S(2)}, u32[]{:S(2)}) collective-permute-start(bf16[1536,768]{1,0:T(8,128)(2,1)} %get-tuple-element.365.refs_4_), channel_id=1, source_target_pairs={{0,32},{32,0},{64,96},{96,64},{128,160},{160,128},{192,224},{224,1... | collective-permute-start | bytes 7077896 | tf_op jit(solution)/shard_map/ppermute | solution.py:485
  738.5 45.7 %collective-permute-start.31 = (bf16[1536,768]{1,0:T(8,128)(2,1)}, bf16[1536,768]{1,0:T(8,128)(2,1)}, u32[]{:S(2)}, u32[]{:S(2)}) collective-permute-start(bf16[1536,768]{1,0:T(8,128)(2,1)} %get-tuple-element.375.refs_4_), channel_id=1, source_target_pairs={{0,32},{32,0},{64,96},{96,64},{128,160},{160,128},{192,224},{224,1... | collective-permute-start | bytes 7077896 | tf_op jit(solution)/shard_map/ppermute | solution.py:485
  790.3 45.6 %collective-permute-start.32 = (bf16[1536,768]{1,0:T(8,128)(2,1)}, bf16[1536,768]{1,0:T(8,128)(2,1)}, u32[]{:S(2)}, u32[]{:S(2)}) collective-permute-start(bf16[1536,768]{1,0:T(8,128)(2,1)} %get-tuple-element.386.refs_4_), channel_id=1, source_target_pairs={{0,32},{32,0},{64,96},{96,64},{128,160},{160,128},{192,224},{224,1... | collective-permute-start | bytes 7077896 | tf_op jit(solution)/shard_map/ppermute | solution.py:485
  841.9 45.8 %collective-permute-start.33 = (bf16[1536,768]{1,0:T(8,128)(2,1)}, bf16[1536,768]{1,0:T(8,128)(2,1)}, u32[]{:S(2)}, u32[]{:S(2)}) collective-permute-start(bf16[1536,768]{1,0:T(8,128)(2,1)} %get-tuple-element.396.refs_4_), channel_id=1, source_target_pairs={{0,32},{32,0},{64,96},{96,64},{128,160},{160,128},{192,224},{224,1... | collective-permute-start | bytes 7077896 | tf_op jit(solution)/shard_map/ppermute | solution.py:485
  893.6 45.5 %collective-permute-start.34 = (bf16[1536,768]{1,0:T(8,128)(2,1)}, bf16[1536,768]{1,0:T(8,128)(2,1)}, u32[]{:S(2)}, u32[]{:S(2)}) collective-permute-start(bf16[1536,768]{1,0:T(8,128)(2,1)} %get-tuple-element.406.refs_4_), channel_id=1, source_target_pairs={{0,32},{32,0},{64,96},{96,64},{128,160},{160,128},{192,224},{224,1... | collective-permute-start | bytes 7077896 | tf_op jit(solution)/shard_map/ppermute | solution.py:485
  (28 other events, 223.5 us)

commit v8 on v6

--- a/solution.py
+++ b/solution.py
@@ -377,10 +377,10 @@
 
 
 def place_tokens(routes, experts):
-    tokens = routes.shape[1]
+    tokens = routes.shape[2]
     ids = jnp.arange(experts, dtype=jnp.int32)
-    first = routes[:, :, 0:1] == ids
-    second = routes[:, :, 1:2] == ids
+    first = routes[:, 0, :, None] == ids
+    second = routes[:, 1, :, None] == ids
     named = (first | second).astype(jnp.bfloat16)
     earlier = jnp.tril(jnp.ones((tokens, tokens), jnp.bfloat16), -1)
     rank = jnp.einsum("ut,lte->lue", earlier, named, preferred_element_type=jnp.float32)
@@ -474,18 +474,24 @@
         parts = range(q * PARTS, (q + 1) * PARTS)
         return max(stock[i][0] for lane in held for stock in lane for i in parts)
 
-    mine = lax.all_to_all(routes[:, 0], "section", split_axis=1, concat_axis=0, tiled=False)
-    mine = jnp.transpose(mine, (1, 0, 2, 3)).reshape(layers, -1, 2)
+    sent = jnp.transpose(routes[:, 0], (1, 0, 3, 2)).astype(jnp.bfloat16).reshape(sections, -1)
+    cut = sent.shape[1]
+    small = jnp.stack([norm_gains[:, 0], routers[:, 0, 0]]).reshape(1, -1)
+    small = jnp.broadcast_to(small, (sections, small.shape[1]))
+    sent = jnp.concatenate([sent, small], axis=1).reshape(sections, -1, LANES)
+    got = lax.all_to_all(sent, "section", split_axis=0, concat_axis=0, tiled=True)
+    h = jnp.transpose(inputs[0], (1, 0))
+
+    ours, later = swapped(picked(swap_rows[0], tab)), swapped(picked(swap_rows[1], tab))
+    ours, tab, got = join(ours, tab, got)
+    buffers[("swapped", 0)] = (ours, ())
+    got = got.reshape(sections, -1)
+    mine = got[:, 0:cut].astype(jnp.int32).reshape(sections, repeats, 2, -1)
+    mine = jnp.transpose(mine, (1, 0, 2, 3)).reshape(layers, 2, -1)
     rows = place_tokens(mine, experts)
-    small = jnp.stack([norm_gains[:, 0], routers[:, 0, 0]])
-    small = jnp.broadcast_to(small[None], (sections,) + small.shape)
-    small = lax.all_to_all(small, "section", split_axis=0, concat_axis=0, tiled=True)
+    small = got[:, cut:].reshape(sections, 2, repeats, width)
     small = jnp.transpose(small, (1, 2, 0, 3)).reshape(2, layers, 1, width).astype(jnp.float32)
     gains, gate_rows = small[0], small[1]
-    h = jnp.transpose(inputs[0], (1, 0))
-
-    buffers[("swapped", 0)] = (swapped(picked(swap_rows[0], tab)), ())
-    later = swapped(picked(swap_rows[1], tab))
     flying = None
     for number in range(1, LEAD + 1):
         started = ring(number, picked(ring_rows[number - 1], tab))
@@ -502,9 +508,11 @@
         flying = started
     flying, tab, blocks = join(flying, tab, blocks)
     buffers[("ring", LEAD)] = (flying, ())
+    onward = picked(ring_rows[LEAD], tab)
+    flying = ring(LEAD + 1, onward)
+    onward, tab = join(onward, tab)
     lane_w = picked(layer_rows[0], tab)
     coming = (lane_w, swapped(lane_w))
-    flying = ring(LEAD + 1, picked(ring_rows[LEAD], tab))
     blocks, tab, *coming = join(blocks, tab, *coming)
 
     for q in range(layers):

time: 822 us -> 818 us (level)
    ppermute x17, waiting for transfers between devices: 99.6 us -> 115 us  [ring(): return lax.ppermute(value, 'section', pairs)]
    all_to_all x2 -> x1, waiting for transfers between devices: 17.5 us -> 4.11 us  [local(): lax.all_to_all(sent, 'section', split_axis=0, concat_axis=0, tiled=True)]
  transfers between devices with their start and end apart: 54 -> 53, of which waited for: 28 -> 32; matrix products, arithmetic and copies ran while one was open for 1% -> 1% of each run, Pallas kernels for 18% -> 18%
where the time goes in v8:
time: 818 us; the launch traced here: 806 us
  blocking collectives  239 us (29%)
  waiting for transfers between devices  213 us (26%)
  Pallas kernels  205 us (25%)
  starting transfers between devices  131 us (16%)
  local copies, waits for them, and re-layouts  14.4 us (2%)
    all_to_all x15, blocking collectives, send_blocks(): lax.all_to_all(value, 'expert', split_axis=0, concat_axis=0, tiled=True)  239 us
    pallas_call x43, Pallas kernels, call_with_side(): pl.pallas_call(body, out_shape=tuple(shapes) + tuple(beside.out_shapes),...  205 us
    ppermute x17, waiting for transfers between devices, ring(): return lax.ppermute(value, 'section', pairs)  115 us
    all_to_all x17, starting transfers between devices, send_blocks(): lax.all_to_all(value, 'expert', split_axis=0, concat_axis=0, tiled=True)  93.1 us
    all_to_all x17, waiting for transfers between devices, send_blocks(): lax.all_to_all(value, 'expert', split_axis=0, concat_axis=0, tiled=True)  92.6 us
    ppermute x17, starting transfers between devices, ring(): return lax.ppermute(value, 'section', pairs)  27.5 us
  transfers between devices with their start and end apart: 53, of which 32 were waited for; matrix products, arithmetic and copies ran while one was open for 1% of the time, Pallas kernels for 18%

profile of v8, /device:TPU:8, one launch (start us, length us, event | category | flops | bytes accessed | tf_op | source)
XLA Modules:
  0.0 806.2 jit_solution(1393774866765674401)
XLA Ops:
  30.9 11.3 %collective-permute-done.2.refs_2_.refs_1_.refs_7_.refs_8_ = bf16[768,768]{1,0:T(8,128)(2,1)} collective-permute-done((bf16[768,768]{1,0:T(8,128)(2,1)}, bf16[768,768]{1,0:T(8,128)(2,1)}, u32[]{:S(2)}, u32[]{:S(2)}) %collective-permute-start.2) | collective-permute-done | bytes 1179680 | tf_op jit(solution)/shard_map/ppermute | solution.py:471
  45.5 9.2 %collective-permute-done.3.refs_2_.refs_1_.refs_3_.refs_8_.refs_9_ = bf16[768,768]{1,0:T(8,128)(2,1)} collective-permute-done((bf16[768,768]{1,0:T(8,128)(2,1)}, bf16[768,768]{1,0:T(8,128)(2,1)}, u32[]{:S(2)}, u32[]{:S(2)}) %collective-permute-start.3) | collective-permute-done | bytes 1179680 | tf_op jit(solution)/shard_map/ppermute | solution.py:471
  58.2 9.2 %collective-permute-done.5.refs_2_.refs_3_.refs_4_.refs_9_.refs_10_.refs_8_.refs_7_ = bf16[768,768]{1,0:T(8,128)(2,1)} collective-permute-done((bf16[768,768]{1,0:T(8,128)(2,1)}, bf16[768,768]{1,0:T(8,128)(2,1)}, u32[]{:S(2)}, u32[]{:S(2)}) %collective-permute-start.5) | collective-permute-done | bytes 1179680 | tf_op jit(solution)/shard_map/ppermute | solution.py:471
  70.4 9.7 %collective-permute-done.4.refs_2_.refs_4_.refs_5_.refs_10_.refs_11_.refs_9_.refs_8_ = bf16[768,768]{1,0:T(8,128)(2,1)} collective-permute-done((bf16[768,768]{1,0:T(8,128)(2,1)}, bf16[768,768]{1,0:T(8,128)(2,1)}, u32[]{:S(2)}, u32[]{:S(2)}) %collective-permute-start.4) | collective-permute-done | bytes 1179680 | tf_op jit(solution)/shard_map/ppermute | solution.py:471
  88.0 21.0 %all_to_all.165.refs_1_ = bf16[160,2,128]{2,1,0:T(2,128)(2,1)} all-to-all(bf16[160,2,128]{2,1,0:T(2,128)(2,1)} %get-tuple-element.225), channel_id=1, replica_groups=mesh['section'=8,'expert'=32] {'expert'}, dimensions={0} | all-to-all | bytes 163840 | tf_op jit(solution)/shard_map/all_to_all | solution.py:238
  126.6 10.8 %all-to-all-start.2 = ((bf16[160,2,128]{2,1,0:T(2,128)(2,1)}), bf16[160,2,128]{2,1,0:T(2,128)(2,1)S(1)}, u32[]{:S(2)}, u32[]{:S(2)}) async-start(bf16[160,2,128]{2,1,0:T(2,128)(2,1)} %expert.16), calls=%async_computation.2 | async-start | bytes 163840 | tf_op jit(solution)/shard_map/all_to_all | solution.py:238
  137.4 10.0 %collective-permute-done.9.refs_13_.refs_14_.refs_7_.refs_10_.refs_9_.refs_8_ = bf16[1536,768]{1,0:T(8,128)(2,1)} collective-permute-done((bf16[1536,768]{1,0:T(8,128)(2,1)}, bf16[1536,768]{1,0:T(8,128)(2,1)}, u32[]{:S(2)}, u32[]{:S(2)}) %collective-permute-start.9) | collective-permute-done | bytes 2359328 | tf_op jit(solution)/shard_map/ppermute | solution.py:471
  155.7 19.8 %all_to_all.166.refs_1_ = bf16[160,2,128]{2,1,0:T(2,128)(2,1)} all-to-all(bf16[160,2,128]{2,1,0:T(2,128)(2,1)} %get-tuple-element.245), channel_id=1, replica_groups=mesh['section'=8,'expert'=32] {'expert'}, dimensions={0} | all-to-all | bytes 163840 | tf_op jit(solution)/shard_map/all_to_all | solution.py:238
  187.8 10.1 %all-to-all-done.4.refs_1_ = bf16[160,2,128]{2,1,0:T(2,128)(2,1)S(1)} async-done(((bf16[160,2,128]{2,1,0:T(2,128)(2,1)}), bf16[160,2,128]{2,1,0:T(2,128)(2,1)S(1)}, u32[]{:S(2)}, u32[]{:S(2)}) %all-to-all-start.4) | async-done | bytes 81952 | tf_op jit(solution)/shard_map/all_to_all | solution.py:238
  205.4 15.0 %all_to_all.167.refs_1_ = bf16[160,2,128]{2,1,0:T(2,128)(2,1)} all-to-all(bf16[160,2,128]{2,1,0:T(2,128)(2,1)} %get-tuple-element.257), channel_id=1, replica_groups=mesh['section'=8,'expert'=32] {'expert'}, dimensions={0} | all-to-all | bytes 163840 | tf_op jit(solution)/shard_map/all_to_all | solution.py:238
  250.0 14.6 %all_to_all.168.refs_1_ = bf16[160,2,128]{2,1,0:T(2,128)(2,1)} all-to-all(bf16[160,2,128]{2,1,0:T(2,128)(2,1)} %get-tuple-element.268), channel_id=1, replica_groups=mesh['section'=8,'expert'=32] {'expert'}, dimensions={0} | all-to-all | bytes 163840 | tf_op jit(solution)/shard_map/all_to_all | solution.py:238
  276.6 8.4 %all-to-all-done.8.refs_1_ = bf16[160,2,128]{2,1,0:T(2,128)(2,1)S(1)} async-done(((bf16[160,2,128]{2,1,0:T(2,128)(2,1)}), bf16[160,2,128]{2,1,0:T(2,128)(2,1)S(1)}, u32[]{:S(2)}, u32[]{:S(2)}) %all-to-all-start.8) | async-done | bytes 81952 | tf_op jit(solution)/shard_map/all_to_all | solution.py:238
  292.0 14.8 %all_to_all.169.refs_1_ = bf16[160,2,128]{2,1,0:T(2,128)(2,1)} all-to-all(bf16[160,2,128]{2,1,0:T(2,128)(2,1)} %get-tuple-element.280), channel_id=1, replica_groups=mesh['section'=8,'expert'=32] {'expert'}, dimensions={0} | all-to-all | bytes 163840 | tf_op jit(solution)/shard_map/all_to_all | solution.py:238
  337.7 9.9 %all-to-all-done.11.refs_1_ = bf16[160,2,128]{2,1,0:T(2,128)(2,1)S(1)} async-done(((bf16[160,2,128]{2,1,0:T(2,128)(2,1)}), bf16[160,2,128]{2,1,0:T(2,128)(2,1)S(1)}, u32[]{:S(2)}, u32[]{:S(2)}) %all-to-all-start.11) | async-done | bytes 81952 | tf_op jit(solution)/shard_map/all_to_all | solution.py:238
  403.0 10.3 %collective-permute-done.21.refs_7_.refs_6_.refs_11_.refs_10_.refs_9_ = bf16[1536,768]{1,0:T(8,128)(2,1)} collective-permute-done((bf16[1536,768]{1,0:T(8,128)(2,1)}, bf16[1536,768]{1,0:T(8,128)(2,1)}, u32[]{:S(2)}, u32[]{:S(2)}) %collective-permute-start.21) | collective-permute-done | bytes 2359328 | tf_op jit(solution)/shard_map/ppermute | solution.py:471
  419.7 9.6 %all-to-all-start.15 = ((bf16[160,2,128]{2,1,0:T(2,128)(2,1)}), bf16[160,2,128]{2,1,0:T(2,128)(2,1)S(1)}, u32[]{:S(2)}, u32[]{:S(2)}) async-start(bf16[160,2,128]{2,1,0:T(2,128)(2,1)} %get-tuple-element.315), calls=%async_computation.15 | async-start | bytes 163840 | tf_op jit(solution)/shard_map/all_to_all | solution.py:238
  450.0 10.4 %collective-permute-done.23.refs_7_.refs_11_.refs_10_.refs_12_.refs_9_ = bf16[1536,768]{1,0:T(8,128)(2,1)} collective-permute-done((bf16[1536,768]{1,0:T(8,128)(2,1)}, bf16[1536,768]{1,0:T(8,128)(2,1)}, u32[]{:S(2)}, u32[]{:S(2)}) %collective-permute-start.23) | collective-permute-done | bytes 2359328 | tf_op jit(solution)/shard_map/ppermute | solution.py:471
  466.6 9.7 %all-to-all-start.17 = ((bf16[160,2,128]{2,1,0:T(2,128)(2,1)}), bf16[160,2,128]{2,1,0:T(2,128)(2,1)S(1)}, u32[]{:S(2)}, u32[]{:S(2)}) async-start(bf16[160,2,128]{2,1,0:T(2,128)(2,1)} %get-tuple-element.327), calls=%async_computation.17 | async-start | bytes 163840 | tf_op jit(solution)/shard_map/all_to_all | solution.py:238
  497.1 8.3 %collective-permute-done.25.refs_5_.refs_11_.refs_10_.refs_12_ = bf16[1536,768]{1,0:T(8,128)(2,1)} collective-permute-done((bf16[1536,768]{1,0:T(8,128)(2,1)}, bf16[1536,768]{1,0:T(8,128)(2,1)}, u32[]{:S(2)}, u32[]{:S(2)}) %collective-permute-start.25) | collective-permute-done | bytes 2359328 | tf_op jit(solution)/shard_map/ppermute | solution.py:471
  541.2 10.5 %all-to-all-done.20.refs_1_ = bf16[160,2,128]{2,1,0:T(2,128)(2,1)S(1)} async-done(((bf16[160,2,128]{2,1,0:T(2,128)(2,1)}), bf16[160,2,128]{2,1,0:T(2,128)(2,1)S(1)}, u32[]{:S(2)}, u32[]{:S(2)}) %all-to-all-start.20) | async-done | bytes 81952 | tf_op jit(solution)/shard_map/all_to_all | solution.py:238
  562.3 9.0 %all-to-all-done.21.refs_1_ = bf16[160,2,128]{2,1,0:T(2,128)(2,1)S(1)} async-done(((bf16[160,2,128]{2,1,0:T(2,128)(2,1)}), bf16[160,2,128]{2,1,0:T(2,128)(2,1)S(1)}, u32[]{:S(2)}, u32[]{:S(2)}) %all-to-all-start.21) | async-done | bytes 81952 | tf_op jit(solution)/shard_map/all_to_all | solution.py:238
  583.6 16.5 %collective-permute-done.29.refs_12_ = bf16[1536,768]{1,0:T(8,128)(2,1)} collective-permute-done((bf16[1536,768]{1,0:T(8,128)(2,1)}, bf16[1536,768]{1,0:T(8,128)(2,1)}, u32[]{:S(2)}, u32[]{:S(2)}) %collective-permute-start.29) | collective-permute-done | bytes 2359328 | tf_op jit(solution)/shard_map/ppermute | solution.py:471
  604.6 20.0 %all_to_all.170.refs_1_ = bf16[160,2,128]{2,1,0:T(2,128)(2,1)} all-to-all(bf16[160,2,128]{2,1,0:T(2,128)(2,1)} %get-tuple-element.362), channel_id=1, replica_groups=mesh['section'=8,'expert'=32] {'expert'}, dimensions={0} | all-to-all | bytes 163840 | tf_op jit(solution)/shard_map/all_to_all | solution.py:238
  630.6 15.1 %all_to_all.171.refs_1_ = bf16[160,2,128]{2,1,0:T(2,128)(2,1)} all-to-all(bf16[160,2,128]{2,1,0:T(2,128)(2,1)} %get-tuple-element.368), channel_id=1, replica_groups=mesh['section'=8,'expert'=32] {'expert'}, dimensions={0} | all-to-all | bytes 163840 | tf_op jit(solution)/shard_map/all_to_all | solution.py:238
  649.5 14.7 %all_to_all.172.refs_1_ = bf16[160,2,128]{2,1,0:T(2,128)(2,1)} all-to-all(bf16[160,2,128]{2,1,0:T(2,128)(2,1)} %get-tuple-element.372), channel_id=1, replica_groups=mesh['section'=8,'expert'=32] {'expert'}, dimensions={0} | all-to-all | bytes 163840 | tf_op jit(solution)/shard_map/all_to_all | solution.py:238
  670.5 15.0 %all_to_all.173.refs_1_ = bf16[160,2,128]{2,1,0:T(2,128)(2,1)} all-to-all(bf16[160,2,128]{2,1,0:T(2,128)(2,1)} %get-tuple-element.379), channel_id=1, replica_groups=mesh['section'=8,'expert'=32] {'expert'}, dimensions={0} | all-to-all | bytes 163840 | tf_op jit(solution)/shard_map/all_to_all | solution.py:238
  689.3 14.7 %all_to_all.174.refs_1_ = bf16[160,2,128]{2,1,0:T(2,128)(2,1)} all-to-all(bf16[160,2,128]{2,1,0:T(2,128)(2,1)} %get-tuple-element.383), channel_id=1, replica_groups=mesh['section'=8,'expert'=32] {'expert'}, dimensions={0} | all-to-all | bytes 163840 | tf_op jit(solution)/shard_map/all_to_all | solution.py:238
  710.1 15.0 %all_to_all.175.refs_1_ = bf16[160,2,128]{2,1,0:T(2,128)(2,1)} all-to-all(bf16[160,2,128]{2,1,0:T(2,128)(2,1)} %get-tuple-element.389), channel_id=1, replica_groups=mesh['section'=8,'expert'=32] {'expert'}, dimensions={0} | all-to-all | bytes 163840 | tf_op jit(solution)/shard_map/all_to_all | solution.py:238
  728.9 14.7 %all_to_all.176.refs_1_ = bf16[160,2,128]{2,1,0:T(2,128)(2,1)} all-to-all(bf16[160,2,128]{2,1,0:T(2,128)(2,1)} %get-tuple-element.393), channel_id=1, replica_groups=mesh['section'=8,'expert'=32] {'expert'}, dimensions={0} | all-to-all | bytes 163840 | tf_op jit(solution)/shard_map/all_to_all | solution.py:238
  749.7 15.3 %all_to_all.177.refs_1_ = bf16[160,2,128]{2,1,0:T(2,128)(2,1)} all-to-all(bf16[160,2,128]{2,1,0:T(2,128)(2,1)} %get-tuple-element.399), channel_id=1, replica_groups=mesh['section'=8,'expert'=32] {'expert'}, dimensions={0} | all-to-all | bytes 163840 | tf_op jit(solution)/shard_map/all_to_all | solution.py:238
  768.8 14.7 %all_to_all.178.refs_1_ = bf16[160,2,128]{2,1,0:T(2,128)(2,1)} all-to-all(bf16[160,2,128]{2,1,0:T(2,128)(2,1)} %get-tuple-element.403), channel_id=1, replica_groups=mesh['section'=8,'expert'=32] {'expert'}, dimensions={0} | all-to-all | bytes 163840 | tf_op jit(solution)/shard_map/all_to_all | solution.py:238
  788.5 14.7 %all_to_all.179.refs_1_ = bf16[160,2,128]{2,1,0:T(2,128)(2,1)} all-to-all(bf16[160,2,128]{2,1,0:T(2,128)(2,1)} %expert.31), channel_id=1, replica_groups=mesh['section'=8,'expert'=32] {'expert'}, dimensions={0} | all-to-all | bytes 163840 | tf_op jit(solution)/shard_map/all_to_all | solution.py:238
  (202 shorter events, 393.2 us)
Async XLA Ops:
  8.3 33.9 %collective-permute-start = (bf16[1536,768]{1,0:T(8,128)(2,1)}, bf16[1536,768]{1,0:T(8,128)(2,1)}, u32[]{:S(2)}, u32[]{:S(2)}) collective-permute-start(bf16[1536,768]{1,0:T(8,128)(2,1)} %pick.10), channel_id=1, source_target_pairs={{0,32},{32,0},{64,96},{96,64},{128,160},{160,128},{192,224},{224,1... | collective-permute-start | bytes 7077896 | tf_op jit(solution)/shard_map/ppermute | solution.py:466
  26.0 28.8 %collective-permute-start.3 = (bf16[768,768]{1,0:T(8,128)(2,1)}, bf16[768,768]{1,0:T(8,128)(2,1)}, u32[]{:S(2)}, u32[]{:S(2)}) collective-permute-start(bf16[768,768]{1,0:T(8,128)(2,1)} %pick.13), channel_id=1, source_target_pairs={{0,64},{32,224},{64,128},{96,32},{128,192},{160,96},{192,0},{224,1... | collective-permute-start | bytes 3538952 | tf_op jit(solution)/shard_map/ppermute | solution.py:471
  45.1 22.3 %collective-permute-start.5 = (bf16[768,768]{1,0:T(8,128)(2,1)}, bf16[768,768]{1,0:T(8,128)(2,1)}, u32[]{:S(2)}, u32[]{:S(2)}) collective-permute-start(bf16[768,768]{1,0:T(8,128)(2,1)} %pick.15), channel_id=1, source_target_pairs={{0,64},{32,224},{64,128},{96,32},{128,192},{160,96},{192,0},{224,1... | collective-permute-start | bytes 3538952 | tf_op jit(solution)/shard_map/ppermute | solution.py:471
  57.8 22.3 %collective-permute-start.4 = (bf16[768,768]{1,0:T(8,128)(2,1)}, bf16[768,768]{1,0:T(8,128)(2,1)}, u32[]{:S(2)}, u32[]{:S(2)}) collective-permute-start(bf16[768,768]{1,0:T(8,128)(2,1)} %pick.14), channel_id=1, source_target_pairs={{0,64},{32,224},{64,128},{96,32},{128,192},{160,96},{192,0},{224,1... | collective-permute-start | bytes 3538952 | tf_op jit(solution)/shard_map/ppermute | solution.py:471
  80.1 28.9 %collective-permute-start.7 = (bf16[768,768]{1,0:T(8,128)(2,1)}, bf16[768,768]{1,0:T(8,128)(2,1)}, u32[]{:S(2)}, u32[]{:S(2)}) collective-permute-start(bf16[768,768]{1,0:T(8,128)(2,1)} %pick.17), channel_id=1, source_target_pairs={{0,64},{32,224},{64,128},{96,32},{128,192},{160,96},{192,0},{224,1... | collective-permute-start | bytes 3538952 | tf_op jit(solution)/shard_map/ppermute | solution.py:471
  83.4 26.4 %collective-permute-start.6 = (bf16[768,768]{1,0:T(8,128)(2,1)}, bf16[768,768]{1,0:T(8,128)(2,1)}, u32[]{:S(2)}, u32[]{:S(2)}) collective-permute-start(bf16[768,768]{1,0:T(8,128)(2,1)} %pick.16), channel_id=1, source_target_pairs={{0,64},{32,224},{64,128},{96,32},{128,192},{160,96},{192,0},{224,1... | collective-permute-start | bytes 3538952 | tf_op jit(solution)/shard_map/ppermute | solution.py:471
  116.7 30.7 %collective-permute-start.9 = (bf16[1536,768]{1,0:T(8,128)(2,1)}, bf16[1536,768]{1,0:T(8,128)(2,1)}, u32[]{:S(2)}, u32[]{:S(2)}) collective-permute-start(bf16[1536,768]{1,0:T(8,128)(2,1)} %pick.18), channel_id=1, source_target_pairs={{0,64},{32,224},{64,128},{96,32},{128,192},{160,96},{192,0},{224,1... | collective-permute-start | bytes 7077896 | tf_op jit(solution)/shard_map/ppermute | solution.py:471
  126.6 20.9 %all-to-all-start.2 = ((bf16[160,2,128]{2,1,0:T(2,128)(2,1)}), bf16[160,2,128]{2,1,0:T(2,128)(2,1)S(1)}, u32[]{:S(2)}, u32[]{:S(2)}) async-start(bf16[160,2,128]{2,1,0:T(2,128)(2,1)} %expert.16), calls=%async_computation.2 | async-start | bytes 163840 | tf_op jit(solution)/shard_map/all_to_all | solution.py:238
  154.4 21.1 %collective-permute-start.10 = (bf16[1536,768]{1,0:T(8,128)(2,1)}, bf16[1536,768]{1,0:T(8,128)(2,1)}, u32[]{:S(2)}, u32[]{:S(2)}) collective-permute-start(bf16[1536,768]{1,0:T(8,128)(2,1)} %get-tuple-element.248.refs_4_), channel_id=1, source_target_pairs={{0,32},{32,0},{64,96},{96,64},{128,160},{160,128},{192,224},{224,1... | collective-permute-start | bytes 7077896 | tf_op jit(solution)/shard_map/ppermute | solution.py:466
  154.5 33.2 %collective-permute-start.11 = (bf16[1536,768]{1,0:T(8,128)(2,1)}, bf16[1536,768]{1,0:T(8,128)(2,1)}, u32[]{:S(2)}, u32[]{:S(2)}) collective-permute-start(bf16[1536,768]{1,0:T(8,128)(2,1)} %get-tuple-element.252), channel_id=1, source_target_pairs={{0,64},{32,224},{64,128},{96,32},{128,192},{160,96},{192,0},{224,1... | collective-permute-start | bytes 7077896 | tf_op jit(solution)/shard_map/ppermute | solution.py:471
  181.9 38.6 %collective-permute-start.12 = (bf16[1536,768]{1,0:T(8,128)(2,1)}, bf16[1536,768]{1,0:T(8,128)(2,1)}, u32[]{:S(2)}, u32[]{:S(2)}) collective-permute-start(bf16[1536,768]{1,0:T(8,128)(2,1)} %get-tuple-element.260.refs_4_), channel_id=1, source_target_pairs={{0,32},{32,0},{64,96},{96,64},{128,160},{160,128},{192,224},{224,1... | collective-permute-start | bytes 7077896 | tf_op jit(solution)/shard_map/ppermute | solution.py:466
  204.4 29.2 %collective-permute-start.13 = (bf16[1536,768]{1,0:T(8,128)(2,1)}, bf16[1536,768]{1,0:T(8,128)(2,1)}, u32[]{:S(2)}, u32[]{:S(2)}) collective-permute-start(bf16[1536,768]{1,0:T(8,128)(2,1)} %get-tuple-element.263), channel_id=1, source_target_pairs={{0,64},{32,224},{64,128},{96,32},{128,192},{160,96},{192,0},{224,1... | collective-permute-start | bytes 7077896 | tf_op jit(solution)/shard_map/ppermute | solution.py:471
  246.5 30.1 %collective-permute-start.15 = (bf16[1536,768]{1,0:T(8,128)(2,1)}, bf16[1536,768]{1,0:T(8,128)(2,1)}, u32[]{:S(2)}, u32[]{:S(2)}) collective-permute-start(bf16[1536,768]{1,0:T(8,128)(2,1)} %get-tuple-element.275), channel_id=1, source_target_pairs={{0,64},{32,224},{64,128},{96,32},{128,192},{160,96},{192,0},{224,1... | collective-permute-start | bytes 7077896 | tf_op jit(solution)/shard_map/ppermute | solution.py:471
  270.6 36.2 %collective-permute-start.16 = (bf16[1536,768]{1,0:T(8,128)(2,1)}, bf16[1536,768]{1,0:T(8,128)(2,1)}, u32[]{:S(2)}, u32[]{:S(2)}) collective-permute-start(bf16[1536,768]{1,0:T(8,128)(2,1)} %get-tuple-element.283.refs_4_), channel_id=1, source_target_pairs={{0,32},{32,0},{64,96},{96,64},{128,160},{160,128},{192,224},{224,1... | collective-permute-start | bytes 7077896 | tf_op jit(solution)/shard_map/ppermute | solution.py:466
  291.2 29.2 %collective-permute-start.17 = (bf16[1536,768]{1,0:T(8,128)(2,1)}, bf16[1536,768]{1,0:T(8,128)(2,1)}, u32[]{:S(2)}, u32[]{:S(2)}) collective-permute-start(bf16[1536,768]{1,0:T(8,128)(2,1)} %get-tuple-element.286), channel_id=1, source_target_pairs={{0,64},{32,224},{64,128},{96,32},{128,192},{160,96},{192,0},{224,1... | collective-permute-start | bytes 7077896 | tf_op jit(solution)/shard_map/ppermute | solution.py:471
  337.1 29.2 %collective-permute-start.19 = (bf16[1536,768]{1,0:T(8,128)(2,1)}, bf16[1536,768]{1,0:T(8,128)(2,1)}, u32[]{:S(2)}, u32[]{:S(2)}) collective-permute-start(bf16[1536,768]{1,0:T(8,128)(2,1)} %get-tuple-element.298), channel_id=1, source_target_pairs={{0,64},{32,224},{64,128},{96,32},{128,192},{160,96},{192,0},{224,1... | collective-permute-start | bytes 7077896 | tf_op jit(solution)/shard_map/ppermute | solution.py:471
  354.2 38.2 %collective-permute-start.20 = (bf16[1536,768]{1,0:T(8,128)(2,1)}, bf16[1536,768]{1,0:T(8,128)(2,1)}, u32[]{:S(2)}, u32[]{:S(2)}) collective-permute-start(bf16[1536,768]{1,0:T(8,128)(2,1)} %get-tuple-element.306.refs_4_), channel_id=1, source_target_pairs={{0,32},{32,0},{64,96},{96,64},{128,160},{160,128},{192,224},{224,1... | collective-permute-start | bytes 7077896 | tf_op jit(solution)/shard_map/ppermute | solution.py:466
  382.3 31.1 %collective-permute-start.21 = (bf16[1536,768]{1,0:T(8,128)(2,1)}, bf16[1536,768]{1,0:T(8,128)(2,1)}, u32[]{:S(2)}, u32[]{:S(2)}) collective-permute-start(bf16[1536,768]{1,0:T(8,128)(2,1)} %get-tuple-element.310), channel_id=1, source_target_pairs={{0,64},{32,224},{64,128},{96,32},{128,192},{160,96},{224,160},{1,6... | collective-permute-start | bytes 7077896 | tf_op jit(solution)/shard_map/ppermute | solution.py:471
  399.1 40.4 %collective-permute-start.22 = (bf16[1536,768]{1,0:T(8,128)(2,1)}, bf16[1536,768]{1,0:T(8,128)(2,1)}, u32[]{:S(2)}, u32[]{:S(2)}) collective-permute-start(bf16[1536,768]{1,0:T(8,128)(2,1)} %get-tuple-element.318.refs_4_), channel_id=1, source_target_pairs={{0,32},{32,0},{64,96},{96,64},{128,160},{160,128},{192,224},{224,1... | collective-permute-start | bytes 7077896 | tf_op jit(solution)/shard_map/ppermute | solution.py:466
  429.3 31.1 %collective-permute-start.23 = (bf16[1536,768]{1,0:T(8,128)(2,1)}, bf16[1536,768]{1,0:T(8,128)(2,1)}, u32[]{:S(2)}, u32[]{:S(2)}) collective-permute-start(bf16[1536,768]{1,0:T(8,128)(2,1)} %get-tuple-element.322), channel_id=1, source_target_pairs={{0,64},{32,224},{64,128},{128,192},{160,96},{192,0},{224,160},{1,6... | collective-permute-start | bytes 7077896 | tf_op jit(solution)/shard_map/ppermute | solution.py:471
  446.0 40.4 %collective-permute-start.24 = (bf16[1536,768]{1,0:T(8,128)(2,1)}, bf16[1536,768]{1,0:T(8,128)(2,1)}, u32[]{:S(2)}, u32[]{:S(2)}) collective-permute-start(bf16[1536,768]{1,0:T(8,128)(2,1)} %get-tuple-element.330.refs_4_), channel_id=1, source_target_pairs={{0,32},{32,0},{64,96},{96,64},{128,160},{160,128},{192,224},{224,1... | collective-permute-start | bytes 7077896 | tf_op jit(solution)/shard_map/ppermute | solution.py:466
  476.3 29.1 %collective-permute-start.25 = (bf16[1536,768]{1,0:T(8,128)(2,1)}, bf16[1536,768]{1,0:T(8,128)(2,1)}, u32[]{:S(2)}, u32[]{:S(2)}) collective-permute-start(bf16[1536,768]{1,0:T(8,128)(2,1)} %get-tuple-element.334), channel_id=1, source_target_pairs={{32,224},{64,128},{96,32},{128,192},{192,0},{224,160},{33,225},{65... | collective-permute-start | bytes 7077896 | tf_op jit(solution)/shard_map/ppermute | solution.py:471
  493.0 37.5 %collective-permute-start.26 = (bf16[1536,768]{1,0:T(8,128)(2,1)}, bf16[1536,768]{1,0:T(8,128)(2,1)}, u32[]{:S(2)}, u32[]{:S(2)}) collective-permute-start(bf16[1536,768]{1,0:T(8,128)(2,1)} %get-tuple-element.342.refs_4_), channel_id=1, source_target_pairs={{0,32},{32,0},{64,96},{96,64},{128,160},{160,128},{192,224},{224,1... | collective-permute-start | bytes 7077896 | tf_op jit(solution)/shard_map/ppermute | solution.py:466
  520.5 20.7 %collective-permute-start.27 = (bf16[1536,768]{1,0:T(8,128)(2,1)}, bf16[1536,768]{1,0:T(8,128)(2,1)}, u32[]{:S(2)}, u32[]{:S(2)}) collective-permute-start(bf16[1536,768]{1,0:T(8,128)(2,1)} %get-tuple-element.346), channel_id=1, source_target_pairs={{160,96},{192,0},{161,97},{193,1},{162,98},{194,2},{163,99},{195,3... | collective-permute-start | bytes 7077896 | tf_op jit(solution)/shard_map/ppermute | solution.py:471
  537.2 34.0 %collective-permute-start.28 = (bf16[1536,768]{1,0:T(8,128)(2,1)}, bf16[1536,768]{1,0:T(8,128)(2,1)}, u32[]{:S(2)}, u32[]{:S(2)}) collective-permute-start(bf16[1536,768]{1,0:T(8,128)(2,1)} %get-tuple-element.354.refs_4_), channel_id=1, source_target_pairs={{0,32},{32,0},{64,96},{96,64},{128,160},{160,128},{192,224},{224,1... | collective-permute-start | bytes 7077896 | tf_op jit(solution)/shard_map/ppermute | solution.py:466
  560.8 39.4 %collective-permute-start.29 = (bf16[1536,768]{1,0:T(8,128)(2,1)}, bf16[1536,768]{1,0:T(8,128)(2,1)}, u32[]{:S(2)}, u32[]{:S(2)}) collective-permute-start(bf16[1536,768]{1,0:T(8,128)(2,1)} %get-tuple-element.358), channel_id=1, source_target_pairs={{0,64},{96,32},{1,65},{97,33},{2,66},{98,34},{3,67},{99,35},{4,68}... | collective-permute-start | bytes 7077896 | tf_op jit(solution)/shard_map/ppermute | solution.py:471
  577.8 46.8 %collective-permute-start.30 = (bf16[1536,768]{1,0:T(8,128)(2,1)}, bf16[1536,768]{1,0:T(8,128)(2,1)}, u32[]{:S(2)}, u32[]{:S(2)}) collective-permute-start(bf16[1536,768]{1,0:T(8,128)(2,1)} %get-tuple-element.365.refs_4_), channel_id=1, source_target_pairs={{0,32},{32,0},{64,96},{96,64},{128,160},{160,128},{192,224},{224,1... | collective-permute-start | bytes 7077896 | tf_op jit(solution)/shard_map/ppermute | solution.py:466
  578.4 21.8 %all-to-all-start.22 = ((bf16[160,2,128]{2,1,0:T(2,128)(2,1)}), bf16[160,2,128]{2,1,0:T(2,128)(2,1)S(1)}, u32[]{:S(2)}, u32[]{:S(2)}) async-start(bf16[160,2,128]{2,1,0:T(2,128)(2,1)} %get-tuple-element.357), calls=%async_computation.22 | async-start | bytes 163840 | tf_op jit(solution)/shard_map/all_to_all | solution.py:238
  630.5 33.6 %collective-permute-start.31 = (bf16[1536,768]{1,0:T(8,128)(2,1)}, bf16[1536,768]{1,0:T(8,128)(2,1)}, u32[]{:S(2)}, u32[]{:S(2)}) collective-permute-start(bf16[1536,768]{1,0:T(8,128)(2,1)} %get-tuple-element.375.refs_4_), channel_id=1, source_target_pairs={{0,32},{32,0},{64,96},{96,64},{128,160},{160,128},{192,224},{224,1... | collective-permute-start | bytes 7077896 | tf_op jit(solution)/shard_map/ppermute | solution.py:466
  670.2 33.8 %collective-permute-start.32 = (bf16[1536,768]{1,0:T(8,128)(2,1)}, bf16[1536,768]{1,0:T(8,128)(2,1)}, u32[]{:S(2)}, u32[]{:S(2)}) collective-permute-start(bf16[1536,768]{1,0:T(8,128)(2,1)} %get-tuple-element.386.refs_4_), channel_id=1, source_target_pairs={{0,32},{32,0},{64,96},{96,64},{128,160},{160,128},{192,224},{224,1... | collective-permute-start | bytes 7077896 | tf_op jit(solution)/shard_map/ppermute | solution.py:466
  710.0 33.6 %collective-permute-start.33 = (bf16[1536,768]{1,0:T(8,128)(2,1)}, bf16[1536,768]{1,0:T(8,128)(2,1)}, u32[]{:S(2)}, u32[]{:S(2)}) collective-permute-start(bf16[1536,768]{1,0:T(8,128)(2,1)} %get-tuple-element.396.refs_4_), channel_id=1, source_target_pairs={{0,32},{32,0},{64,96},{96,64},{128,160},{160,128},{192,224},{224,1... | collective-permute-start | bytes 7077896 | tf_op jit(solution)/shard_map/ppermute | solution.py:466
  749.6 33.9 %collective-permute-start.34 = (bf16[1536,768]{1,0:T(8,128)(2,1)}, bf16[1536,768]{1,0:T(8,128)(2,1)}, u32[]{:S(2)}, u32[]{:S(2)}) collective-permute-start(bf16[1536,768]{1,0:T(8,128)(2,1)} %get-tuple-element.406.refs_4_), channel_id=1, source_target_pairs={{0,32},{32,0},{64,96},{96,64},{128,160},{160,128},{192,224},{224,1... | collective-permute-start | bytes 7077896 | tf_op jit(solution)/shard_map/ppermute | solution.py:466
  (41 other events, 333.3 us)
